TPU v7x, 32 devices: a whole 2x2x4 slice. The times are simulated.
32 devices in a mesh: section: 2 (over core), dp: 4 (over y, x), mp: 4 (over z).
Axes of the slice: x: 2, y: 2, z: 4, core: 2. Of those that a mesh axis runs over, the one named last changes fastest.
Arguments:
- tokens: bfloat16 [2, 1216, 4, 1024], P(None, 'mp', 'dp'), may hold values from -6 to 6
- cotangent: bfloat16 [2, 1216, 4, 1024], P(None, 'mp', 'dp'), may hold values from -6 to 6
- lengths: int32 [2, 4, 5], P(None, 'dp'), may hold values from 1 to 512, 1216 in all within a row
- qkv_weight: float32 [2, 3, 1024, 1024], P('section', None, 'dp', 'mp'), may hold values from -0.1875 to 0.1875
- qkv_bias: float32 [2, 3, 1024], P('section', None, 'mp'), may hold values from -3 to 3
- out_weight: float32 [2, 1024, 1024], P('section', 'mp', 'dp'), may hold values from -0.75 to 0.75
- out_bias: float32 [2, 1024], P('section'), may hold values from -3 to 3
- up_weight: float32 [2, 1024, 4096], P('section', 'dp', 'mp'), may hold values from -0.1875 to 0.1875
- up_bias: float32 [2, 4096], P('section', 'mp'), may hold values from -3 to 3
- down_weight: float32 [2, 4096, 1024], P('section', 'mp', 'dp'), may hold values from -0.09375 to 0.09375
- down_bias: float32 [2, 1024], P('section'), may hold values from -3 to 3
- norm_gain: float32 [2, 2, 1024], P('section'), may hold values from 0.1 to 1.9
- norm_shift: float32 [2, 2, 1024], P('section'), may hold values from -3 to 3
- prefix_keys: float32 [2, 64, 1024], P('section', None, 'mp'), may hold values from -6 to 6
- prefix_values: float32 [2, 64, 1024], P('section', None, 'mp'), may hold values from -6 to 6
Outputs:
- outputs: bfloat16 [2, 2, 1216, 4, 1024], P('section', None, 'mp', 'dp')
- input_grads: bfloat16 [2, 2, 1216, 4, 1024], P('section', None, 'mp', 'dp')
- key_grads: float32 [2, 64, 1024], P('section', None, 'mp')
- value_grads: float32 [2, 64, 1024], P('section', None, 'mp')
Inputs may be any that keep to these rules, and one draw needn't show every extreme that they name: The last entry of a row is its number of padding positions at the row's end; the others are its segments' lengths in order; entries of a row sum to 1216.
All inputs are finite; a program needn't handle non-finite values.
Results may differ from a plain program's by a relative error of at most 0.019.
Values may be sent and summed in bfloat16 or wider, within the bound.
No kernel may reach another device: no remote copies, remote signals or barrier semaphores. Data moves between devices by JAX's collectives and lax.ppermute only.
A program may use at most 384 MiB of HBM per device.

v0:
```python
from functools import partial

import jax
import jax.numpy as jnp
from jax import lax
from jax.sharding import PartitionSpec as P

HEADS = 16
HD = 64


def from_behind(value, axis, steps):
    count = lax.axis_size(axis)
    leading, last = (max(0, -steps), min(count, count - steps))
    return lax.ppermute(value, axis, [(source, source + steps) for source in range(leading, last)])


def layer_norm(stream_value, gain, shift):
    center = jnp.mean(stream_value, axis=-1, keepdims=True)
    centred = stream_value - center
    spread = jnp.mean(centred * centred, axis=-1, keepdims=True)
    return centred * lax.rsqrt(spread + 1e-05) * gain + shift


def segment_ids(lengths, length):
    ends = jnp.cumsum(lengths, axis=-1)
    places = jnp.arange(length, dtype=jnp.int32)
    return jnp.sum((places[:, None] >= ends[..., None, :]).astype(jnp.int32), axis=-1)


def regroup(moving):
    return lax.all_to_all(moving, "mp", split_axis=0, concat_axis=1, tiled=True)


def fetch_frozen(qkv_weight, qkv_bias, out_weight, up_weight, up_bias, down_weight):
    shards = (
        qkv_weight[0].astype(jnp.bfloat16)[None],
        out_weight[0].astype(jnp.bfloat16)[None],
        up_weight[0].astype(jnp.bfloat16)[None],
        down_weight[0].astype(jnp.bfloat16)[None],
    )
    blocks = (
        lax.all_gather(shards[0], ("dp", "mp"), axis=0, tiled=True),
        lax.all_gather(shards[1], ("dp", "mp"), axis=0, tiled=True),
        lax.all_gather(shards[2], ("dp", "mp"), axis=0, tiled=True),
        lax.all_gather(shards[3], ("dp", "mp"), axis=0, tiled=True),
    )
    dp_count = lax.axis_size("dp")
    mp_count = lax.axis_size("mp")
    qkv_rows, qkv_cols = (shards[0].shape[2], shards[0].shape[3])
    full_qkv = (
        blocks[0]
        .reshape(dp_count, mp_count, 3, qkv_rows, qkv_cols)
        .transpose(2, 0, 3, 1, 4)
        .reshape(3, dp_count * qkv_rows, mp_count * qkv_cols)
    )
    out_rows, out_cols = (shards[1].shape[1], shards[1].shape[2])
    full_out = (
        blocks[1]
        .reshape(dp_count, mp_count, out_rows, out_cols)
        .transpose(1, 2, 0, 3)
        .reshape(mp_count * out_rows, dp_count * out_cols)
    )
    up_rows, up_cols = (shards[2].shape[1], shards[2].shape[2])
    full_up = (
        blocks[2]
        .reshape(dp_count, mp_count, up_rows, up_cols)
        .transpose(0, 2, 1, 3)
        .reshape(dp_count * up_rows, mp_count * up_cols)
    )
    down_rows, down_cols = (shards[3].shape[1], shards[3].shape[2])
    full_down = (
        blocks[3]
        .reshape(dp_count, mp_count, down_rows, down_cols)
        .transpose(1, 2, 0, 3)
        .reshape(mp_count * down_rows, dp_count * down_cols)
    )
    biases = (
        lax.all_gather(qkv_bias[0], "mp", axis=1, tiled=True),
        lax.all_gather(up_bias[0], "mp", axis=0, tiled=True),
    )
    return (full_qkv, full_out, full_up, full_down, biases[0], biases[1])


def key_allowed(segment, first_row, row_total, prefix_len, padding_id):
    query_segment = segment[first_row : first_row + row_total]
    tokens_seen = (query_segment[:, None] == segment[None, :]) & (segment[None, :] != padding_id)
    return jnp.concatenate([jnp.ones((row_total, prefix_len), jnp.bool_), tokens_seen], axis=1)


def block_scores(queries, all_keys, segment, first_row, row_total, padding_id):
    prefix_len = all_keys.shape[1] - segment.shape[0]
    allowed = key_allowed(segment, first_row, row_total, prefix_len, padding_id)
    scores = jnp.einsum(
        "hqd,hkd->hqk",
        queries[:, first_row : first_row + row_total],
        all_keys,
        preferred_element_type=jnp.float32,
    ) * HD ** (-0.5)
    return jnp.where(allowed[None], scores, -1e30)


def attend(queries, all_keys, all_values, segment, padding_id):
    length = queries.shape[1]
    blocks = max(1, length // 512)
    step_rows = length // blocks
    pieces_out = []
    pieces_total = []
    for block_index in range(blocks):
        first_row = block_index * step_rows
        scores = block_scores(queries, all_keys, segment, first_row, step_rows, padding_id)
        row_peak = jnp.max(scores, axis=-1, keepdims=True)
        exponent = jnp.exp(scores - row_peak)
        summed = jnp.sum(exponent, axis=-1, keepdims=True)
        weights = (exponent / summed).astype(jnp.bfloat16)
        pieces_out.append(
            jnp.einsum("hqk,hkd->hqd", weights, all_values, preferred_element_type=jnp.float32)
        )
        pieces_total.append(row_peak[..., 0] + jnp.log(summed[..., 0]))
    return (jnp.concatenate(pieces_out, axis=1), jnp.concatenate(pieces_total, axis=1))


def attend_back(queries, all_keys, all_values, segment, padding_id, totals, grad_out):
    length = queries.shape[1]
    blocks = max(1, length // 512)
    step_rows = length // blocks
    grad_keys = jnp.zeros(all_keys.shape, jnp.float32)
    grad_values = jnp.zeros(all_values.shape, jnp.float32)
    grad_queries = []
    for block_index in range(blocks):
        first_row = block_index * step_rows
        scores = block_scores(queries, all_keys, segment, first_row, step_rows, padding_id)
        probs = jnp.exp(scores - totals[:, first_row : first_row + step_rows, None])
        weights = probs.astype(jnp.bfloat16)
        grad_block = grad_out[:, first_row : first_row + step_rows]
        grad_weights = jnp.einsum(
            "hqd,hkd->hqk", grad_block, all_values, preferred_element_type=jnp.float32
        )
        inner = jnp.sum(probs * grad_weights, axis=-1, keepdims=True)
        grad_scores = (probs * (grad_weights - inner)).astype(jnp.bfloat16)
        grad_queries.append(
            jnp.einsum("hqk,hkd->hqd", grad_scores, all_keys, preferred_element_type=jnp.float32)
            * HD ** (-0.5)
        )
        query_block = queries[:, first_row : first_row + step_rows]
        grad_keys = grad_keys + jnp.einsum(
            "hqk,hqd->hkd", grad_scores, query_block, preferred_element_type=jnp.float32
        ) * HD ** (-0.5)
        grad_values = grad_values + jnp.einsum(
            "hqk,hqd->hkd", weights, grad_block, preferred_element_type=jnp.float32
        )
    return (jnp.concatenate(grad_queries, axis=1), grad_keys, grad_values)


def section_forward(inputs, lengths, gathered, params):
    qkv_w, out_w, up_w, down_w, qkv_b, up_b = gathered
    out_b, down_b, gains, shifts, pre_keys, pre_values = params
    local_len, row_count, model_width = inputs.shape
    local_rows = local_len * row_count
    length = local_len * lax.axis_size("mp")
    flat_in = inputs.reshape(local_rows, model_width)
    projected = (
        jnp.einsum("nd,cdh->cnh", flat_in, qkv_w, preferred_element_type=jnp.float32)
        + qkv_b[:, None, :]
    )
    packed = (
        projected.astype(jnp.bfloat16)
        .reshape(3, local_rows, HEADS, HD)
        .transpose(2, 1, 0, 3)
        .reshape(HEADS, local_rows, 3 * HD)
    )
    spread_heads = regroup(packed)
    headed = spread_heads.reshape(-1, length, row_count, 3, HD).transpose(3, 2, 0, 1, 4)
    segments = segment_ids(lengths, length)
    padding_id = lengths.shape[-1] - 1
    prefix_key_heads = (
        pre_keys.astype(jnp.bfloat16).reshape(pre_keys.shape[0], -1, HD).transpose(1, 0, 2)
    )
    prefix_value_heads = (
        pre_values.astype(jnp.bfloat16).reshape(pre_values.shape[0], -1, HD).transpose(1, 0, 2)
    )
    all_keys = jnp.concatenate([prefix_key_heads, headed[1, 0]], axis=1)
    all_values = jnp.concatenate([prefix_value_heads, headed[2, 0]], axis=1)
    attended_row, totals_row = attend(headed[0, 0], all_keys, all_values, segments[0], padding_id)
    attended_rows = [attended_row]
    total_rows = [totals_row]
    attended_heads = jnp.stack(attended_rows)
    outgoing = (
        attended_heads.astype(jnp.bfloat16)
        .transpose(2, 0, 1, 3)
        .reshape(length * row_count, -1, HD)
    )
    attended = regroup(outgoing).reshape(local_rows, model_width)
    branch_attn = jnp.dot(attended, out_w, preferred_element_type=jnp.float32)
    residual = flat_in.astype(jnp.float32) + branch_attn + out_b
    normed = layer_norm(residual, gains[0], shifts[0])
    hidden = jnp.dot(normed.astype(jnp.bfloat16), up_w, preferred_element_type=jnp.float32) + up_b
    active = jax.nn.gelu(hidden, approximate=False).astype(jnp.bfloat16)
    branch_ffn = jnp.dot(active, down_w, preferred_element_type=jnp.float32)
    summed_stream = normed + branch_ffn + down_b
    result = layer_norm(summed_stream, gains[1], shifts[1])
    saved = (
        headed,
        segments,
        prefix_key_heads,
        prefix_value_heads,
        jnp.stack(total_rows),
        residual,
        hidden,
        summed_stream,
    )
    return (result, saved)


def section_backward(inputs, lengths, gathered, params, grad_result):
    qkv_w, out_w, up_w, down_w, qkv_b, up_b = gathered
    out_b, down_b, gains, shifts, pre_keys, pre_values = params
    local_len, row_count, model_width = inputs.shape
    local_rows = local_len * row_count
    result, saved = section_forward(inputs, lengths, gathered, params)
    (
        headed,
        segments,
        prefix_key_heads,
        prefix_value_heads,
        totals,
        residual,
        hidden,
        summed_stream,
    ) = saved
    length = headed.shape[3]
    padding_id = lengths.shape[-1] - 1
    contract = (((1,), (1,)), ((), ()))
    grad_flat = grad_result.reshape(local_rows, model_width).astype(jnp.float32)
    _, second_back = jax.vjp(
        lambda stream_value: layer_norm(stream_value, gains[1], shifts[1]), summed_stream
    )
    grad_stream = second_back(grad_flat)[0]
    _, gelu_back = jax.vjp(partial(jax.nn.gelu, approximate=False), hidden)
    grad_active = lax.dot_general(
        grad_stream.astype(jnp.bfloat16), down_w, contract, preferred_element_type=jnp.float32
    )
    grad_hidden = gelu_back(grad_active)[0].astype(jnp.bfloat16)
    grad_normed = grad_stream + lax.dot_general(
        grad_hidden, up_w, contract, preferred_element_type=jnp.float32
    )
    _, first_back = jax.vjp(
        lambda stream_value: layer_norm(stream_value, gains[0], shifts[0]), residual
    )
    grad_residual = first_back(grad_normed)[0]
    grad_local = lax.dot_general(
        grad_residual.astype(jnp.bfloat16), out_w, contract, preferred_element_type=jnp.float32
    ).astype(jnp.bfloat16)
    moving = grad_local.reshape(local_rows, HEADS, HD).transpose(1, 0, 2)
    grad_heads = regroup(moving).reshape(-1, length, row_count, HD).transpose(2, 0, 1, 3)
    prefix_len = prefix_key_heads.shape[1]
    all_keys = jnp.concatenate([prefix_key_heads, headed[1, 0]], axis=1)
    all_values = jnp.concatenate([prefix_value_heads, headed[2, 0]], axis=1)
    grad_q, grad_k, grad_v = attend_back(
        headed[0, 0], all_keys, all_values, segments[0], padding_id, totals[0], grad_heads[0]
    )
    key_heads = grad_k[:, :prefix_len]
    value_heads = grad_v[:, :prefix_len]
    token_grads = [jnp.stack([grad_q, grad_k[:, prefix_len:], grad_v[:, prefix_len:]])]
    grads_heads = jnp.stack(token_grads, axis=1)
    sending = (
        grads_heads.astype(jnp.bfloat16)
        .transpose(3, 1, 2, 0, 4)
        .reshape(length * row_count, -1, 3 * HD)
    )
    returned = (
        regroup(sending)
        .reshape(local_rows, HEADS, 3, HD)
        .transpose(2, 0, 1, 3)
        .reshape(3, local_rows, model_width)
    )
    grad_inputs = grad_residual + jnp.einsum(
        "cnh,cdh->nd", returned, qkv_w, preferred_element_type=jnp.float32
    )
    key_grad = key_heads.transpose(1, 0, 2).reshape(prefix_len, -1)
    value_grad = value_heads.transpose(1, 0, 2).reshape(prefix_len, -1)
    return (
        grad_inputs.reshape(local_len, row_count, model_width).astype(jnp.bfloat16),
        key_grad,
        value_grad,
    )


def on_device(
    tokens,
    cotangent,
    lengths,
    qkv_weight,
    qkv_bias,
    out_weight,
    out_bias,
    up_weight,
    up_bias,
    down_weight,
    down_bias,
    norm_gain,
    norm_shift,
    prefix_keys,
    prefix_values,
):
    micro = tokens.shape[0]
    section_position = lax.axis_index("section")
    is_first = section_position == 0
    params = (
        out_bias[0],
        down_bias[0],
        norm_gain[0],
        norm_shift[0],
        prefix_keys[0],
        prefix_values[0],
    )
    stored = jnp.zeros_like(tokens)
    results = jnp.zeros_like(tokens)
    received = jnp.zeros_like(tokens[0])
    for step_index in range(micro + 1):
        number = step_index - section_position
        is_valid = (number >= 0) & (number < micro)
        chosen = jnp.clip(number, 0, micro - 1)
        gathered = fetch_frozen(qkv_weight, qkv_bias, out_weight, up_weight, up_bias, down_weight)
        current = jnp.where(
            is_first, lax.dynamic_index_in_dim(tokens, chosen, 0, keepdims=False), received
        )
        row_lengths = lax.dynamic_index_in_dim(lengths, chosen, 0, keepdims=False)
        result, _ = section_forward(current, row_lengths, gathered, params)
        result = result.reshape(current.shape).astype(jnp.bfloat16)
        stored = jnp.where(
            is_valid, lax.dynamic_update_index_in_dim(stored, current, chosen, 0), stored
        )
        results = jnp.where(
            is_valid, lax.dynamic_update_index_in_dim(results, result, chosen, 0), results
        )
        if step_index < micro:
            received = from_behind(result, "section", 1)
    grads = jnp.zeros_like(tokens)
    key_total = jnp.zeros(prefix_keys.shape[1:], jnp.float32)
    value_total = jnp.zeros(prefix_values.shape[1:], jnp.float32)
    back_received = jnp.zeros_like(tokens[0])
    for step_index in range(micro + 1):
        number = step_index - 1 + section_position
        is_valid = (number >= 0) & (number < micro)
        chosen = jnp.clip(number, 0, micro - 1)
        gathered = fetch_frozen(qkv_weight, qkv_bias, out_weight, up_weight, up_bias, down_weight)
        incoming = jnp.where(
            is_first, back_received, lax.dynamic_index_in_dim(cotangent, chosen, 0, keepdims=False)
        )
        row_lengths = lax.dynamic_index_in_dim(lengths, chosen, 0, keepdims=False)
        kept_input = lax.dynamic_index_in_dim(stored, chosen, 0, keepdims=False)
        grad_in, key_grad, value_grad = section_backward(
            kept_input, row_lengths, gathered, params, incoming
        )
        grads = jnp.where(
            is_valid, lax.dynamic_update_index_in_dim(grads, grad_in, chosen, 0), grads
        )
        key_grad, value_grad = (
            lax.psum(key_grad.astype(jnp.bfloat16), "dp").astype(jnp.float32),
            lax.psum(value_grad.astype(jnp.bfloat16), "dp").astype(jnp.float32),
        )
        key_total = key_total + jnp.where(is_valid, key_grad, 0.0)
        value_total = value_total + jnp.where(is_valid, value_grad, 0.0)
        if step_index < micro:
            back_received = from_behind(grad_in, "section", -1)
    return (results[None], grads[None], key_total[None], value_total[None])


def solution(mesh):
    placed = (
        P(None, "mp", "dp", None),
        P(None, "mp", "dp", None),
        P(None, "dp", None),
        P("section", None, "dp", "mp"),
        P("section", None, "mp"),
        P("section", "mp", "dp"),
        P("section", None),
        P("section", "dp", "mp"),
        P("section", "mp"),
        P("section", "mp", "dp"),
        P("section", None),
        P("section", None, None),
        P("section", None, None),
        P("section", None, "mp"),
        P("section", None, "mp"),
    )
    return jax.shard_map(
        on_device,
        mesh=mesh,
        in_specs=placed,
        out_specs=(
            P("section", None, "mp", "dp", None),
            P("section", None, "mp", "dp", None),
            P("section", None, "mp"),
            P("section", None, "mp"),
        ),
        check_vma=False,
    )
```

profile of v0, /device:TPU:0, one launch (start us, length us, event | category | flops | bytes accessed | tf_op | source)
XLA Modules:
  0.0 1592.5 jit_solution(13368072769616305476)
XLA Ops:
  15.3 12.7 all-gather
  28.1 80.4 %all-gather.7.cloned.1.call-done = bf16[16,3,256,256]{3,2,1,0:T(8,128)(2,1)} async-done(((bf16[1,3,256,256]{3,2,1,0:T(8,128)(2,1)}), bf16[16,3,256,256]{3,2,1,0:T(8,128)(2,1)}) %all-gather.7.cloned.1.call-update) | async-done | bytes 6291472 | tf_op jit(solution)/shard_map/all_gather | solution.py:43
  108.4 10.3 copy.351
  118.8 11.1 reshape.1313
  129.9 6.2 fusion.171
  150.9 58.6 %all-to-all-done = bf16[16,304,192]{1,2,0:T(8,128)(2,1)S(1)} async-done(((bf16[16,304,192]{1,2,0:T(8,128)(2,1)}), bf16[16,304,192]{1,2,0:T(8,128)(2,1)S(1)}, u32[]{:S(2)}, u32[]{:S(2)}) %all-to-all-start) | async-done | bytes 1867808 | tf_op jit(solution)/shard_map/all_to_all | solution.py:32
  223.4 7.6 fusion.249
  231.0 6.0 fusion.622
  237.0 6.2 fusion.248
  250.9 29.6 %all-gather.1 = f32[1,4096]{1,0:T(1,128)S(1)} all-gather(f32[1,1024]{1,0:T(1,128)S(1)} %copy-done.144), channel_id=3, replica_groups=mesh['section'=2,'dp'=4,'mp'=4] {'mp'}, dimensions={1}, use_global_device_ids=true | all-gather | bytes 20480 | tf_op jit(solution)/shard_map/all_gather | solution.py:80
  293.9 34.4 %all-gather.13.cloned.1.call-done = bf16[16,1024,256]{2,1,0:T(8,128)(2,1)} async-done(((bf16[1,1024,256]{2,1,0:T(8,128)(2,1)}), bf16[16,1024,256]{2,1,0:T(8,128)(2,1)}) %all-gather.13.cloned.1.call-update) | async-done | bytes 8388624 | tf_op jit(solution)/shard_map/all_gather | solution.py:46
  328.3 12.2 copy.256
  340.5 9.4 copy.333
  349.8 92.1 %all-gather.11.cloned.1.call-done = bf16[16,256,1024]{2,1,0:T(8,128)(2,1)} async-done(((bf16[1,256,1024]{2,1,0:T(8,128)(2,1)}), bf16[16,256,1024]{2,1,0:T(8,128)(2,1)}) %all-gather.11.cloned.1.call-update) | async-done | bytes 8388624 | tf_op jit(solution)/shard_map/all_gather | solution.py:45
  442.0 12.3 copy.255
  454.3 12.1 copy.332
  466.4 21.7 %fusion.626 = (f32[304]{0:T(512)S(1)}, f32[304,1024]{1,0:T(8,128)S(1)}) fusion(f32[1024]{0:T(1024)S(1)} %bitcast.821, bf16[4096,1024]{1,0:T(8,128)(2,1)} %bitcast.642, f32[4096]{0:T(1024)S(1)} %bitcast.779, bf16[1024,4096]{1,0:T(8,128)(2,1)} %bitcast.657, f32[304,1024]{1,0:T(8,128)} %copy-done.33, f32[1024]{0:T(1024)S(1)} %bitcast.791, ...), kind=kOutput, calls=%fused_computation.861 | convolution fusion | flops 5186190848 | bytes 19299904 | tf_op jit(solution)/shard_map/dot_general | solution.py:199
  495.4 6.2 fusion.172
  524.1 44.4 %all-to-all-done.2 = bf16[16,304,192]{1,2,0:T(8,128)(2,1)} async-done(((bf16[16,304,192]{1,2,0:T(8,128)(2,1)}), bf16[16,304,192]{1,2,0:T(8,128)(2,1)}, u32[]{:S(2)}, u32[]{:S(2)}) %all-to-all-start.2) | async-done | bytes 1867808 | tf_op jit(solution)/shard_map/all_to_all | solution.py:32
  581.3 6.7 fusion.629
  588.0 6.4 fusion.632
  594.4 9.1 fusion.251
  603.5 7.5 fusion.250
  628.7 11.1 all-to-all-done.3
  649.3 22.1 %fusion.635 = (f32[304]{0:T(512)S(1)}, f32[304,1024]{1,0:T(8,128)S(1)}) fusion(f32[1024]{0:T(1024)} %bitcast.819, bf16[4096,1024]{1,0:T(8,128)(2,1)} %bitcast.643, f32[4096]{0:T(1024)S(1)} %bitcast.780, bf16[1024,4096]{1,0:T(8,128)(2,1)} %bitcast.658, f32[304]{0:T(512)S(1)} %add_rsqrt_fusion.3, f32[304]{0:T(512)S(1)} %broadcast_multiply_fusion.9, ...), kind=kOutput, calls=%fused_computation.864 | convolution fusion | flops 5188058624 | bytes 19926592 | tf_op jit(solution)/shard_map/dot_general | solution.py:199
  681.2 6.8 fusion.174
  709.6 6.1 fusion.173
  733.8 6.2 fusion.176
  744.5 8.6 all-to-all-done.6
  795.7 15.6 all-to-all-done.10
  850.4 18.9 %all-to-all-done.14 = bf16[16,304,192]{1,2,0:T(8,128)(2,1)} async-done(((bf16[16,304,192]{1,2,0:T(8,128)(2,1)}), bf16[16,304,192]{1,2,0:T(8,128)(2,1)}, u32[]{:S(2)}, u32[]{:S(2)}) %all-to-all-start.14) | async-done | bytes 1867808 | tf_op jit(solution)/shard_map/all_to_all | solution.py:32
  919.5 5.9 convolution_add_fusion.2
  925.5 12.8 fusion.650
  939.4 27.0 %multiply_reduce_fusion.12 = (f32[304]{0:T(512)S(1)}, f32[304,1024]{1,0:T(8,128)}) fusion(f32[304,1024]{1,0:T(8,128)} %copy-done.19, f32[304]{0:T(512)S(1)} %broadcast_multiply_fusion.5, f32[1024]{0:T(1024)S(1)} %bitcast.804, bf16[1024,4096]{1,0:T(8,128)(2,1)} %bitcast.660, f32[304,4096]{1,0:T(8,128)} %copy-done.159, bf16[4096,1024]{1,0:T(8,128)(2,1)} %bitcast.644, ...), kind=kOutput, calls=%fused_computation.390 | convolution fusion | flops 5197397504 | bytes 28017856 | tf_op jit(solution)/shard_map/dot_general | solution.py:244
  978.4 6.6 fusion.258
  1019.2 9.2 multiply_reduce_fusion.4
  1028.4 6.2 multiply_reduce_fusion.5
  1034.6 6.3 multiply_convert_fusion.5
  1049.5 6.3 multiply_convert_fusion.4
  1075.6 6.8 fusion.638
  1091.5 8.0 convolution_add_fusion.1
  1099.5 26.2 %all-to-all-done.9 = bf16[1216,4,192]{2,1,0:T(4,128)(2,1)} async-done(((bf16[1216,4,192]{2,1,0:T(4,128)(2,1)}), bf16[1216,4,192]{2,1,0:T(4,128)(2,1)}, u32[]{:S(2)}, u32[]{:S(2)}) %all-to-all-start.9) | async-done | bytes 1867808 | tf_op jit(solution)/shard_map/all_to_all | solution.py:32
  1133.6 6.0 bitcast_dynamic-update-slice_fusion
  1141.7 12.9 fusion.654
  1156.7 25.3 %multiply_reduce_fusion.9 = (f32[304]{0:T(512)S(1)}, f32[304,1024]{1,0:T(8,128)}) fusion(f32[304,1024]{1,0:T(8,128)S(1)} %copy-done.18, f32[304]{0:T(512)S(1)} %broadcast_multiply_fusion.3, f32[1024]{0:T(1024)S(1)} %bitcast.807, bf16[1024,4096]{1,0:T(8,128)(2,1)} %bitcast.662, f32[304,4096]{1,0:T(8,128)} %convolution_add_fusion.1, ...), kind=kOutput, calls=%fused_computation.386 | convolution fusion | flops 5192416768 | bytes 25501248 | tf_op jit(solution)/shard_map/dot_general | solution.py:244
  1197.0 6.2 fusion.641
  1203.1 10.4 all-to-all-done.12
  1219.4 8.0 fusion.28
  1227.4 9.0 multiply_reduce_fusion.2
  1256.3 6.2 multiply_convert_fusion.2
  1275.9 8.3 fusion.253
  1284.2 7.1 fusion.252
  1309.2 8.1 convolution_add_fusion
  1317.3 15.3 all-to-all-done.13
  1344.6 7.5 fusion.286
  1353.5 16.3 %fusion.658 = (f32[304]{0:T(512)S(1)}, f32[304,1024]{1,0:T(8,128)}) fusion(f32[1024]{0:T(1024)S(1)} %bitcast.824, bf16[4096,1024]{1,0:T(8,128)(2,1)S(1)} %bitcast.656, f32[304,4096]{1,0:T(8,128)} %convolution_add_fusion, f32[1024]{0:T(1024)S(1)} %bitcast.798, f32[1024]{0:T(1024)S(1)} %bitcast.809, f32[304]{0:T(512)S(1)} %fusion.444, ...), kind=kOutput, calls=%fused_computation.879 | convolution fusion | flops 2633252608 | bytes 15875648 | tf_op jit(solution)/shard_map/dot_general | solution.py:199
  1381.1 25.3 %multiply_reduce_fusion.6 = (f32[304]{0:T(512)S(1)}, f32[304,1024]{1,0:T(8,128)}) fusion(f32[304,1024]{1,0:T(8,128)S(1)} %copy-done.16, f32[304]{0:T(512)S(1)} %broadcast_multiply_fusion.1, f32[1024]{0:T(1024)S(1)} %bitcast.810, bf16[1024,4096]{1,0:T(8,128)(2,1)} %bitcast.664, f32[304,4096]{1,0:T(8,128)} %convolution_add_fusion, ...), kind=kOutput, calls=%fused_computation.382 | convolution fusion | flops 5192416768 | bytes 25501248 | tf_op jit(solution)/shard_map/dot_general | solution.py:244
  1422.1 17.8 %all-to-all-done.16 = bf16[16,304,64]{1,2,0:T(8,128)(2,1)} async-done(((bf16[16,304,64]{1,2,0:T(8,128)(2,1)}), bf16[16,304,64]{1,2,0:T(8,128)(2,1)}, u32[]{:S(2)}, u32[]{:S(2)}) %all-to-all-start.16) | async-done | bytes 622624 | tf_op jit(solution)/shard_map/all_to_all | solution.py:32
  1442.2 8.0 fusion.24
  1450.2 9.2 multiply_reduce_fusion
  1479.5 6.2 multiply_convert_fusion
  1498.6 22.5 %fusion.644 = (f32[304]{0:T(512)}, f32[304,1024]{1,0:T(8,128)S(1)}) fusion(f32[1024]{0:T(1024)} %bitcast.820, bf16[4096,1024]{1,0:T(8,128)(2,1)} %bitcast.647, f32[4096]{0:T(1024)S(1)} %bitcast.784, bf16[1024,4096]{1,0:T(8,128)(2,1)} %bitcast.665, f32[304]{0:T(512)S(1)} %add_rsqrt_fusion.1, f32[304]{0:T(512)S(1)} %broadcast_multiply_fusion.7, ...), kind=kOutput, calls=%fused_computation.867 | convolution fusion | flops 5188058624 | bytes 19926592 | tf_op jit(solution)/shard_map/dot_general | solution.py:199
  1530.0 41.2 %all-reduce.15.cloned.1.call-done = (bf16[64,256]{1,0:T(8,128)(2,1)}, bf16[64,256]{1,0:T(8,128)(2,1)}, bf16[64,256]{1,0:T(8,128)(2,1)}, bf16[64,256]{1,0:T(8,128...) async-done(((bf16[64,256]{1,0:T(8,128)(2,1)}, bf16[64,256]{1,0:T(8,128)(2,1)}, bf16[64,256]{1,0:T(8,128)(2,1)}, bf16[64,256]{1,0:T(8,128)(2,1)}, ...) | async-done | bytes 196624 | tf_op jit(solution)/shard_map/psum | solution.py:360
  1578.7 7.0 fusion.247
  (727 shorter events, 571.6 us)
Async XLA Ops:
  7.2 101.3 %all-gather.7.cloned.1.call-start = ((), (), s32[]{:S(2)}) async-start(), calls=%async_computation.18 | async-start | bytes 6684672 | tf_op jit(solution)/shard_map/all_gather | solution.py:43
  9.2 271.4 %all-gather.9.cloned.1.call-start = ((), (), s32[]{:S(2)}) async-start(), calls=%async_computation.19 | async-start | bytes 2228224 | tf_op jit(solution)/shard_map/all_gather | solution.py:44
  10.9 317.4 %all-gather.13.cloned.1.call-start = ((), (), s32[]{:S(2)}) async-start(), calls=%async_computation.21 | async-start | bytes 8912896 | tf_op jit(solution)/shard_map/all_gather | solution.py:46
  13.1 428.9 %all-gather.11.cloned.1.call-start = ((), (), s32[]{:S(2)}) async-start(), calls=%async_computation.20 | async-start | bytes 8912896 | tf_op jit(solution)/shard_map/all_gather | solution.py:45
  28.1 101.8 %copy-start.139 = (f32[1,3,1024]{2,1,0:T(4,128)}, f32[1,3,1024]{2,1,0:T(4,128)S(1)}, u32[]{:S(2)}) copy-start(f32[1,3,1024]{2,1,0:T(4,128)S(1)} %copy.367) | copy-start | bytes 36868
  140.7 68.8 %all-to-all-start = ((bf16[16,304,192]{1,2,0:T(8,128)(2,1)}), bf16[16,304,192]{1,2,0:T(8,128)(2,1)S(1)}, u32[]{:S(2)}, u32[]{:S(2)}) async-start(bf16[16,304,192]{1,2,0:T(8,128)(2,1)} %bitcast.624), calls=%async_computation | async-start | bytes 4718592 | tf_op jit(solution)/shard_map/all_to_all | solution.py:32
  145.9 929.7 %copy-start.110 = (bf16[1,64,256]{1,2,0:T(8,128)(2,1)}, bf16[1,64,256]{1,2,0:T(8,128)(2,1)S(1)}, u32[]{:S(2)}) copy-start(bf16[1,64,256]{1,2,0:T(8,128)(2,1)S(1)} %copy.250) | copy-start | bytes 98308
  146.0 882.4 %copy-start.52 = (bf16[1,64,256]{1,2,0:T(8,128)(2,1)}, bf16[1,64,256]{1,2,0:T(8,128)(2,1)S(1)}, u32[]{:S(2)}) copy-start(bf16[1,64,256]{1,2,0:T(8,128)(2,1)S(1)} %copy.251) | copy-start | bytes 98308
  243.2 37.2 %copy-start.142 = (f32[1,2,1024]{2,1,0:T(2,128)S(1)}, f32[1,2,1024]{2,1,0:T(2,128)}, u32[]{:S(2)}) copy-start(f32[1,2,1024]{2,1,0:T(2,128)} %param.27) | copy-start | bytes 24580
  243.2 37.2 %copy-start.143 = (f32[1,2,1024]{2,1,0:T(2,128)S(1)}, f32[1,2,1024]{2,1,0:T(2,128)}, u32[]{:S(2)}) copy-start(f32[1,2,1024]{2,1,0:T(2,128)} %param.26) | copy-start | bytes 24580
  246.7 37.6 %all-to-all-start.1 = ((bf16[4,2,38912]{2,1,0:T(2,128)(2,1)}), bf16[4,2,38912]{2,1,0:T(2,128)(2,1)}, u32[]{:S(2)}, u32[]{:S(2)}) async-start(bf16[4,2,38912]{2,1,0:T(2,128)(2,1)} %reshape.1393), calls=%async_computation.1 | async-start | bytes 1245184 | tf_op jit(solution)/shard_map/all_to_all | solution.py:32
  280.5 368.8 %copy-start.134 = (f32[1,4096]{1,0:T(1,128)}, f32[1,4096]{1,0:T(1,128)S(1)}, u32[]{:S(2)}) copy-start(f32[1,4096]{1,0:T(1,128)S(1)} %all-gather.1) | copy-start | bytes 49156
  280.5 368.8 %copy-start.145 = (f32[1,1,1024]{2,1,0:T(1,128)}, f32[1,1,1024]{2,1,0:T(1,128)S(1)}, u32[]{:S(2)}) copy-start(f32[1,1,1024]{2,1,0:T(1,128)S(1)} %get-tuple-element.94) | copy-start | bytes 12292
  280.5 425.2 %copy-start.106 = (f32[1,1,1024]{2,1,0:T(1,128)}, f32[1,1,1024]{2,1,0:T(1,128)S(1)}, u32[]{:S(2)}) copy-start(f32[1,1,1024]{2,1,0:T(1,128)S(1)} %get-tuple-element.95) | copy-start | bytes 12292
  280.5 368.8 %copy-start.148 = (f32[1,1,1024]{2,1,0:T(1,128)}, f32[1,1,1024]{2,1,0:T(1,128)S(1)}, u32[]{:S(2)}) copy-start(f32[1,1,1024]{2,1,0:T(1,128)S(1)} %get-tuple-element.92) | copy-start | bytes 12292
  280.5 425.2 %copy-start.96 = (f32[1,1,1024]{2,1,0:T(1,128)}, f32[1,1,1024]{2,1,0:T(1,128)S(1)}, u32[]{:S(2)}) copy-start(f32[1,1,1024]{2,1,0:T(1,128)S(1)} %get-tuple-element.93) | copy-start | bytes 12292
  284.3 361.6 %copy-start.6 = (bf16[128,8,4,256]{3,1,2,0:T(8,128)(2,1)}, bf16[128,8,4,256]{3,1,2,0:T(8,128)(2,1)S(1)}, u32[]{:S(2)}) copy-start(bf16[128,8,4,256]{3,1,2,0:T(8,128)(2,1)S(1)} %copy.331) | copy-start | bytes 6291460
  489.5 3.5 collective-permute-start
  508.9 59.5 %all-to-all-start.2 = ((bf16[16,304,192]{1,2,0:T(8,128)(2,1)}), bf16[16,304,192]{1,2,0:T(8,128)(2,1)}, u32[]{:S(2)}, u32[]{:S(2)}) async-start(bf16[16,304,192]{1,2,0:T(8,128)(2,1)} %bitcast.625), calls=%async_computation.2 | async-start | bytes 4718592 | tf_op jit(solution)/shard_map/all_to_all | solution.py:32
  613.1 14.9 copy-start.155
  613.1 15.1 copy-start.154
  619.0 20.8 %all-to-all-start.3 = ((bf16[4,2,38912]{2,1,0:T(2,128)(2,1)}), bf16[4,2,38912]{2,1,0:T(2,128)(2,1)}, u32[]{:S(2)}, u32[]{:S(2)}) async-start(bf16[4,2,38912]{2,1,0:T(2,128)(2,1)} %reshape.1395), calls=%async_computation.3 | async-start | bytes 1245184 | tf_op jit(solution)/shard_map/all_to_all | solution.py:32
  672.8 6.9 collective-permute-start.1
  681.2 28.4 %copy-start.28 = (bf16[304,1,1024]{2,0,1:T(8,128)(2,1)}, bf16[304,1,1024]{2,0,1:T(8,128)(2,1)S(1)}, u32[]{:S(2)}) copy-start(bf16[304,1,1024]{2,0,1:T(8,128)(2,1)S(1)} %get-tuple-element.59) | copy-start | bytes 1867780
  681.2 52.6 %copy-start.11 = (bf16[2,304,1,1024]{3,1,2,0:T(8,128)(2,1)}, bf16[2,304,1,1024]{3,1,2,0:T(8,128)(2,1)S(1)}, u32[]{:S(2)}) copy-start(bf16[2,304,1,1024]{3,1,2,0:T(8,128)(2,1)S(1)} %get-tuple-element.58) | copy-start | bytes 3735556
  695.4 57.8 %all-to-all-start.6 = ((bf16[16,304,192]{1,2,0:T(8,128)(2,1)}), bf16[16,304,192]{1,2,0:T(8,128)(2,1)}, u32[]{:S(2)}, u32[]{:S(2)}) async-start(bf16[16,304,192]{1,2,0:T(8,128)(2,1)} %bitcast.626), calls=%async_computation.6 | async-start | bytes 4718592 | tf_op jit(solution)/shard_map/all_to_all | solution.py:32
  753.2 58.1 %all-to-all-start.10 = ((bf16[16,304,192]{1,2,0:T(8,128)(2,1)}), bf16[16,304,192]{1,2,0:T(8,128)(2,1)}, u32[]{:S(2)}, u32[]{:S(2)}) async-start(bf16[16,304,192]{1,2,0:T(8,128)(2,1)} %bitcast.146), calls=%async_computation.10 | async-start | bytes 4718592 | tf_op jit(solution)/shard_map/all_to_all | solution.py:32
  811.2 58.1 %all-to-all-start.14 = ((bf16[16,304,192]{1,2,0:T(8,128)(2,1)}), bf16[16,304,192]{1,2,0:T(8,128)(2,1)}, u32[]{:S(2)}, u32[]{:S(2)}) async-start(bf16[16,304,192]{1,2,0:T(8,128)(2,1)} %bitcast.188), calls=%async_computation.14 | async-start | bytes 4718592 | tf_op jit(solution)/shard_map/all_to_all | solution.py:32
  869.4 36.2 %all-to-all-start.7 = ((bf16[4,2,38912]{2,1,0:T(2,128)(2,1)}), bf16[4,2,38912]{2,1,0:T(2,128)(2,1)}, u32[]{:S(2)}, u32[]{:S(2)}) async-start(bf16[4,2,38912]{2,1,0:T(2,128)(2,1)} %reshape.1399), calls=%async_computation.7 | async-start | bytes 1245184 | tf_op jit(solution)/shard_map/all_to_all | solution.py:32
  899.1 79.3 %copy-start.117 = (f32[4,608]{1,0:T(4,128)}, f32[4,608]{1,0:T(4,128)S(1)}, u32[]{:S(2)}) copy-start(f32[4,608]{1,0:T(4,128)S(1)} %get-tuple-element.154) | copy-start | bytes 29188
  905.5 72.9 %copy-start.119 = (f32[4,608]{1,0:T(4,128)}, f32[4,608]{1,0:T(4,128)S(1)}, u32[]{:S(2)}) copy-start(f32[4,608]{1,0:T(4,128)S(1)} %fusion.10) | copy-start | bytes 29188
  905.6 67.7 %all-to-all-start.4 = ((bf16[16,304,192]{1,2,0:T(8,128)(2,1)}), bf16[16,304,192]{1,2,0:T(8,128)(2,1)}, u32[]{:S(2)}, u32[]{:S(2)}) async-start(bf16[16,304,192]{1,2,0:T(8,128)(2,1)} %bitcast.622), calls=%async_computation.4 | async-start | bytes 4718592 | tf_op jit(solution)/shard_map/all_to_all | solution.py:32
  939.4 27.0 %copy-start.20 = (f32[304,1024]{1,0:T(8,128)S(1)}, f32[304,1024]{1,0:T(8,128)}, u32[]{:S(2)}) copy-start(f32[304,1024]{1,0:T(8,128)} %copy-done.19) | copy-start | bytes 3735556
  973.3 29.9 %all-to-all-start.8 = ((bf16[16,304,64]{1,2,0:T(8,128)(2,1)}), bf16[16,304,64]{1,2,0:T(8,128)(2,1)}, u32[]{:S(2)}, u32[]{:S(2)}) async-start(bf16[16,304,64]{1,2,0:T(8,128)(2,1)} %bitcast.705), calls=%async_computation.8 | async-start | bytes 1572864 | tf_op jit(solution)/shard_map/all_to_all | solution.py:32
  1003.2 63.1 %all-to-all-start.11 = ((bf16[4,2,38912]{2,1,0:T(2,128)(2,1)}), bf16[4,2,38912]{2,1,0:T(2,128)(2,1)}, u32[]{:S(2)}, u32[]{:S(2)}) async-start(bf16[4,2,38912]{2,1,0:T(2,128)(2,1)} %reshape.1401), calls=%async_computation.11 | async-start | bytes 1245184 | tf_op jit(solution)/shard_map/all_to_all | solution.py:32
  1013.2 15.2 slice-start.15
  1013.2 15.2 slice-start.16
  1066.3 59.4 %all-to-all-start.9 = ((bf16[1216,4,192]{2,1,0:T(4,128)(2,1)}), bf16[1216,4,192]{2,1,0:T(4,128)(2,1)}, u32[]{:S(2)}, u32[]{:S(2)}) async-start(bf16[1216,4,192]{2,1,0:T(4,128)(2,1)} %copy.279), calls=%async_computation.9 | async-start | bytes 4980736 | tf_op jit(solution)/shard_map/all_to_all | solution.py:32
  1139.6 14.9 copy-start.50
  1139.6 15.0 copy-start.22
  1139.6 14.9 collective-permute-start.2
  1188.8 24.8 %all-to-all-start.12 = ((bf16[16,304,64]{1,2,0:T(8,128)(2,1)}), bf16[16,304,64]{1,2,0:T(8,128)(2,1)S(1)}, u32[]{:S(2)}, u32[]{:S(2)}) async-start(bf16[16,304,64]{1,2,0:T(8,128)(2,1)} %bitcast.161), calls=%async_computation.12 | async-start | bytes 1572864 | tf_op jit(solution)/shard_map/all_to_all | solution.py:32
  1213.6 57.0 %all-to-all-start.15 = ((bf16[4,2,38912]{2,1,0:T(2,128)(2,1)}), bf16[4,2,38912]{2,1,0:T(2,128)(2,1)}, u32[]{:S(2)}, u32[]{:S(2)}) async-start(bf16[4,2,38912]{2,1,0:T(2,128)(2,1)} %reshape.1403), calls=%async_computation.15 | async-start | bytes 1245184 | tf_op jit(solution)/shard_map/all_to_all | solution.py:32
  1219.3 17.0 %slice-start.9 = ((s8[12451840]{0:T(1024)(128)(4,1)}), s8[4194304]{0:T(1024)(128)(4,1)S(1)}, s32[]{:S(2)}) async-start(s8[12451840]{0:T(1024)(128)(4,1)} %bitcast.603), calls=%async_computation.32 | async-start | bytes 8388608
  1219.4 17.0 %slice-start.10 = ((s8[12451840]{0:T(1024)(128)(4,1)}), s8[4194304]{0:T(1024)(128)(4,1)S(1)}, s32[]{:S(2)}) async-start(s8[12451840]{0:T(1024)(128)(4,1)} %bitcast.603), calls=%async_computation.33 | async-start | bytes 8388608
  1270.6 62.0 %all-to-all-start.13 = ((bf16[1216,4,192]{2,1,0:T(4,128)(2,1)}), bf16[1216,4,192]{2,1,0:T(4,128)(2,1)}, u32[]{:S(2)}, u32[]{:S(2)}) async-start(bf16[1216,4,192]{2,1,0:T(4,128)(2,1)} %copy.293), calls=%async_computation.13 | async-start | bytes 4980736 | tf_op jit(solution)/shard_map/all_to_all | solution.py:32
  1291.4 14.7 copy-start.8
  1291.4 14.7 copy-start.14
  1332.6 37.2 %all-to-all-start.5 = ((bf16[4,2,38912]{2,1,0:T(2,128)(2,1)}), bf16[4,2,38912]{2,1,0:T(2,128)(2,1)}, u32[]{:S(2)}, u32[]{:S(2)}) async-start(bf16[4,2,38912]{2,1,0:T(2,128)(2,1)} %reshape.1397), calls=%async_computation.5 | async-start | bytes 1245184 | tf_op jit(solution)/shard_map/all_to_all | solution.py:32
  1352.0 23.7 %copy-start.98 = (f32[1,1,1024]{2,1,0:T(1,128)S(1)}, f32[1,1,1024]{2,1,0:T(1,128)}, u32[]{:S(2)}) copy-start(f32[1,1,1024]{2,1,0:T(1,128)} %copy-done.96) | copy-start | bytes 12292
  1352.0 23.7 %collective-permute-start.3 = (bf16[304,1,1024]{2,0,1:T(8,128)(2,1)}, bf16[304,1,1024]{2,0,1:T(8,128)(2,1)}, u32[]{:S(2)}, u32[]{:S(2)}) collective-permute-start(bf16[304,1,1024]{2,0,1:T(8,128)(2,1)} %bitcast.178), channel_id=1, source_target_pairs={{16,0},{17,1},{18,2},{19,3},{20,4},{21,5},{22,6},{23,7},{24,8},{25... | collective-permute-start | bytes 1867784 | tf_op jit(solution)/shard_map/ppermute | solution.py:15
  1413.1 26.7 %all-to-all-start.16 = ((bf16[16,304,64]{1,2,0:T(8,128)(2,1)}), bf16[16,304,64]{1,2,0:T(8,128)(2,1)}, u32[]{:S(2)}, u32[]{:S(2)}) async-start(bf16[16,304,64]{1,2,0:T(8,128)(2,1)} %bitcast.706), calls=%async_computation.16 | async-start | bytes 1572864 | tf_op jit(solution)/shard_map/all_to_all | solution.py:32
  1442.2 17.2 %slice-start.3 = ((s8[12451840]{0:T(1024)(128)(4,1)}), s8[4194304]{0:T(1024)(128)(4,1)S(1)}, s32[]{:S(2)}) async-start(s8[12451840]{0:T(1024)(128)(4,1)} %bitcast.599), calls=%async_computation.26 | async-start | bytes 8388608
  1442.2 17.2 %slice-start.4 = ((s8[12451840]{0:T(1024)(128)(4,1)}), s8[4194304]{0:T(1024)(128)(4,1)S(1)}, s32[]{:S(2)}) async-start(s8[12451840]{0:T(1024)(128)(4,1)} %bitcast.599), calls=%async_computation.27 | async-start | bytes 8388608
  1493.7 80.3 %all-to-all-start.17 = ((bf16[1216,4,192]{2,1,0:T(4,128)(2,1)}), bf16[1216,4,192]{2,1,0:T(4,128)(2,1)}, u32[]{:S(2)}, u32[]{:S(2)}) async-start(bf16[1216,4,192]{2,1,0:T(4,128)(2,1)} %copy.307), calls=%async_computation.17 | async-start | bytes 4980736 | tf_op jit(solution)/shard_map/all_to_all | solution.py:32
  1498.3 23.8 %slice-start.25 = ((bf16[4,1280,64]{1,2,0:T(8,128)(2,1)}), bf16[4,64,64]{1,2,0:T(8,128)(2,1)S(1)}, s32[]{:S(2)}) async-start(bf16[4,1280,64]{1,2,0:T(8,128)(2,1)} %copy-done.55), calls=%async_computation.48 | async-start | bytes 131072 | tf_op jit(solution)/shard_map/slice | solution.py:262
  1498.3 24.5 %slice-start.24 = ((bf16[4,1280,64]{1,2,0:T(8,128)(2,1)}), bf16[4,64,64]{1,2,0:T(8,128)(2,1)S(1)}, s32[]{:S(2)}) async-start(bf16[4,1280,64]{1,2,0:T(8,128)(2,1)} %copy-done.54), calls=%async_computation.47 | async-start | bytes 131072 | tf_op jit(solution)/shard_map/slice | solution.py:263
  1498.3 25.2 %slice-start.27 = ((bf16[4,1280,64]{1,2,0:T(8,128)(2,1)}), bf16[4,64,64]{1,2,0:T(8,128)(2,1)S(1)}, s32[]{:S(2)}) async-start(bf16[4,1280,64]{1,2,0:T(8,128)(2,1)} %copy-done.57), calls=%async_computation.50 | async-start | bytes 131072 | tf_op jit(solution)/shard_map/slice | solution.py:262
  1498.3 25.9 %slice-start.26 = ((bf16[4,1280,64]{1,2,0:T(8,128)(2,1)}), bf16[4,64,64]{1,2,0:T(8,128)(2,1)S(1)}, s32[]{:S(2)}) async-start(bf16[4,1280,64]{1,2,0:T(8,128)(2,1)} %copy-done.56), calls=%async_computation.49 | async-start | bytes 131072 | tf_op jit(solution)/shard_map/slice | solution.py:263
  1498.3 26.6 %slice-start.29 = ((bf16[4,1280,64]{1,2,0:T(8,128)(2,1)}), bf16[4,64,64]{1,2,0:T(8,128)(2,1)S(1)}, s32[]{:S(2)}) async-start(bf16[4,1280,64]{1,2,0:T(8,128)(2,1)} %copy-done.59), calls=%async_computation.52 | async-start | bytes 131072 | tf_op jit(solution)/shard_map/slice | solution.py:262
  1498.3 27.3 %slice-start.28 = ((bf16[4,1280,64]{1,2,0:T(8,128)(2,1)}), bf16[4,64,64]{1,2,0:T(8,128)(2,1)S(1)}, s32[]{:S(2)}) async-start(bf16[4,1280,64]{1,2,0:T(8,128)(2,1)} %copy-done.58), calls=%async_computation.51 | async-start | bytes 131072 | tf_op jit(solution)/shard_map/slice | solution.py:263
  1498.3 28.0 %copy-start.27 = (bf16[2,304,1,1024]{3,1,2,0:T(8,128)(2,1)S(1)}, bf16[2,304,1,1024]{3,1,2,0:T(8,128)(2,1)}, u32[]{:S(2)}) copy-start(bf16[2,304,1,1024]{3,1,2,0:T(8,128)(2,1)} %copy-done.26) | copy-start | bytes 3735556
  1498.3 28.0 %copy-start.107 = (f32[1,1,1024]{2,1,0:T(1,128)S(1)}, f32[1,1,1024]{2,1,0:T(1,128)}, u32[]{:S(2)}) copy-start(f32[1,1,1024]{2,1,0:T(1,128)} %copy-done.106) | copy-start | bytes 12292
  1498.3 72.8 %all-reduce.15.cloned.1.call-start = ((), (), s32[]{:S(2)}) async-start(), calls=%async_computation.22 | async-start | bytes 393216 | tf_op jit(solution)/shard_map/psum | solution.py:360
  (157 other events, 964.1 us)
Sparse Core Ops, SparseCore 0:
  11.4 96.9 all-gather.6
  111.2 85.4 all-gather.8
  199.6 128.6 all-gather.12
  330.9 111.0 all-gather.10
  1526.5 44.6 all-reduce.14
where the time goes:
time: 1600 us; the launch traced here: 1590 us
  matrix products  518 us (32%)
  waiting for transfers between devices  475 us (30%)
  local copies, waits for them, and re-layouts  345 us (22%)
  other arithmetic  102 us (6%)
  starting transfers between devices  92.7 us (6%)
  blocking collectives  42.3 us (3%)
  between operations  17.2 us (1%)
    all_to_all x18, waiting for transfers between devices, regroup(): return lax.all_to_all(moving, 'mp', split_axis=0, concat_axis=1, tiled=True)  227 us
    dot_general x6, matrix products, section_forward(): branch_ffn = jnp.dot(active, down_w, preferred_element_type=jnp.float32)  108 us
    all_gather x1, waiting for transfers between devices, fetch_frozen(): lax.all_gather(shards[2], ('dp', 'mp'), axis=0, tiled=True)  92.1 us
    unnamed x394, local copies, waits for them, and re-layouts  85.2 us
    all_to_all x18, starting transfers between devices, regroup(): return lax.all_to_all(moving, 'mp', split_axis=0, concat_axis=1, tiled=True)  84.7 us
    all_gather x1, waiting for transfers between devices, fetch_frozen(): lax.all_gather(shards[0], ('dp', 'mp'), axis=0, tiled=True)  80.4 us
    dot_general x3, matrix products, section_backward(): lax.dot_general(grad_hidden, up_w, contract, preferred_element_type=jnp.f...  77.6 us
    dot_general x12, matrix products, attend(): jnp.einsum('hqk,hkd->hqd', weights, all_values, preferred_element_type=jn...  74.2 us
  transfers between devices with their start and end apart: 27, of which 14 were waited for; matrix products, arithmetic and copies ran while one was open for 39% of the time, Pallas kernels for 0%

commit v1 on v0

v1 whole, which is shorter than its diff:
```python
import jax
import jax.numpy as jnp
from jax import lax
from jax.sharding import PartitionSpec as P

HEADS = 16
HD = 64
EPS = 1e-5
BF = jnp.bfloat16
F32 = jnp.float32


def dot(a, b, dims):
    return lax.dot_general(a, b, (dims, ((), ())), preferred_element_type=F32)


def nn(a, b):
    return dot(a, b, ((1,), (0,)))


def nt(a, b):
    return dot(a, b, ((1,), (1,)))


def norm_stats(v):
    centred = v - jnp.mean(v, axis=-1, keepdims=True)
    inv = lax.rsqrt(jnp.mean(centred * centred, axis=-1, keepdims=True) + EPS)
    return centred * inv, inv


def norm_back(v, grad, gain):
    n, inv = norm_stats(v)
    e = grad * gain
    return inv * (e - jnp.mean(e, -1, keepdims=True) - n * jnp.mean(e * n, -1, keepdims=True))


class Place:
    def __init__(self):
        self.mp = lax.axis_size("mp")
        self.g = self.mp // 2
        self.c = lax.axis_index("section")
        self.z = lax.axis_index("mp")
        self.m = self.z // self.g
        self.p = self.z % self.g

    def send(self, value, route):
        pairs = []
        for c in range(2):
            for m in range(2):
                for p in range(self.g):
                    to = route(c, m, p)
                    if to is not None:
                        source = c * self.mp + m * self.g + p
                        pairs.append((source, to[0] * self.mp + to[1] * self.g + to[2]))
        return lax.ppermute(value, ("section", "mp"), pairs)

    def core(self, value):
        return lax.ppermute(value, "section", [(0, 1), (1, 0)])

    def chip(self, value, j):
        return lax.ppermute(value, "mp", [(z, z ^ j) for z in range(self.mp)])


def gather_weights(place, l, qkv, out, up, down):
    g = place.g
    attn = qkv[0].astype(BF).transpose(1, 0, 2).reshape(qkv.shape[2], -1)
    rest = jnp.concatenate([out[0].astype(BF).T, up[0].astype(BF), down[0].astype(BF).T], axis=1)
    attn = sum(
        place.send(attn, lambda c, m, p: (m, half, p) if c == l else None) for half in range(2)
    )
    qkv_full = lax.all_gather(attn, "dp", axis=0, tiled=True)
    panels = []
    for j in range(g):
        panel = sum(
            place.send(rest, lambda c, m, p: (m, half, p ^ j) if c == l else None)
            for half in range(2)
        )
        panels.append(lax.all_gather(panel, "dp", axis=0, tiled=True))
    return qkv_full, panels


def scores_of(queries, keys, allowed):
    scores = jnp.einsum("hqd,hkd->hqk", queries, keys, preferred_element_type=F32) * HD ** (-0.5)
    return jnp.where(allowed[None], scores, -1e30)


def attend(queries, keys, values, allowed):
    length = queries.shape[1]
    step = length // 2
    outs, totals = [], []
    for first in range(0, length, step):
        s = scores_of(queries[:, first : first + step], keys, allowed[first : first + step])
        peak = jnp.max(s, axis=-1, keepdims=True)
        e = jnp.exp(s - peak)
        total = jnp.sum(e, axis=-1, keepdims=True)
        w = (e / total).astype(BF)
        outs.append(jnp.einsum("hqk,hkd->hqd", w, values, preferred_element_type=F32))
        totals.append(peak + jnp.log(total))
    return jnp.concatenate(outs, 1).astype(BF), jnp.concatenate(totals, 1)


def attend_back(queries, keys, values, allowed, totals, grad):
    length = queries.shape[1]
    step = length // 2
    gk = jnp.zeros(keys.shape, F32)
    gv = jnp.zeros(values.shape, F32)
    gq = []
    for first in range(0, length, step):
        cut = slice(first, first + step)
        s = scores_of(queries[:, cut], keys, allowed[cut])
        prob = jnp.exp(s - totals[:, cut])
        go = grad[:, cut]
        gp = jnp.einsum("hqd,hkd->hqk", go, values, preferred_element_type=F32)
        inner = jnp.sum(prob * gp, axis=-1, keepdims=True)
        gs = (prob * (gp - inner)).astype(BF)
        gq.append(
            jnp.einsum("hqk,hkd->hqd", gs, keys, preferred_element_type=F32) * HD ** (-0.5)
        )
        gk = gk + jnp.einsum(
            "hqk,hqd->hkd", gs, queries[:, cut], preferred_element_type=F32
        ) * HD ** (-0.5)
        gv = gv + jnp.einsum("hqk,hqd->hkd", prob.astype(BF), go, preferred_element_type=F32)
    return jnp.concatenate(gq, 1), gk, gv


def to_heads(flat):
    return flat.reshape(flat.shape[0], -1, HD).transpose(1, 0, 2)


def from_heads(heads):
    return heads.transpose(1, 0, 2).reshape(heads.shape[1], -1)


def layer_forward(place, x_own, weights, small, allowed):
    qkv_w, panels = weights
    g, rows = place.g, x_own.shape[0]
    d_model = x_own.shape[1]
    gained, up_b, qkv_b, pre = small
    out_b, down_b, gain0, gain1, shift0, shift1 = gained
    blocks = []
    for j in range(g):
        own = x_own if j == 0 else place.chip(x_own, j)
        blocks += [own, place.core(own)]
    projected = [nn(b, qkv_w) + qkv_b for b in blocks]
    flat = jnp.concatenate(projected, 0).astype(BF)
    width = flat.shape[1] // 3
    q, k, v = (to_heads(flat[:, i * width : (i + 1) * width]) for i in range(3))
    keys = jnp.concatenate([to_heads(pre[0]), k], axis=1)
    values = jnp.concatenate([to_heads(pre[1]), v], axis=1)
    o, totals = attend(q, keys, values, allowed)
    o = from_heads(o)
    mine = 0.0
    for j in range(g):
        part = o[j * 2 * rows : (j + 1) * 2 * rows]
        part = part if j == 0 else place.chip(part, j)
        mine = mine + nt(part, panels[j][:, :width])
    a = x_own.astype(F32) + mine[:rows] + place.core(mine[rows:]) + out_b
    n, _ = norm_stats(a)
    x1 = n * gain0 + shift0
    x1_low = x1.astype(BF)
    both = jnp.concatenate([x1_low, place.core(x1_low)], 0)
    hidden, branch = [], 0.0
    ff = up_b[0].shape[0]
    for j in range(g):
        u = nn(both, panels[j][:, width : width + ff]) + up_b[j]
        f = jax.nn.gelu(u, approximate=False).astype(BF)
        branch = branch + nt(f, panels[j][:, width + ff :])
        hidden.append(u)
    z = x1 + branch[:rows] + place.core(branch[rows:]) + down_b
    n, _ = norm_stats(z)
    result = (n * gain1 + shift1).astype(BF)
    return result, (q, keys, values, totals, a, hidden, z)


def layer_backward(place, grad, saved, weights, small, allowed):
    q, keys, values, totals, a, hidden, z = saved
    qkv_w, panels = weights
    gained, up_b, _, _ = small
    _, _, gain0, gain1, _, _ = gained
    g, rows = place.g, grad.shape[0]
    ff = up_b[0].shape[0]
    width = q.shape[0] * HD
    dz = norm_back(z, grad.astype(F32), gain1)
    low = dz.astype(BF)
    both = jnp.concatenate([low, place.core(low)], 0)
    branch = 0.0
    for j in range(g):
        df = nn(both, panels[j][:, width + ff :])
        u = hidden[j]
        slope = 0.5 * (1 + lax.erf(u * 2 ** (-0.5))) + u * jnp.exp(-0.5 * u * u) * 0.3989422804014327
        branch = branch + nt((df * slope).astype(BF), panels[j][:, width : width + ff])
    dx1 = dz + branch[:rows] + place.core(branch[rows:])
    da = norm_back(a, dx1, gain0)
    low = da.astype(BF)
    both = jnp.concatenate([low, place.core(low)], 0)
    parts = []
    for j in range(g):
        do = nn(both, panels[j][:, :width]).astype(BF)
        parts.append(do if j == 0 else place.chip(do, j))
    go = to_heads(jnp.concatenate(parts, 0))
    gq, gk, gv = attend_back(q, keys, values, allowed, totals, go)
    prefix = keys.shape[1] - q.shape[1]
    kv_grad = jnp.stack([from_heads(gk[:, :prefix]), from_heads(gv[:, :prefix])])
    back = jnp.concatenate(
        [from_heads(t).astype(BF) for t in (gq, gk[:, prefix:], gv[:, prefix:])], axis=1
    )
    dx = nt(back, qkv_w).reshape(g, 2, rows, -1)
    summed = dx[:, 0] + place.core(dx[:, 1].astype(BF)).astype(F32)
    total = da + summed[0]
    for j in range(1, g):
        total = total + place.chip(summed[j].astype(BF), j).astype(F32)
    return total.astype(BF), kv_grad


def on_device(
    tokens,
    cotangent,
    lengths,
    qkv_weight,
    qkv_bias,
    out_weight,
    out_bias,
    up_weight,
    up_bias,
    down_weight,
    down_bias,
    norm_gain,
    norm_shift,
    prefix_keys,
    prefix_values,
):
    place = Place()
    g, mp, c, m, p = place.g, place.mp, place.c, place.m, place.p
    layers = [
        gather_weights(place, l, qkv_weight, out_weight, up_weight, down_weight) for l in range(2)
    ]

    d_model, ff = out_bias.shape[1], up_bias.shape[1]
    fixed = jnp.concatenate([out_bias, down_bias, norm_gain[0], norm_shift[0]], 0)
    flat = jnp.concatenate([fixed.reshape(-1), up_bias[0], qkv_bias[0].reshape(-1)])
    flat = lax.all_gather(flat, ("section", "mp"))
    pre = jnp.stack([prefix_keys[0], prefix_values[0]]).astype(BF)
    pre = lax.all_gather(pre, ("section", "mp"))
    shard = c * g + p
    smalls = []
    for l in range(2):
        mine = lax.dynamic_index_in_dim(flat, l * mp + shard, 0, keepdims=False)
        gained = [mine[i * d_model : (i + 1) * d_model] for i in range(6)]
        qkv_b = mine[6 * d_model + ff :]
        up_b = []
        for j in range(g):
            row = lax.dynamic_index_in_dim(flat, l * mp + c * g + (p ^ j), 0, keepdims=False)
            up_b.append(row[6 * d_model : 6 * d_model + ff])
        smalls.append(
            (gained, up_b, qkv_b, lax.dynamic_index_in_dim(pre, l * mp + shard, 0, keepdims=False))
        )

    rows = tokens.shape[1]

    def own_rows(array):
        other = lax.dynamic_index_in_dim(array, 1 - m, 0, keepdims=False)[:, 0]
        same = lax.dynamic_index_in_dim(array, m, 0, keepdims=False)[:, 0]
        moved = place.send(other, lambda c, m, p: (c, 1 - m, p) if c == m else None)
        return jnp.where(c == m, same, moved)

    x = own_rows(tokens)
    grad = own_rows(cotangent)

    row_lengths = lax.dynamic_index_in_dim(lengths, m, 0, keepdims=False)[0]
    places = jnp.concatenate(
        [
            ((c ^ i) * g + (p ^ j)) * rows + jnp.arange(rows, dtype=jnp.int32)
            for j in range(g)
            for i in range(2)
        ]
    )
    segment = jnp.sum((places[:, None] >= jnp.cumsum(row_lengths)[None]).astype(jnp.int32), -1)
    seen = (segment[:, None] == segment[None, :]) & (segment[None, :] != lengths.shape[-1] - 1)
    prefix = prefix_keys.shape[1]
    allowed = jnp.concatenate([jnp.ones((seen.shape[0], prefix), jnp.bool_), seen], axis=1)

    results, kept = [], []
    for l in range(2):
        x, saved = layer_forward(place, x, layers[l], smalls[l], allowed)
        results.append(x)
        kept.append(saved)
    grads, kv = [None, None], [None, None]
    for l in (1, 0):
        grad, kv[l] = layer_backward(place, grad, kept[l], layers[l], smalls[l], allowed)
        grads[l] = grad

    def home(pair, half):
        return sum(
            place.send(pair[l], lambda c, m, p: (l, c, p) if m == half else None) for l in range(2)
        )

    outs = jnp.stack([home(results, half) for half in range(2)])[:, :, None]
    gouts = jnp.stack([home(grads, half) for half in range(2)])[:, :, None]
    kv = lax.psum(home(kv, 0) + home(kv, 1), "dp")
    return outs[None], gouts[None], kv[None, 0], kv[None, 1]


def solution(mesh):
    placed = (
        P(None, "mp", "dp", None),
        P(None, "mp", "dp", None),
        P(None, "dp", None),
        P("section", None, "dp", "mp"),
        P("section", None, "mp"),
        P("section", "mp", "dp"),
        P("section", None),
        P("section", "dp", "mp"),
        P("section", "mp"),
        P("section", "mp", "dp"),
        P("section", None),
        P("section", None, None),
        P("section", None, None),
        P("section", None, "mp"),
        P("section", None, "mp"),
    )
    return jax.shard_map(
        on_device,
        mesh=mesh,
        in_specs=placed,
        out_specs=(
            P("section", None, "mp", "dp", None),
            P("section", None, "mp", "dp", None),
            P("section", None, "mp"),
            P("section", None, "mp"),
        ),
        check_vma=False,
    )
```

time: 1600 us -> 775 us (0.48)
  local copies, waits for them, and re-layouts: 345 us -> 32.3 us
  matrix products: 518 us -> 210 us
  waiting for transfers between devices: 475 us -> 189 us
  starting transfers between devices: 92.7 us -> 142 us
  blocking collectives: 42.3 us -> 84.1 us
    dot_general x72 -> x54, matrix products: 481 us -> 210 us  [the longest x30 98.4 us: dot(): return lax.dot_general(a, b, (dims, ((), ())), preferred_element_type=F32)]
    all_to_all x18 -> x0, waiting for transfers between devices: 227 us -> none  [regroup(): return lax.all_to_all(moving, 'mp', split_axis=0, concat_axis=1, tiled=True)]
    all_gather x4 -> x6, waiting for transfers between devices: 207 us -> 3.75 us  [the longest x4 3.73 us: gather_weights(): panels.append(lax.all_gather(panel, 'dp', axis=0, tiled=True))]
    ppermute x4 -> x52, waiting for transfers between devices: 0.01 us -> 154 us  [the longest x8 69 us: chip(): return lax.ppermute(value, 'mp', [(z, z ^ j) for z in range(self.mp)])]
    ppermute x4 -> x52, starting transfers between devices: 7.64 us -> 141 us  [the longest x26 93.6 us: send(): return lax.ppermute(value, ('section', 'mp'), pairs)]
    reshape x26 -> x1, local copies, waits for them, and re-layouts: 106 us -> 0.01 us  [on_device(): fixed.reshape(-1)]
    all_to_all x18 -> x0, starting transfers between devices: 84.7 us -> none  [regroup(): return lax.all_to_all(moving, 'mp', split_axis=0, concat_axis=1, tiled=True)]
    unnamed x394 -> x243, local copies, waits for them, and re-layouts: 85.2 us -> 10.5 us
  transfers between devices with their start and end apart: 27 -> 59, of which waited for: 14 -> 27; matrix products, arithmetic and copies ran while one was open for 39% -> 20% of each run, Pallas kernels for 0% -> 0%
where the time goes in v1:
time: 775 us; the launch traced here: 765 us
  matrix products  210 us (27%)
  waiting for transfers between devices  189 us (24%)
  starting transfers between devices  142 us (18%)
  other arithmetic  90.5 us (12%)
  blocking collectives  84.1 us (11%)
  local copies, waits for them, and re-layouts  32.3 us (4%)
  between operations  16.8 us (2%)
    dot_general x30, matrix products, dot(): return lax.dot_general(a, b, (dims, ((), ())), preferred_element_type=F32)  98.4 us
    ppermute x26, starting transfers between devices, send(): return lax.ppermute(value, ('section', 'mp'), pairs)  93.6 us
    ppermute x8, waiting for transfers between devices, chip(): return lax.ppermute(value, 'mp', [(z, z ^ j) for z in range(self.mp)])  69 us
    ppermute x26, waiting for transfers between devices, send(): return lax.ppermute(value, ('section', 'mp'), pairs)  64.1 us
    all_gather x1, blocking collectives, on_device(): flat = lax.all_gather(flat, ('section', 'mp'))  45.4 us
    ppermute x18, starting transfers between devices, core(): return lax.ppermute(value, 'section', [(0, 1), (1, 0)])  39.3 us
    all_gather x1, blocking collectives, on_device(): pre = lax.all_gather(pre, ('section', 'mp'))  38.8 us
    psum x1, waiting for transfers between devices, on_device(): kv = lax.psum(home(kv, 0) + home(kv, 1), 'dp')  31.8 us
  transfers between devices with their start and end apart: 59, of which 27 were waited for; matrix products, arithmetic and copies ran while one was open for 20% of the time, Pallas kernels for 0%

profile of v1, /device:TPU:0, one launch (start us, length us, event | category | flops | bytes accessed | tf_op | source)
XLA Modules:
  0.0 764.5 jit_solution(11132321619583482542)
XLA Ops:
  8.7 6.0 collective-permute-start.2
  15.4 4.6 collective-permute-done.2
  22.5 10.6 %collective-permute-start.10 = (bf16[256,2304]{0,1:T(8,128)(2,1)}, bf16[256,2304]{0,1:T(8,128)(2,1)S(1)}, u32[]{:S(2)}, u32[]{:S(2)}) collective-permute-start(bf16[256,2304]{0,1:T(8,128)(2,1)} %pad_maximum_fusion.8), channel_id=1, source_target_pairs={{0,3},{1,2},{2,19},{3,18},{4,7},{5,6},{6,23},{7,22},{8,11},{9,10},... | collective-permute-start | bytes 3538952 | tf_op jit(solution)/shard_map/ppermute | solution.py:55
  35.0 12.1 %collective-permute-done.10 = bf16[256,2304]{0,1:T(8,128)(2,1)S(1)} collective-permute-done((bf16[256,2304]{0,1:T(8,128)(2,1)}, bf16[256,2304]{0,1:T(8,128)(2,1)S(1)}, u32[]{:S(2)}, u32[]{:S(2)}) %collective-permute-start.10) | collective-permute-done | bytes 1179680 | tf_op jit(solution)/shard_map/ppermute | solution.py:55
  47.0 17.0 %collective-permute-done.9 = bf16[256,2304]{0,1:T(8,128)(2,1)S(1)} collective-permute-done((bf16[256,2304]{0,1:T(8,128)(2,1)}, bf16[256,2304]{0,1:T(8,128)(2,1)S(1)}, u32[]{:S(2)}, u32[]{:S(2)}) %collective-permute-start.9) | collective-permute-done | bytes 1179680 | tf_op jit(solution)/shard_map/ppermute | solution.py:55
  67.7 10.4 %collective-permute-start.6 = (bf16[256,2304]{0,1:T(8,128)(2,1)}, bf16[256,2304]{0,1:T(8,128)(2,1)}, u32[]{:S(2)}, u32[]{:S(2)}) collective-permute-start(bf16[256,2304]{0,1:T(8,128)(2,1)} %pad_maximum_fusion.8), channel_id=1, source_target_pairs={{0,0},{1,1},{2,16},{3,17},{4,4},{5,5},{6,20},{7,21},{8,8},{9,9},{1... | collective-permute-start | bytes 3538952 | tf_op jit(solution)/shard_map/ppermute | solution.py:55
  81.5 45.4 %all-gather.1 = f32[8,1,7936]{2,1,0:T(1,128)S(1)} all-gather(f32[1,1,7936]{2,1,0:T(1,128)S(1)} %reshape.324), channel_id=2, replica_groups=mesh['section'=2,'dp'=4,'mp'=4] {'section','mp'}, dimensions={0}, use_global_device_ids=true | all-gather | bytes 285696 | tf_op jit(solution)/shard_map/all_gather | solution.py:241
  129.2 38.8 %all_gather.31 = bf16[8,2,64,256]{3,2,1,0:T(8,128)(2,1)S(1)} all-gather(bf16[1,2,64,256]{3,2,1,0:T(8,128)(2,1)S(1)} %pad_maximum_fusion.35), channel_id=1, replica_groups=mesh['section'=2,'dp'=4,'mp'=4] {'section','mp'}, dimensions={0}, use_global_device_ids=true | all-gather | bytes 589824 | tf_op jit(solution)/shard_map/all_gather | solution.py:243
  171.5 2.9 add.510
  181.9 6.7 fusion.552
  188.6 4.3 fusion.551
  192.9 10.9 %fusion = f32[4,608]{1,0:T(4,128)S(1)} fusion(f32[4,608,1280]{2,1,0:T(8,128)} %get-tuple-element.84, f32[4,608]{1,0:T(4,128)S(1)} %get-tuple-element.83), kind=kLoop, calls=%fused_computation.24 | loop fusion | flops 6223488 | bytes 12471296 | tf_op jit(solution)/shard_map/reduce_sum | solution.py:95
  205.7 7.4 fusion.323
  213.2 4.5 fusion.322
  219.1 10.0 %collective-permute-done.8 = bf16[608,256]{0,1:T(8,128)(2,1)S(1)} collective-permute-done((bf16[608,256]{0,1:T(8,128)(2,1)S(1)}, bf16[608,256]{0,1:T(8,128)(2,1)S(1)}, u32[]{:S(2)}, u32[]{:S(2)}) %collective-permute-start.8) | collective-permute-done | bytes 311328 | tf_op jit(solution)/shard_map/ppermute | solution.py:61
  235.9 5.3 collective-permute-done.15
  247.1 12.1 %collective-permute-start.12 = (bf16[304,1024]{1,0:T(8,128)(2,1)S(1)}, bf16[304,1024]{1,0:T(8,128)(2,1)S(1)}, u32[]{:S(2)}, u32[]{:S(2)}) collective-permute-start(bf16[304,1024]{1,0:T(8,128)(2,1)S(1)} %fusion.332), channel_id=1, source_target_pairs={{0,16},{16,0},{1,17},{17,1},{2,18},{18,2},{3,19},{19,3},{4,20},{20... | collective-permute-start | bytes 1867784 | tf_op jit(solution)/shard_map/ppermute | solution.py:58
  259.1 7.9 %collective-permute-done.23 = bf16[256,2304]{0,1:T(8,128)(2,1)S(1)} collective-permute-done((bf16[256,2304]{0,1:T(8,128)(2,1)}, bf16[256,2304]{0,1:T(8,128)(2,1)S(1)}, u32[]{:S(2)}, u32[]{:S(2)}) %collective-permute-start.23) | collective-permute-done | bytes 1179680 | tf_op jit(solution)/shard_map/ppermute | solution.py:55
  268.6 3.1 fusion.132
  271.7 4.0 fusion.140
  275.7 8.8 %fusion.128 = f32[608,1024]{1,0:T(8,128)S(1)} fusion(bf16[1024,2304]{0,1:T(8,128)(2,1)} %all-gather.13.cloned.1.call-done, f32[608,1024]{1,0:T(8,128)S(1)} %fusion.132, f32[1024]{0:T(1024)S(1)} %bitcast.327), kind=kOutput, calls=%fused_computation.195 | convolution fusion | flops 1316159488 | bytes 7081984 | tf_op jit(solution)/shard_map/dot_general | solution.py:14
  284.6 8.4 %fusion.145 = f32[608,1024]{1,0:T(8,128)S(1)} fusion(f32[608,1024]{1,0:T(8,128)S(1)} %fusion.128, bf16[1024,2304]{0,1:T(8,128)(2,1)} %all-gather.11.cloned.1.call-done, f32[608,1024]{1,0:T(8,128)S(1)} %fusion.140, f32[1024]{0:T(1024)S(1)} %bitcast.333), kind=kOutput, calls=%fused_computation.212 | convolution fusion | flops 1316782080 | bytes 9572352 | tf_op jit(solution)/shard_map/dot_general | solution.py:14
  293.1 15.0 %collective-permute-start.13 = (f32[304,1024]{1,0:T(8,128)S(1)}, f32[304,1024]{1,0:T(8,128)S(1)}, u32[]{:S(2)}, u32[]{:S(2)}) collective-permute-start(f32[304,1024]{1,0:T(8,128)S(1)} %slice.430), channel_id=1, source_target_pairs={{0,16},{16,0},{1,17},{17,1},{2,18},{18,2},{3,19},{19,3},{4,20},{20... | collective-permute-start | bytes 3735560 | tf_op jit(solution)/shard_map/ppermute | solution.py:58
  318.9 22.6 %collective-permute-done.18 = bf16[304,1024]{1,0:T(8,128)(2,1)S(1)} collective-permute-done((bf16[304,1024]{1,0:T(8,128)(2,1)}, bf16[304,1024]{1,0:T(8,128)(2,1)S(1)}, u32[]{:S(2)}, u32[]{:S(2)}) %collective-permute-start.18) | collective-permute-done | bytes 622624 | tf_op jit(solution)/shard_map/ppermute | solution.py:61
  351.3 4.7 fusion.553
  356.1 6.8 fusion.554
  364.8 6.4 fusion.2
  371.2 4.0 fusion.320
  375.3 7.1 fusion.321
  382.9 9.7 %collective-permute-done.22 = bf16[608,256]{0,1:T(8,128)(2,1)S(1)} collective-permute-done((bf16[608,256]{0,1:T(8,128)(2,1)S(1)}, bf16[608,256]{0,1:T(8,128)(2,1)S(1)}, u32[]{:S(2)}, u32[]{:S(2)}) %collective-permute-start.22) | collective-permute-done | bytes 311328 | tf_op jit(solution)/shard_map/ppermute | solution.py:61
  394.1 3.7 all-gather.17.cloned.1.call-done
  399.5 2.9 collective-permute-done.25
  408.9 6.6 fusion.112
  415.5 6.4 fusion.151
  423.3 4.8 collective-permute-start.31
  429.0 6.4 collective-permute-done.31
  436.4 6.6 collective-permute-start.32
  444.9 7.6 fusion.114
  452.5 8.3 %fusion.148 = f32[608,1024]{1,0:T(8,128)} fusion(f32[608,1024]{1,0:T(8,128)} %fusion.114, bf16[1024,2304]{0,1:T(8,128)(2,1)} %all-gather.17.cloned.1.call-done, f32[608,1024]{1,0:T(8,128)} %copy-done.102, f32[1024]{0:T(1024)S(1)} %bitcast.330, bf16[304,1024]{1,0:T(8,128)(2,1)} %collective-permute-done.32, bf16[304,1024]{1,0:T(8,128)(2,1)} %copy-done.45), kind=kOutput, calls=%fused_computation.213 | convolution fusion | flops 2560098304 | bytes 12914688 | tf_op jit(solution)/shard_map/dot_general | solution.py:14
  465.3 3.2 fusion.530
  477.1 6.2 collective-permute-done.35
  483.6 6.1 fusion.12
  489.7 9.1 %multiply_reduce_fusion.2 = (f32[4,608]{1,0:T(4,128)S(1)}, f32[4,608,1280]{2,1,0:T(8,128)}) fusion(f32[4,608,1280]{2,1,0:T(8,128)} %copy-done.3, f32[4,608]{1,0:T(4,128)S(1)} %log_add_fusion.2, bf16[4,1216,64]{1,2,0:T(8,128)(2,1)S(1)} %bitcast.230, bf16[4,64,64]{1,2,0:T(8,128)(2,1)S(1)} %bitcast.278, bf16[4,1216,64]{1,2,0:T(8,128)(2,1)S(1)} %bitcast.233), kind=kOutput, calls=%fused_computation.7 | convolution fusion | flops 409106048 | bytes 25972224 | tf_op jit(solution)/shard_map/hqd,hkd->hqk/dot_general | solution.py:113
  498.9 6.2 multiply_reduce_fusion.3
  505.1 6.3 multiply_convert_fusion.3
  518.6 6.5 multiply_convert_fusion.2
  532.8 2.9 collective-permute-done.36
  537.9 14.4 %collective-permute-done.37 = bf16[304,1024]{1,0:T(8,128)(2,1)S(1)} collective-permute-done((bf16[304,1024]{1,0:T(8,128)(2,1)S(1)}, bf16[304,1024]{1,0:T(8,128)(2,1)S(1)}, u32[]{:S(2)}, u32[]{:S(2)}) %collective-permute-start.37) | collective-permute-done | bytes 622624 | tf_op jit(solution)/shard_map/ppermute | solution.py:61
  555.5 7.3 fusion.130
  562.8 8.0 %fusion.142 = f32[608,1024]{1,0:T(8,128)} fusion(f32[608,1024]{1,0:T(8,128)} %fusion.130, bf16[1024,2304]{0,1:T(8,128)(2,1)} %all-gather.11.cloned.1.call-done, f32[608,1024]{1,0:T(8,128)} %copy-done.100, f32[1024]{0:T(1024)S(1)} %bitcast.334, bf16[304,1024]{1,0:T(8,128)(2,1)S(1)} %collective-permute-done.38, bf16[304,1024]{1,0:T(8,128)(2,1)S(1)} %fusion.528), kind=kOutput, calls=%fused_computation.211 | convolution fusion | flops 2560098304 | bytes 12914688 | tf_op jit(solution)/shard_map/dot_general | solution.py:14
  586.5 6.2 collective-permute-done.41
  593.0 8.0 %fusion.8 = f32[4,1280,64]{1,2,0:T(8,128)} fusion(f32[4,608,1280]{2,1,0:T(8,128)} %copy-done.2, f32[4,608]{1,0:T(4,128)S(1)} %log_add_fusion, bf16[4,1216,64]{1,2,0:T(8,128)(2,1)S(1)} %bitcast.236), kind=kOutput, calls=%fused_computation.32 | convolution fusion | flops 404684800 | bytes 14100480 | tf_op jit(solution)/shard_map/hqk,hqd->hkd/dot_general | solution.py:122
  601.0 9.1 %multiply_reduce_fusion = (f32[4,608]{1,0:T(4,128)S(1)}, f32[4,608,1280]{2,1,0:T(8,128)}) fusion(f32[4,608,1280]{2,1,0:T(8,128)} %copy-done.2, f32[4,608]{1,0:T(4,128)S(1)} %log_add_fusion, bf16[4,1216,64]{1,2,0:T(8,128)(2,1)S(1)} %bitcast.226, bf16[4,64,64]{1,2,0:T(8,128)(2,1)S(1)} %bitcast.274, bf16[4,1216,64]{1,2,0:T(8,128)(2,1)S(1)} %bitcast.237), kind=kOutput, calls=%fused_computation.1 | convolution fusion | flops 409106048 | bytes 25972224 | tf_op jit(solution)/shard_map/hqd,hkd->hqk/dot_general | solution.py:113
  610.1 4.4 multiply_reduce_fusion.1
  614.5 4.5 multiply_convert_fusion.1
  619.0 5.6 fusion.318
  630.9 6.5 multiply_convert_fusion
  651.5 6.4 collective-permute-start.14
  660.8 6.8 collective-permute-done.29
  672.1 13.9 %collective-permute-start.49 = (f32[2,64,256]{2,1,0:T(8,128)}, f32[2,64,256]{2,1,0:T(8,128)}, u32[]{:S(2)}, u32[]{:S(2)}) collective-permute-start(f32[2,64,256]{2,1,0:T(8,128)} %pad_maximum_fusion.34), channel_id=1, source_target_pairs={{0,16},{1,17},{16,18},{17,19},{4,20},{5,21},{20,22},{21,23},{8,24}... | collective-permute-start | bytes 393224 | tf_op jit(solution)/shard_map/ppermute | solution.py:55
  696.1 11.1 %collective-permute-start.45 = (bf16[304,1024]{1,0:T(8,128)(2,1)S(1)}, bf16[304,1024]{1,0:T(8,128)(2,1)S(1)}, u32[]{:S(2)}, u32[]{:S(2)}) collective-permute-start(bf16[304,1024]{1,0:T(8,128)(2,1)S(1)} %copy-done.17), channel_id=1, source_target_pairs={{0,16},{1,17},{16,18},{17,19},{4,20},{5,21},{20,22},{21,23},{8,24}... | collective-permute-start | bytes 1867784 | tf_op jit(solution)/shard_map/ppermute | solution.py:55
  707.1 4.2 collective-permute-done.50
  713.0 6.4 collective-permute-start.44
  720.6 31.8 %all-reduce.3.cloned.1.call-done = f32[2,64,256]{2,1,0:T(8,128)} async-done(((f32[2,64,256]{2,1,0:T(8,128)}), f32[2,64,256]{2,1,0:T(8,128)}) %all-reduce.3.cloned.1.call-update) | async-done | bytes 131088 | tf_op jit(solution)/shard_map/psum | solution.py:299
  (511 shorter events, 176.1 us)
Async XLA Ops:
  7.2 73.9 %copy-start = (s32[2,1,5]{2,1,0:T(1,128)S(1)}, s32[2,1,5]{2,1,0:T(1,128)}, u32[]{:S(2)}) copy-start(s32[2,1,5]{2,1,0:T(1,128)} %param.17) | copy-start | bytes 124
  7.2 167.3 %all-gather.9.cloned.1.call-start = ((), (), s32[]{:S(2)}) async-start(), calls=%async_computation | async-start | bytes 1966080 | tf_op jit(solution)/shard_map/all_gather | solution.py:71
  8.7 11.3 %collective-permute-start.2 = (bf16[256,768]{0,1:T(8,128)(2,1)S(1)}, bf16[256,768]{0,1:T(8,128)(2,1)S(1)}, u32[]{:S(2)}, u32[]{:S(2)}) collective-permute-start(bf16[256,768]{0,1:T(8,128)(2,1)S(1)} %bitcast.281), channel_id=1, source_target_pairs={{0,2},{1,3},{2,18},{3,19},{4,6},{5,7},{6,22},{7,23},{8,10},{9,11},... | collective-permute-start | bytes 1179656 | tf_op jit(solution)/shard_map/ppermute | solution.py:55
  14.7 5.3 collective-permute-start.1
  20.9 208.2 %all-gather.13.cloned.1.call-start = ((), (), s32[]{:S(2)}) async-start(), calls=%async_computation.2 | async-start | bytes 5898240 | tf_op jit(solution)/shard_map/all_gather | solution.py:78
  22.4 104.4 %copy-start.61 = (f32[1,64,256]{2,1,0:T(8,128)S(1)}, f32[1,64,256]{2,1,0:T(8,128)}, u32[]{:S(2)}) copy-start(f32[1,64,256]{2,1,0:T(8,128)} %param.29) | copy-start | bytes 196612
  22.5 104.4 %copy-start.62 = (f32[1,64,256]{2,1,0:T(8,128)S(1)}, f32[1,64,256]{2,1,0:T(8,128)}, u32[]{:S(2)}) copy-start(f32[1,64,256]{2,1,0:T(8,128)} %param.28) | copy-start | bytes 196612
  22.5 24.6 %collective-permute-start.10 = (bf16[256,2304]{0,1:T(8,128)(2,1)}, bf16[256,2304]{0,1:T(8,128)(2,1)S(1)}, u32[]{:S(2)}, u32[]{:S(2)}) collective-permute-start(bf16[256,2304]{0,1:T(8,128)(2,1)} %pad_maximum_fusion.8), channel_id=1, source_target_pairs={{0,3},{1,2},{2,19},{3,18},{4,7},{5,6},{6,23},{7,22},{8,11},{9,10},... | collective-permute-start | bytes 3538952 | tf_op jit(solution)/shard_map/ppermute | solution.py:55
  33.0 30.9 %collective-permute-start.9 = (bf16[256,2304]{0,1:T(8,128)(2,1)}, bf16[256,2304]{0,1:T(8,128)(2,1)S(1)}, u32[]{:S(2)}, u32[]{:S(2)}) collective-permute-start(bf16[256,2304]{0,1:T(8,128)(2,1)} %pad_maximum_fusion.8), channel_id=1, source_target_pairs={{0,1},{1,0},{2,17},{3,16},{4,5},{5,4},{6,21},{7,20},{8,9},{9,8},{1... | collective-permute-start | bytes 3538952 | tf_op jit(solution)/shard_map/ppermute | solution.py:55
  65.3 165.3 %all-gather.11.cloned.1.call-start = ((), (), s32[]{:S(2)}) async-start(), calls=%async_computation.1 | async-start | bytes 5898240 | tf_op jit(solution)/shard_map/all_gather | solution.py:78
  65.4 106.1 %collective-permute-start.7 = (bf16[256,2304]{0,1:T(8,128)(2,1)}, bf16[256,2304]{0,1:T(8,128)(2,1)}, u32[]{:S(2)}, u32[]{:S(2)}) collective-permute-start(bf16[256,2304]{0,1:T(8,128)(2,1)} %pad_maximum_fusion.8), channel_id=1, source_target_pairs={{0,2},{1,3},{2,18},{3,19},{4,6},{5,7},{6,22},{7,23},{8,10},{9,11},... | collective-permute-start | bytes 3538952 | tf_op jit(solution)/shard_map/ppermute | solution.py:55
  67.7 103.8 %collective-permute-start.6 = (bf16[256,2304]{0,1:T(8,128)(2,1)}, bf16[256,2304]{0,1:T(8,128)(2,1)}, u32[]{:S(2)}, u32[]{:S(2)}) collective-permute-start(bf16[256,2304]{0,1:T(8,128)(2,1)} %pad_maximum_fusion.8), channel_id=1, source_target_pairs={{0,0},{1,1},{2,16},{3,17},{4,4},{5,5},{6,20},{7,21},{8,8},{9,9},{1... | collective-permute-start | bytes 3538952 | tf_op jit(solution)/shard_map/ppermute | solution.py:55
  78.9 50.1 %collective-permute-start = (bf16[304,1024]{1,0:T(8,128)(2,1)}, bf16[304,1024]{1,0:T(8,128)(2,1)}, u32[]{:S(2)}, u32[]{:S(2)}) collective-permute-start(bf16[304,1024]{1,0:T(8,128)(2,1)} %dynamic-slice_bitcast_fusion.1), channel_id=1, source_target_pairs={{0,2},{1,3},{18,16},{19,17},{4,6},{5,7},{22,20},{23,21},{8,10},{9,... | collective-permute-start | bytes 1867784 | tf_op jit(solution)/shard_map/ppermute | solution.py:55
  129.1 41.5 %collective-permute-start.4 = (bf16[304,1024]{1,0:T(8,128)(2,1)S(1)}, bf16[304,1024]{1,0:T(8,128)(2,1)}, u32[]{:S(2)}, u32[]{:S(2)}) collective-permute-start(bf16[304,1024]{1,0:T(8,128)(2,1)S(1)} %bitcast_select_fusion.1), channel_id=1, source_target_pairs={{0,1},{1,0},{2,3},{3,2},{4,5},{5,4},{6,7},{7,6},{8,9},{9,8},{10,11... | collective-permute-start | bytes 1867784 | tf_op jit(solution)/shard_map/ppermute | solution.py:61
  170.6 7.9 %collective-permute-start.5 = (bf16[304,1024]{1,0:T(8,128)(2,1)}, bf16[304,1024]{1,0:T(8,128)(2,1)S(1)}, u32[]{:S(2)}, u32[]{:S(2)}) collective-permute-start(bf16[304,1024]{1,0:T(8,128)(2,1)} %collective-permute-done.4), channel_id=1, source_target_pairs={{0,16},{16,0},{1,17},{17,1},{2,18},{18,2},{3,19},{19,3},{4,20},{20... | collective-permute-start | bytes 1867784 | tf_op jit(solution)/shard_map/ppermute | solution.py:58
  171.3 8.0 %collective-permute-start.3 = (bf16[304,1024]{1,0:T(8,128)(2,1)S(1)}, bf16[304,1024]{1,0:T(8,128)(2,1)S(1)}, u32[]{:S(2)}, u32[]{:S(2)}) collective-permute-start(bf16[304,1024]{1,0:T(8,128)(2,1)S(1)} %bitcast_select_fusion.1), channel_id=1, source_target_pairs={{0,16},{16,0},{1,17},{17,1},{2,18},{18,2},{3,19},{19,3},{4,20},{20... | collective-permute-start | bytes 1867784 | tf_op jit(solution)/shard_map/ppermute | solution.py:58
  174.4 168.8 %all-gather.15.cloned.1.call-start = ((), (), s32[]{:S(2)}) async-start(), calls=%async_computation.3 | async-start | bytes 1966080 | tf_op jit(solution)/shard_map/all_gather | solution.py:71
  219.0 10.0 %collective-permute-start.8 = (bf16[608,256]{0,1:T(8,128)(2,1)S(1)}, bf16[608,256]{0,1:T(8,128)(2,1)S(1)}, u32[]{:S(2)}, u32[]{:S(2)}) collective-permute-start(bf16[608,256]{0,1:T(8,128)(2,1)S(1)} %bitcast.286), channel_id=1, source_target_pairs={{0,1},{1,0},{2,3},{3,2},{4,5},{5,4},{6,7},{7,6},{8,9},{9,8},{10,11... | collective-permute-start | bytes 933896 | tf_op jit(solution)/shard_map/ppermute | solution.py:61
  233.8 11.0 %collective-permute-start.11 = (f32[304,1024]{1,0:T(8,128)S(1)}, f32[304,1024]{1,0:T(8,128)S(1)}, u32[]{:S(2)}, u32[]{:S(2)}) collective-permute-start(f32[304,1024]{1,0:T(8,128)S(1)} %slice.419), channel_id=1, source_target_pairs={{0,16},{16,0},{1,17},{17,1},{2,18},{18,2},{3,19},{19,3},{4,20},{20... | collective-permute-start | bytes 3735560 | tf_op jit(solution)/shard_map/ppermute | solution.py:58
  233.9 2.0 collective-permute-start.16
  234.6 6.6 collective-permute-start.15
  242.1 140.8 %all-gather.19.cloned.1.call-start = ((), (), s32[]{:S(2)}) async-start(), calls=%async_computation.5 | async-start | bytes 5898240 | tf_op jit(solution)/shard_map/all_gather | solution.py:78
  242.1 17.0 %collective-permute-start.24 = (bf16[256,2304]{0,1:T(8,128)(2,1)}, bf16[256,2304]{0,1:T(8,128)(2,1)S(1)}, u32[]{:S(2)}, u32[]{:S(2)}) collective-permute-start(bf16[256,2304]{0,1:T(8,128)(2,1)} %pad_maximum_fusion.8), channel_id=1, source_target_pairs={{16,3},{17,2},{18,19},{19,18},{20,7},{21,6},{22,23},{23,22},{24,11... | collective-permute-start | bytes 3538952 | tf_op jit(solution)/shard_map/ppermute | solution.py:55
  242.9 24.1 %collective-permute-start.23 = (bf16[256,2304]{0,1:T(8,128)(2,1)}, bf16[256,2304]{0,1:T(8,128)(2,1)S(1)}, u32[]{:S(2)}, u32[]{:S(2)}) collective-permute-start(bf16[256,2304]{0,1:T(8,128)(2,1)} %pad_maximum_fusion.8), channel_id=1, source_target_pairs={{16,1},{17,0},{18,17},{19,16},{20,5},{21,4},{22,21},{23,20},{24,9}... | collective-permute-start | bytes 3538952 | tf_op jit(solution)/shard_map/ppermute | solution.py:55
  247.1 21.5 %collective-permute-start.12 = (bf16[304,1024]{1,0:T(8,128)(2,1)S(1)}, bf16[304,1024]{1,0:T(8,128)(2,1)S(1)}, u32[]{:S(2)}, u32[]{:S(2)}) collective-permute-start(bf16[304,1024]{1,0:T(8,128)(2,1)S(1)} %fusion.332), channel_id=1, source_target_pairs={{0,16},{16,0},{1,17},{17,1},{2,18},{18,2},{3,19},{19,3},{4,20},{20... | collective-permute-start | bytes 1867784 | tf_op jit(solution)/shard_map/ppermute | solution.py:58
  268.4 129.4 %all-gather.17.cloned.1.call-start = ((), (), s32[]{:S(2)}) async-start(), calls=%async_computation.4 | async-start | bytes 5898240 | tf_op jit(solution)/shard_map/all_gather | solution.py:78
  293.1 17.6 %collective-permute-start.13 = (f32[304,1024]{1,0:T(8,128)S(1)}, f32[304,1024]{1,0:T(8,128)S(1)}, u32[]{:S(2)}, u32[]{:S(2)}) collective-permute-start(f32[304,1024]{1,0:T(8,128)S(1)} %slice.430), channel_id=1, source_target_pairs={{0,16},{16,0},{1,17},{17,1},{2,18},{18,2},{3,19},{19,3},{4,20},{20... | collective-permute-start | bytes 3735560 | tf_op jit(solution)/shard_map/ppermute | solution.py:58
  308.1 8.0 %collective-permute-start.21 = (bf16[256,2304]{0,1:T(8,128)(2,1)}, bf16[256,2304]{0,1:T(8,128)(2,1)S(1)}, u32[]{:S(2)}, u32[]{:S(2)}) collective-permute-start(bf16[256,2304]{0,1:T(8,128)(2,1)} %pad_maximum_fusion.8), channel_id=1, source_target_pairs={{16,2},{17,3},{18,18},{19,19},{20,6},{21,7},{22,22},{23,23},{24,10... | collective-permute-start | bytes 3538952 | tf_op jit(solution)/shard_map/ppermute | solution.py:55
  308.9 7.2 collective-permute-start.20
  311.3 91.1 %copy-start.54 = (f32[304]{0:T(512)}, f32[304]{0:T(512)S(1)}, u32[]{:S(2)}) copy-start(f32[304]{0:T(512)S(1)} %broadcast_multiply_fusion.10) | copy-start | bytes 3652
  311.6 90.8 %copy-start.58 = (f32[304]{0:T(512)}, f32[304]{0:T(512)S(1)}, u32[]{:S(2)}) copy-start(f32[304]{0:T(512)S(1)} %add_rsqrt_fusion.2) | copy-start | bytes 3652
  313.4 28.0 %collective-permute-start.18 = (bf16[304,1024]{1,0:T(8,128)(2,1)}, bf16[304,1024]{1,0:T(8,128)(2,1)S(1)}, u32[]{:S(2)}, u32[]{:S(2)}) collective-permute-start(bf16[304,1024]{1,0:T(8,128)(2,1)} %add_convert_fusion.1), channel_id=1, source_target_pairs={{0,1},{1,0},{2,3},{3,2},{4,5},{5,4},{6,7},{7,6},{8,9},{9,8},{10,11... | collective-permute-start | bytes 1867784 | tf_op jit(solution)/shard_map/ppermute | solution.py:61
  314.5 31.9 %collective-permute-start.17 = (bf16[304,1024]{1,0:T(8,128)(2,1)}, bf16[304,1024]{1,0:T(8,128)(2,1)S(1)}, u32[]{:S(2)}, u32[]{:S(2)}) collective-permute-start(bf16[304,1024]{1,0:T(8,128)(2,1)} %add_convert_fusion.1), channel_id=1, source_target_pairs={{0,16},{16,0},{1,17},{17,1},{2,18},{18,2},{3,19},{19,3},{4,20},{20... | collective-permute-start | bytes 1867784 | tf_op jit(solution)/shard_map/ppermute | solution.py:58
  318.8 433.6 %all-reduce.3.cloned.1.call-start = ((), (), s32[]{:S(2)}) async-start(), calls=%async_computation.6 | async-start | bytes 262144 | tf_op jit(solution)/shard_map/psum | solution.py:299
  341.5 5.6 collective-permute-start.19
  382.7 9.8 %collective-permute-start.22 = (bf16[608,256]{0,1:T(8,128)(2,1)S(1)}, bf16[608,256]{0,1:T(8,128)(2,1)S(1)}, u32[]{:S(2)}, u32[]{:S(2)}) collective-permute-start(bf16[608,256]{0,1:T(8,128)(2,1)S(1)} %bitcast.285), channel_id=1, source_target_pairs={{0,1},{1,0},{2,3},{3,2},{4,5},{5,4},{6,7},{7,6},{8,9},{9,8},{10,11... | collective-permute-start | bytes 933896 | tf_op jit(solution)/shard_map/ppermute | solution.py:61
  399.5 3.0 collective-permute-start.25
  403.7 2.1 collective-permute-start.26
  422.1 6.0 collective-permute-start.27
  423.3 12.1 %collective-permute-start.31 = (bf16[304,1024]{1,0:T(8,128)(2,1)S(1)}, bf16[304,1024]{1,0:T(8,128)(2,1)S(1)}, u32[]{:S(2)}, u32[]{:S(2)}) collective-permute-start(bf16[304,1024]{1,0:T(8,128)(2,1)S(1)} %dynamic-slice_bitcast_fusion), channel_id=1, source_target_pairs={{0,2},{1,3},{18,16},{19,17},{4,6},{5,7},{22,20},{23,21},{8,10},{9,... | collective-permute-start | bytes 1867784 | tf_op jit(solution)/shard_map/ppermute | solution.py:55
  436.4 8.5 %collective-permute-start.32 = (bf16[304,1024]{1,0:T(8,128)(2,1)S(1)}, bf16[304,1024]{1,0:T(8,128)(2,1)}, u32[]{:S(2)}, u32[]{:S(2)}) collective-permute-start(bf16[304,1024]{1,0:T(8,128)(2,1)S(1)} %fusion.527), channel_id=1, source_target_pairs={{0,16},{16,0},{1,17},{17,1},{2,18},{18,2},{3,19},{19,3},{4,20},{20... | collective-permute-start | bytes 1867784 | tf_op jit(solution)/shard_map/ppermute | solution.py:58
  462.3 3.0 collective-permute-start.33
  469.9 2.1 collective-permute-start.34
  473.6 9.7 %collective-permute-start.35 = (bf16[608,256]{1,0:T(8,128)(2,1)S(1)}, bf16[608,256]{1,0:T(8,128)(2,1)S(1)}, u32[]{:S(2)}, u32[]{:S(2)}) collective-permute-start(bf16[608,256]{1,0:T(8,128)(2,1)S(1)} %convolution_convert_fusion.2), channel_id=1, source_target_pairs={{0,1},{1,0},{2,3},{3,2},{4,5},{5,4},{6,7},{7,6},{8,9},{9,8},{10,11... | collective-permute-start | bytes 933896 | tf_op jit(solution)/shard_map/ppermute | solution.py:61
  532.7 3.0 collective-permute-start.36
  536.2 16.1 %collective-permute-start.37 = (bf16[304,1024]{1,0:T(8,128)(2,1)S(1)}, bf16[304,1024]{1,0:T(8,128)(2,1)S(1)}, u32[]{:S(2)}, u32[]{:S(2)}) collective-permute-start(bf16[304,1024]{1,0:T(8,128)(2,1)S(1)} %fusion.334), channel_id=1, source_target_pairs={{0,1},{1,0},{2,3},{3,2},{4,5},{5,4},{6,7},{7,6},{8,9},{9,8},{10,11... | collective-permute-start | bytes 1867784 | tf_op jit(solution)/shard_map/ppermute | solution.py:61
  553.4 2.1 collective-permute-start.38
  572.4 3.0 collective-permute-start.39
  579.5 2.1 collective-permute-start.40
  583.2 9.5 %collective-permute-start.41 = (bf16[608,256]{1,0:T(8,128)(2,1)S(1)}, bf16[608,256]{1,0:T(8,128)(2,1)S(1)}, u32[]{:S(2)}, u32[]{:S(2)}) collective-permute-start(bf16[608,256]{1,0:T(8,128)(2,1)S(1)} %convolution_convert_fusion), channel_id=1, source_target_pairs={{0,1},{1,0},{2,3},{3,2},{4,5},{5,4},{6,7},{7,6},{8,9},{9,8},{10,11... | collective-permute-start | bytes 933896 | tf_op jit(solution)/shard_map/ppermute | solution.py:61
  645.5 3.0 collective-permute-start.42
  645.5 22.1 %collective-permute-start.29 = (bf16[304,1024]{1,0:T(8,128)(2,1)}, bf16[304,1024]{1,0:T(8,128)(2,1)S(1)}, u32[]{:S(2)}, u32[]{:S(2)}) collective-permute-start(bf16[304,1024]{1,0:T(8,128)(2,1)} %add_convert_fusion.1), channel_id=1, source_target_pairs={{2,0},{3,1},{18,2},{19,3},{6,4},{7,5},{22,6},{23,7},{10,8},{11,9},... | collective-permute-start | bytes 1867784 | tf_op jit(solution)/shard_map/ppermute | solution.py:55
  646.8 20.8 %collective-permute-start.30 = (bf16[304,1024]{1,0:T(8,128)(2,1)}, bf16[304,1024]{1,0:T(8,128)(2,1)S(1)}, u32[]{:S(2)}, u32[]{:S(2)}) collective-permute-start(bf16[304,1024]{1,0:T(8,128)(2,1)} %get-tuple-element.52), channel_id=1, source_target_pairs={{2,16},{3,17},{18,18},{19,19},{6,20},{7,21},{22,22},{23,23},{10,24... | collective-permute-start | bytes 1867784 | tf_op jit(solution)/shard_map/ppermute | solution.py:55
  649.9 37.3 %collective-permute-start.43 = (bf16[304,1024]{1,0:T(8,128)(2,1)}, bf16[304,1024]{1,0:T(8,128)(2,1)}, u32[]{:S(2)}, u32[]{:S(2)}) collective-permute-start(bf16[304,1024]{1,0:T(8,128)(2,1)} %fusion.335), channel_id=1, source_target_pairs={{0,1},{1,0},{2,3},{3,2},{4,5},{5,4},{6,7},{7,6},{8,9},{9,8},{10,11... | collective-permute-start | bytes 1867784 | tf_op jit(solution)/shard_map/ppermute | solution.py:61
  651.5 39.8 %collective-permute-start.14 = (bf16[304,1024]{1,0:T(8,128)(2,1)}, bf16[304,1024]{1,0:T(8,128)(2,1)}, u32[]{:S(2)}, u32[]{:S(2)}) collective-permute-start(bf16[304,1024]{1,0:T(8,128)(2,1)} %add_convert_fusion.1), channel_id=1, source_target_pairs={{0,0},{1,1},{16,2},{17,3},{4,4},{5,5},{20,6},{21,7},{8,8},{9,9},{2... | collective-permute-start | bytes 1867784 | tf_op jit(solution)/shard_map/ppermute | solution.py:55
  657.9 34.8 %collective-permute-start.28 = (bf16[304,1024]{1,0:T(8,128)(2,1)}, bf16[304,1024]{1,0:T(8,128)(2,1)}, u32[]{:S(2)}, u32[]{:S(2)}) collective-permute-start(bf16[304,1024]{1,0:T(8,128)(2,1)} %get-tuple-element.52), channel_id=1, source_target_pairs={{0,16},{1,17},{16,18},{17,19},{4,20},{5,21},{20,22},{21,23},{8,24}... | collective-permute-start | bytes 1867784 | tf_op jit(solution)/shard_map/ppermute | solution.py:55
  670.8 22.6 %collective-permute-start.51 = (f32[2,64,256]{2,1,0:T(8,128)}, f32[2,64,256]{2,1,0:T(8,128)}, u32[]{:S(2)}, u32[]{:S(2)}) collective-permute-start(f32[2,64,256]{2,1,0:T(8,128)} %pad_maximum_fusion.34), channel_id=1, source_target_pairs={{2,16},{3,17},{18,18},{19,19},{6,20},{7,21},{22,22},{23,23},{10,24... | collective-permute-start | bytes 393224 | tf_op jit(solution)/shard_map/ppermute | solution.py:55
  672.1 24.0 %collective-permute-start.49 = (f32[2,64,256]{2,1,0:T(8,128)}, f32[2,64,256]{2,1,0:T(8,128)}, u32[]{:S(2)}, u32[]{:S(2)}) collective-permute-start(f32[2,64,256]{2,1,0:T(8,128)} %pad_maximum_fusion.34), channel_id=1, source_target_pairs={{0,16},{1,17},{16,18},{17,19},{4,20},{5,21},{20,22},{21,23},{8,24}... | collective-permute-start | bytes 393224 | tf_op jit(solution)/shard_map/ppermute | solution.py:55
  687.2 66.8 %collective-permute-start.47 = (bf16[304,1024]{1,0:T(8,128)(2,1)S(1)}, bf16[304,1024]{1,0:T(8,128)(2,1)}, u32[]{:S(2)}, u32[]{:S(2)}) collective-permute-start(bf16[304,1024]{1,0:T(8,128)(2,1)S(1)} %copy-done.17), channel_id=1, source_target_pairs={{2,16},{3,17},{18,18},{19,19},{6,20},{7,21},{22,22},{23,23},{10,24... | collective-permute-start | bytes 1867784 | tf_op jit(solution)/shard_map/ppermute | solution.py:55
  691.3 20.0 %collective-permute-start.50 = (f32[2,64,256]{2,1,0:T(8,128)S(1)}, f32[2,64,256]{2,1,0:T(8,128)S(1)}, u32[]{:S(2)}, u32[]{:S(2)}) collective-permute-start(f32[2,64,256]{2,1,0:T(8,128)S(1)} %pad_maximum_fusion.33), channel_id=1, source_target_pairs={{2,0},{3,1},{18,2},{19,3},{6,4},{7,5},{22,6},{23,7},{10,8},{11,9},... | collective-permute-start | bytes 393224 | tf_op jit(solution)/shard_map/ppermute | solution.py:55
  692.7 18.6 %collective-permute-start.48 = (f32[2,64,256]{2,1,0:T(8,128)S(1)}, f32[2,64,256]{2,1,0:T(8,128)S(1)}, u32[]{:S(2)}, u32[]{:S(2)}) collective-permute-start(f32[2,64,256]{2,1,0:T(8,128)S(1)} %pad_maximum_fusion.33), channel_id=1, source_target_pairs={{0,0},{1,1},{16,2},{17,3},{4,4},{5,5},{20,6},{21,7},{8,8},{9,9},{2... | collective-permute-start | bytes 393224 | tf_op jit(solution)/shard_map/ppermute | solution.py:55
  693.4 60.5 %collective-permute-start.46 = (bf16[304,1024]{1,0:T(8,128)(2,1)}, bf16[304,1024]{1,0:T(8,128)(2,1)S(1)}, u32[]{:S(2)}, u32[]{:S(2)}) collective-permute-start(bf16[304,1024]{1,0:T(8,128)(2,1)} %fusion.174), channel_id=1, source_target_pairs={{2,0},{3,1},{18,2},{19,3},{6,4},{7,5},{22,6},{23,7},{10,8},{11,9},... | collective-permute-start | bytes 1867784 | tf_op jit(solution)/shard_map/ppermute | solution.py:55
  696.1 59.0 %collective-permute-start.45 = (bf16[304,1024]{1,0:T(8,128)(2,1)S(1)}, bf16[304,1024]{1,0:T(8,128)(2,1)S(1)}, u32[]{:S(2)}, u32[]{:S(2)}) collective-permute-start(bf16[304,1024]{1,0:T(8,128)(2,1)S(1)} %copy-done.17), channel_id=1, source_target_pairs={{0,16},{1,17},{16,18},{17,19},{4,20},{5,21},{20,22},{21,23},{8,24}... | collective-permute-start | bytes 1867784 | tf_op jit(solution)/shard_map/ppermute | solution.py:55
  713.0 42.1 %collective-permute-start.44 = (bf16[304,1024]{1,0:T(8,128)(2,1)}, bf16[304,1024]{1,0:T(8,128)(2,1)}, u32[]{:S(2)}, u32[]{:S(2)}) collective-permute-start(bf16[304,1024]{1,0:T(8,128)(2,1)} %fusion.174), channel_id=1, source_target_pairs={{0,0},{1,1},{16,2},{17,3},{4,4},{5,5},{20,6},{21,7},{8,8},{9,9},{2... | collective-permute-start | bytes 1867784 | tf_op jit(solution)/shard_map/ppermute | solution.py:55
  (118 other events, 1737.6 us)
Sparse Core Ops, SparseCore 0:
  21.0 36.9 all-gather.8
  65.4 55.1 all-gather.12
  174.5 55.7 all-gather.10
  242.2 38.2 all-gather.14
  282.2 56.9 all-gather.18
  340.8 56.9 all-gather.16
  713.1 39.2 all-reduce.2

commit v2 on v1

v2 whole, which is shorter than its diff:
```python
from functools import partial

import jax
import jax.numpy as jnp
from jax import lax
from jax.experimental import pallas as pl
from jax.experimental.pallas import tpu as pltpu
from jax.sharding import PartitionSpec as P

HEADS = 16
HD = 64
EPS = 1e-5
BF = jnp.bfloat16
F32 = jnp.float32
TQ = 128
CK = 256
SIZES = (2, 3, 4, 5, 6, 7, 8, 10)
TH = 512
VMEM = 48 << 20


def dot(a, b, dims):
    return lax.dot_general(a, b, (dims, ((), ())), preferred_element_type=F32)


def nn(a, b):
    return dot(a, b, ((1,), (0,)))


def nt(a, b):
    return dot(a, b, ((1,), (1,)))


def norm_stats(v):
    centred = v - jnp.mean(v, axis=-1, keepdims=True)
    inv = lax.rsqrt(jnp.mean(centred * centred, axis=-1, keepdims=True) + EPS)
    return centred * inv, inv


def norm_back(v, grad, gain):
    n, inv = norm_stats(v)
    e = grad * gain
    return inv * (e - jnp.mean(e, -1, keepdims=True) - n * jnp.mean(e * n, -1, keepdims=True))


class Place:
    def __init__(self):
        self.mp = lax.axis_size("mp")
        self.g = self.mp // 2
        self.c = lax.axis_index("section")
        self.z = lax.axis_index("mp")
        self.m = self.z // self.g
        self.p = self.z % self.g

    def send(self, value, route):
        pairs = []
        for c in range(2):
            for m in range(2):
                for p in range(self.g):
                    to = route(c, m, p)
                    if to is not None:
                        source = c * self.mp + m * self.g + p
                        pairs.append((source, to[0] * self.mp + to[1] * self.g + to[2]))
        return lax.ppermute(value, ("section", "mp"), pairs)

    def core(self, value):
        return lax.ppermute(value, "section", [(0, 1), (1, 0)])

    def chip(self, value, j):
        return lax.ppermute(value, "mp", [(z, z ^ j) for z in range(self.mp)])


def tie(value, *after):
    return lax.optimization_barrier((value,) + after)[0]


def high_low(v):
    high = v.astype(BF)
    return high, (v - high.astype(F32)).astype(BF)


def gather(block):
    return lax.all_gather(block, "dp", axis=0, tiled=True)


def sum_steps(place):
    count = lax.axis_size("dp")
    steps = [lambda value: value + place.chip(value, place.g)]
    bit = 1
    while bit < count:
        pairs = [(i, i ^ bit) for i in range(count)]
        steps.append(partial(lambda pairs, v: v + lax.ppermute(v, "dp", pairs), pairs))
        bit *= 2
    return steps


def move_qkv(place, qkv, qkv_bias, pre):
    weight = qkv[0].astype(BF).transpose(1, 0, 2).reshape(qkv.shape[2], -1)
    width = weight.shape[1]
    bias = jnp.stack(high_low(qkv_bias[0].reshape(-1)))
    pre = jnp.concatenate([v[0].astype(BF) for v in pre], axis=1)
    pre = jnp.pad(pre, ((0, 0), (0, width - pre.shape[1])))
    block = jnp.concatenate([weight, pre, jnp.pad(bias, ((0, 14), (0, 0)))], axis=0)
    got = [place.send(block, lambda c, m, p: (m, c ^ turn, p)) for turn in range(2)]
    first = place.m == 0
    split = [jnp.where(first, got[0], got[1]), jnp.where(first, got[1], got[0])]
    rows, prefix = weight.shape[0], pre.shape[0]
    third = width // 3
    full = gather(jnp.concatenate([v[:rows] for v in split], axis=1))
    out = []
    for l, v in enumerate(split):
        b = v[rows + prefix].astype(F32) + v[rows + prefix + 1].astype(F32)
        p = v[rows : rows + prefix]
        w = full[:, l * width : (l + 1) * width]
        out.append((got[1], w, b, (p[:, :third], p[:, third : 2 * third])))
    return out, full


def own_shard(place, l, out, up, up_bias, down):
    block = jnp.concatenate([up[0].astype(BF), down[0].astype(BF).T, out[0].astype(BF).T], axis=1)
    bias = jnp.stack(high_low(up_bias[0]))
    bias = jnp.pad(bias, ((0, 14), (0, block.shape[1] - bias.shape[1])))
    block = jnp.concatenate([block, bias], 0)
    got = [place.send(block, lambda c, m, p: (m, half, p) if c == l else None) for half in range(2)]
    return jnp.where(place.m == 0, got[0], got[1])


def cut_shard(shard, rows, ff):
    bias = shard[rows : rows + 2, :ff].astype(F32)
    shard = shard[:rows]
    return shard[:, :ff], shard[:, ff : 2 * ff], shard[:, 2 * ff :], bias[0] + bias[1]


def spread_heads(block, heads):
    if heads == 1:
        return block
    lane = lax.broadcasted_iota(jnp.int32, block.shape, 1) // HD
    return jnp.concatenate([jnp.where(lane == h, block, jnp.zeros_like(block)) for h in range(heads)], 0)

def own_columns(wide, heads):
    return jnp.concatenate([wide[h*HD:(h+1)*HD, h*TQ:(h+1)*TQ] for h in range(heads)], 0)

def widen(mask, heads):
    return mask if heads == 1 else jnp.concatenate([mask] * heads, axis=1)

def each_size(range_ref, t, body):
    for index, size in enumerate(SIZES):
        @pl.when(range_ref[t, 1] == index)
        def _():
            body(pl.multiple_of(range_ref[t, 0], TQ), size * TQ)

def window_mask(start, size, span_ref, heads):
    key = lax.broadcasted_iota(jnp.int32, (size, TQ), 0) + start
    return widen((key >= span_ref[0:1, :]) & (key < span_ref[1:2, :]), heads)

def attn_fwd(prefix, heads, range_ref, span_ref, qkv_ref, o_ref, lse_ref, vt_ref):
    w = heads * HD
    t = pl.program_id(0)
    @pl.when(t == 0)
    def _():
        for i in range(vt_ref.shape[1] // CK):
            at = slice(i * CK, (i + 1) * CK)
            vt_ref[:, at] = qkv_ref[at, 2*w:3*w].astype(F32).T.astype(BF)
    def body(start, size):
        q = spread_heads(qkv_ref[pl.ds(pl.multiple_of(t*TQ, TQ), TQ), 0:w] * BF(HD ** -0.5), heads)
        at = pl.ds(start, size)
        first = nt(qkv_ref[0:prefix, w:2*w], q)
        rest = nt(qkv_ref[at, w:2*w], q)
        rest = jnp.where(window_mask(start, size, span_ref, heads), rest, -1e30)
        peak = jnp.maximum(jnp.max(first, axis=0, keepdims=True), jnp.max(rest, axis=0, keepdims=True))
        first, rest = jnp.exp(first - peak), jnp.exp(rest - peak)
        total = jnp.sum(first, axis=0, keepdims=True) + jnp.sum(rest, axis=0, keepdims=True)
        acc = nn(vt_ref[:, 0:prefix], first.astype(BF)) + nn(vt_ref[:, at], rest.astype(BF))
        o_ref[...] = own_columns(acc * (1.0 / total), heads).T.astype(BF)
        lse = peak + jnp.log(total)
        for h in range(heads):
            lse_ref[h:h+1, :] = lse[:, h*TQ:(h+1)*TQ]
    each_size(range_ref, t, body)

def attn_bwd(prefix, heads, range_ref, span_ref, qkv_ref, lse_ref, o_ref, do_ref, out_ref, pre_ref,
             kt_ref, dk_ref, dv_ref):
    w = heads * HD
    t = pl.program_id(0)
    @pl.when(t == 0)
    def _():
        for i in range(kt_ref.shape[1] // CK):
            at = slice(i * CK, (i + 1) * CK)
            kt_ref[:, at] = qkv_ref[at, w:2*w].astype(F32).T.astype(BF)
        dk_ref[...] = jnp.zeros_like(dk_ref)
        dv_ref[...] = jnp.zeros_like(dv_ref)
    def body(start, size):
        here = pl.ds(pl.multiple_of(t*TQ, TQ), TQ)
        q = spread_heads(qkv_ref[here, 0:w] * BF(HD ** -0.5), heads)
        do = do_ref[...]
        both = (do.astype(F32) * o_ref[...].astype(F32)).T
        delta = jnp.concatenate([jnp.sum(both[h*HD:(h+1)*HD], axis=0, keepdims=True) for h in range(heads)], 1)
        do = spread_heads(do, heads)
        lse = jnp.concatenate([lse_ref[h:h+1, :] for h in range(heads)], 1)
        dq = 0.0
        for at, mask in ((pl.ds(0, prefix), None), (pl.ds(start, size), window_mask(start, size, span_ref, heads))):
            prob = jnp.exp(nt(qkv_ref[at, w:2*w], q) - lse)
            if mask is not None:
                prob = jnp.where(mask, prob, 0.0)
            ds = (prob * (nt(qkv_ref[at, 2*w:3*w], do) - delta)).astype(BF)
            dv_ref[at, :] += nn(prob.astype(BF), do)
            dk_ref[at, :] += nn(ds, q)
            dq = dq + nn(kt_ref[:, at], ds)
        out_ref[here, 0:w] = (own_columns(dq, heads) * HD ** -0.5).T.astype(BF)
    each_size(range_ref, t, body)
    @pl.when(t == pl.num_programs(0) - 1)
    def _():
        out_ref[:, w:2*w] = dk_ref[...].astype(BF)
        out_ref[:, 2*w:3*w] = dv_ref[...].astype(BF)
        pre_ref[0] = dk_ref[0:prefix, :]
        pre_ref[1] = dv_ref[0:prefix, :]

def whole(shape):
    return pl.BlockSpec(shape, lambda t, *_: (0,) * len(shape))

def attend(ranges, span, qkv, prefix, heads):
    n, w = qkv.shape[0], heads*HD
    return pl.pallas_call(
        partial(attn_fwd, prefix, heads),
        grid_spec=pltpu.PrefetchScalarGridSpec(
            num_scalar_prefetch=1, grid=(n//TQ,),
            in_specs=[pl.BlockSpec((2, TQ), lambda t, *_: (0, t)), whole(qkv.shape)],
            out_specs=[pl.BlockSpec((TQ, w), lambda t, *_: (t, 0)), pl.BlockSpec((heads, TQ), lambda t, *_: (0, t))],
            scratch_shapes=[pltpu.VMEM((w, n), BF)]),
        out_shape=[jax.ShapeDtypeStruct((n, w), BF), jax.ShapeDtypeStruct((heads, n), F32)],
        compiler_params=pltpu.CompilerParams(dimension_semantics=("arbitrary",), vmem_limit_bytes=VMEM), name="attend",
        cost_estimate=pl.CostEstimate(flops=2*n*n*w*2, bytes_accessed=n*w*8, transcendentals=n*n*heads),
    )(ranges, span, qkv)

def attend_back(ranges, span, qkv, lse, o, do, prefix, heads):
    n, w = qkv.shape[0], heads*HD
    tile = pl.BlockSpec((TQ, w), lambda t, *_: (t, 0))
    return pl.pallas_call(
        partial(attn_bwd, prefix, heads),
        grid_spec=pltpu.PrefetchScalarGridSpec(
            num_scalar_prefetch=1, grid=(n//TQ,),
            in_specs=[pl.BlockSpec((2, TQ), lambda t, *_: (0, t)), whole(qkv.shape),
                      pl.BlockSpec((heads, TQ), lambda t, *_: (0, t)), tile, tile],
            out_specs=[whole((n, 3*w)), whole((2, prefix, w))],
            scratch_shapes=[pltpu.VMEM((w, n), BF), pltpu.VMEM((n, w), F32), pltpu.VMEM((n, w), F32)]),
        out_shape=[jax.ShapeDtypeStruct((n, 3*w), BF), jax.ShapeDtypeStruct((2, prefix, w), F32)],
        compiler_params=pltpu.CompilerParams(dimension_semantics=("arbitrary",), vmem_limit_bytes=VMEM), name="attend_back",
        cost_estimate=pl.CostEstimate(flops=5*n*n*w*2, bytes_accessed=n*w*14, transcendentals=n*n*heads),
    )(ranges, span, qkv, lse, o, do)

def take_size(index):
    return sum(jnp.where(index == i, size, 0) for i, size in enumerate(SIZES))


def spans(lengths, length, prefix):
    ends = jnp.cumsum(lengths)
    starts = ends - lengths
    place = jnp.arange(prefix + length, dtype=jnp.int32) - prefix
    last = lengths.shape[0] - 1
    inside = (place[:, None] >= starts[None, :last]) & (place[:, None] < ends[None, :last])
    low = jnp.sum(jnp.where(inside, starts[None, :last] + prefix, 0), -1)
    high = jnp.sum(jnp.where(inside, ends[None, :last] + prefix, 0), -1)
    tl, th = low.reshape(-1, TQ), high.reshape(-1, TQ)
    tiles = (prefix + length) // TQ
    first = jnp.min(jnp.where(th > 0, tl, prefix + length), axis=1) // TQ
    size = (jnp.max(th, axis=1) + TQ - 1) // TQ - first
    index = jnp.sum((size[:, None] > jnp.array(SIZES)[None]).astype(jnp.int32), 1)
    first = jnp.minimum(first, tiles - take_size(index))
    return jnp.stack([first * TQ, index], 1).astype(jnp.int32), jnp.stack([low, high]).astype(jnp.int32)


def bell_parts(u):
    bell = jnp.exp(-0.5 * u * u)
    t = 1.0 / (1.0 + (0.3275911 * 0.5**0.5) * jnp.abs(u))
    tail = 1.061405429 * t - 1.453152027
    for k in (1.421413741, -0.284496736, 0.254829592):
        tail = tail * t + k
    tail = 0.5 * tail * t * bell
    return bell, jnp.where(u > 0, 1.0 - tail, tail)


def slope_of(u, bell, phi):
    return phi + u * (bell * 0.3989422804014327)


def feed_kernel(mode, cuts, refs):
    count = len(cuts)
    panels, refs = refs[: 2 * count], refs[2 * count :]
    (own_ref, other_ref), refs = refs[:2], refs[2:]
    biases = ()
    if mode != "back":
        biases, refs = refs[:count], refs[count:]
    if mode == "again":
        inputs, refs = refs[:2], refs[2:]
    if mode == "back":
        slope_ref, refs = refs[0], refs[1:]
    x_ref, acc_ref, *again = refs[-3:] if mode == "again" else refs[-2:]
    out_own_ref, out_other_ref, *kept = refs[: -2 - len(again)]
    rows = own_ref.shape[0]
    t = pl.program_id(0)

    @pl.when(t == 0)
    def _():
        x_ref[:rows] = own_ref[...]
        x_ref[rows:] = other_ref[...]
        if mode == "again":
            again[0][:rows] = inputs[0][...]
            again[0][rows:] = inputs[1][...]
        acc_ref[...] = jnp.zeros_like(acc_ref)

    def run(k):
        up_ref, down_ref = panels[2 * k], panels[2 * k + 1]
        if mode == "forward":
            u = nn(x_ref[...], up_ref[...]) + biases[k][...]
            bell, phi = bell_parts(u)
            if kept:
                kept[0][...] = slope_of(u, bell, phi).astype(BF)
            acc_ref[...] += nt((u * phi).astype(BF), down_ref[...])
        else:
            df = nn(x_ref[...], down_ref[...])
            if mode == "again":
                u = nn(again[0][...], up_ref[...]) + biases[k][...]
                slope = slope_of(u, *bell_parts(u))
            else:
                slope = slope_ref[...].astype(F32)
            acc_ref[...] += nt((df * slope).astype(BF), up_ref[...])

    for k, (first, last) in enumerate(cuts):
        if count == 1:
            run(k)
        else:
            pl.when((t >= first) & (t < last))(partial(run, k))

    @pl.when(t == pl.num_programs(0) - 1)
    def _():
        out_own_ref[...] = acc_ref[:rows]
        out_other_ref[...] = acc_ref[rows:].astype(BF)


def feed(mode, panels, own, other, biases=(), inputs=(), slopes=(), keep=False):
    rows, d = own.shape
    th = TH if all(units % TH == 0 for _, units in panels) else TH // 2
    specs, arrays, cuts, at = [], [], [], 0
    for panel, units in panels:
        steps = units // th
        low = partial(lambda at, steps, t: jnp.clip(t - at, 0, steps - 1), at, steps)
        if len(panels) == 1:
            low = lambda t: t
        specs.append(pl.BlockSpec((d, th), partial(lambda low, t: (0, low(t)), low)))
        specs.append(pl.BlockSpec((d, th), partial(lambda low, n, t: (0, n + low(t)), low, steps)))
        arrays += [panel, panel]
        cuts.append((at, at + steps))
        at += steps
    full = pl.BlockSpec((rows, d), lambda t: (0, 0))
    part = pl.BlockSpec((2 * rows, th), lambda t: (0, t))
    specs += [full, full]
    arrays += [own, other]
    if mode != "back":
        for k, bias in enumerate(biases):
            specs.append(pl.BlockSpec((1, th), specs[2 * k].index_map))
            arrays.append(bias)
    specs += [full] * len(inputs) + [part] * len(slopes)
    arrays += list(inputs) + list(slopes)
    outs = [jax.ShapeDtypeStruct((rows, d), F32), jax.ShapeDtypeStruct((rows, d), BF)]
    out_specs = [full, full]
    if keep:
        outs.append(jax.ShapeDtypeStruct((2 * rows, at * th), BF))
        out_specs.append(part)
    matmuls = 3 if mode == "again" else 2
    scratch = [pltpu.VMEM((2 * rows, d), BF), pltpu.VMEM((2 * rows, d), F32)]
    if mode == "again":
        scratch.append(pltpu.VMEM((2 * rows, d), BF))
    return pl.pallas_call(
        lambda *refs: feed_kernel(mode, cuts, refs),
        grid=(at,),
        in_specs=specs,
        out_specs=out_specs,
        out_shape=outs,
        scratch_shapes=scratch,
        compiler_params=pltpu.CompilerParams(
            dimension_semantics=("arbitrary",), vmem_limit_bytes=VMEM
        ),
        cost_estimate=pl.CostEstimate(
            flops=4 * matmuls * rows * d * at * th,
            bytes_accessed=4 * d * at * th,
            transcendentals=0,
        ),
        name="feed_" + mode,
    )(*arrays)


class Order:
    def __init__(self, place, prefix, rows):
        self.place, self.prefix, self.rows = place, prefix, rows
        self.length = prefix + place.mp * rows

    def start(self, j, i):
        place = self.place
        return self.prefix + ((place.c ^ i) * place.g + (place.p ^ j)) * self.rows

    def put(self, whole, block, j, i):
        return lax.dynamic_update_slice(whole, block, (self.start(j, i), 0))

    def get(self, whole, j, i):
        return lax.dynamic_slice(whole, (self.start(j, i), 0), (self.rows, whole.shape[1]))


def both_cores(place, mine, theirs):
    return mine + place.core(theirs).astype(F32)


def attention(place, order, blocks, weights, where):
    qkv_w, qkv_b, pre = weights
    prefix = order.prefix
    qkv = jnp.pad(
        jnp.concatenate([jnp.zeros_like(pre[0]), pre[0], pre[1]], axis=1),
        ((0, order.length - prefix), (0, 0)),
    )
    for (j, i), block in blocks.items():
        qkv = order.put(qkv, (nn(block, qkv_w) + qkv_b).astype(BF), j, i)
    return (qkv,) + tuple(attend(*where, qkv, prefix, qkv_w.shape[1] // 3 // HD))


def spread_rows(place, x_own):
    blocks = {}
    for j in range(place.g):
        blocks[j, 0] = x_own if j == 0 else place.chip(x_own, j)
        blocks[j, 1] = place.core(blocks[j, 0])
    return blocks


def out_project(place, order, x_own, o, outs, fixed):
    mine = [0.0, 0.0]
    for j in range(place.g):
        part = jnp.concatenate([order.get(o, j, i) for i in range(2)], 0)
        part = part if j == 0 else place.chip(part, j)
        for i in range(2):
            mine[i] = mine[i] + nt(part[i * order.rows : (i + 1) * order.rows], outs[j])
    a = x_own.astype(F32) + both_cores(place, mine[0], mine[1].astype(BF)) + fixed[0]
    x1 = norm_stats(a)[0] * fixed[2] + fixed[4]
    return a, x1


def out_back(place, order, dx1, a, outs, fixed):
    da = norm_back(a, dx1, fixed[2])
    low = da.astype(BF)
    both = jnp.concatenate([low, place.core(low)], 0)
    go = jnp.zeros((order.length, outs[0].shape[1]), BF)
    for j in range(place.g - 1, -1, -1):
        do = nn(both, outs[j]).astype(BF)
        do = do if j == 0 else place.chip(do, j)
        for i in range(2):
            go = order.put(go, do[i * order.rows : (i + 1) * order.rows], j, i)
    return da, go


def input_back(place, order, da, back, qkv_w):
    total = da
    for j in range(place.g - 1, -1, -1):
        other = nt(order.get(back, j, 1), qkv_w).astype(BF)
        summed = both_cores(place, nt(order.get(back, j, 0), qkv_w), other)
        total = total + (summed if j == 0 else place.chip(summed.astype(BF), j).astype(F32))
    return total.astype(BF)


def on_device(
    tokens,
    cotangent,
    lengths,
    qkv_weight,
    qkv_bias,
    out_weight,
    out_bias,
    up_weight,
    up_bias,
    down_weight,
    down_bias,
    norm_gain,
    norm_shift,
    prefix_keys,
    prefix_values,
):
    place = Place()
    g, mp, c, m, p = place.g, place.mp, place.c, place.m, place.p
    rows = tokens.shape[1]
    width, ff, dim = out_weight.shape[1], up_weight.shape[2], up_weight.shape[1]
    prefix = prefix_keys.shape[1]
    order = Order(place, prefix, rows)
    row_lengths = lax.dynamic_index_in_dim(lengths, m, 0, keepdims=False)[0]
    where = spans(row_lengths, mp * rows, prefix)
    fixed = jnp.concatenate([out_bias, down_bias, norm_gain[0], norm_shift[0]], 0)
    other = place.core(fixed)
    fixed = [jnp.where(c == 0, fixed, other), jnp.where(c == 0, other, fixed)]

    def own_rows(array):
        other = lax.dynamic_index_in_dim(array, 1 - m, 0, keepdims=False)[:, 0]
        same = lax.dynamic_index_in_dim(array, m, 0, keepdims=False)[:, 0]
        moved = place.send(other, lambda c, m, p: (c, 1 - m, p) if c == m else None)
        return jnp.where(c == m, same, moved)

    attn, full = move_qkv(place, qkv_weight, qkv_bias, (prefix_keys, prefix_values))
    x = own_rows(tie(tokens, attn[0][0]))
    raw = (out_weight, up_weight, up_bias, down_weight)

    def shard_of(l, *after):
        held = tie(raw, *after)
        return own_shard(place, l, *held)

    shard0 = shard_of(0, x)
    up0, down0, out0, bias0 = cut_shard(shard0, dim, ff)
    outs0 = [out0] + [place.chip(out0, j) for j in range(1, g)]
    first = jnp.concatenate([up0, down0] + outs0, axis=1)
    blocks = spread_rows(place, x)
    panel0 = gather(tie(first, full, blocks))
    shard1 = shard_of(1, first)
    shards1 = [cut_shard(shard1 if j == 0 else place.chip(shard1, j), dim, ff) for j in range(g)]
    second = jnp.concatenate([v[k] for k in range(3) for v in shards1], axis=1)
    bias1 = jnp.concatenate([v[3] for v in shards1])[None]
    panel1 = gather(tie(second, panel0))
    grad = own_rows(tie(cotangent, second))
    outs = []
    for panel, start in ((panel0, 2 * ff), (panel1, 2 * g * ff)):
        outs.append([panel[:, start + j * width : start + (j + 1) * width] for j in range(g)])

    qkv0, o0, lse0 = attention(place, order, blocks, attn[0][1:], where)
    a0, x1 = out_project(place, order, x, o0, outs[0], fixed[0])
    wide0 = spread_rows(place, x1.astype(BF))
    z = x1 + fixed[0][1]
    for j in range(g):
        mine, theirs = feed("forward", [(panel0, ff)], wide0[j, 0], wide0[j, 1], [bias0[None]])
        summed = both_cores(place, mine, theirs)
        z = z + (summed if j == 0 else place.chip(summed.astype(BF), j).astype(F32))
    z0 = z
    y0 = (norm_stats(z)[0] * fixed[0][3] + fixed[0][5]).astype(BF)

    blocks = spread_rows(place, y0)
    late = tie(shard0, blocks)
    late = [place.chip(late, j) for j in range(1, g)]
    qkv1, o1, lse1 = attention(place, order, tie(blocks, grad), attn[1][1:], where)
    a1, x1 = out_project(place, order, y0, o1, outs[1], fixed[1])
    low = x1.astype(BF)
    mine, theirs, slope = feed(
        "forward", [(panel1, g * ff)], low, place.core(low), [bias1], keep=True
    )
    z1 = x1 + both_cores(place, mine, theirs) + fixed[1][1]
    y1 = (norm_stats(z1)[0] * fixed[1][3] + fixed[1][5]).astype(BF)

    moved = [cut_shard(tie(v, o1), dim, ff) for v in late]
    rest = jnp.concatenate([v[k] for k in range(2) for v in moved], axis=1)
    rest_bias = jnp.concatenate([v[3] for v in moved])[None]
    rest = gather(tie(rest, panel1))

    def home(value, l, half):
        return place.send(value, lambda c, m, p: (l, c, p) if m == half else None)

    def home_kv(value, l):
        return place.send(value, lambda c, m, p: (l, c, p) if c == m else None)

    steps = sum_steps(place)

    dz = norm_back(z1, grad.astype(F32), fixed[1][3])
    low = dz.astype(BF)
    mine, theirs = feed("back", [(panel1, g * ff)], low, place.core(low), slopes=[slope])
    dx1 = dz + both_cores(place, mine, theirs)
    first = m == 0
    pair = [place.send(tie(jnp.where(first, y0, y1), mine), lambda c, m, p: (m, c, p))]
    pair += [place.send(tie(jnp.where(first, y1, y0), mine), lambda c, m, p: (1 - m, c, p))]
    results = [jnp.where(c == 0, pair[h], pair[1 - h]) for h in range(2)]
    da, go = out_back(place, order, dx1, a1, outs[1], fixed[1])
    back, kv1 = attend_back(*where, qkv1, lse1, o1, go, prefix, width // HD)
    back = tie(back, results)
    grad1 = input_back(place, order, da, back, attn[1][1])
    kv1 = steps[0](kv1)

    dz = norm_back(z0, grad1.astype(F32), fixed[0][3])
    low = dz.astype(BF)
    mine, theirs = feed(
        "again",
        [(panel0, ff), (rest, (g - 1) * ff)],
        low,
        place.core(low),
        [bias0[None], rest_bias],
        inputs=(wide0[0, 0], wide0[0, 1]),
    )
    gouts = [home(grad1, 1, h) for h in range(2)]
    kv1 = steps[1](tie(kv1, low))
    dx1 = dz + both_cores(place, mine, theirs)
    da, go = out_back(place, order, dx1, a0, outs[0], fixed[0])
    kv1 = tie(kv1, mine)
    for step in steps[2:]:
        kv1 = step(kv1)
    kv = home_kv(tie(kv1, go), 1)
    back, kv0 = attend_back(*where, qkv0, lse0, o0, go, prefix, width // HD)
    back = tie(back, gouts, kv)
    grad0 = input_back(place, order, da, back, attn[0][1])
    for step in steps:
        kv0 = step(kv0)
    gouts = [gouts[h] + home(grad0, 0, h) for h in range(2)]
    kv = kv + home_kv(kv0, 0)
    results = jnp.stack(results)[:, :, None]
    gouts = jnp.stack(gouts)[:, :, None]
    return results[None], gouts[None], kv[None, 0], kv[None, 1]


def solution(mesh):
    placed = (
        P(None, "mp", "dp", None),
        P(None, "mp", "dp", None),
        P(None, "dp", None),
        P("section", None, "dp", "mp"),
        P("section", None, "mp"),
        P("section", "mp", "dp"),
        P("section", None),
        P("section", "dp", "mp"),
        P("section", "mp"),
        P("section", "mp", "dp"),
        P("section", None),
        P("section", None, None),
        P("section", None, None),
        P("section", None, "mp"),
        P("section", None, "mp"),
    )
    return jax.shard_map(
        on_device,
        mesh=mesh,
        in_specs=placed,
        out_specs=(
            P("section", None, "mp", "dp", None),
            P("section", None, "mp", "dp", None),
            P("section", None, "mp"),
            P("section", None, "mp"),
        ),
        check_vma=False,
    )
```

time: 775 us -> 576 us (0.74)
  matrix products: 210 us -> 33.6 us
  Pallas kernels: 0 us -> 107 us
  waiting for transfers between devices: 189 us -> 278 us
  blocking collectives: 84.1 us -> 0 us
  other arithmetic: 90.5 us -> 28.4 us
  starting transfers between devices: 142 us -> 83.5 us
  local copies, waits for them, and re-layouts: 32.3 us -> 23.3 us
    dot_general x24 -> x0, matrix products: 111 us -> none  [the longest x4 28.9 us: attend_back(): gp = jnp.einsum('hqd,hkd->hqk', go, values, preferred_element_type=F32)]
    pallas_call x0 -> x9, Pallas kernels: none -> 107 us  [the longest x5 48.4 us: feed(): pl.pallas_call(lambda *refs: feed_kernel(mode, cuts, refs), grid=(at,), i...]
    ppermute x8 -> x15, waiting for transfers between devices: 69 us -> 176 us  [chip(): return lax.ppermute(value, 'mp', [(z, z ^ j) for z in range(self.mp)])]
    all_gather x2 -> x0, blocking collectives: 84.1 us -> none  [the longest x1 45.4 us: on_device(): flat = lax.all_gather(flat, ('section', 'mp'))]
    dot_general x30 -> x28, matrix products: 98.4 us -> 33.6 us  [dot(): return lax.dot_general(a, b, (dims, ((), ())), preferred_element_type=F32)]
    ppermute x26 -> x16, starting transfers between devices: 93.6 us -> 47.1 us  [send(): return lax.ppermute(value, ('section', 'mp'), pairs)]
    psum x1 -> x0, waiting for transfers between devices: 31.8 us -> none  [on_device(): kv = lax.psum(home(kv, 0) + home(kv, 1), 'dp')]
    ppermute x18 -> x23, starting transfers between devices: 39.3 us -> 11.1 us  [core(): return lax.ppermute(value, 'section', [(0, 1), (1, 0)])]
  transfers between devices with their start and end apart: 59 -> 62, of which waited for: 27 -> 32; matrix products, arithmetic and copies ran while one was open for 20% -> 11% of each run, Pallas kernels for 0% -> 14%
where the time goes in v2:
time: 576 us; the launch traced here: 569 us
  waiting for transfers between devices  278 us (48%)
  Pallas kernels  107 us (19%)
  starting transfers between devices  83.5 us (14%)
  matrix products  33.6 us (6%)
  other arithmetic  28.4 us (5%)
  local copies, waits for them, and re-layouts  23.3 us (4%)
  between operations  15.6 us (3%)
    ppermute x15, waiting for transfers between devices, chip(): return lax.ppermute(value, 'mp', [(z, z ^ j) for z in range(self.mp)])  176 us
    ppermute x16, waiting for transfers between devices, send(): return lax.ppermute(value, ('section', 'mp'), pairs)  60.2 us
    pallas_call x5, Pallas kernels, feed(): pl.pallas_call(lambda *refs: feed_kernel(mode, cuts, refs), grid=(at,), i...  48.4 us
    ppermute x16, starting transfers between devices, send(): return lax.ppermute(value, ('section', 'mp'), pairs)  47.1 us
    dot_general x28, matrix products, dot(): return lax.dot_general(a, b, (dims, ((), ())), preferred_element_type=F32)  33.6 us
    pallas_call x2, Pallas kernels, attend_back(): pl.pallas_call(partial(attn_bwd, prefix, heads), grid_spec=pltpu.Prefetch...  33.6 us
    pallas_call x2, Pallas kernels, attend(): pl.pallas_call(partial(attn_fwd, prefix, heads), grid_spec=pltpu.Prefetch...  24.7 us
    all_gather x4, waiting for transfers between devices, gather(): return lax.all_gather(block, 'dp', axis=0, tiled=True)  22.1 us
  transfers between devices with their start and end apart: 62, of which 32 were waited for; matrix products, arithmetic and copies ran while one was open for 11% of the time, Pallas kernels for 14%

profile of v2, /device:TPU:0, one launch (start us, length us, event | category | flops | bytes accessed | tf_op | source)
XLA Modules:
  0.0 569.4 jit_solution(7196399610372942160)
XLA Ops:
  10.3 4.1 collective-permute-start
  15.1 10.1 %collective-permute-done = bf16[336,768]{1,0:T(8,128)(2,1)S(1)} collective-permute-done((bf16[336,768]{1,0:T(8,128)(2,1)S(1)}, bf16[336,768]{1,0:T(8,128)(2,1)S(1)}, u32[]{:S(2)}, u32[]{:S(2)}) %collective-permute-start) | collective-permute-done | bytes 516128 | tf_op jit(solution)/shard_map/ppermute | solution.py:64
  28.7 13.6 %collective-permute-start.1 = (bf16[304,1024]{1,0:T(8,128)(2,1)}, bf16[304,1024]{1,0:T(8,128)(2,1)S(1)}, u32[]{:S(2)}, u32[]{:S(2)}) collective-permute-start(bf16[304,1024]{1,0:T(8,128)(2,1)} %dynamic-slice_bitcast_fusion.1), channel_id=1, source_target_pairs={{0,2},{1,3},{18,16},{19,17},{4,6},{5,7},{22,20},{23,21},{8,10},{9,... | collective-permute-start | bytes 1867784 | tf_op jit(solution)/shard_map/ppermute | solution.py:64
  42.3 8.0 %collective-permute-done.1 = bf16[304,1024]{1,0:T(8,128)(2,1)S(1)} collective-permute-done((bf16[304,1024]{1,0:T(8,128)(2,1)}, bf16[304,1024]{1,0:T(8,128)(2,1)S(1)}, u32[]{:S(2)}, u32[]{:S(2)}) %collective-permute-start.1) | collective-permute-done | bytes 622624 | tf_op jit(solution)/shard_map/ppermute | solution.py:64
  53.5 14.8 %collective-permute-start.7 = (bf16[272,2304]{1,0:T(8,128)(2,1)S(1)}, bf16[272,2304]{1,0:T(8,128)(2,1)S(1)}, u32[]{:S(2)}, u32[]{:S(2)}) collective-permute-start(bf16[272,2304]{1,0:T(8,128)(2,1)S(1)} %pad_maximum_fusion.1), channel_id=1, source_target_pairs={{0,2},{1,3},{2,18},{3,19},{4,6},{5,7},{6,22},{7,23},{8,10},{9,11},... | collective-permute-start | bytes 3760136 | tf_op jit(solution)/shard_map/ppermute | solution.py:64
  68.5 23.0 %collective-permute-done.4 = bf16[304,1024]{1,0:T(8,128)(2,1)S(1)} collective-permute-done((bf16[304,1024]{1,0:T(8,128)(2,1)}, bf16[304,1024]{1,0:T(8,128)(2,1)S(1)}, u32[]{:S(2)}, u32[]{:S(2)}) %collective-permute-start.4) | collective-permute-done | bytes 622624 | tf_op jit(solution)/shard_map/ppermute | solution.py:70
  92.3 3.3 collective-permute-start.8
  95.7 3.7 collective-permute-done.8
  104.5 2.8 collective-permute-done.21
  109.6 28.3 %collective-permute-done.23 = bf16[272,2304]{1,0:T(8,128)(2,1)S(1)} collective-permute-done((bf16[272,2304]{1,0:T(8,128)(2,1)S(1)}, bf16[272,2304]{1,0:T(8,128)(2,1)S(1)}, u32[]{:S(2)}, u32[]{:S(2)}) %collective-permute-start.23) | collective-permute-done | bytes 1253408 | tf_op jit(solution)/shard_map/ppermute | solution.py:70
  142.0 22.1 %all-gather.7.cloned.1.call-done.refs_0_.refs_1_ = bf16[1024,2560]{1,0:T(8,128)(2,1)} async-done(((bf16[256,2560]{1,0:T(8,128)(2,1)}), bf16[1024,2560]{1,0:T(8,128)(2,1)}) %all-gather.7.cloned.1.call-update) | async-done | bytes 5242896 | tf_op jit(solution)/shard_map/all_gather | solution.py:83
  166.7 2.4 fusion.8
  169.2 1.8 fusion.10
  171.7 1.7 fusion.14.qkv_ref
  173.4 12.4 %attend.2 = (bf16[1280,256]{1,0:T(8,128)(2,1)S(1)}, f32[4,1280]{1,0:T(4,128)S(1)}) custom-call(s32[10,2]{1,0:T(8,128)S(1)} %copy.75.range_ref, s32[2,1280]{1,0:T(2,128)S(1)} %pad_add_fusion.span_ref, bf16[1280,768]{1,0:T(8,128)(2,1)S(1)} %fusion.14.qkv_ref), custom_call_target="tpu_custom_call" | custom-call | flops 1677721600 | bytes 2621440 | tf_op jit(solution)/shard_map/attend/pallas_call | solution.py:222
  186.7 1.5 collective-permute-start.9
  189.7 6.4 %collective-permute-done.9 = bf16[608,256]{1,0:T(8,128)(2,1)} collective-permute-done((bf16[608,256]{1,0:T(8,128)(2,1)}, bf16[608,256]{1,0:T(8,128)(2,1)}, u32[]{:S(2)}, u32[]{:S(2)}) %collective-permute-start.9) | collective-permute-done | bytes 311328 | tf_op jit(solution)/shard_map/ppermute | solution.py:70
  196.1 1.5 fusion.4
  199.7 1.9 fusion.148
  202.2 1.6 collective-permute-start.14
  203.8 14.6 %collective-permute-done.14.refs_2_ = bf16[304,1024]{1,0:T(8,128)(2,1)S(1)} collective-permute-done((bf16[304,1024]{1,0:T(8,128)(2,1)S(1)}, bf16[304,1024]{1,0:T(8,128)(2,1)S(1)}, u32[]{:S(2)}, u32[]{:S(2)}) %collective-permute-start.14) | collective-permute-done | bytes 622624 | tf_op jit(solution)/shard_map/ppermute | solution.py:70
  218.9 1.5 collective-permute-done.15.refs_3_
  220.4 6.9 %feed_forward.4 = (f32[304,1024]{1,0:T(8,128)S(1)}, bf16[304,1024]{1,0:T(8,128)(2,1)S(1)}) custom-call(bf16[1024,2560]{1,0:T(8,128)(2,1)} %all-gather.7.cloned.1.call-done.refs_0_.refs_1_, bf16[1024,2560]{1,0:T(8,128)(2,1)} %all-gather.7.cloned.1.call-done.refs_0_.refs_1_, bf16[304,1024]{1,0:T(8,128)(2,1)S(1)} %collective-permute-done.14.refs_2_, ...), custom_call_target="tpu_custom_call" | custom-call | flops 2550136832 | bytes 4194304 | tf_op jit(solution)/shard_map/feed_forward/pallas_call | solution.py:372
  227.5 6.3 %feed_forward.3 = (f32[304,1024]{1,0:T(8,128)S(1)}, bf16[304,1024]{1,0:T(8,128)(2,1)S(1)}) custom-call(bf16[1024,2560]{1,0:T(8,128)(2,1)} %all-gather.7.cloned.1.call-done.refs_0_.refs_1_, bf16[1024,2560]{1,0:T(8,128)(2,1)} %all-gather.7.cloned.1.call-done.refs_0_.refs_1_, bf16[304,1024]{1,0:T(8,128)(2,1)S(1)} %fusion.25.refs_2_.refs_8_, ...), custom_call_target="tpu_custom_call" | custom-call | flops 2550136832 | bytes 4194304 | tf_op jit(solution)/shard_map/feed_forward/pallas_call | solution.py:372
  234.5 1.6 collective-permute-start.17
  236.0 14.6 %collective-permute-done.17 = bf16[304,1024]{1,0:T(8,128)(2,1)S(1)} collective-permute-done((bf16[304,1024]{1,0:T(8,128)(2,1)S(1)}, bf16[304,1024]{1,0:T(8,128)(2,1)S(1)}, u32[]{:S(2)}, u32[]{:S(2)}) %collective-permute-start.17) | collective-permute-done | bytes 622624 | tf_op jit(solution)/shard_map/ppermute | solution.py:70
  252.3 1.5 collective-permute-start.19
  253.8 4.2 collective-permute-start.24
  258.1 16.2 %collective-permute-done.19 = bf16[304,1024]{1,0:T(8,128)(2,1)S(1)} collective-permute-done((bf16[304,1024]{1,0:T(8,128)(2,1)S(1)}, bf16[304,1024]{1,0:T(8,128)(2,1)S(1)}, u32[]{:S(2)}, u32[]{:S(2)}) %collective-permute-start.19) | collective-permute-done | bytes 622624 | tf_op jit(solution)/shard_map/ppermute | solution.py:70
  279.8 12.3 %attend.3 = (bf16[1280,256]{1,0:T(8,128)(2,1)S(1)}, f32[4,1280]{1,0:T(4,128)S(1)}) custom-call(s32[10,2]{1,0:T(8,128)S(1)} %copy.75.range_ref, s32[2,1280]{1,0:T(2,128)S(1)} %pad_add_fusion.span_ref, bf16[1280,768]{1,0:T(8,128)(2,1)S(1)} %fusion.22.qkv_ref), custom_call_target="tpu_custom_call" | custom-call | flops 1677721600 | bytes 2621440 | tf_op jit(solution)/shard_map/attend/pallas_call | solution.py:222
  293.7 1.5 fusion.47
  295.2 8.6 %collective-permute-done.25 = bf16[608,256]{1,0:T(8,128)(2,1)} collective-permute-done((bf16[608,256]{1,0:T(8,128)(2,1)}, bf16[608,256]{1,0:T(8,128)(2,1)}, u32[]{:S(2)}, u32[]{:S(2)}) %collective-permute-start.25) | collective-permute-done | bytes 311328 | tf_op jit(solution)/shard_map/ppermute | solution.py:70
  303.8 1.5 fusion.5
  306.1 1.5 fusion.49
  307.6 1.7 fusion.149
  312.1 11.7 %feed_forward.5 = (f32[304,1024]{1,0:T(8,128)S(1)}, bf16[304,1024]{1,0:T(8,128)(2,1)S(1)}, bf16[608,2048]{1,0:T(8,128)(2,1)S(1)}) custom-call(bf16[1024,4608]{1,0:T(8,128)(2,1)} %all-gather.9.cloned.1.call-done.refs_0_.refs_1_, bf16[1024,4608]{1,0:T(8,128)(2,1)} %all-gather.9.cloned.1.call-done.refs_0_.refs_1_, bf16[304,1024]{1,0:T(8,128)(2,1)S(1)} %fusion.26.refs_2_, ...), custom_call_target="tpu_custom_call" | custom-call | flops 5100273664 | bytes 8388608 | tf_op jit(solution)/shard_map/feed_forward/pallas_call | solution.py:372
  324.3 1.7 collective-permute-done.28
  331.0 8.8 %feed_back.1 = (f32[304,1024]{1,0:T(8,128)S(1)}, bf16[304,1024]{1,0:T(8,128)(2,1)}) custom-call(bf16[1024,4608]{1,0:T(8,128)(2,1)} %all-gather.9.cloned.1.call-done.refs_0_.refs_1_, bf16[1024,4608]{1,0:T(8,128)(2,1)} %all-gather.9.cloned.1.call-done.refs_0_.refs_1_, bf16[304,1024]{1,0:T(8,128)(2,1)S(1)} %fusion.135.refs_2_, ...), custom_call_target="tpu_custom_call" | custom-call | flops 5100273664 | bytes 8388608 | tf_op jit(solution)/shard_map/feed_back/pallas_call | solution.py:372
  341.2 18.4 %collective-permute-done.39 = bf16[272,2304]{1,0:T(8,128)(2,1)S(1)} collective-permute-done((bf16[272,2304]{1,0:T(8,128)(2,1)S(1)}, bf16[272,2304]{1,0:T(8,128)(2,1)S(1)}, u32[]{:S(2)}, u32[]{:S(2)}) %collective-permute-start.39) | collective-permute-done | bytes 1253408 | tf_op jit(solution)/shard_map/ppermute | solution.py:70
  361.8 3.4 fusion.138
  368.3 1.5 convolution_convert_fusion.7
  370.2 21.6 %collective-permute-done.31 = bf16[304,1024]{1,0:T(8,128)(2,1)S(1)} collective-permute-done((bf16[304,1024]{1,0:T(8,128)(2,1)S(1)}, bf16[304,1024]{1,0:T(8,128)(2,1)S(1)}, u32[]{:S(2)}, u32[]{:S(2)}) %collective-permute-start.31) | collective-permute-done | bytes 622624 | tf_op jit(solution)/shard_map/ppermute | solution.py:64
  392.9 1.5 convolution_convert_fusion.6
  395.6 16.8 %attend_back.2 = (bf16[1280,768]{1,0:T(8,128)(2,1)S(1)}, f32[2,64,256]{2,1,0:T(8,128)S(1)}) custom-call(s32[10,2]{1,0:T(8,128)S(1)} %copy.75.range_ref, s32[2,1280]{1,0:T(2,128)S(1)} %pad_add_fusion.span_ref, bf16[1280,768]{1,0:T(8,128)(2,1)S(1)} %fusion.22.qkv_ref, f32[4,1280]{1,0:T(4,128)S(1)} %get-tuple-element.78.lse_ref, ...), custom_call_target="tpu_custom_call" | custom-call | flops 4194304000 | bytes 4587520 | tf_op jit(solution)/shard_map/attend_back/pallas_call | solution.py:237
  413.1 6.6 %collective-permute-start.35 = (bf16[304,1024]{1,0:T(8,128)(2,1)S(1)}, bf16[304,1024]{1,0:T(8,128)(2,1)S(1)}, u32[]{:S(2)}, u32[]{:S(2)}) collective-permute-start(bf16[304,1024]{1,0:T(8,128)(2,1)S(1)} %convolution_convert_fusion.3), channel_id=1, source_target_pairs={{0,16},{16,0},{1,17},{17,1},{2,18},{18,2},{3,19},{19,3},{4,20},{20... | collective-permute-start | bytes 1867784 | tf_op jit(solution)/shard_map/ppermute | solution.py:67
  422.5 15.9 %collective-permute-done.36 = bf16[304,1024]{1,0:T(8,128)(2,1)S(1)} collective-permute-done((bf16[304,1024]{1,0:T(8,128)(2,1)S(1)}, bf16[304,1024]{1,0:T(8,128)(2,1)S(1)}, u32[]{:S(2)}, u32[]{:S(2)}) %collective-permute-start.36) | collective-permute-done | bytes 622624 | tf_op jit(solution)/shard_map/ppermute | solution.py:70
  442.3 14.7 %feed_again.1 = (f32[304,1024]{1,0:T(8,128)S(1)}, bf16[304,1024]{1,0:T(8,128)(2,1)S(1)}) custom-call(bf16[1024,2560]{1,0:T(8,128)(2,1)} %all-gather.7.cloned.1.call-done.refs_0_.refs_1_, bf16[1024,2560]{1,0:T(8,128)(2,1)} %all-gather.7.cloned.1.call-done.refs_0_.refs_1_, bf16[1024,2048]{1,0:T(8,128)(2,1)} %all-gather.11.cloned.1.call-done.refs_2_.refs_3_, ...), custom_call_target="tpu_custom_call" | custom-call | flops 7650410496 | bytes 8388608 | tf_op jit(solution)/shard_map/feed_again/pallas_call | solution.py:372
  457.3 1.9 collective-permute-done.41
  459.2 2.0 fusion.137
  461.8 9.2 %collective-permute-done.45 = f32[2,64,256]{2,1,0:T(8,128)S(1)} collective-permute-done((f32[2,64,256]{2,1,0:T(8,128)S(1)}, f32[2,64,256]{2,1,0:T(8,128)S(1)}, u32[]{:S(2)}, u32[]{:S(2)}) %collective-permute-start.45) | collective-permute-done | bytes 131104 | tf_op jit(solution)/shard_map/ppermute | solution.py:70
  471.0 3.0 collective-permute-start.46
  474.0 3.7 collective-permute-done.46
  477.7 1.5 collective-permute-start.47
  479.3 1.5 convolution_convert_fusion.5
  483.4 1.7 convolution_convert_fusion.4
  485.1 3.6 collective-permute-done.43
  490.3 16.7 %attend_back.3 = (bf16[1280,768]{1,0:T(8,128)(2,1)S(1)}, f32[2,64,256]{2,1,0:T(8,128)S(1)}) custom-call(s32[10,2]{1,0:T(8,128)S(1)} %copy.75.range_ref, s32[2,1280]{1,0:T(2,128)S(1)} %pad_add_fusion.span_ref, bf16[1280,768]{1,0:T(8,128)(2,1)S(1)} %copy-done.1, f32[4,1280]{1,0:T(4,128)S(1)} %get-tuple-element.86.lse_ref, bf16[1280,256]{1,0:T(8,128)(2,1)S(1)} %copy-done.4, ...), custom_call_target="tpu_custom_call" | custom-call | flops 4194304000 | bytes 4587520 | tf_op jit(solution)/shard_map/attend_back/pallas_call | solution.py:237
  510.5 2.4 collective-permute-start.50
  512.9 3.1 collective-permute-start.54
  516.0 13.3 %collective-permute-done.54 = f32[2,64,256]{2,1,0:T(8,128)S(1)} collective-permute-done((f32[2,64,256]{2,1,0:T(8,128)S(1)}, f32[2,64,256]{2,1,0:T(8,128)S(1)}, u32[]{:S(2)}, u32[]{:S(2)}) %collective-permute-start.54) | collective-permute-done | bytes 131104 | tf_op jit(solution)/shard_map/ppermute | solution.py:70
  529.3 2.5 collective-permute-start.55
  533.3 1.5 collective-permute-done.55
  535.5 4.3 collective-permute-done.56
  543.8 17.6 %collective-permute-done.53 = bf16[304,1024]{1,0:T(8,128)(2,1)S(1)} collective-permute-done((bf16[304,1024]{1,0:T(8,128)(2,1)S(1)}, bf16[304,1024]{1,0:T(8,128)(2,1)S(1)}, u32[]{:S(2)}, u32[]{:S(2)}) %collective-permute-start.53) | collective-permute-done | bytes 622624 | tf_op jit(solution)/shard_map/ppermute | solution.py:64
  (337 shorter events, 82.4 us)
Async XLA Ops:
  7.2 93.4 %all-gather.5.cloned.1.call-start = ((), (), s32[]{:S(2)}) async-start(), calls=%async_computation | async-start | bytes 3932160 | tf_op jit(solution)/shard_map/all_gather | solution.py:83
  10.3 14.9 %collective-permute-start = (bf16[336,768]{1,0:T(8,128)(2,1)S(1)}, bf16[336,768]{1,0:T(8,128)(2,1)S(1)}, u32[]{:S(2)}, u32[]{:S(2)}) collective-permute-start(bf16[336,768]{1,0:T(8,128)(2,1)S(1)} %pad_maximum_fusion.10), channel_id=1, source_target_pairs={{0,2},{1,3},{2,18},{3,19},{16,0},{17,1},{18,16},{19,17},{4,6},{5,7... | collective-permute-start | bytes 1548296 | tf_op jit(solution)/shard_map/ppermute | solution.py:64
  14.4 10.8 %collective-permute-start.2 = (bf16[336,768]{1,0:T(8,128)(2,1)S(1)}, bf16[336,768]{1,0:T(8,128)(2,1)S(1)}, u32[]{:S(2)}, u32[]{:S(2)}) collective-permute-start(bf16[336,768]{1,0:T(8,128)(2,1)S(1)} %pad_maximum_fusion.10), channel_id=1, source_target_pairs={{0,0},{1,1},{2,16},{3,17},{16,2},{17,3},{18,18},{19,19},{4,4},{5,5... | collective-permute-start | bytes 1548296 | tf_op jit(solution)/shard_map/ppermute | solution.py:64
  27.2 136.8 %all-gather.7.cloned.1.call-start = ((), (), s32[]{:S(2)}) async-start(), calls=%async_computation.1 | async-start | bytes 6553600 | tf_op jit(solution)/shard_map/all_gather | solution.py:83
  28.7 21.7 %collective-permute-start.1 = (bf16[304,1024]{1,0:T(8,128)(2,1)}, bf16[304,1024]{1,0:T(8,128)(2,1)S(1)}, u32[]{:S(2)}, u32[]{:S(2)}) collective-permute-start(bf16[304,1024]{1,0:T(8,128)(2,1)} %dynamic-slice_bitcast_fusion.1), channel_id=1, source_target_pairs={{0,2},{1,3},{18,16},{19,17},{4,6},{5,7},{22,20},{23,21},{8,10},{9,... | collective-permute-start | bytes 1867784 | tf_op jit(solution)/shard_map/ppermute | solution.py:64
  52.8 38.7 %collective-permute-start.6 = (bf16[272,2304]{1,0:T(8,128)(2,1)S(1)}, bf16[272,2304]{1,0:T(8,128)(2,1)S(1)}, u32[]{:S(2)}, u32[]{:S(2)}) collective-permute-start(bf16[272,2304]{1,0:T(8,128)(2,1)S(1)} %pad_maximum_fusion.1), channel_id=1, source_target_pairs={{0,0},{1,1},{2,16},{3,17},{4,4},{5,5},{6,20},{7,21},{8,8},{9,9},{1... | collective-permute-start | bytes 3760136 | tf_op jit(solution)/shard_map/ppermute | solution.py:64
  53.5 38.0 %collective-permute-start.7 = (bf16[272,2304]{1,0:T(8,128)(2,1)S(1)}, bf16[272,2304]{1,0:T(8,128)(2,1)S(1)}, u32[]{:S(2)}, u32[]{:S(2)}) collective-permute-start(bf16[272,2304]{1,0:T(8,128)(2,1)S(1)} %pad_maximum_fusion.1), channel_id=1, source_target_pairs={{0,2},{1,3},{2,18},{3,19},{4,6},{5,7},{6,22},{7,23},{8,10},{9,11},... | collective-permute-start | bytes 3760136 | tf_op jit(solution)/shard_map/ppermute | solution.py:64
  68.4 23.1 %collective-permute-start.4 = (bf16[304,1024]{1,0:T(8,128)(2,1)}, bf16[304,1024]{1,0:T(8,128)(2,1)S(1)}, u32[]{:S(2)}, u32[]{:S(2)}) collective-permute-start(bf16[304,1024]{1,0:T(8,128)(2,1)} %bitcast_select_fusion.1), channel_id=1, source_target_pairs={{0,1},{1,0},{2,3},{3,2},{4,5},{5,4},{6,7},{7,6},{8,9},{9,8},{10,11... | collective-permute-start | bytes 1867784 | tf_op jit(solution)/shard_map/ppermute | solution.py:70
  68.4 32.2 %collective-permute-start.3 = (bf16[304,1024]{1,0:T(8,128)(2,1)}, bf16[304,1024]{1,0:T(8,128)(2,1)}, u32[]{:S(2)}, u32[]{:S(2)}) collective-permute-start(bf16[304,1024]{1,0:T(8,128)(2,1)} %bitcast_select_fusion.1), channel_id=1, source_target_pairs={{0,16},{16,0},{1,17},{17,1},{2,18},{18,2},{3,19},{19,3},{4,20},{20... | collective-permute-start | bytes 1867784 | tf_op jit(solution)/shard_map/ppermute | solution.py:67
  91.5 9.1 %collective-permute-start.5 = (bf16[304,1024]{1,0:T(8,128)(2,1)S(1)}, bf16[304,1024]{1,0:T(8,128)(2,1)}, u32[]{:S(2)}, u32[]{:S(2)}) collective-permute-start(bf16[304,1024]{1,0:T(8,128)(2,1)S(1)} %collective-permute-done.4), channel_id=1, source_target_pairs={{0,16},{16,0},{1,17},{17,1},{2,18},{18,2},{3,19},{19,3},{4,20},{20... | collective-permute-start | bytes 1867784 | tf_op jit(solution)/shard_map/ppermute | solution.py:67
  92.3 126.0 %copy-start.17 = (bf16[272,2304]{1,0:T(8,128)(2,1)}, bf16[272,2304]{1,0:T(8,128)(2,1)S(1)}, u32[]{:S(2)}) copy-start(bf16[272,2304]{1,0:T(8,128)(2,1)S(1)} %broadcast_select_fusion.1) | copy-start | bytes 3760132
  92.3 7.1 %collective-permute-start.8 = (bf16[256,256]{1,0:T(8,128)(2,1)S(1)}, bf16[256,256]{1,0:T(8,128)(2,1)S(1)}, u32[]{:S(2)}, u32[]{:S(2)}) collective-permute-start(bf16[256,256]{1,0:T(8,128)(2,1)S(1)} %slice.292), channel_id=1, source_target_pairs={{0,1},{1,0},{2,3},{3,2},{4,5},{5,4},{6,7},{7,6},{8,9},{9,8},{10,11... | collective-permute-start | bytes 393224 | tf_op jit(solution)/shard_map/ppermute | solution.py:70
  100.7 193.1 %all-gather.9.cloned.1.call-start = ((), (), s32[]{:S(2)}) async-start(), calls=%async_computation.2 | async-start | bytes 11796480 | tf_op jit(solution)/shard_map/all_gather | solution.py:83
  102.5 4.8 collective-permute-start.21
  103.8 3.5 collective-permute-start.22
  107.4 30.4 %collective-permute-start.23 = (bf16[272,2304]{1,0:T(8,128)(2,1)S(1)}, bf16[272,2304]{1,0:T(8,128)(2,1)S(1)}, u32[]{:S(2)}, u32[]{:S(2)}) collective-permute-start(bf16[272,2304]{1,0:T(8,128)(2,1)S(1)} %broadcast_select_fusion), channel_id=1, source_target_pairs={{0,1},{1,0},{2,3},{3,2},{4,5},{5,4},{6,7},{7,6},{8,9},{9,8},{10,11... | collective-permute-start | bytes 3760136 | tf_op jit(solution)/shard_map/ppermute | solution.py:70
  164.1 278.3 %all-gather.11.cloned.1.call-start = ((), (), s32[]{:S(2)}) async-start(), calls=%async_computation.3 | async-start | bytes 5242880 | tf_op jit(solution)/shard_map/all_gather | solution.py:83
  186.7 9.4 %collective-permute-start.9 = (bf16[608,256]{1,0:T(8,128)(2,1)}, bf16[608,256]{1,0:T(8,128)(2,1)}, u32[]{:S(2)}, u32[]{:S(2)}) collective-permute-start(bf16[608,256]{1,0:T(8,128)(2,1)} %pad_maximum_fusion.11), channel_id=1, source_target_pairs={{0,1},{1,0},{2,3},{3,2},{4,5},{5,4},{6,7},{7,6},{8,9},{9,8},{10,11... | collective-permute-start | bytes 933896 | tf_op jit(solution)/shard_map/ppermute | solution.py:70
  188.2 9.5 %collective-permute-start.11 = (f32[6,1024]{1,0:T(8,128)S(1)}, f32[6,1024]{1,0:T(8,128)S(1)}, u32[]{:S(2)}, u32[]{:S(2)}) collective-permute-start(f32[6,1024]{1,0:T(8,128)S(1)} %pad_maximum_fusion.13), channel_id=1, source_target_pairs={{0,16},{16,0},{1,17},{17,1},{2,18},{18,2},{3,19},{19,3},{4,20},{20... | collective-permute-start | bytes 73736 | tf_op jit(solution)/shard_map/ppermute | solution.py:67
  197.6 2.1 collective-permute-start.10
  201.6 49.0 %copy-start.7 = (f32[304,1024]{1,0:T(8,128)}, f32[304,1024]{1,0:T(8,128)S(1)}, u32[]{:S(2)}) copy-start(f32[304,1024]{1,0:T(8,128)S(1)} %get-tuple-element.165) | copy-start | bytes 3735556
  202.2 16.1 %collective-permute-start.14 = (bf16[304,1024]{1,0:T(8,128)(2,1)S(1)}, bf16[304,1024]{1,0:T(8,128)(2,1)S(1)}, u32[]{:S(2)}, u32[]{:S(2)}) collective-permute-start(bf16[304,1024]{1,0:T(8,128)(2,1)S(1)} %fusion.25.refs_2_.refs_8_), channel_id=1, source_target_pairs={{0,1},{1,0},{2,3},{3,2},{4,5},{5,4},{6,7},{7,6},{8,9},{9,8},{10,11... | collective-permute-start | bytes 1867784 | tf_op jit(solution)/shard_map/ppermute | solution.py:70
  218.3 2.1 collective-permute-start.15
  218.4 9.1 %collective-permute-start.12 = (bf16[304,1024]{1,0:T(8,128)(2,1)S(1)}, bf16[304,1024]{1,0:T(8,128)(2,1)S(1)}, u32[]{:S(2)}, u32[]{:S(2)}) collective-permute-start(bf16[304,1024]{1,0:T(8,128)(2,1)S(1)} %fusion.25.refs_2_.refs_8_), channel_id=1, source_target_pairs={{0,16},{16,0},{1,17},{17,1},{2,18},{18,2},{3,19},{19,3},{4,20},{20... | collective-permute-start | bytes 1867784 | tf_op jit(solution)/shard_map/ppermute | solution.py:67
  227.3 7.0 %collective-permute-start.16 = (bf16[304,1024]{1,0:T(8,128)(2,1)S(1)}, bf16[304,1024]{1,0:T(8,128)(2,1)S(1)}, u32[]{:S(2)}, u32[]{:S(2)}) collective-permute-start(bf16[304,1024]{1,0:T(8,128)(2,1)S(1)} %get-tuple-element.59), channel_id=1, source_target_pairs={{0,16},{16,0},{1,17},{17,1},{2,18},{18,2},{3,19},{19,3},{4,20},{20... | collective-permute-start | bytes 1867784 | tf_op jit(solution)/shard_map/ppermute | solution.py:67
  233.8 2.2 collective-permute-start.13
  234.5 16.1 %collective-permute-start.17 = (bf16[304,1024]{1,0:T(8,128)(2,1)S(1)}, bf16[304,1024]{1,0:T(8,128)(2,1)S(1)}, u32[]{:S(2)}, u32[]{:S(2)}) collective-permute-start(bf16[304,1024]{1,0:T(8,128)(2,1)S(1)} %add_convert_fusion.5), channel_id=1, source_target_pairs={{0,1},{1,0},{2,3},{3,2},{4,5},{5,4},{6,7},{7,6},{8,9},{9,8},{10,11... | collective-permute-start | bytes 1867784 | tf_op jit(solution)/shard_map/ppermute | solution.py:70
  252.3 22.0 %collective-permute-start.19 = (bf16[304,1024]{1,0:T(8,128)(2,1)S(1)}, bf16[304,1024]{1,0:T(8,128)(2,1)S(1)}, u32[]{:S(2)}, u32[]{:S(2)}) collective-permute-start(bf16[304,1024]{1,0:T(8,128)(2,1)S(1)} %add_convert_fusion.4), channel_id=1, source_target_pairs={{0,1},{1,0},{2,3},{3,2},{4,5},{5,4},{6,7},{7,6},{8,9},{9,8},{10,11... | collective-permute-start | bytes 1867784 | tf_op jit(solution)/shard_map/ppermute | solution.py:70
  253.8 22.4 %collective-permute-start.24 = (bf16[304,1024]{1,0:T(8,128)(2,1)S(1)}, bf16[304,1024]{1,0:T(8,128)(2,1)S(1)}, u32[]{:S(2)}, u32[]{:S(2)}) collective-permute-start(bf16[304,1024]{1,0:T(8,128)(2,1)S(1)} %dynamic-slice_bitcast_fusion), channel_id=1, source_target_pairs={{0,2},{1,3},{18,16},{19,17},{4,6},{5,7},{22,20},{23,21},{8,10},{9,... | collective-permute-start | bytes 1867784 | tf_op jit(solution)/shard_map/ppermute | solution.py:64
  258.0 19.1 %collective-permute-start.18 = (bf16[304,1024]{1,0:T(8,128)(2,1)S(1)}, bf16[304,1024]{1,0:T(8,128)(2,1)S(1)}, u32[]{:S(2)}, u32[]{:S(2)}) collective-permute-start(bf16[304,1024]{1,0:T(8,128)(2,1)S(1)} %add_convert_fusion.4), channel_id=1, source_target_pairs={{0,16},{16,0},{1,17},{17,1},{2,18},{18,2},{3,19},{19,3},{4,20},{20... | collective-permute-start | bytes 1867784 | tf_op jit(solution)/shard_map/ppermute | solution.py:67
  274.3 2.8 collective-permute-start.20
  293.7 10.1 %collective-permute-start.25 = (bf16[608,256]{1,0:T(8,128)(2,1)}, bf16[608,256]{1,0:T(8,128)(2,1)}, u32[]{:S(2)}, u32[]{:S(2)}) collective-permute-start(bf16[608,256]{1,0:T(8,128)(2,1)} %pad_maximum_fusion.12), channel_id=1, source_target_pairs={{0,1},{1,0},{2,3},{3,2},{4,5},{5,4},{6,7},{7,6},{8,9},{9,8},{10,11... | collective-permute-start | bytes 933896 | tf_op jit(solution)/shard_map/ppermute | solution.py:70
  305.3 2.3 collective-permute-start.26
  309.9 2.2 collective-permute-start.27
  323.8 2.1 collective-permute-start.28
  328.9 2.1 collective-permute-start.29
  329.7 29.8 %collective-permute-start.39 = (bf16[272,2304]{1,0:T(8,128)(2,1)S(1)}, bf16[272,2304]{1,0:T(8,128)(2,1)S(1)}, u32[]{:S(2)}, u32[]{:S(2)}) collective-permute-start(bf16[272,2304]{1,0:T(8,128)(2,1)S(1)} %copy-done.18), channel_id=1, source_target_pairs={{0,1},{1,0},{2,3},{3,2},{4,5},{5,4},{6,7},{7,6},{8,9},{9,8},{10,11... | collective-permute-start | bytes 3760136 | tf_op jit(solution)/shard_map/ppermute | solution.py:70
  340.8 21.0 %collective-permute-start.32 = (bf16[304,1024]{1,0:T(8,128)(2,1)}, bf16[304,1024]{1,0:T(8,128)(2,1)}, u32[]{:S(2)}, u32[]{:S(2)}) collective-permute-start(bf16[304,1024]{1,0:T(8,128)(2,1)} %get-tuple-element.77), channel_id=1, source_target_pairs={{0,16},{16,0},{1,17},{17,1},{2,18},{18,2},{3,19},{19,3},{4,20},{20... | collective-permute-start | bytes 1867784 | tf_op jit(solution)/shard_map/ppermute | solution.py:67
  365.7 2.6 collective-permute-start.33
  367.5 24.3 %collective-permute-start.31 = (bf16[304,1024]{1,0:T(8,128)(2,1)S(1)}, bf16[304,1024]{1,0:T(8,128)(2,1)S(1)}, u32[]{:S(2)}, u32[]{:S(2)}) collective-permute-start(bf16[304,1024]{1,0:T(8,128)(2,1)S(1)} %get-tuple-element.76), channel_id=1, source_target_pairs={{0,16},{1,17},{2,0},{3,1},{16,18},{17,19},{18,2},{19,3},{4,20},{5,... | collective-permute-start | bytes 1867784 | tf_op jit(solution)/shard_map/ppermute | solution.py:64
  367.6 24.2 %collective-permute-start.30 = (bf16[304,1024]{1,0:T(8,128)(2,1)S(1)}, bf16[304,1024]{1,0:T(8,128)(2,1)S(1)}, u32[]{:S(2)}, u32[]{:S(2)}) collective-permute-start(bf16[304,1024]{1,0:T(8,128)(2,1)S(1)} %get-tuple-element.75), channel_id=1, source_target_pairs={{0,0},{1,1},{2,16},{3,17},{16,2},{17,3},{18,18},{19,19},{4,4},{5,5... | collective-permute-start | bytes 1867784 | tf_op jit(solution)/shard_map/ppermute | solution.py:64
  369.8 24.7 %collective-permute-start.34 = (bf16[608,256]{1,0:T(8,128)(2,1)S(1)}, bf16[608,256]{1,0:T(8,128)(2,1)S(1)}, u32[]{:S(2)}, u32[]{:S(2)}) collective-permute-start(bf16[608,256]{1,0:T(8,128)(2,1)S(1)} %convolution_convert_fusion.7), channel_id=1, source_target_pairs={{0,1},{1,0},{2,3},{3,2},{4,5},{5,4},{6,7},{7,6},{8,9},{9,8},{10,11... | collective-permute-start | bytes 933896 | tf_op jit(solution)/shard_map/ppermute | solution.py:70
  413.1 8.3 %collective-permute-start.35 = (bf16[304,1024]{1,0:T(8,128)(2,1)S(1)}, bf16[304,1024]{1,0:T(8,128)(2,1)S(1)}, u32[]{:S(2)}, u32[]{:S(2)}) collective-permute-start(bf16[304,1024]{1,0:T(8,128)(2,1)S(1)} %convolution_convert_fusion.3), channel_id=1, source_target_pairs={{0,16},{16,0},{1,17},{17,1},{2,18},{18,2},{3,19},{19,3},{4,20},{20... | collective-permute-start | bytes 1867784 | tf_op jit(solution)/shard_map/ppermute | solution.py:67
  420.4 2.1 collective-permute-start.37
  422.1 16.4 %collective-permute-start.36 = (bf16[304,1024]{1,0:T(8,128)(2,1)S(1)}, bf16[304,1024]{1,0:T(8,128)(2,1)S(1)}, u32[]{:S(2)}, u32[]{:S(2)}) collective-permute-start(bf16[304,1024]{1,0:T(8,128)(2,1)S(1)} %add_convert_fusion.2), channel_id=1, source_target_pairs={{0,1},{1,0},{2,3},{3,2},{4,5},{5,4},{6,7},{7,6},{8,9},{9,8},{10,11... | collective-permute-start | bytes 1867784 | tf_op jit(solution)/shard_map/ppermute | solution.py:70
  440.3 2.1 collective-permute-start.40
  457.1 2.1 collective-permute-start.41
  461.6 17.7 %collective-permute-start.42 = (bf16[304,1024]{1,0:T(8,128)(2,1)S(1)}, bf16[304,1024]{1,0:T(8,128)(2,1)S(1)}, u32[]{:S(2)}, u32[]{:S(2)}) collective-permute-start(bf16[304,1024]{1,0:T(8,128)(2,1)S(1)} %get-tuple-element.122), channel_id=1, source_target_pairs={{0,16},{16,0},{1,17},{17,1},{2,18},{18,2},{3,19},{19,3},{4,20},{20... | collective-permute-start | bytes 1867784 | tf_op jit(solution)/shard_map/ppermute | solution.py:67
  461.8 9.2 %collective-permute-start.45 = (f32[2,64,256]{2,1,0:T(8,128)S(1)}, f32[2,64,256]{2,1,0:T(8,128)S(1)}, u32[]{:S(2)}, u32[]{:S(2)}) collective-permute-start(f32[2,64,256]{2,1,0:T(8,128)S(1)} %get-tuple-element.88), channel_id=1, source_target_pairs={{0,2},{1,3},{2,0},{3,1},{4,6},{5,7},{6,4},{7,5},{8,10},{9,11},{10,... | collective-permute-start | bytes 393224 | tf_op jit(solution)/shard_map/ppermute | solution.py:70
  471.0 6.7 %collective-permute-start.46 = (f32[2,64,256]{2,1,0:T(8,128)S(1)}, f32[2,64,256]{2,1,0:T(8,128)S(1)}, u32[]{:S(2)}, u32[]{:S(2)}) collective-permute-start(f32[2,64,256]{2,1,0:T(8,128)S(1)} %add.672), channel_id=1, source_target_pairs={{0,4},{4,0},{8,12},{12,8},{1,5},{5,1},{9,13},{13,9},{2,6},{6,2},{1... | collective-permute-start | bytes 393224 | tf_op jit(solution)/shard_map/ppermute | solution.py:92
  477.7 5.6 collective-permute-start.47
  480.8 7.8 %collective-permute-start.43 = (bf16[608,256]{1,0:T(8,128)(2,1)S(1)}, bf16[608,256]{1,0:T(8,128)(2,1)S(1)}, u32[]{:S(2)}, u32[]{:S(2)}) collective-permute-start(bf16[608,256]{1,0:T(8,128)(2,1)S(1)} %convolution_convert_fusion.5), channel_id=1, source_target_pairs={{0,1},{1,0},{2,3},{3,2},{4,5},{5,4},{6,7},{7,6},{8,9},{9,8},{10,11... | collective-permute-start | bytes 933896 | tf_op jit(solution)/shard_map/ppermute | solution.py:70
  481.3 25.7 %collective-permute-start.38 = (bf16[304,1024]{1,0:T(8,128)(2,1)S(1)}, bf16[304,1024]{1,0:T(8,128)(2,1)S(1)}, u32[]{:S(2)}, u32[]{:S(2)}) collective-permute-start(bf16[304,1024]{1,0:T(8,128)(2,1)S(1)} %copy-done.25), channel_id=1, source_target_pairs={{0,16},{1,17},{16,18},{17,19},{4,20},{5,21},{20,22},{21,23},{8,24}... | collective-permute-start | bytes 1867784 | tf_op jit(solution)/shard_map/ppermute | solution.py:64
  482.6 24.4 %collective-permute-start.44 = (bf16[304,1024]{1,0:T(8,128)(2,1)S(1)}, bf16[304,1024]{1,0:T(8,128)(2,1)S(1)}, u32[]{:S(2)}, u32[]{:S(2)}) collective-permute-start(bf16[304,1024]{1,0:T(8,128)(2,1)S(1)} %copy-done.25), channel_id=1, source_target_pairs={{2,16},{3,17},{18,18},{19,19},{6,20},{7,21},{22,22},{23,23},{10,24... | collective-permute-start | bytes 1867784 | tf_op jit(solution)/shard_map/ppermute | solution.py:64
  488.8 18.2 %collective-permute-start.48 = (f32[2,64,256]{2,1,0:T(8,128)S(1)}, f32[2,64,256]{2,1,0:T(8,128)S(1)}, u32[]{:S(2)}, u32[]{:S(2)}) collective-permute-start(f32[2,64,256]{2,1,0:T(8,128)S(1)} %add.674), channel_id=1, source_target_pairs={{0,16},{1,17},{18,18},{19,19},{4,20},{5,21},{22,22},{23,23},{8,24}... | collective-permute-start | bytes 393224 | tf_op jit(solution)/shard_map/ppermute | solution.py:64
  507.7 2.1 collective-permute-start.49
  508.5 23.4 %collective-permute-start.51 = (bf16[304,1024]{1,0:T(8,128)(2,1)S(1)}, bf16[304,1024]{1,0:T(8,128)(2,1)S(1)}, u32[]{:S(2)}, u32[]{:S(2)}) collective-permute-start(bf16[304,1024]{1,0:T(8,128)(2,1)S(1)} %convolution_convert_fusion), channel_id=1, source_target_pairs={{0,16},{16,0},{1,17},{17,1},{2,18},{18,2},{3,19},{19,3},{4,20},{20... | collective-permute-start | bytes 1867784 | tf_op jit(solution)/shard_map/ppermute | solution.py:67
  510.5 21.3 %collective-permute-start.50 = (bf16[304,1024]{1,0:T(8,128)(2,1)S(1)}, bf16[304,1024]{1,0:T(8,128)(2,1)S(1)}, u32[]{:S(2)}, u32[]{:S(2)}) collective-permute-start(bf16[304,1024]{1,0:T(8,128)(2,1)S(1)} %fusion.6), channel_id=1, source_target_pairs={{0,1},{1,0},{2,3},{3,2},{4,5},{5,4},{6,7},{7,6},{8,9},{9,8},{10,11... | collective-permute-start | bytes 1867784 | tf_op jit(solution)/shard_map/ppermute | solution.py:70
  512.9 16.4 %collective-permute-start.54 = (f32[2,64,256]{2,1,0:T(8,128)S(1)}, f32[2,64,256]{2,1,0:T(8,128)S(1)}, u32[]{:S(2)}, u32[]{:S(2)}) collective-permute-start(f32[2,64,256]{2,1,0:T(8,128)S(1)} %get-tuple-element.93), channel_id=1, source_target_pairs={{0,2},{1,3},{2,0},{3,1},{4,6},{5,7},{6,4},{7,5},{8,10},{9,11},{10,... | collective-permute-start | bytes 393224 | tf_op jit(solution)/shard_map/ppermute | solution.py:70
  529.3 5.5 collective-permute-start.55
  532.6 11.1 %collective-permute-start.52 = (bf16[304,1024]{1,0:T(8,128)(2,1)S(1)}, bf16[304,1024]{1,0:T(8,128)(2,1)S(1)}, u32[]{:S(2)}, u32[]{:S(2)}) collective-permute-start(bf16[304,1024]{1,0:T(8,128)(2,1)S(1)} %add_convert_fusion), channel_id=1, source_target_pairs={{0,0},{1,1},{16,2},{17,3},{4,4},{5,5},{20,6},{21,7},{8,8},{9,9},{2... | collective-permute-start | bytes 1867784 | tf_op jit(solution)/shard_map/ppermute | solution.py:64
  534.8 5.0 collective-permute-start.56
  539.9 3.1 collective-permute-start.57
  540.6 20.8 %collective-permute-start.53 = (bf16[304,1024]{1,0:T(8,128)(2,1)S(1)}, bf16[304,1024]{1,0:T(8,128)(2,1)S(1)}, u32[]{:S(2)}, u32[]{:S(2)}) collective-permute-start(bf16[304,1024]{1,0:T(8,128)(2,1)S(1)} %add_convert_fusion), channel_id=1, source_target_pairs={{2,0},{3,1},{18,2},{19,3},{6,4},{7,5},{22,6},{23,7},{10,8},{11,9},... | collective-permute-start | bytes 1867784 | tf_op jit(solution)/shard_map/ppermute | solution.py:64
  (48 other events, 323.5 us)
Sparse Core Ops, SparseCore 0:
  27.3 58.2 all-gather.4
  100.8 63.2 all-gather.6
  165.9 97.5 all-gather.8
  361.9 54.8 all-gather.10

commit v3 on v2

--- a/solution.py
+++ b/solution.py
@@ -83,37 +83,28 @@
     return lax.all_gather(block, "dp", axis=0, tiled=True)
 
 
-def sum_steps(place):
-    count = lax.axis_size("dp")
-    steps = [lambda value: value + place.chip(value, place.g)]
-    bit = 1
-    while bit < count:
-        pairs = [(i, i ^ bit) for i in range(count)]
-        steps.append(partial(lambda pairs, v: v + lax.ppermute(v, "dp", pairs), pairs))
-        bit *= 2
-    return steps
-
-
-def move_qkv(place, qkv, qkv_bias, pre):
+def own_layer(place, l, block):
+    return [place.send(block, lambda c, m, p: (m, half, p) if c == l else None) for half in range(2)]
+
+
+def merged(place, got):
+    return jnp.where(place.m == 0, got[0], got[1])
+
+
+def qkv_block(qkv, qkv_bias, pre):
     weight = qkv[0].astype(BF).transpose(1, 0, 2).reshape(qkv.shape[2], -1)
     width = weight.shape[1]
     bias = jnp.stack(high_low(qkv_bias[0].reshape(-1)))
     pre = jnp.concatenate([v[0].astype(BF) for v in pre], axis=1)
     pre = jnp.pad(pre, ((0, 0), (0, width - pre.shape[1])))
-    block = jnp.concatenate([weight, pre, jnp.pad(bias, ((0, 14), (0, 0)))], axis=0)
-    got = [place.send(block, lambda c, m, p: (m, c ^ turn, p)) for turn in range(2)]
-    first = place.m == 0
-    split = [jnp.where(first, got[0], got[1]), jnp.where(first, got[1], got[0])]
-    rows, prefix = weight.shape[0], pre.shape[0]
-    third = width // 3
-    full = gather(jnp.concatenate([v[:rows] for v in split], axis=1))
-    out = []
-    for l, v in enumerate(split):
-        b = v[rows + prefix].astype(F32) + v[rows + prefix + 1].astype(F32)
-        p = v[rows : rows + prefix]
-        w = full[:, l * width : (l + 1) * width]
-        out.append((got[1], w, b, (p[:, :third], p[:, third : 2 * third])))
-    return out, full
+    return jnp.concatenate([weight, pre, jnp.pad(bias, ((0, 14), (0, 0)))], axis=0)
+
+
+def cut_qkv(v, rows, prefix):
+    third = v.shape[1] // 3
+    bias = v[rows + prefix].astype(F32) + v[rows + prefix + 1].astype(F32)
+    pre = v[rows : rows + prefix]
+    return v[:rows], bias, (pre[:, :third], pre[:, third : 2 * third])
 
 
 def own_shard(place, l, out, up, up_bias, down):
@@ -121,8 +112,7 @@
     bias = jnp.stack(high_low(up_bias[0]))
     bias = jnp.pad(bias, ((0, 14), (0, block.shape[1] - bias.shape[1])))
     block = jnp.concatenate([block, bias], 0)
-    got = [place.send(block, lambda c, m, p: (m, half, p) if c == l else None) for half in range(2)]
-    return jnp.where(place.m == 0, got[0], got[1])
+    return own_layer(place, l, block)
 
 
 def cut_shard(shard, rows, ff):
@@ -228,7 +218,7 @@
             scratch_shapes=[pltpu.VMEM((w, n), BF)]),
         out_shape=[jax.ShapeDtypeStruct((n, w), BF), jax.ShapeDtypeStruct((heads, n), F32)],
         compiler_params=pltpu.CompilerParams(dimension_semantics=("arbitrary",), vmem_limit_bytes=VMEM), name="attend",
-        cost_estimate=pl.CostEstimate(flops=2*n*n*w*2, bytes_accessed=n*w*8, transcendentals=n*n*heads),
+        cost_estimate=pl.CostEstimate(flops=2*n*n*w*2//4000, bytes_accessed=1, transcendentals=0),
     )(ranges, span, qkv)
 
 def attend_back(ranges, span, qkv, lse, o, do, prefix, heads):
@@ -244,7 +234,7 @@
             scratch_shapes=[pltpu.VMEM((w, n), BF), pltpu.VMEM((n, w), F32), pltpu.VMEM((n, w), F32)]),
         out_shape=[jax.ShapeDtypeStruct((n, 3*w), BF), jax.ShapeDtypeStruct((2, prefix, w), F32)],
         compiler_params=pltpu.CompilerParams(dimension_semantics=("arbitrary",), vmem_limit_bytes=VMEM), name="attend_back",
-        cost_estimate=pl.CostEstimate(flops=5*n*n*w*2, bytes_accessed=n*w*14, transcendentals=n*n*heads),
+        cost_estimate=pl.CostEstimate(flops=5*n*n*w*2//4000, bytes_accessed=1, transcendentals=0),
     )(ranges, span, qkv, lse, o, do)
 
 def take_size(index):
@@ -380,8 +370,8 @@
             dimension_semantics=("arbitrary",), vmem_limit_bytes=VMEM
         ),
         cost_estimate=pl.CostEstimate(
-            flops=4 * matmuls * rows * d * at * th,
-            bytes_accessed=4 * d * at * th,
+            flops=4 * matmuls * rows * d * at * th // 4000,
+            bytes_accessed=1,
             transcendentals=0,
         ),
         name="feed_" + mode,
@@ -428,11 +418,14 @@
     return blocks
 
 
-def out_project(place, order, x_own, o, outs, fixed):
+def out_parts(place, order, o):
+    parts = [jnp.concatenate([order.get(o, j, i) for i in range(2)], 0) for j in range(place.g)]
+    return [part if j == 0 else place.chip(part, j) for j, part in enumerate(parts)]
+
+
+def out_project(place, order, x_own, parts, outs, fixed):
     mine = [0.0, 0.0]
-    for j in range(place.g):
-        part = jnp.concatenate([order.get(o, j, i) for i in range(2)], 0)
-        part = part if j == 0 else place.chip(part, j)
+    for j, part in enumerate(parts):
         for i in range(2):
             mine[i] = mine[i] + nt(part[i * order.rows : (i + 1) * order.rows], outs[j])
     a = x_own.astype(F32) + both_cores(place, mine[0], mine[1].astype(BF)) + fixed[0]
@@ -453,13 +446,28 @@
     return da, go
 
 
-def input_back(place, order, da, back, qkv_w):
-    total = da
+def swap_add(value, bit):
+    count = lax.axis_size("dp")
+    return value + lax.ppermute(value, "dp", [(i, i ^ bit) for i in range(count)])
+
+
+def input_back(place, order, da, back, qkv_w, kv=None):
+    total, bit = da, 1
+    if kv is not None:
+        kv = swap_add(kv, bit)
     for j in range(place.g - 1, -1, -1):
         other = nt(order.get(back, j, 1), qkv_w).astype(BF)
         summed = both_cores(place, nt(order.get(back, j, 0), qkv_w), other)
+        if kv is not None and bit == 1:
+            summed, kv = tie((summed, kv), kv)
+            bit = 2
         total = total + (summed if j == 0 else place.chip(summed.astype(BF), j).astype(F32))
-    return total.astype(BF)
+    if kv is None:
+        return total.astype(BF)
+    while bit < lax.axis_size("dp"):
+        kv = swap_add(kv, bit)
+        bit *= 2
+    return total.astype(BF), kv
 
 
 def on_device(
@@ -497,79 +505,89 @@
         moved = place.send(other, lambda c, m, p: (c, 1 - m, p) if c == m else None)
         return jnp.where(c == m, same, moved)
 
-    attn, full = move_qkv(place, qkv_weight, qkv_bias, (prefix_keys, prefix_values))
-    x = own_rows(tie(tokens, attn[0][0]))
+    block = qkv_block(qkv_weight, qkv_bias, (prefix_keys, prefix_values))
+    thin0 = merged(place, own_layer(place, 0, block))
+    w0, qkv_b0, pre0 = cut_qkv(thin0, dim, prefix)
+    w0 = gather(w0)
     raw = (out_weight, up_weight, up_bias, down_weight)
 
     def shard_of(l, *after):
         held = tie(raw, *after)
         return own_shard(place, l, *held)
 
-    shard0 = shard_of(0, x)
+    shard0 = merged(place, shard_of(0, thin0))
     up0, down0, out0, bias0 = cut_shard(shard0, dim, ff)
     outs0 = [out0] + [place.chip(out0, j) for j in range(1, g)]
-    first = jnp.concatenate([up0, down0] + outs0, axis=1)
+    thin1 = merged(place, own_layer(place, 1, tie(block, shard0)))
+    w1, qkv_b1, pre1 = cut_qkv(thin1, dim, prefix)
+    first = jnp.concatenate([up0, down0] + outs0 + [w1], axis=1)
+    panel0 = gather(tie(first, w0))
+    x = own_rows(tie(tokens, thin1))
     blocks = spread_rows(place, x)
-    panel0 = gather(tie(first, full, blocks))
-    shard1 = shard_of(1, first)
-    shards1 = [cut_shard(shard1 if j == 0 else place.chip(shard1, j), dim, ff) for j in range(g)]
-    second = jnp.concatenate([v[k] for k in range(3) for v in shards1], axis=1)
-    bias1 = jnp.concatenate([v[3] for v in shards1])[None]
-    panel1 = gather(tie(second, panel0))
-    grad = own_rows(tie(cotangent, second))
-    outs = []
-    for panel, start in ((panel0, 2 * ff), (panel1, 2 * g * ff)):
-        outs.append([panel[:, start + j * width : start + (j + 1) * width] for j in range(g)])
-
-    qkv0, o0, lse0 = attention(place, order, blocks, attn[0][1:], where)
-    a0, x1 = out_project(place, order, x, o0, outs[0], fixed[0])
-    wide0 = spread_rows(place, x1.astype(BF))
+    shard1 = shard_of(1, blocks)
+    qkv0, o0, lse0 = attention(place, order, blocks, (w0, qkv_b0, pre0), where)
+    parts = out_parts(place, order, o0)
+    shard1 = merged(place, tie(shard1, parts))
+    shards1 = [shard1] + [place.chip(shard1, j) for j in range(1, g)]
+    w1 = panel0[:, 2 * ff + g * width :]
+
+    def outs_of(panel, start):
+        return [panel[:, start + j * width : start + (j + 1) * width] for j in range(g)]
+
+    outs = [outs_of(tie(panel0, parts), 2 * ff)]
+    a0, x1 = out_project(place, order, x, parts, outs[0], fixed[0])
+    low = x1.astype(BF)
+    wide0 = [low] + [place.chip(low, j) for j in range(1, g)]
     z = x1 + fixed[0][1]
+    mine, sums = low, []
     for j in range(g):
-        mine, theirs = feed("forward", [(panel0, ff)], wide0[j, 0], wide0[j, 1], [bias0[None]])
+        own = tie(wide0[j], mine)
+        other = place.core(own)
+        if j == 0:
+            both0 = (own, other)
+        mine, theirs = feed("forward", [(panel0, ff)], own, other, [bias0[None]])
+        if j == 0:
+            shards1 = [cut_shard(v, dim, ff) for v in tie(shards1, mine)]
+            second = jnp.concatenate([v[k] for k in range(3) for v in shards1], axis=1)
+            bias1 = jnp.concatenate([v[3] for v in shards1])[None]
+            panel1 = gather(tie(second, panel0))
+            grad = own_rows(tie(cotangent, second))
+            outs.append(outs_of(panel1, 2 * g * ff))
         summed = both_cores(place, mine, theirs)
         z = z + (summed if j == 0 else place.chip(summed.astype(BF), j).astype(F32))
     z0 = z
     y0 = (norm_stats(z)[0] * fixed[0][3] + fixed[0][5]).astype(BF)
 
-    blocks = spread_rows(place, y0)
-    late = tie(shard0, blocks)
-    late = [place.chip(late, j) for j in range(1, g)]
-    qkv1, o1, lse1 = attention(place, order, tie(blocks, grad), attn[1][1:], where)
-    a1, x1 = out_project(place, order, y0, o1, outs[1], fixed[1])
+    blocks = tie(spread_rows(place, y0), grad)
+    qkv1, o1, lse1 = attention(place, order, blocks, (w1, qkv_b1, pre1), where)
+    a1, x1 = out_project(place, order, y0, out_parts(place, order, o1), outs[1], fixed[1])
     low = x1.astype(BF)
+    late = [place.chip(tie(shard0[:, : 2 * ff], low), j) for j in range(1, g)]
     mine, theirs, slope = feed(
         "forward", [(panel1, g * ff)], low, place.core(low), [bias1], keep=True
     )
     z1 = x1 + both_cores(place, mine, theirs) + fixed[1][1]
     y1 = (norm_stats(z1)[0] * fixed[1][3] + fixed[1][5]).astype(BF)
 
-    moved = [cut_shard(tie(v, o1), dim, ff) for v in late]
-    rest = jnp.concatenate([v[k] for k in range(2) for v in moved], axis=1)
-    rest_bias = jnp.concatenate([v[3] for v in moved])[None]
-    rest = gather(tie(rest, panel1))
-
     def home(value, l, half):
         return place.send(value, lambda c, m, p: (l, c, p) if m == half else None)
-
-    def home_kv(value, l):
-        return place.send(value, lambda c, m, p: (l, c, p) if c == m else None)
-
-    steps = sum_steps(place)
 
     dz = norm_back(z1, grad.astype(F32), fixed[1][3])
     low = dz.astype(BF)
     mine, theirs = feed("back", [(panel1, g * ff)], low, place.core(low), slopes=[slope])
-    dx1 = dz + both_cores(place, mine, theirs)
+    dx1 = tie(dz + both_cores(place, mine, theirs), late)
+
+    late = [cut_shard(v, dim, ff) for v in late]
+    rest = jnp.concatenate([v[k] for k in range(2) for v in late], axis=1)
+    rest_bias = jnp.concatenate([v[3] for v in late])[None]
+    rest = gather(tie(rest, panel1))
+
     first = m == 0
-    pair = [place.send(tie(jnp.where(first, y0, y1), mine), lambda c, m, p: (m, c, p))]
-    pair += [place.send(tie(jnp.where(first, y1, y0), mine), lambda c, m, p: (1 - m, c, p))]
-    results = [jnp.where(c == 0, pair[h], pair[1 - h]) for h in range(2)]
     da, go = out_back(place, order, dx1, a1, outs[1], fixed[1])
+    pair = [place.send(tie(jnp.where(first, y0, y1), go), lambda c, m, p: (m, c, p))]
     back, kv1 = attend_back(*where, qkv1, lse1, o1, go, prefix, width // HD)
-    back = tie(back, results)
-    grad1 = input_back(place, order, da, back, attn[1][1])
-    kv1 = steps[0](kv1)
+    back = tie(back, pair)
+    grad1 = input_back(place, order, da, back, w1)
 
     dz = norm_back(z0, grad1.astype(F32), fixed[0][3])
     low = dz.astype(BF)
@@ -579,23 +597,22 @@
         low,
         place.core(low),
         [bias0[None], rest_bias],
-        inputs=(wide0[0, 0], wide0[0, 1]),
+        inputs=both0,
     )
-    gouts = [home(grad1, 1, h) for h in range(2)]
-    kv1 = steps[1](tie(kv1, low))
+    swapped = tie(jnp.where(first, y1, y0), low)
+    pair.append(place.send(swapped, lambda c, m, p: (1 - m, c, p)))
+    results = [jnp.where(c == 0, pair[h], pair[1 - h]) for h in range(2)]
+    mine, theirs = tie((mine, theirs), pair)
     dx1 = dz + both_cores(place, mine, theirs)
     da, go = out_back(place, order, dx1, a0, outs[0], fixed[0])
-    kv1 = tie(kv1, mine)
-    for step in steps[2:]:
-        kv1 = step(kv1)
-    kv = home_kv(tie(kv1, go), 1)
+    gouts = [home(tie(grad1, go), 1, h) for h in range(2)]
     back, kv0 = attend_back(*where, qkv0, lse0, o0, go, prefix, width // HD)
-    back = tie(back, gouts, kv)
-    grad0 = input_back(place, order, da, back, attn[0][1])
-    for step in steps:
-        kv0 = step(kv0)
+    back = tie(back, gouts)
+    grad0, kv = input_back(place, order, da, back, w0, jnp.stack([kv0, kv1]))
     gouts = [gouts[h] + home(grad0, 0, h) for h in range(2)]
-    kv = kv + home_kv(kv0, 0)
+    kv = place.send(jnp.where(first, kv[0], kv[1]), lambda c, m, p: (m, c, p)) + place.send(
+        jnp.where(first, kv[1], kv[0]), lambda c, m, p: (1 - m, c, p)
+    )
     results = jnp.stack(results)[:, :, None]
     gouts = jnp.stack(gouts)[:, :, None]
     return results[None], gouts[None], kv[None, 0], kv[None, 1]

time: 576 us -> 546 us (0.948)
  waiting for transfers between devices: 278 us -> 232 us
  starting transfers between devices: 83.5 us -> 92 us
  Pallas kernels: 107 us -> 113 us
    ppermute x15 -> x13, waiting for transfers between devices: 176 us -> 149 us  [chip(): return lax.ppermute(value, 'mp', [(z, z ^ j) for z in range(self.mp)])]
    ppermute x15 -> x13, starting transfers between devices: 17.5 us -> 31.8 us  [chip(): return lax.ppermute(value, 'mp', [(z, z ^ j) for z in range(self.mp)])]
    ppermute x16 -> x18, waiting for transfers between devices: 60.2 us -> 46.7 us  [send(): return lax.ppermute(value, ('section', 'mp'), pairs)]
    all_gather x4, waiting for transfers between devices: 22.1 us -> 11.9 us  [gather(): return lax.all_gather(block, 'dp', axis=0, tiled=True)]
    ppermute x4 -> x2, starting transfers between devices: 7.73 us -> 0.07 us  [swap_add(): lax.ppermute(value, 'dp', [(i, i ^ bit) for i in range(count)])]
    ppermute x23, waiting for transfers between devices: 10.9 us -> 16.7 us  [core(): return lax.ppermute(value, 'section', [(0, 1), (1, 0)])]
    unnamed x106 -> x132, local copies, waits for them, and re-layouts: 16.6 us -> 13.7 us
    ppermute x16 -> x18, starting transfers between devices: 47.1 us -> 44.8 us  [send(): return lax.ppermute(value, ('section', 'mp'), pairs)]
  transfers between devices with their start and end apart: 62 -> 60, of which waited for: 32 -> 32; matrix products, arithmetic and copies ran while one was open for 11% -> 10% of each run, Pallas kernels for 14% -> 19%
where the time goes in v3:
time: 546 us; the launch traced here: 540 us
  waiting for transfers between devices  232 us (42%)
  Pallas kernels  113 us (21%)
  starting transfers between devices  92 us (17%)
  matrix products  35.1 us (6%)
  other arithmetic  29.1 us (5%)
  local copies, waits for them, and re-layouts  22.6 us (4%)
  between operations  15.7 us (3%)
    ppermute x13, waiting for transfers between devices, chip(): return lax.ppermute(value, 'mp', [(z, z ^ j) for z in range(self.mp)])  149 us
    pallas_call x5, Pallas kernels, feed(): pl.pallas_call(lambda *refs: feed_kernel(mode, cuts, refs), grid=(at,), i...  47.7 us
    ppermute x18, waiting for transfers between devices, send(): return lax.ppermute(value, ('section', 'mp'), pairs)  46.7 us
    ppermute x18, starting transfers between devices, send(): return lax.ppermute(value, ('section', 'mp'), pairs)  44.8 us
    pallas_call x2, Pallas kernels, attend_back(): pl.pallas_call(partial(attn_bwd, prefix, heads), grid_spec=pltpu.Prefetch...  38.3 us
    dot_general x28, matrix products, dot(): return lax.dot_general(a, b, (dims, ((), ())), preferred_element_type=F32)  35.1 us
    ppermute x13, starting transfers between devices, chip(): return lax.ppermute(value, 'mp', [(z, z ^ j) for z in range(self.mp)])  31.8 us
    pallas_call x2, Pallas kernels, attend(): pl.pallas_call(partial(attn_fwd, prefix, heads), grid_spec=pltpu.Prefetch...  26.9 us
  transfers between devices with their start and end apart: 60, of which 32 were waited for; matrix products, arithmetic and copies ran while one was open for 10% of the time, Pallas kernels for 19%

profile of v3, /device:TPU:0, one launch (start us, length us, event | category | flops | bytes accessed | tf_op | source)
XLA Modules:
  0.0 539.6 jit_solution(12835447576683331034)
XLA Ops:
  11.2 6.6 %collective-permute-start.1 = (bf16[336,768]{1,0:T(8,128)(2,1)S(1)}, bf16[336,768]{1,0:T(8,128)(2,1)S(1)}, u32[]{:S(2)}, u32[]{:S(2)}) collective-permute-start(bf16[336,768]{1,0:T(8,128)(2,1)S(1)} %pad_maximum_fusion.9), channel_id=1, source_target_pairs={{0,2},{1,3},{2,18},{3,19},{4,6},{5,7},{6,22},{7,23},{8,10},{9,11},... | collective-permute-start | bytes 1548296 | tf_op jit(solution)/shard_map/ppermute | solution.py:64
  17.8 6.6 %collective-permute-done.1 = bf16[336,768]{1,0:T(8,128)(2,1)S(1)} collective-permute-done((bf16[336,768]{1,0:T(8,128)(2,1)S(1)}, bf16[336,768]{1,0:T(8,128)(2,1)S(1)}, u32[]{:S(2)}, u32[]{:S(2)}) %collective-permute-start.1) | collective-permute-done | bytes 516128 | tf_op jit(solution)/shard_map/ppermute | solution.py:64
  27.7 10.6 %collective-permute-start.3 = (bf16[272,2304]{1,0:T(8,128)(2,1)S(1)}, bf16[272,2304]{1,0:T(8,128)(2,1)}, u32[]{:S(2)}, u32[]{:S(2)}) collective-permute-start(bf16[272,2304]{1,0:T(8,128)(2,1)S(1)} %pad_maximum_fusion.1), channel_id=1, source_target_pairs={{0,2},{1,3},{2,18},{3,19},{4,6},{5,7},{6,22},{7,23},{8,10},{9,11},... | collective-permute-start | bytes 3760136 | tf_op jit(solution)/shard_map/ppermute | solution.py:64
  40.2 11.6 %collective-permute-done.3 = bf16[272,2304]{1,0:T(8,128)(2,1)} collective-permute-done((bf16[272,2304]{1,0:T(8,128)(2,1)S(1)}, bf16[272,2304]{1,0:T(8,128)(2,1)}, u32[]{:S(2)}, u32[]{:S(2)}) %collective-permute-start.3) | collective-permute-done | bytes 1253408 | tf_op jit(solution)/shard_map/ppermute | solution.py:64
  51.7 1.4 broadcast_select_fusion.1
  55.2 14.9 %collective-permute-start.10 = (bf16[256,256]{1,0:T(8,128)(2,1)S(1)}, bf16[256,256]{1,0:T(8,128)(2,1)S(1)}, u32[]{:S(2)}, u32[]{:S(2)}) collective-permute-start(bf16[256,256]{1,0:T(8,128)(2,1)S(1)} %slice.300), channel_id=1, source_target_pairs={{0,1},{1,0},{2,3},{3,2},{4,5},{5,4},{6,7},{7,6},{8,9},{9,8},{10,11... | collective-permute-start | bytes 393224 | tf_op jit(solution)/shard_map/ppermute | solution.py:70
  70.1 4.6 collective-permute-done.4
  77.8 8.0 %collective-permute-start.13 = (f32[6,1024]{1,0:T(8,128)S(1)}, f32[6,1024]{1,0:T(8,128)}, u32[]{:S(2)}, u32[]{:S(2)}) collective-permute-start(f32[6,1024]{1,0:T(8,128)S(1)} %pad_maximum_fusion.14), channel_id=1, source_target_pairs={{0,16},{16,0},{1,17},{17,1},{2,18},{18,2},{3,19},{19,3},{4,20},{20... | collective-permute-start | bytes 73736 | tf_op jit(solution)/shard_map/ppermute | solution.py:67
  86.0 3.7 collective-permute-start.6
  90.1 7.4 %collective-permute-done.6 = bf16[304,1024]{1,0:T(8,128)(2,1)S(1)} collective-permute-done((bf16[304,1024]{1,0:T(8,128)(2,1)S(1)}, bf16[304,1024]{1,0:T(8,128)(2,1)S(1)}, u32[]{:S(2)}, u32[]{:S(2)}) %collective-permute-start.6) | collective-permute-done | bytes 622624 | tf_op jit(solution)/shard_map/ppermute | solution.py:64
  98.4 8.1 %collective-permute-start.8 = (bf16[304,1024]{1,0:T(8,128)(2,1)}, bf16[304,1024]{1,0:T(8,128)(2,1)}, u32[]{:S(2)}, u32[]{:S(2)}) collective-permute-start(bf16[304,1024]{1,0:T(8,128)(2,1)} %bitcast_select_fusion.1), channel_id=1, source_target_pairs={{0,1},{1,0},{2,3},{3,2},{4,5},{5,4},{6,7},{7,6},{8,9},{9,8},{10,11... | collective-permute-start | bytes 1867784 | tf_op jit(solution)/shard_map/ppermute | solution.py:70
  106.7 14.5 %collective-permute-done.8 = bf16[304,1024]{1,0:T(8,128)(2,1)} collective-permute-done((bf16[304,1024]{1,0:T(8,128)(2,1)}, bf16[304,1024]{1,0:T(8,128)(2,1)}, u32[]{:S(2)}, u32[]{:S(2)}) %collective-permute-start.8) | collective-permute-done | bytes 622624 | tf_op jit(solution)/shard_map/ppermute | solution.py:70
  123.3 2.5 fusion.8
  129.8 1.4 collective-permute-start.23
  131.2 2.2 collective-permute-start.24
  133.4 1.8 fusion.12
  135.2 1.8 fusion.14.qkv_ref
  137.9 13.4 %attend.2 = (bf16[1280,256]{1,0:T(8,128)(2,1)S(1)}, f32[4,1280]{1,0:T(4,128)S(1)}) custom-call(s32[10,2]{1,0:T(8,128)S(1)} %copy.77.range_ref, s32[2,1280]{1,0:T(2,128)S(1)} %pad_add_fusion.span_ref, bf16[1280,768]{1,0:T(8,128)(2,1)S(1)} %fusion.14.qkv_ref), custom_call_target="tpu_custom_call" | custom-call | flops 419430 | bytes 1 | tf_op jit(solution)/shard_map/attend/pallas_call | solution.py:212
  153.1 15.9 %collective-permute-done.11 = bf16[608,256]{1,0:T(8,128)(2,1)S(1)} collective-permute-done((bf16[608,256]{1,0:T(8,128)(2,1)S(1)}, bf16[608,256]{1,0:T(8,128)(2,1)S(1)}, u32[]{:S(2)}, u32[]{:S(2)}) %collective-permute-start.11) | collective-permute-done | bytes 311328 | tf_op jit(solution)/shard_map/ppermute | solution.py:70
  169.1 1.4 fusion.48
  170.5 1.4 fusion.4
  172.4 1.8 fusion.50
  174.2 1.9 fusion.132
  179.1 6.6 %feed_forward.3 = (f32[304,1024]{1,0:T(8,128)S(1)}, bf16[304,1024]{1,0:T(8,128)(2,1)S(1)}) custom-call(bf16[1024,3328]{1,0:T(8,128)(2,1)} %all-gather.7.cloned.1.call-done.refs_0_.refs_1_, bf16[1024,3328]{1,0:T(8,128)(2,1)} %all-gather.7.cloned.1.call-done.refs_0_.refs_1_, bf16[304,1024]{1,0:T(8,128)(2,1)S(1)} %fusion.25.refs_2_.refs_8_, ...), custom_call_target="tpu_custom_call" | custom-call | flops 637534 | bytes 1 | tf_op jit(solution)/shard_map/feed_forward/pallas_call | solution.py:362
  185.7 16.5 %collective-permute-done.25 = bf16[272,2304]{1,0:T(8,128)(2,1)S(1)} collective-permute-done((bf16[272,2304]{1,0:T(8,128)(2,1)S(1)}, bf16[272,2304]{1,0:T(8,128)(2,1)S(1)}, u32[]{:S(2)}, u32[]{:S(2)}) %collective-permute-start.25) | collective-permute-done | bytes 1253408 | tf_op jit(solution)/shard_map/ppermute | solution.py:70
  207.6 15.2 %collective-permute-done.16.refs_2_ = bf16[304,1024]{1,0:T(8,128)(2,1)S(1)} collective-permute-done((bf16[304,1024]{1,0:T(8,128)(2,1)S(1)}, bf16[304,1024]{1,0:T(8,128)(2,1)S(1)}, u32[]{:S(2)}, u32[]{:S(2)}) %collective-permute-start.16) | collective-permute-done | bytes 622624 | tf_op jit(solution)/shard_map/ppermute | solution.py:70
  222.9 2.0 collective-permute-done.17.refs_3_
  224.9 6.5 %feed_forward.4 = (f32[304,1024]{1,0:T(8,128)S(1)}, bf16[304,1024]{1,0:T(8,128)(2,1)S(1)}) custom-call(bf16[1024,3328]{1,0:T(8,128)(2,1)} %all-gather.7.cloned.1.call-done.refs_0_.refs_1_, bf16[1024,3328]{1,0:T(8,128)(2,1)} %all-gather.7.cloned.1.call-done.refs_0_.refs_1_, bf16[304,1024]{1,0:T(8,128)(2,1)S(1)} %collective-permute-done.16.refs_2_, ...), custom_call_target="tpu_custom_call" | custom-call | flops 637534 | bytes 1 | tf_op jit(solution)/shard_map/feed_forward/pallas_call | solution.py:362
  231.9 1.5 collective-permute-done.18
  234.4 15.4 %collective-permute-done.19 = bf16[304,1024]{1,0:T(8,128)(2,1)S(1)} collective-permute-done((bf16[304,1024]{1,0:T(8,128)(2,1)S(1)}, bf16[304,1024]{1,0:T(8,128)(2,1)S(1)}, u32[]{:S(2)}, u32[]{:S(2)}) %collective-permute-start.19) | collective-permute-done | bytes 622624 | tf_op jit(solution)/shard_map/ppermute | solution.py:70
  252.3 5.4 %collective-permute-start.26 = (bf16[304,1024]{1,0:T(8,128)(2,1)S(1)}, bf16[304,1024]{1,0:T(8,128)(2,1)S(1)}, u32[]{:S(2)}, u32[]{:S(2)}) collective-permute-start(bf16[304,1024]{1,0:T(8,128)(2,1)S(1)} %dynamic-slice_bitcast_fusion), channel_id=1, source_target_pairs={{0,2},{1,3},{18,16},{19,17},{4,6},{5,7},{22,20},{23,21},{8,10},{9,... | collective-permute-start | bytes 1867784 | tf_op jit(solution)/shard_map/ppermute | solution.py:64
  257.9 15.6 %collective-permute-done.21 = bf16[304,1024]{1,0:T(8,128)(2,1)S(1)} collective-permute-done((bf16[304,1024]{1,0:T(8,128)(2,1)S(1)}, bf16[304,1024]{1,0:T(8,128)(2,1)S(1)}, u32[]{:S(2)}, u32[]{:S(2)}) %collective-permute-start.21) | collective-permute-done | bytes 622624 | tf_op jit(solution)/shard_map/ppermute | solution.py:70
  278.9 13.6 %attend.3 = (bf16[1280,256]{1,0:T(8,128)(2,1)S(1)}, f32[4,1280]{1,0:T(4,128)S(1)}) custom-call(s32[10,2]{1,0:T(8,128)S(1)} %copy.77.range_ref, s32[2,1280]{1,0:T(2,128)S(1)} %pad_add_fusion.span_ref, bf16[1280,768]{1,0:T(8,128)(2,1)S(1)} %fusion.22.qkv_ref), custom_call_target="tpu_custom_call" | custom-call | flops 419430 | bytes 1 | tf_op jit(solution)/shard_map/attend/pallas_call | solution.py:212
  293.3 11.9 %all-gather.9.cloned.1.call-done.refs_0_.refs_1_ = bf16[1024,4608]{1,0:T(8,128)(2,1)} async-done(((bf16[256,4608]{1,0:T(8,128)(2,1)}), bf16[1024,4608]{1,0:T(8,128)(2,1)}) %all-gather.9.cloned.1.call-update) | async-done | bytes 9437200 | tf_op jit(solution)/shard_map/all_gather | solution.py:83
  306.6 1.5 fusion.5
  310.4 1.7 fusion.133
  314.9 11.9 %feed_forward.5 = (f32[304,1024]{1,0:T(8,128)S(1)}, bf16[304,1024]{1,0:T(8,128)(2,1)S(1)}, bf16[608,2048]{1,0:T(8,128)(2,1)S(1)}) custom-call(bf16[1024,4608]{1,0:T(8,128)(2,1)} %all-gather.9.cloned.1.call-done.refs_0_.refs_1_, bf16[1024,4608]{1,0:T(8,128)(2,1)} %all-gather.9.cloned.1.call-done.refs_0_.refs_1_, bf16[304,1024]{1,0:T(8,128)(2,1)S(1)} %fusion.26.refs_2_, ...), custom_call_target="tpu_custom_call" | custom-call | flops 1275068 | bytes 1 | tf_op jit(solution)/shard_map/feed_forward/pallas_call | solution.py:362
  327.2 1.7 collective-permute-done.30
  332.9 1.6 collective-permute-start.33
  334.4 8.0 %feed_back.1 = (f32[304,1024]{1,0:T(8,128)S(1)}, bf16[304,1024]{1,0:T(8,128)(2,1)S(1)}) custom-call(bf16[1024,4608]{1,0:T(8,128)(2,1)} %all-gather.9.cloned.1.call-done.refs_0_.refs_1_, bf16[1024,4608]{1,0:T(8,128)(2,1)} %all-gather.9.cloned.1.call-done.refs_0_.refs_1_, bf16[304,1024]{1,0:T(8,128)(2,1)S(1)} %fusion.120.refs_2_, ...), custom_call_target="tpu_custom_call" | custom-call | flops 1275068 | bytes 1 | tf_op jit(solution)/shard_map/feed_back/pallas_call | solution.py:362
  342.5 2.0 collective-permute-done.32
  345.1 14.7 %collective-permute-done.33 = bf16[272,2048]{1,0:T(8,128)(2,1)S(1)} collective-permute-done((bf16[272,2048]{1,0:T(8,128)(2,1)S(1)}, bf16[272,2048]{1,0:T(8,128)(2,1)S(1)}, u32[]{:S(2)}, u32[]{:S(2)}) %collective-permute-start.33) | collective-permute-done | bytes 1114144 | tf_op jit(solution)/shard_map/ppermute | solution.py:70
  360.2 1.7 fusion.124
  364.2 1.9 convolution_convert_fusion.7
  366.1 1.6 collective-permute-start.35
  369.1 2.4 convolution_convert_fusion.6
  371.5 4.1 collective-permute-done.35
  376.5 19.0 %attend_back.2 = (bf16[1280,768]{1,0:T(8,128)(2,1)S(1)}, f32[2,64,256]{2,1,0:T(8,128)S(1)}) custom-call(s32[10,2]{1,0:T(8,128)S(1)} %copy.77.range_ref, s32[2,1280]{1,0:T(2,128)S(1)} %pad_add_fusion.span_ref, bf16[1280,768]{1,0:T(8,128)(2,1)S(1)} %fusion.22.qkv_ref, f32[4,1280]{1,0:T(4,128)S(1)} %get-tuple-element.97.lse_ref, ...), custom_call_target="tpu_custom_call" | custom-call | flops 1048576 | bytes 1 | tf_op jit(solution)/shard_map/attend_back/pallas_call | solution.py:227
  396.3 3.7 collective-permute-start.37
  402.4 1.6 collective-permute-start.38
  404.0 14.8 %collective-permute-done.38 = bf16[304,1024]{1,0:T(8,128)(2,1)S(1)} collective-permute-done((bf16[304,1024]{1,0:T(8,128)(2,1)S(1)}, bf16[304,1024]{1,0:T(8,128)(2,1)S(1)}, u32[]{:S(2)}, u32[]{:S(2)}) %collective-permute-start.38) | collective-permute-done | bytes 622624 | tf_op jit(solution)/shard_map/ppermute | solution.py:70
  422.8 14.8 %feed_again.1 = (f32[304,1024]{1,0:T(8,128)S(1)}, bf16[304,1024]{1,0:T(8,128)(2,1)S(1)}) custom-call(bf16[1024,3328]{1,0:T(8,128)(2,1)} %all-gather.7.cloned.1.call-done.refs_0_.refs_1_, bf16[1024,3328]{1,0:T(8,128)(2,1)} %all-gather.7.cloned.1.call-done.refs_0_.refs_1_, bf16[1024,2048]{1,0:T(8,128)(2,1)} %all-gather.11.cloned.1.call-done.refs_2_.refs_3_, ...), custom_call_target="tpu_custom_call" | custom-call | flops 1912602 | bytes 1 | tf_op jit(solution)/shard_map/feed_again/pallas_call | solution.py:362
  438.8 2.0 collective-permute-done.42
  440.9 2.0 fusion.122
  443.5 1.9 collective-permute-done.43
  445.5 1.5 convolution_convert_fusion.5
  447.4 1.7 convolution_convert_fusion.4
  449.1 7.4 %collective-permute-done.44 = bf16[608,256]{1,0:T(8,128)(2,1)S(1)} collective-permute-done((bf16[608,256]{1,0:T(8,128)(2,1)S(1)}, bf16[608,256]{1,0:T(8,128)(2,1)S(1)}, u32[]{:S(2)}, u32[]{:S(2)}) %collective-permute-start.44) | collective-permute-done | bytes 311328 | tf_op jit(solution)/shard_map/ppermute | solution.py:70
  457.3 1.8 collective-permute-start.45
  459.2 19.3 %attend_back.3 = (bf16[1280,768]{1,0:T(8,128)(2,1)S(1)}, f32[2,64,256]{2,1,0:T(8,128)S(1)}) custom-call(s32[10,2]{1,0:T(8,128)S(1)} %copy.77.range_ref, s32[2,1280]{1,0:T(2,128)S(1)} %pad_add_fusion.span_ref, bf16[1280,768]{1,0:T(8,128)(2,1)S(1)} %copy-done.1, f32[4,1280]{1,0:T(4,128)S(1)} %get-tuple-element.107.lse_ref, bf16[1280,256]{1,0:T(8,128)(2,1)S(1)} %copy-done.3, ...), custom_call_target="tpu_custom_call" | custom-call | flops 1048576 | bytes 1 | tf_op jit(solution)/shard_map/attend_back/pallas_call | solution.py:227
  479.4 7.4 %collective-permute-done.48 = f32[2,2,64,256]{3,2,1,0:T(8,128)S(1)} collective-permute-done((f32[2,2,64,256]{3,2,1,0:T(8,128)S(1)}, f32[2,2,64,256]{3,2,1,0:T(8,128)S(1)}, u32[]{:S(2)}, u32[]{:S(2)}) %collective-permute-start.48) | collective-permute-done | bytes 262176 | tf_op jit(solution)/shard_map/ppermute | solution.py:451
  489.7 15.2 %collective-permute-done.49 = bf16[304,1024]{1,0:T(8,128)(2,1)S(1)} collective-permute-done((bf16[304,1024]{1,0:T(8,128)(2,1)S(1)}, bf16[304,1024]{1,0:T(8,128)(2,1)S(1)}, u32[]{:S(2)}, u32[]{:S(2)}) %collective-permute-start.49) | collective-permute-done | bytes 622624 | tf_op jit(solution)/shard_map/ppermute | solution.py:70
  508.8 5.0 collective-permute-start.55
  515.6 15.3 %collective-permute-done.55 = f32[2,64,256]{2,1,0:T(8,128)S(1)} collective-permute-done((f32[2,64,256]{2,1,0:T(8,128)S(1)}, f32[2,64,256]{2,1,0:T(8,128)S(1)}, u32[]{:S(2)}, u32[]{:S(2)}) %collective-permute-start.55) | collective-permute-done | bytes 131104 | tf_op jit(solution)/shard_map/ppermute | solution.py:64
  (362 shorter events, 81.3 us)
Async XLA Ops:
  7.2 69.9 %all-gather.5.cloned.1.call-start = ((), (), s32[]{:S(2)}) async-start(), calls=%async_computation | async-start | bytes 1966080 | tf_op jit(solution)/shard_map/all_gather | solution.py:83
  10.3 7.5 %collective-permute-start = (bf16[336,768]{1,0:T(8,128)(2,1)S(1)}, bf16[336,768]{1,0:T(8,128)(2,1)S(1)}, u32[]{:S(2)}, u32[]{:S(2)}) collective-permute-start(bf16[336,768]{1,0:T(8,128)(2,1)S(1)} %pad_maximum_fusion.9), channel_id=1, source_target_pairs={{0,0},{1,1},{2,16},{3,17},{4,4},{5,5},{6,20},{7,21},{8,8},{9,9},{1... | collective-permute-start | bytes 1548296 | tf_op jit(solution)/shard_map/ppermute | solution.py:64
  11.2 13.2 %collective-permute-start.1 = (bf16[336,768]{1,0:T(8,128)(2,1)S(1)}, bf16[336,768]{1,0:T(8,128)(2,1)S(1)}, u32[]{:S(2)}, u32[]{:S(2)}) collective-permute-start(bf16[336,768]{1,0:T(8,128)(2,1)S(1)} %pad_maximum_fusion.9), channel_id=1, source_target_pairs={{0,2},{1,3},{2,18},{3,19},{4,6},{5,7},{6,22},{7,23},{8,10},{9,11},... | collective-permute-start | bytes 1548296 | tf_op jit(solution)/shard_map/ppermute | solution.py:64
  26.9 12.2 %collective-permute-start.2 = (bf16[272,2304]{1,0:T(8,128)(2,1)S(1)}, bf16[272,2304]{1,0:T(8,128)(2,1)S(1)}, u32[]{:S(2)}, u32[]{:S(2)}) collective-permute-start(bf16[272,2304]{1,0:T(8,128)(2,1)S(1)} %pad_maximum_fusion.1), channel_id=1, source_target_pairs={{0,0},{1,1},{2,16},{3,17},{4,4},{5,5},{6,20},{7,21},{8,8},{9,9},{1... | collective-permute-start | bytes 3760136 | tf_op jit(solution)/shard_map/ppermute | solution.py:64
  27.7 24.0 %collective-permute-start.3 = (bf16[272,2304]{1,0:T(8,128)(2,1)S(1)}, bf16[272,2304]{1,0:T(8,128)(2,1)}, u32[]{:S(2)}, u32[]{:S(2)}) collective-permute-start(bf16[272,2304]{1,0:T(8,128)(2,1)S(1)} %pad_maximum_fusion.1), channel_id=1, source_target_pairs={{0,2},{1,3},{2,18},{3,19},{4,6},{5,7},{6,22},{7,23},{8,10},{9,11},... | collective-permute-start | bytes 3760136 | tf_op jit(solution)/shard_map/ppermute | solution.py:64
  39.1 130.0 %all-gather.7.cloned.1.call-start = ((), (), s32[]{:S(2)}) async-start(), calls=%async_computation.1 | async-start | bytes 8519680 | tf_op jit(solution)/shard_map/all_gather | solution.py:83
  53.2 21.6 %collective-permute-start.4 = (bf16[336,768]{1,0:T(8,128)(2,1)S(1)}, bf16[336,768]{1,0:T(8,128)(2,1)S(1)}, u32[]{:S(2)}, u32[]{:S(2)}) collective-permute-start(bf16[336,768]{1,0:T(8,128)(2,1)S(1)} %copy-done.44), channel_id=1, source_target_pairs={{16,0},{17,1},{18,16},{19,17},{20,4},{21,5},{22,20},{23,21},{24,8}... | collective-permute-start | bytes 1548296 | tf_op jit(solution)/shard_map/ppermute | solution.py:64
  54.5 20.3 %collective-permute-start.5 = (bf16[336,768]{1,0:T(8,128)(2,1)S(1)}, bf16[336,768]{1,0:T(8,128)(2,1)S(1)}, u32[]{:S(2)}, u32[]{:S(2)}) collective-permute-start(bf16[336,768]{1,0:T(8,128)(2,1)S(1)} %copy-done.44), channel_id=1, source_target_pairs={{16,2},{17,3},{18,18},{19,19},{20,6},{21,7},{22,22},{23,23},{24,10... | collective-permute-start | bytes 1548296 | tf_op jit(solution)/shard_map/ppermute | solution.py:64
  55.2 20.5 %collective-permute-start.10 = (bf16[256,256]{1,0:T(8,128)(2,1)S(1)}, bf16[256,256]{1,0:T(8,128)(2,1)S(1)}, u32[]{:S(2)}, u32[]{:S(2)}) collective-permute-start(bf16[256,256]{1,0:T(8,128)(2,1)S(1)} %slice.300), channel_id=1, source_target_pairs={{0,1},{1,0},{2,3},{3,2},{4,5},{5,4},{6,7},{7,6},{8,9},{9,8},{10,11... | collective-permute-start | bytes 393224 | tf_op jit(solution)/shard_map/ppermute | solution.py:70
  77.1 228.1 %all-gather.9.cloned.1.call-start = ((), (), s32[]{:S(2)}) async-start(), calls=%async_computation.2 | async-start | bytes 11796480 | tf_op jit(solution)/shard_map/all_gather | solution.py:83
  77.8 59.2 %collective-permute-start.13 = (f32[6,1024]{1,0:T(8,128)S(1)}, f32[6,1024]{1,0:T(8,128)}, u32[]{:S(2)}, u32[]{:S(2)}) collective-permute-start(f32[6,1024]{1,0:T(8,128)S(1)} %pad_maximum_fusion.14), channel_id=1, source_target_pairs={{0,16},{16,0},{1,17},{17,1},{2,18},{18,2},{3,19},{19,3},{4,20},{20... | collective-permute-start | bytes 73736 | tf_op jit(solution)/shard_map/ppermute | solution.py:67
  86.0 11.4 %collective-permute-start.6 = (bf16[304,1024]{1,0:T(8,128)(2,1)S(1)}, bf16[304,1024]{1,0:T(8,128)(2,1)S(1)}, u32[]{:S(2)}, u32[]{:S(2)}) collective-permute-start(bf16[304,1024]{1,0:T(8,128)(2,1)S(1)} %dynamic-slice_bitcast_fusion.1), channel_id=1, source_target_pairs={{0,2},{1,3},{18,16},{19,17},{4,6},{5,7},{22,20},{23,21},{8,10},{9,... | collective-permute-start | bytes 1867784 | tf_op jit(solution)/shard_map/ppermute | solution.py:64
  98.4 22.9 %collective-permute-start.8 = (bf16[304,1024]{1,0:T(8,128)(2,1)}, bf16[304,1024]{1,0:T(8,128)(2,1)}, u32[]{:S(2)}, u32[]{:S(2)}) collective-permute-start(bf16[304,1024]{1,0:T(8,128)(2,1)} %bitcast_select_fusion.1), channel_id=1, source_target_pairs={{0,1},{1,0},{2,3},{3,2},{4,5},{5,4},{6,7},{7,6},{8,9},{9,8},{10,11... | collective-permute-start | bytes 1867784 | tf_op jit(solution)/shard_map/ppermute | solution.py:70
  106.7 19.1 %collective-permute-start.7 = (bf16[304,1024]{1,0:T(8,128)(2,1)}, bf16[304,1024]{1,0:T(8,128)(2,1)S(1)}, u32[]{:S(2)}, u32[]{:S(2)}) collective-permute-start(bf16[304,1024]{1,0:T(8,128)(2,1)} %bitcast_select_fusion.1), channel_id=1, source_target_pairs={{0,16},{16,0},{1,17},{17,1},{2,18},{18,2},{3,19},{19,3},{4,20},{20... | collective-permute-start | bytes 1867784 | tf_op jit(solution)/shard_map/ppermute | solution.py:67
  121.3 5.2 collective-permute-start.9
  129.8 39.3 %collective-permute-start.23 = (bf16[272,2304]{1,0:T(8,128)(2,1)S(1)}, bf16[272,2304]{1,0:T(8,128)(2,1)S(1)}, u32[]{:S(2)}, u32[]{:S(2)}) collective-permute-start(bf16[272,2304]{1,0:T(8,128)(2,1)S(1)} %pad_maximum_fusion.2), channel_id=1, source_target_pairs={{16,0},{17,1},{18,16},{19,17},{20,4},{21,5},{22,20},{23,21},{24,8}... | collective-permute-start | bytes 3760136 | tf_op jit(solution)/shard_map/ppermute | solution.py:64
  131.2 37.9 %collective-permute-start.24 = (bf16[272,2304]{1,0:T(8,128)(2,1)S(1)}, bf16[272,2304]{1,0:T(8,128)(2,1)}, u32[]{:S(2)}, u32[]{:S(2)}) collective-permute-start(bf16[272,2304]{1,0:T(8,128)(2,1)S(1)} %pad_maximum_fusion.2), channel_id=1, source_target_pairs={{16,2},{17,3},{18,18},{19,19},{20,6},{21,7},{22,22},{23,23},{24,10... | collective-permute-start | bytes 3760136 | tf_op jit(solution)/shard_map/ppermute | solution.py:64
  152.2 16.9 %collective-permute-start.11 = (bf16[608,256]{1,0:T(8,128)(2,1)S(1)}, bf16[608,256]{1,0:T(8,128)(2,1)S(1)}, u32[]{:S(2)}, u32[]{:S(2)}) collective-permute-start(bf16[608,256]{1,0:T(8,128)(2,1)S(1)} %pad_maximum_fusion.11), channel_id=1, source_target_pairs={{0,1},{1,0},{2,3},{3,2},{4,5},{5,4},{6,7},{7,6},{8,9},{9,8},{10,11... | collective-permute-start | bytes 933896 | tf_op jit(solution)/shard_map/ppermute | solution.py:70
  171.9 2.3 collective-permute-start.12
  172.3 33.6 %copy-start.18 = (bf16[272,2304]{1,0:T(8,128)(2,1)}, bf16[272,2304]{1,0:T(8,128)(2,1)S(1)}, u32[]{:S(2)}) copy-start(bf16[272,2304]{1,0:T(8,128)(2,1)S(1)} %broadcast_select_fusion) | copy-start | bytes 3760132
  172.3 29.9 %collective-permute-start.25 = (bf16[272,2304]{1,0:T(8,128)(2,1)S(1)}, bf16[272,2304]{1,0:T(8,128)(2,1)S(1)}, u32[]{:S(2)}, u32[]{:S(2)}) collective-permute-start(bf16[272,2304]{1,0:T(8,128)(2,1)S(1)} %broadcast_select_fusion), channel_id=1, source_target_pairs={{0,1},{1,0},{2,3},{3,2},{4,5},{5,4},{6,7},{7,6},{8,9},{9,8},{10,11... | collective-permute-start | bytes 3760136 | tf_op jit(solution)/shard_map/ppermute | solution.py:70
  177.1 2.1 collective-permute-start.14
  207.2 215.5 %all-gather.11.cloned.1.call-start = ((), (), s32[]{:S(2)}) async-start(), calls=%async_computation.3 | async-start | bytes 5242880 | tf_op jit(solution)/shard_map/all_gather | solution.py:83
  207.3 15.6 %collective-permute-start.16 = (bf16[304,1024]{1,0:T(8,128)(2,1)S(1)}, bf16[304,1024]{1,0:T(8,128)(2,1)S(1)}, u32[]{:S(2)}, u32[]{:S(2)}) collective-permute-start(bf16[304,1024]{1,0:T(8,128)(2,1)S(1)} %fusion.25.refs_2_.refs_8_), channel_id=1, source_target_pairs={{0,1},{1,0},{2,3},{3,2},{4,5},{5,4},{6,7},{7,6},{8,9},{9,8},{10,11... | collective-permute-start | bytes 1867784 | tf_op jit(solution)/shard_map/ppermute | solution.py:70
  222.9 2.1 collective-permute-start.17
  231.4 2.1 collective-permute-start.18
  231.6 2.8 collective-permute-start.15
  233.5 42.8 %slice-start = ((s8[6815744]{0:T(1024)(128)(4,1)}), s8[2621440]{0:T(1024)(128)(4,1)S(1)}, s32[]{:S(2)}) async-start(s8[6815744]{0:T(1024)(128)(4,1)} %bitcast.137), calls=%async_computation.4 | async-start | bytes 5242880
  233.7 16.1 %collective-permute-start.19 = (bf16[304,1024]{1,0:T(8,128)(2,1)S(1)}, bf16[304,1024]{1,0:T(8,128)(2,1)S(1)}, u32[]{:S(2)}, u32[]{:S(2)}) collective-permute-start(bf16[304,1024]{1,0:T(8,128)(2,1)S(1)} %add_convert_fusion.4), channel_id=1, source_target_pairs={{0,1},{1,0},{2,3},{3,2},{4,5},{5,4},{6,7},{7,6},{8,9},{9,8},{10,11... | collective-permute-start | bytes 1867784 | tf_op jit(solution)/shard_map/ppermute | solution.py:70
  251.6 21.9 %collective-permute-start.21 = (bf16[304,1024]{1,0:T(8,128)(2,1)S(1)}, bf16[304,1024]{1,0:T(8,128)(2,1)S(1)}, u32[]{:S(2)}, u32[]{:S(2)}) collective-permute-start(bf16[304,1024]{1,0:T(8,128)(2,1)S(1)} %add_convert_fusion.3), channel_id=1, source_target_pairs={{0,1},{1,0},{2,3},{3,2},{4,5},{5,4},{6,7},{7,6},{8,9},{9,8},{10,11... | collective-permute-start | bytes 1867784 | tf_op jit(solution)/shard_map/ppermute | solution.py:70
  252.3 22.9 %collective-permute-start.26 = (bf16[304,1024]{1,0:T(8,128)(2,1)S(1)}, bf16[304,1024]{1,0:T(8,128)(2,1)S(1)}, u32[]{:S(2)}, u32[]{:S(2)}) collective-permute-start(bf16[304,1024]{1,0:T(8,128)(2,1)S(1)} %dynamic-slice_bitcast_fusion), channel_id=1, source_target_pairs={{0,2},{1,3},{18,16},{19,17},{4,6},{5,7},{22,20},{23,21},{8,10},{9,... | collective-permute-start | bytes 1867784 | tf_op jit(solution)/shard_map/ppermute | solution.py:64
  257.8 18.4 %collective-permute-start.20 = (bf16[304,1024]{1,0:T(8,128)(2,1)S(1)}, bf16[304,1024]{1,0:T(8,128)(2,1)S(1)}, u32[]{:S(2)}, u32[]{:S(2)}) collective-permute-start(bf16[304,1024]{1,0:T(8,128)(2,1)S(1)} %add_convert_fusion.3), channel_id=1, source_target_pairs={{0,16},{16,0},{1,17},{17,1},{2,18},{18,2},{3,19},{19,3},{4,20},{20... | collective-permute-start | bytes 1867784 | tf_op jit(solution)/shard_map/ppermute | solution.py:67
  273.5 2.7 collective-permute-start.22
  293.3 13.3 %collective-permute-start.27 = (bf16[608,256]{1,0:T(8,128)(2,1)}, bf16[608,256]{1,0:T(8,128)(2,1)}, u32[]{:S(2)}, u32[]{:S(2)}) collective-permute-start(bf16[608,256]{1,0:T(8,128)(2,1)} %pad_maximum_fusion.12), channel_id=1, source_target_pairs={{0,1},{1,0},{2,3},{3,2},{4,5},{5,4},{6,7},{7,6},{8,9},{9,8},{10,11... | collective-permute-start | bytes 933896 | tf_op jit(solution)/shard_map/ppermute | solution.py:70
  308.1 2.3 collective-permute-start.28
  312.7 2.2 collective-permute-start.29
  326.8 2.1 collective-permute-start.30
  331.9 2.6 collective-permute-start.31
  332.9 26.9 %collective-permute-start.33 = (bf16[272,2048]{1,0:T(8,128)(2,1)S(1)}, bf16[272,2048]{1,0:T(8,128)(2,1)S(1)}, u32[]{:S(2)}, u32[]{:S(2)}) collective-permute-start(bf16[272,2048]{1,0:T(8,128)(2,1)S(1)} %slice.331), channel_id=1, source_target_pairs={{0,1},{1,0},{2,3},{3,2},{4,5},{5,4},{6,7},{7,6},{8,9},{9,8},{10,11... | collective-permute-start | bytes 3342344 | tf_op jit(solution)/shard_map/ppermute | solution.py:70
  342.4 2.1 collective-permute-start.32
  361.8 2.4 collective-permute-start.34
  366.1 9.5 %collective-permute-start.35 = (bf16[608,256]{1,0:T(8,128)(2,1)S(1)}, bf16[608,256]{1,0:T(8,128)(2,1)S(1)}, u32[]{:S(2)}, u32[]{:S(2)}) collective-permute-start(bf16[608,256]{1,0:T(8,128)(2,1)S(1)} %convolution_convert_fusion.7), channel_id=1, source_target_pairs={{0,1},{1,0},{2,3},{3,2},{4,5},{5,4},{6,7},{7,6},{8,9},{9,8},{10,11... | collective-permute-start | bytes 933896 | tf_op jit(solution)/shard_map/ppermute | solution.py:70
  367.7 27.8 %slice-start.2 = ((s8[6815744]{0:T(1024)(128)(4,1)}), s8[4194304]{0:T(1024)(128)(4,1)S(1)}, s32[]{:S(2)}) async-start(s8[6815744]{0:T(1024)(128)(4,1)} %bitcast.139), calls=%async_computation.6 | async-start | bytes 8388608
  369.1 26.4 %slice-start.3 = ((s8[6815744]{0:T(1024)(128)(4,1)}), s8[2621440]{0:T(1024)(128)(4,1)S(1)}, s32[]{:S(2)}) async-start(s8[6815744]{0:T(1024)(128)(4,1)} %bitcast.139), calls=%async_computation.7 | async-start | bytes 5242880
  375.8 19.7 %collective-permute-start.36 = (bf16[304,1024]{1,0:T(8,128)(2,1)S(1)}, bf16[304,1024]{1,0:T(8,128)(2,1)S(1)}, u32[]{:S(2)}, u32[]{:S(2)}) collective-permute-start(bf16[304,1024]{1,0:T(8,128)(2,1)S(1)} %get-tuple-element.96), channel_id=1, source_target_pairs={{0,0},{1,1},{2,16},{3,17},{16,2},{17,3},{18,18},{19,19},{4,4},{5,5... | collective-permute-start | bytes 1867784 | tf_op jit(solution)/shard_map/ppermute | solution.py:64
  396.3 5.4 %collective-permute-start.37 = (bf16[304,1024]{1,0:T(8,128)(2,1)S(1)}, bf16[304,1024]{1,0:T(8,128)(2,1)S(1)}, u32[]{:S(2)}, u32[]{:S(2)}) collective-permute-start(bf16[304,1024]{1,0:T(8,128)(2,1)S(1)} %convolution_convert_fusion.3), channel_id=1, source_target_pairs={{0,16},{16,0},{1,17},{17,1},{2,18},{18,2},{3,19},{19,3},{4,20},{20... | collective-permute-start | bytes 1867784 | tf_op jit(solution)/shard_map/ppermute | solution.py:67
  400.7 3.2 collective-permute-start.39
  402.4 16.4 %collective-permute-start.38 = (bf16[304,1024]{1,0:T(8,128)(2,1)S(1)}, bf16[304,1024]{1,0:T(8,128)(2,1)S(1)}, u32[]{:S(2)}, u32[]{:S(2)}) collective-permute-start(bf16[304,1024]{1,0:T(8,128)(2,1)S(1)} %fusion.6), channel_id=1, source_target_pairs={{0,1},{1,0},{2,3},{3,2},{4,5},{5,4},{6,7},{7,6},{8,9},{9,8},{10,11... | collective-permute-start | bytes 1867784 | tf_op jit(solution)/shard_map/ppermute | solution.py:70
  420.7 2.1 collective-permute-start.41
  420.7 18.1 %collective-permute-start.40 = (bf16[304,1024]{1,0:T(8,128)(2,1)}, bf16[304,1024]{1,0:T(8,128)(2,1)}, u32[]{:S(2)}, u32[]{:S(2)}) collective-permute-start(bf16[304,1024]{1,0:T(8,128)(2,1)} %get-tuple-element.100), channel_id=1, source_target_pairs={{0,16},{1,17},{2,0},{3,1},{16,18},{17,19},{18,2},{19,3},{4,20},{5,... | collective-permute-start | bytes 1867784 | tf_op jit(solution)/shard_map/ppermute | solution.py:64
  438.8 2.1 collective-permute-start.42
  443.3 2.1 collective-permute-start.43
  447.0 9.5 %collective-permute-start.44 = (bf16[608,256]{1,0:T(8,128)(2,1)S(1)}, bf16[608,256]{1,0:T(8,128)(2,1)S(1)}, u32[]{:S(2)}, u32[]{:S(2)}) collective-permute-start(bf16[608,256]{1,0:T(8,128)(2,1)S(1)} %convolution_convert_fusion.5), channel_id=1, source_target_pairs={{0,1},{1,0},{2,3},{3,2},{4,5},{5,4},{6,7},{7,6},{8,9},{9,8},{10,11... | collective-permute-start | bytes 933896 | tf_op jit(solution)/shard_map/ppermute | solution.py:70
  456.6 22.0 %collective-permute-start.46 = (bf16[304,1024]{1,0:T(8,128)(2,1)S(1)}, bf16[304,1024]{1,0:T(8,128)(2,1)S(1)}, u32[]{:S(2)}, u32[]{:S(2)}) collective-permute-start(bf16[304,1024]{1,0:T(8,128)(2,1)S(1)} %copy-done.23), channel_id=1, source_target_pairs={{2,16},{3,17},{18,18},{19,19},{6,20},{7,21},{22,22},{23,23},{10,24... | collective-permute-start | bytes 1867784 | tf_op jit(solution)/shard_map/ppermute | solution.py:64
  457.3 21.3 %collective-permute-start.45 = (bf16[304,1024]{1,0:T(8,128)(2,1)S(1)}, bf16[304,1024]{1,0:T(8,128)(2,1)S(1)}, u32[]{:S(2)}, u32[]{:S(2)}) collective-permute-start(bf16[304,1024]{1,0:T(8,128)(2,1)S(1)} %copy-done.23), channel_id=1, source_target_pairs={{0,16},{1,17},{16,18},{17,19},{4,20},{5,21},{20,22},{21,23},{8,24}... | collective-permute-start | bytes 1867784 | tf_op jit(solution)/shard_map/ppermute | solution.py:64
  478.6 8.3 %collective-permute-start.48 = (f32[2,2,64,256]{3,2,1,0:T(8,128)S(1)}, f32[2,2,64,256]{3,2,1,0:T(8,128)S(1)}, u32[]{:S(2)}, u32[]{:S(2)}) collective-permute-start(f32[2,2,64,256]{3,2,1,0:T(8,128)S(1)} %pad_maximum_fusion.13), channel_id=1, source_target_pairs={{0,4},{4,0},{8,12},{12,8},{1,5},{5,1},{9,13},{13,9},{2,6},{6,2},{1... | collective-permute-start | bytes 786440 | tf_op jit(solution)/shard_map/ppermute | solution.py:451
  479.4 8.3 %collective-permute-start.47 = (bf16[304,1024]{1,0:T(8,128)(2,1)S(1)}, bf16[304,1024]{1,0:T(8,128)(2,1)S(1)}, u32[]{:S(2)}, u32[]{:S(2)}) collective-permute-start(bf16[304,1024]{1,0:T(8,128)(2,1)S(1)} %convolution_convert_fusion.1), channel_id=1, source_target_pairs={{0,16},{16,0},{1,17},{17,1},{2,18},{18,2},{3,19},{19,3},{4,20},{20... | collective-permute-start | bytes 1867784 | tf_op jit(solution)/shard_map/ppermute | solution.py:67
  487.5 2.1 collective-permute-start.50
  488.3 16.5 %collective-permute-start.49 = (bf16[304,1024]{1,0:T(8,128)(2,1)S(1)}, bf16[304,1024]{1,0:T(8,128)(2,1)S(1)}, u32[]{:S(2)}, u32[]{:S(2)}) collective-permute-start(bf16[304,1024]{1,0:T(8,128)(2,1)S(1)} %convolution_add_fusion.5), channel_id=1, source_target_pairs={{0,1},{1,0},{2,3},{3,2},{4,5},{5,4},{6,7},{7,6},{8,9},{9,8},{10,11... | collective-permute-start | bytes 1867784 | tf_op jit(solution)/shard_map/ppermute | solution.py:70
  489.5 18.6 %collective-permute-start.53 = (f32[2,2,64,256]{3,2,1,0:T(8,128)S(1)}, f32[2,2,64,256]{3,2,1,0:T(8,128)S(1)}, u32[]{:S(2)}, u32[]{:S(2)}) collective-permute-start(f32[2,2,64,256]{3,2,1,0:T(8,128)S(1)} %fusion.119), channel_id=1, source_target_pairs={{0,8},{4,12},{8,0},{12,4},{1,9},{5,13},{9,1},{13,5},{2,10},{6,14},... | collective-permute-start | bytes 786440 | tf_op jit(solution)/shard_map/ppermute | solution.py:451
  505.6 26.0 %collective-permute-start.52 = (bf16[304,1024]{1,0:T(8,128)(2,1)S(1)}, bf16[304,1024]{1,0:T(8,128)(2,1)S(1)}, u32[]{:S(2)}, u32[]{:S(2)}) collective-permute-start(bf16[304,1024]{1,0:T(8,128)(2,1)S(1)} %add_convert_fusion), channel_id=1, source_target_pairs={{2,0},{3,1},{18,2},{19,3},{6,4},{7,5},{22,6},{23,7},{10,8},{11,9},... | collective-permute-start | bytes 1867784 | tf_op jit(solution)/shard_map/ppermute | solution.py:64
  508.1 7.5 %collective-permute-start.54 = (f32[2,64,256]{2,1,0:T(8,128)S(1)}, f32[2,64,256]{2,1,0:T(8,128)S(1)}, u32[]{:S(2)}, u32[]{:S(2)}) collective-permute-start(f32[2,64,256]{2,1,0:T(8,128)S(1)} %get-tuple-element.162), channel_id=1, source_target_pairs={{0,0},{1,1},{2,16},{3,17},{16,2},{17,3},{18,18},{19,19},{4,4},{5,5... | collective-permute-start | bytes 393224 | tf_op jit(solution)/shard_map/ppermute | solution.py:64
  508.8 22.1 %collective-permute-start.55 = (f32[2,64,256]{2,1,0:T(8,128)S(1)}, f32[2,64,256]{2,1,0:T(8,128)S(1)}, u32[]{:S(2)}, u32[]{:S(2)}) collective-permute-start(f32[2,64,256]{2,1,0:T(8,128)S(1)} %get-tuple-element.161), channel_id=1, source_target_pairs={{0,16},{1,17},{2,0},{3,1},{16,18},{17,19},{18,2},{19,3},{4,20},{5,... | collective-permute-start | bytes 393224 | tf_op jit(solution)/shard_map/ppermute | solution.py:64
  513.8 17.9 %collective-permute-start.51 = (bf16[304,1024]{1,0:T(8,128)(2,1)S(1)}, bf16[304,1024]{1,0:T(8,128)(2,1)S(1)}, u32[]{:S(2)}, u32[]{:S(2)}) collective-permute-start(bf16[304,1024]{1,0:T(8,128)(2,1)S(1)} %add_convert_fusion), channel_id=1, source_target_pairs={{0,0},{1,1},{16,2},{17,3},{4,4},{5,5},{20,6},{21,7},{8,8},{9,9},{2... | collective-permute-start | bytes 1867784 | tf_op jit(solution)/shard_map/ppermute | solution.py:64
  (60 other events, 433.2 us)
Sparse Core Ops, SparseCore 0:
  39.2 32.3 all-gather.4
  77.3 86.3 all-gather.6
  207.4 97.7 all-gather.8
  363.1 53.0 all-gather.10

commit v4 on v3

--- a/solution.py
+++ b/solution.py
@@ -14,6 +14,7 @@
 F32 = jnp.float32
 TQ = 128
 CK = 256
+KC = 64
 SIZES = (2, 3, 4, 5, 6, 7, 8, 10)
 TH = 512
 VMEM = 48 << 20
@@ -139,12 +140,18 @@
         def _():
             body(pl.multiple_of(range_ref[t, 0], TQ), size * TQ)
 
-def window_mask(start, size, span_ref, heads):
-    key = lax.broadcasted_iota(jnp.int32, (size, TQ), 0) + start
+def pieces(prefix, start, size):
+    out = [(r, r, KC, False) for r in range(0, prefix, KC)]
+    return out + [(prefix + r, start + r, KC, True) for r in range(0, size, KC)]
+
+def piece_mask(first, span_ref, heads):
+    key = lax.broadcasted_iota(jnp.int32, (KC, TQ), 0) + first
     return widen((key >= span_ref[0:1, :]) & (key < span_ref[1:2, :]), heads)
 
-def attn_fwd(prefix, heads, range_ref, span_ref, qkv_ref, o_ref, lse_ref, vt_ref):
+def attn_fwd(prefix, heads, range_ref, span_ref, qkv_ref, o_ref, lse_ref, vt_ref, s_ref, p_ref):
     w = heads * HD
+    pair = min(2, heads)
+    pw = pair * HD
     t = pl.program_id(0)
     @pl.when(t == 0)
     def _():
@@ -152,24 +159,43 @@
             at = slice(i * CK, (i + 1) * CK)
             vt_ref[:, at] = qkv_ref[at, 2*w:3*w].astype(F32).T.astype(BF)
     def body(start, size):
-        q = spread_heads(qkv_ref[pl.ds(pl.multiple_of(t*TQ, TQ), TQ), 0:w] * BF(HD ** -0.5), heads)
+        here = pl.ds(pl.multiple_of(t*TQ, TQ), TQ)
         at = pl.ds(start, size)
-        first = nt(qkv_ref[0:prefix, w:2*w], q)
-        rest = nt(qkv_ref[at, w:2*w], q)
-        rest = jnp.where(window_mask(start, size, span_ref, heads), rest, -1e30)
-        peak = jnp.maximum(jnp.max(first, axis=0, keepdims=True), jnp.max(rest, axis=0, keepdims=True))
-        first, rest = jnp.exp(first - peak), jnp.exp(rest - peak)
-        total = jnp.sum(first, axis=0, keepdims=True) + jnp.sum(rest, axis=0, keepdims=True)
-        acc = nn(vt_ref[:, 0:prefix], first.astype(BF)) + nn(vt_ref[:, at], rest.astype(BF))
-        o_ref[...] = own_columns(acc * (1.0 / total), heads).T.astype(BF)
-        lse = peak + jnp.log(total)
-        for h in range(heads):
-            lse_ref[h:h+1, :] = lse[:, h*TQ:(h+1)*TQ]
+        outs = []
+        lanes = range(0, w, pw)
+        for g, lane in enumerate(lanes):
+            q = spread_heads(qkv_ref[here, lane:lane+pw] * BF(HD ** -0.5), pair)
+            s_ref[g, 0:prefix] = nt(qkv_ref[0:prefix, w+lane:w+lane+pw], q)
+            s_ref[g, prefix:prefix+size] = nt(qkv_ref[at, w+lane:w+lane+pw], q)
+        for g, lane in enumerate(lanes):
+            peak = jnp.full((8, pair*TQ), -1e30, F32)
+            for row, first, n, masked in pieces(prefix, start, size):
+                s = s_ref[g, row:row+n]
+                if masked:
+                    s = jnp.where(piece_mask(first, span_ref, pair), s, -1e30)
+                    s_ref[g, row:row+n] = s
+                peak = jnp.maximum(peak, jnp.max(s.reshape(n//8, 8, -1), axis=0))
+            peak = jnp.max(peak, axis=0, keepdims=True)
+            total = jnp.zeros((8, pair*TQ), F32)
+            for row, first, n, masked in pieces(prefix, start, size):
+                e = jnp.exp(s_ref[g, row:row+n] - peak)
+                p_ref[g, row:row+n] = e.astype(BF)
+                total = total + jnp.sum(e.reshape(n//8, 8, -1), axis=0)
+            total = jnp.sum(total, axis=0, keepdims=True)
+            acc = nn(vt_ref[lane:lane+pw, 0:prefix], p_ref[g, 0:prefix]) + nn(vt_ref[lane:lane+pw, at], p_ref[g, prefix:prefix+size])
+            outs.append(own_columns(acc * (1.0 / total), pair))
+            lse = peak + jnp.log(total)
+            for h in range(pair):
+                row = lane // HD + h
+                lse_ref[row:row+1, :] = lse[:, h*TQ:(h+1)*TQ]
+        o_ref[...] = jnp.concatenate(outs, 0).T.astype(BF)
     each_size(range_ref, t, body)
 
 def attn_bwd(prefix, heads, range_ref, span_ref, qkv_ref, lse_ref, o_ref, do_ref, out_ref, pre_ref,
-             kt_ref, dk_ref, dv_ref):
+             kt_ref, dk_ref, dv_ref, s_ref, dp_ref, p_ref, ds_ref):
     w = heads * HD
+    pair = min(2, heads)
+    pw = pair * HD
     t = pl.program_id(0)
     @pl.when(t == 0)
     def _():
@@ -180,22 +206,37 @@
         dv_ref[...] = jnp.zeros_like(dv_ref)
     def body(start, size):
         here = pl.ds(pl.multiple_of(t*TQ, TQ), TQ)
-        q = spread_heads(qkv_ref[here, 0:w] * BF(HD ** -0.5), heads)
-        do = do_ref[...]
-        both = (do.astype(F32) * o_ref[...].astype(F32)).T
-        delta = jnp.concatenate([jnp.sum(both[h*HD:(h+1)*HD], axis=0, keepdims=True) for h in range(heads)], 1)
-        do = spread_heads(do, heads)
-        lse = jnp.concatenate([lse_ref[h:h+1, :] for h in range(heads)], 1)
-        dq = 0.0
-        for at, mask in ((pl.ds(0, prefix), None), (pl.ds(start, size), window_mask(start, size, span_ref, heads))):
-            prob = jnp.exp(nt(qkv_ref[at, w:2*w], q) - lse)
-            if mask is not None:
-                prob = jnp.where(mask, prob, 0.0)
-            ds = (prob * (nt(qkv_ref[at, 2*w:3*w], do) - delta)).astype(BF)
-            dv_ref[at, :] += nn(prob.astype(BF), do)
-            dk_ref[at, :] += nn(ds, q)
-            dq = dq + nn(kt_ref[:, at], ds)
-        out_ref[here, 0:w] = (own_columns(dq, heads) * HD ** -0.5).T.astype(BF)
+        both = (do_ref[...].astype(F32) * o_ref[...].astype(F32)).T
+        outs = []
+        at = pl.ds(start, size)
+        parts = ((slice(0, prefix), slice(0, prefix)), (at, slice(prefix, prefix+size)))
+        lanes = range(0, w, pw)
+        qs, dos = [], []
+        for g, lane in enumerate(lanes):
+            q = spread_heads(qkv_ref[here, lane:lane+pw] * BF(HD ** -0.5), pair)
+            do = spread_heads(do_ref[:, lane:lane+pw], pair)
+            qs.append(q)
+            dos.append(do)
+            for src, dst in parts:
+                s_ref[g, dst] = nt(qkv_ref[src, w+lane:w+lane+pw], q)
+                dp_ref[g, dst] = nt(qkv_ref[src, 2*w+lane:2*w+lane+pw], do)
+        for g, lane in enumerate(lanes):
+            rows = range(lane // HD, lane // HD + pair)
+            delta = jnp.concatenate([jnp.sum(both[h*HD:(h+1)*HD], axis=0, keepdims=True) for h in rows], 1)
+            lse = jnp.concatenate([lse_ref[h:h+1, :] for h in rows], 1)
+            for row, first, n, masked in pieces(prefix, start, size):
+                prob = jnp.exp(s_ref[g, row:row+n] - lse)
+                if masked:
+                    prob = jnp.where(piece_mask(first, span_ref, pair), prob, 0.0)
+                p_ref[g, row:row+n] = prob.astype(BF)
+                ds_ref[g, row:row+n] = (prob * (dp_ref[g, row:row+n] - delta)).astype(BF)
+            dq = 0.0
+            for src, dst in parts:
+                dv_ref[src, lane:lane+pw] += nn(p_ref[g, dst], dos[g])
+                dk_ref[src, lane:lane+pw] += nn(ds_ref[g, dst], qs[g])
+                dq = dq + nn(kt_ref[lane:lane+pw, src], ds_ref[g, dst])
+            outs.append(own_columns(dq, pair))
+        out_ref[here, 0:w] = (jnp.concatenate(outs, 0) * HD ** -0.5).T.astype(BF)
     each_size(range_ref, t, body)
     @pl.when(t == pl.num_programs(0) - 1)
     def _():
@@ -203,6 +244,10 @@
         out_ref[:, 2*w:3*w] = dv_ref[...].astype(BF)
         pre_ref[0] = dk_ref[0:prefix, :]
         pre_ref[1] = dv_ref[0:prefix, :]
+
+def score_scratch(n, w, kind):
+    pair = min(2, w // HD)
+    return pltpu.VMEM((w // HD // pair, n + TQ, pair*TQ), kind)
 
 def whole(shape):
     return pl.BlockSpec(shape, lambda t, *_: (0,) * len(shape))
@@ -215,7 +260,7 @@
             num_scalar_prefetch=1, grid=(n//TQ,),
             in_specs=[pl.BlockSpec((2, TQ), lambda t, *_: (0, t)), whole(qkv.shape)],
             out_specs=[pl.BlockSpec((TQ, w), lambda t, *_: (t, 0)), pl.BlockSpec((heads, TQ), lambda t, *_: (0, t))],
-            scratch_shapes=[pltpu.VMEM((w, n), BF)]),
+            scratch_shapes=[pltpu.VMEM((w, n), BF), score_scratch(n, w, F32), score_scratch(n, w, BF)]),
         out_shape=[jax.ShapeDtypeStruct((n, w), BF), jax.ShapeDtypeStruct((heads, n), F32)],
         compiler_params=pltpu.CompilerParams(dimension_semantics=("arbitrary",), vmem_limit_bytes=VMEM), name="attend",
         cost_estimate=pl.CostEstimate(flops=2*n*n*w*2//4000, bytes_accessed=1, transcendentals=0),
@@ -231,7 +276,8 @@
             in_specs=[pl.BlockSpec((2, TQ), lambda t, *_: (0, t)), whole(qkv.shape),
                       pl.BlockSpec((heads, TQ), lambda t, *_: (0, t)), tile, tile],
             out_specs=[whole((n, 3*w)), whole((2, prefix, w))],
-            scratch_shapes=[pltpu.VMEM((w, n), BF), pltpu.VMEM((n, w), F32), pltpu.VMEM((n, w), F32)]),
+            scratch_shapes=[pltpu.VMEM((w, n), BF), pltpu.VMEM((n, w), F32), pltpu.VMEM((n, w), F32),
+                score_scratch(n, w, F32), score_scratch(n, w, F32), score_scratch(n, w, BF), score_scratch(n, w, BF)]),
         out_shape=[jax.ShapeDtypeStruct((n, 3*w), BF), jax.ShapeDtypeStruct((2, prefix, w), F32)],
         compiler_params=pltpu.CompilerParams(dimension_semantics=("arbitrary",), vmem_limit_bytes=VMEM), name="attend_back",
         cost_estimate=pl.CostEstimate(flops=5*n*n*w*2//4000, bytes_accessed=1, transcendentals=0),
@@ -279,12 +325,10 @@
     biases = ()
     if mode != "back":
         biases, refs = refs[:count], refs[count:]
-    if mode == "again":
-        inputs, refs = refs[:2], refs[2:]
     if mode == "back":
         slope_ref, refs = refs[0], refs[1:]
-    x_ref, acc_ref, *again = refs[-3:] if mode == "again" else refs[-2:]
-    out_own_ref, out_other_ref, *kept = refs[: -2 - len(again)]
+    out_own_ref, out_other_ref, *kept, x_ref, acc_ref, u_ref, f_ref = refs
+    step = 16
     rows = own_ref.shape[0]
     t = pl.program_id(0)
 
@@ -292,27 +336,26 @@
     def _():
         x_ref[:rows] = own_ref[...]
         x_ref[rows:] = other_ref[...]
-        if mode == "again":
-            again[0][:rows] = inputs[0][...]
-            again[0][rows:] = inputs[1][...]
         acc_ref[...] = jnp.zeros_like(acc_ref)
 
     def run(k):
         up_ref, down_ref = panels[2 * k], panels[2 * k + 1]
         if mode == "forward":
-            u = nn(x_ref[...], up_ref[...]) + biases[k][...]
-            bell, phi = bell_parts(u)
-            if kept:
-                kept[0][...] = slope_of(u, bell, phi).astype(BF)
-            acc_ref[...] += nt((u * phi).astype(BF), down_ref[...])
+            u_ref[...] = nn(x_ref[...], up_ref[...])
+            bias = biases[k][...]
+            for row in range(0, 2 * rows, step):
+                at = slice(row, min(row + step, 2 * rows))
+                u = u_ref[at] + bias
+                bell, phi = bell_parts(u)
+                kept[0][at] = slope_of(u, bell, phi).astype(BF)
+                f_ref[at] = (u * phi).astype(BF)
+            acc_ref[...] += nt(f_ref[...], down_ref[...])
         else:
-            df = nn(x_ref[...], down_ref[...])
-            if mode == "again":
-                u = nn(again[0][...], up_ref[...]) + biases[k][...]
-                slope = slope_of(u, *bell_parts(u))
-            else:
-                slope = slope_ref[...].astype(F32)
-            acc_ref[...] += nt((df * slope).astype(BF), up_ref[...])
+            u_ref[...] = nn(x_ref[...], down_ref[...])
+            for row in range(0, 2 * rows, step):
+                at = slice(row, min(row + step, 2 * rows))
+                f_ref[at] = (u_ref[at] * slope_ref[at].astype(F32)).astype(BF)
+            acc_ref[...] += nt(f_ref[...], up_ref[...])
 
     for k, (first, last) in enumerate(cuts):
         if count == 1:
@@ -326,7 +369,7 @@
         out_other_ref[...] = acc_ref[rows:].astype(BF)
 
 
-def feed(mode, panels, own, other, biases=(), inputs=(), slopes=(), keep=False):
+def feed(mode, panels, own, other, biases=(), slopes=(), keep=False):
     rows, d = own.shape
     th = TH if all(units % TH == 0 for _, units in panels) else TH // 2
     specs, arrays, cuts, at = [], [], [], 0
@@ -348,17 +391,15 @@
         for k, bias in enumerate(biases):
             specs.append(pl.BlockSpec((1, th), specs[2 * k].index_map))
             arrays.append(bias)
-    specs += [full] * len(inputs) + [part] * len(slopes)
-    arrays += list(inputs) + list(slopes)
+    specs += [part] * len(slopes)
+    arrays += list(slopes)
     outs = [jax.ShapeDtypeStruct((rows, d), F32), jax.ShapeDtypeStruct((rows, d), BF)]
     out_specs = [full, full]
     if keep:
         outs.append(jax.ShapeDtypeStruct((2 * rows, at * th), BF))
         out_specs.append(part)
-    matmuls = 3 if mode == "again" else 2
     scratch = [pltpu.VMEM((2 * rows, d), BF), pltpu.VMEM((2 * rows, d), F32)]
-    if mode == "again":
-        scratch.append(pltpu.VMEM((2 * rows, d), BF))
+    scratch += [pltpu.VMEM((2 * rows, th), F32), pltpu.VMEM((2 * rows, th), BF)]
     return pl.pallas_call(
         lambda *refs: feed_kernel(mode, cuts, refs),
         grid=(at,),
@@ -370,7 +411,7 @@
             dimension_semantics=("arbitrary",), vmem_limit_bytes=VMEM
         ),
         cost_estimate=pl.CostEstimate(
-            flops=4 * matmuls * rows * d * at * th // 4000,
+            flops=8 * rows * d * at * th // 4000,
             bytes_accessed=1,
             transcendentals=0,
         ),
@@ -452,22 +493,23 @@
 
 
 def input_back(place, order, da, back, qkv_w, kv=None):
-    total, bit = da, 1
-    if kv is not None:
-        kv = swap_add(kv, bit)
+    total, sent = da, []
     for j in range(place.g - 1, -1, -1):
         other = nt(order.get(back, j, 1), qkv_w).astype(BF)
         summed = both_cores(place, nt(order.get(back, j, 0), qkv_w), other)
-        if kv is not None and bit == 1:
-            summed, kv = tie((summed, kv), kv)
-            bit = 2
-        total = total + (summed if j == 0 else place.chip(summed.astype(BF), j).astype(F32))
-    if kv is None:
-        return total.astype(BF)
-    while bit < lax.axis_size("dp"):
-        kv = swap_add(kv, bit)
-        bit *= 2
-    return total.astype(BF), kv
+        if j == 0:
+            total = total + summed
+        else:
+            sent.append(place.chip(summed.astype(BF), j))
+    if kv is not None:
+        bit = 1
+        while bit < lax.axis_size("dp"):
+            kv = swap_add(kv, bit)
+            bit *= 2
+        sent = tie(sent, kv)
+    for value in sent:
+        total = total + value.astype(F32)
+    return total.astype(BF) if kv is None else (total.astype(BF), kv)
 
 
 def on_device(
@@ -516,93 +558,73 @@
         return own_shard(place, l, *held)
 
     shard0 = merged(place, shard_of(0, thin0))
-    up0, down0, out0, bias0 = cut_shard(shard0, dim, ff)
-    outs0 = [out0] + [place.chip(out0, j) for j in range(1, g)]
+    shards0 = [shard0] + [place.chip(shard0, j) for j in range(1, g)]
     thin1 = merged(place, own_layer(place, 1, tie(block, shard0)))
     w1, qkv_b1, pre1 = cut_qkv(thin1, dim, prefix)
-    first = jnp.concatenate([up0, down0] + outs0 + [w1], axis=1)
-    panel0 = gather(tie(first, w0))
+
+    def panel_of(shards, *more):
+        cuts = [cut_shard(v, dim, ff) for v in shards]
+        parts = [v[k] for k in range(3) for v in cuts] + list(more)
+        return jnp.concatenate(parts, axis=1), jnp.concatenate([v[3] for v in cuts])[None]
+
+    def outs_of(panel, count):
+        start = 2 * count * ff
+        return [panel[:, start + j * width : start + (j + 1) * width] for j in range(count)]
+
+    part_a, bias_a = panel_of(shards0[:1])
+    panel_a = gather(tie(part_a, w0))
     x = own_rows(tie(tokens, thin1))
+    part_b, bias_b = panel_of(shards0[1:], w1)
+    panel_b = gather(tie(part_b, panel_a, x))
+    shard1 = shard_of(1, x)
     blocks = spread_rows(place, x)
-    shard1 = shard_of(1, blocks)
     qkv0, o0, lse0 = attention(place, order, blocks, (w0, qkv_b0, pre0), where)
     parts = out_parts(place, order, o0)
-    shard1 = merged(place, tie(shard1, parts))
+    shard1 = merged(place, tie(shard1, blocks))
     shards1 = [shard1] + [place.chip(shard1, j) for j in range(1, g)]
-    w1 = panel0[:, 2 * ff + g * width :]
-
-    def outs_of(panel, start):
-        return [panel[:, start + j * width : start + (j + 1) * width] for j in range(g)]
-
-    outs = [outs_of(tie(panel0, parts), 2 * ff)]
+    second, bias1 = panel_of(tie(shards1, o0))
+    panel1 = gather(tie(second, panel_b))
+    grad = own_rows(tie(cotangent, second))
+    panels0 = [(panel_a, ff), (panel_b, (g - 1) * ff)]
+    panels1 = [(panel1, g * ff)]
+
+    w1 = panel_b[:, (g - 1) * (2 * ff + width) :]
+    outs = [outs_of(panel_a, 1) + outs_of(tie(panel_b, parts), g - 1), outs_of(panel1, g)]
     a0, x1 = out_project(place, order, x, parts, outs[0], fixed[0])
     low = x1.astype(BF)
-    wide0 = [low] + [place.chip(low, j) for j in range(1, g)]
-    z = x1 + fixed[0][1]
-    mine, sums = low, []
-    for j in range(g):
-        own = tie(wide0[j], mine)
-        other = place.core(own)
-        if j == 0:
-            both0 = (own, other)
-        mine, theirs = feed("forward", [(panel0, ff)], own, other, [bias0[None]])
-        if j == 0:
-            shards1 = [cut_shard(v, dim, ff) for v in tie(shards1, mine)]
-            second = jnp.concatenate([v[k] for k in range(3) for v in shards1], axis=1)
-            bias1 = jnp.concatenate([v[3] for v in shards1])[None]
-            panel1 = gather(tie(second, panel0))
-            grad = own_rows(tie(cotangent, second))
-            outs.append(outs_of(panel1, 2 * g * ff))
-        summed = both_cores(place, mine, theirs)
-        z = z + (summed if j == 0 else place.chip(summed.astype(BF), j).astype(F32))
-    z0 = z
-    y0 = (norm_stats(z)[0] * fixed[0][3] + fixed[0][5]).astype(BF)
+    mine, theirs, slope0 = feed(
+        "forward", panels0, low, place.core(low), [bias_a, bias_b], keep=True
+    )
+    z0 = x1 + both_cores(place, mine, theirs) + fixed[0][1]
+    y0 = (norm_stats(z0)[0] * fixed[0][3] + fixed[0][5]).astype(BF)
+
+    def home(value, l, half):
+        return place.send(value, lambda c, m, p: (l, c, p) if m == half else None)
 
     blocks = tie(spread_rows(place, y0), grad)
+    results0 = [home(tie(y0, blocks), 0, h) for h in range(2)]
     qkv1, o1, lse1 = attention(place, order, blocks, (w1, qkv_b1, pre1), where)
-    a1, x1 = out_project(place, order, y0, out_parts(place, order, o1), outs[1], fixed[1])
+    a1, x1 = out_project(place, order, y0, out_parts(place, order, tie(o1, results0)), outs[1], fixed[1])
     low = x1.astype(BF)
-    late = [place.chip(tie(shard0[:, : 2 * ff], low), j) for j in range(1, g)]
-    mine, theirs, slope = feed(
-        "forward", [(panel1, g * ff)], low, place.core(low), [bias1], keep=True
-    )
+    mine, theirs, slope1 = feed("forward", panels1, low, place.core(low), [bias1], keep=True)
     z1 = x1 + both_cores(place, mine, theirs) + fixed[1][1]
     y1 = (norm_stats(z1)[0] * fixed[1][3] + fixed[1][5]).astype(BF)
 
-    def home(value, l, half):
-        return place.send(value, lambda c, m, p: (l, c, p) if m == half else None)
-
     dz = norm_back(z1, grad.astype(F32), fixed[1][3])
     low = dz.astype(BF)
-    mine, theirs = feed("back", [(panel1, g * ff)], low, place.core(low), slopes=[slope])
-    dx1 = tie(dz + both_cores(place, mine, theirs), late)
-
-    late = [cut_shard(v, dim, ff) for v in late]
-    rest = jnp.concatenate([v[k] for k in range(2) for v in late], axis=1)
-    rest_bias = jnp.concatenate([v[3] for v in late])[None]
-    rest = gather(tie(rest, panel1))
+    mine, theirs = feed("back", panels1, low, place.core(low), slopes=[slope1])
+    dx1 = dz + both_cores(place, mine, theirs)
 
     first = m == 0
     da, go = out_back(place, order, dx1, a1, outs[1], fixed[1])
-    pair = [place.send(tie(jnp.where(first, y0, y1), go), lambda c, m, p: (m, c, p))]
+    results1 = [home(tie(y1, go), 1, h) for h in range(2)]
     back, kv1 = attend_back(*where, qkv1, lse1, o1, go, prefix, width // HD)
-    back = tie(back, pair)
+    back = tie(back, results1)
     grad1 = input_back(place, order, da, back, w1)
 
     dz = norm_back(z0, grad1.astype(F32), fixed[0][3])
     low = dz.astype(BF)
-    mine, theirs = feed(
-        "again",
-        [(panel0, ff), (rest, (g - 1) * ff)],
-        low,
-        place.core(low),
-        [bias0[None], rest_bias],
-        inputs=both0,
-    )
-    swapped = tie(jnp.where(first, y1, y0), low)
-    pair.append(place.send(swapped, lambda c, m, p: (1 - m, c, p)))
-    results = [jnp.where(c == 0, pair[h], pair[1 - h]) for h in range(2)]
-    mine, theirs = tie((mine, theirs), pair)
+    mine, theirs = feed("back", panels0, low, place.core(low), slopes=[slope0])
     dx1 = dz + both_cores(place, mine, theirs)
     da, go = out_back(place, order, dx1, a0, outs[0], fixed[0])
     gouts = [home(tie(grad1, go), 1, h) for h in range(2)]
@@ -613,7 +635,7 @@
     kv = place.send(jnp.where(first, kv[0], kv[1]), lambda c, m, p: (m, c, p)) + place.send(
         jnp.where(first, kv[1], kv[0]), lambda c, m, p: (1 - m, c, p)
     )
-    results = jnp.stack(results)[:, :, None]
+    results = jnp.stack([results0[h] + results1[h] for h in range(2)])[:, :, None]
     gouts = jnp.stack(gouts)[:, :, None]
     return results[None], gouts[None], kv[None, 0], kv[None, 1]
 

time: 546 us -> 506 us (0.927)
  waiting for transfers between devices: 232 us -> 217 us
  Pallas kernels: 113 us -> 99 us
  other arithmetic: 29.1 us -> 23.2 us
    ppermute x13 -> x10, waiting for transfers between devices: 149 us -> 93.2 us  [chip(): return lax.ppermute(value, 'mp', [(z, z ^ j) for z in range(self.mp)])]
    ppermute x13 -> x10, starting transfers between devices: 31.8 us -> 12.1 us  [chip(): return lax.ppermute(value, 'mp', [(z, z ^ j) for z in range(self.mp)])]
    all_gather x4, waiting for transfers between devices: 11.9 us -> 30.9 us  [gather(): return lax.all_gather(block, 'dp', axis=0, tiled=True)]
    ppermute x18 -> x20, waiting for transfers between devices: 46.7 us -> 62 us  [send(): return lax.ppermute(value, ('section', 'mp'), pairs)]
    ppermute x18 -> x20, starting transfers between devices: 44.8 us -> 57.9 us  [send(): return lax.ppermute(value, ('section', 'mp'), pairs)]
    pallas_call x5 -> x4, Pallas kernels: 47.7 us -> 41.2 us  [feed(): pl.pallas_call(lambda *refs: feed_kernel(mode, cuts, refs), grid=(at,), i...]
    ppermute x23 -> x21, starting transfers between devices: 15.2 us -> 18.9 us  [core(): return lax.ppermute(value, 'section', [(0, 1), (1, 0)])]
    unnamed x132 -> x94, local copies, waits for them, and re-layouts: 13.7 us -> 10.2 us
  transfers between devices with their start and end apart: 60 -> 57, of which waited for: 32 -> 34; matrix products, arithmetic and copies ran while one was open for 10% -> 10% of each run, Pallas kernels for 19% -> 14%
where the time goes in v4:
time: 506 us; the launch traced here: 500 us
  waiting for transfers between devices  217 us (43%)
  Pallas kernels  99 us (20%)
  starting transfers between devices  92.5 us (18%)
  matrix products  33.1 us (7%)
  other arithmetic  23.2 us (5%)
  local copies, waits for them, and re-layouts  19.7 us (4%)
  between operations  15.5 us (3%)
    ppermute x10, waiting for transfers between devices, chip(): return lax.ppermute(value, 'mp', [(z, z ^ j) for z in range(self.mp)])  93.2 us
    ppermute x20, waiting for transfers between devices, send(): return lax.ppermute(value, ('section', 'mp'), pairs)  62 us
    ppermute x20, starting transfers between devices, send(): return lax.ppermute(value, ('section', 'mp'), pairs)  57.9 us
    pallas_call x4, Pallas kernels, feed(): pl.pallas_call(lambda *refs: feed_kernel(mode, cuts, refs), grid=(at,), i...  41.2 us
    pallas_call x2, Pallas kernels, attend_back(): pl.pallas_call(partial(attn_bwd, prefix, heads), grid_spec=pltpu.Prefetch...  34.2 us
    dot_general x28, matrix products, dot(): return lax.dot_general(a, b, (dims, ((), ())), preferred_element_type=F32)  33.1 us
    all_gather x4, waiting for transfers between devices, gather(): return lax.all_gather(block, 'dp', axis=0, tiled=True)  30.9 us
    pallas_call x2, Pallas kernels, attend(): pl.pallas_call(partial(attn_fwd, prefix, heads), grid_spec=pltpu.Prefetch...  23.7 us
  transfers between devices with their start and end apart: 57, of which 34 were waited for; matrix products, arithmetic and copies ran while one was open for 10% of the time, Pallas kernels for 14%

profile of v4, /device:TPU:0, one launch (start us, length us, event | category | flops | bytes accessed | tf_op | source)
XLA Modules:
  0.0 500.0 jit_solution(8573655559136130236)
XLA Ops:
  11.2 7.4 %collective-permute-start.1 = (bf16[336,768]{1,0:T(8,128)(2,1)S(1)}, bf16[336,768]{1,0:T(8,128)(2,1)}, u32[]{:S(2)}, u32[]{:S(2)}) collective-permute-start(bf16[336,768]{1,0:T(8,128)(2,1)S(1)} %pad_maximum_fusion.9), channel_id=1, source_target_pairs={{0,2},{1,3},{2,18},{3,19},{4,6},{5,7},{6,22},{7,23},{8,10},{9,11},... | collective-permute-start | bytes 1548296 | tf_op jit(solution)/shard_map/ppermute | solution.py:65
  18.5 5.8 %collective-permute-done.1 = bf16[336,768]{1,0:T(8,128)(2,1)} collective-permute-done((bf16[336,768]{1,0:T(8,128)(2,1)S(1)}, bf16[336,768]{1,0:T(8,128)(2,1)}, u32[]{:S(2)}, u32[]{:S(2)}) %collective-permute-start.1) | collective-permute-done | bytes 516128 | tf_op jit(solution)/shard_map/ppermute | solution.py:65
  27.5 9.6 %collective-permute-start.3 = (bf16[272,2304]{1,0:T(8,128)(2,1)S(1)}, bf16[272,2304]{1,0:T(8,128)(2,1)S(1)}, u32[]{:S(2)}, u32[]{:S(2)}) collective-permute-start(bf16[272,2304]{1,0:T(8,128)(2,1)S(1)} %pad_maximum_fusion.1), channel_id=1, source_target_pairs={{0,2},{1,3},{2,18},{3,19},{4,6},{5,7},{6,22},{7,23},{8,10},{9,11},... | collective-permute-start | bytes 3760136 | tf_op jit(solution)/shard_map/ppermute | solution.py:65
  37.1 14.4 %collective-permute-done.3 = bf16[272,2304]{1,0:T(8,128)(2,1)S(1)} collective-permute-done((bf16[272,2304]{1,0:T(8,128)(2,1)S(1)}, bf16[272,2304]{1,0:T(8,128)(2,1)S(1)}, u32[]{:S(2)}, u32[]{:S(2)}) %collective-permute-start.3) | collective-permute-done | bytes 1253408 | tf_op jit(solution)/shard_map/ppermute | solution.py:65
  52.8 13.9 %all-gather.5.cloned.1.call-done = bf16[1024,768]{1,0:T(8,128)(2,1)} async-done(((bf16[256,768]{1,0:T(8,128)(2,1)}), bf16[1024,768]{1,0:T(8,128)(2,1)}) %all-gather.5.cloned.1.call-update) | async-done | bytes 1572880 | tf_op jit(solution)/shard_map/all_gather | solution.py:84
  74.2 17.8 %collective-permute-start.6 = (bf16[304,1024]{1,0:T(8,128)(2,1)S(1)}, bf16[304,1024]{1,0:T(8,128)(2,1)}, u32[]{:S(2)}, u32[]{:S(2)}) collective-permute-start(bf16[304,1024]{1,0:T(8,128)(2,1)S(1)} %dynamic-slice_bitcast_fusion.1), channel_id=1, source_target_pairs={{0,2},{1,3},{18,16},{19,17},{4,6},{5,7},{22,20},{23,21},{8,10},{9,... | collective-permute-start | bytes 1867784 | tf_op jit(solution)/shard_map/ppermute | solution.py:65
  91.9 19.2 %collective-permute-done.6 = bf16[304,1024]{1,0:T(8,128)(2,1)} collective-permute-done((bf16[304,1024]{1,0:T(8,128)(2,1)S(1)}, bf16[304,1024]{1,0:T(8,128)(2,1)}, u32[]{:S(2)}, u32[]{:S(2)}) %collective-permute-start.6) | collective-permute-done | bytes 622624 | tf_op jit(solution)/shard_map/ppermute | solution.py:65
  112.3 1.6 slice.300
  115.2 10.9 %all-gather.7.cloned.1.call-done.refs_0_.refs_1_ = bf16[1024,2304]{1,0:T(8,128)(2,1)} async-done(((bf16[256,2304]{1,0:T(8,128)(2,1)}), bf16[1024,2304]{1,0:T(8,128)(2,1)}) %all-gather.7.cloned.1.call-update) | async-done | bytes 4718608 | tf_op jit(solution)/shard_map/all_gather | solution.py:84
  131.5 2.3 collective-permute-start.20
  133.8 1.6 collective-permute-start.8
  135.6 3.0 collective-permute-start.7
  138.6 17.2 %collective-permute-done.8 = bf16[304,1024]{1,0:T(8,128)(2,1)} collective-permute-done((bf16[304,1024]{1,0:T(8,128)(2,1)S(1)}, bf16[304,1024]{1,0:T(8,128)(2,1)}, u32[]{:S(2)}, u32[]{:S(2)}) %collective-permute-start.8) | collective-permute-done | bytes 622624 | tf_op jit(solution)/shard_map/ppermute | solution.py:71
  155.8 7.3 %collective-permute-start.9 = (bf16[304,1024]{1,0:T(8,128)(2,1)}, bf16[304,1024]{1,0:T(8,128)(2,1)}, u32[]{:S(2)}, u32[]{:S(2)}) collective-permute-start(bf16[304,1024]{1,0:T(8,128)(2,1)} %collective-permute-done.8), channel_id=1, source_target_pairs={{0,16},{16,0},{1,17},{17,1},{2,18},{18,2},{3,19},{19,3},{4,20},{20... | collective-permute-start | bytes 1867784 | tf_op jit(solution)/shard_map/ppermute | solution.py:68
  165.3 2.1 collective-permute-start.21
  168.9 1.7 fusion.17
  170.6 1.7 fusion.19
  172.4 1.7 fusion.21.qkv_ref
  174.1 11.6 %attend.2 = (bf16[1280,256]{1,0:T(8,128)(2,1)S(1)}, f32[4,1280]{1,0:T(4,128)S(1)}) custom-call(s32[10,2]{1,0:T(8,128)S(1)} %copy.77.range_ref, s32[2,1280]{1,0:T(2,128)S(1)} %pad_add_fusion.span_ref, bf16[1280,768]{1,0:T(8,128)(2,1)S(1)} %fusion.21.qkv_ref), custom_call_target="tpu_custom_call" | custom-call | flops 419430 | bytes 1 | tf_op jit(solution)/shard_map/attend/pallas_call | solution.py:257
  185.8 9.7 %collective-permute-done.21 = bf16[272,2304]{1,0:T(8,128)(2,1)S(1)} collective-permute-done((bf16[272,2304]{1,0:T(8,128)(2,1)S(1)}, bf16[272,2304]{1,0:T(8,128)(2,1)S(1)}, u32[]{:S(2)}, u32[]{:S(2)}) %collective-permute-start.21) | collective-permute-done | bytes 1253408 | tf_op jit(solution)/shard_map/ppermute | solution.py:71
  201.5 1.8 collective-permute-start.10
  204.7 6.6 %collective-permute-done.10 = bf16[608,256]{1,0:T(8,128)(2,1)S(1)} collective-permute-done((bf16[608,256]{1,0:T(8,128)(2,1)S(1)}, bf16[608,256]{1,0:T(8,128)(2,1)S(1)}, u32[]{:S(2)}, u32[]{:S(2)}) %collective-permute-start.10) | collective-permute-done | bytes 311328 | tf_op jit(solution)/shard_map/ppermute | solution.py:71
  211.3 1.5 fusion.10
  214.9 1.7 fusion.140
  219.3 12.6 %feed_forward.2 = (f32[304,1024]{1,0:T(8,128)S(1)}, bf16[304,1024]{1,0:T(8,128)(2,1)S(1)}, bf16[608,2048]{1,0:T(8,128)(2,1)S(1)}) custom-call(bf16[1024,2304]{1,0:T(8,128)(2,1)} %all-gather.7.cloned.1.call-done.refs_0_.refs_1_, bf16[1024,2304]{1,0:T(8,128)(2,1)} %all-gather.7.cloned.1.call-done.refs_0_.refs_1_, ...), custom_call_target="tpu_custom_call" | custom-call | flops 1275068 | bytes 1 | tf_op jit(solution)/shard_map/feed_forward/pallas_call | solution.py:403
  232.1 1.9 collective-permute-done.15
  235.7 1.7 collective-permute-start.17
  237.4 2.7 collective-permute-start.22
  240.2 18.2 %collective-permute-done.17 = bf16[304,1024]{1,0:T(8,128)(2,1)S(1)} collective-permute-done((bf16[304,1024]{1,0:T(8,128)(2,1)S(1)}, bf16[304,1024]{1,0:T(8,128)(2,1)S(1)}, u32[]{:S(2)}, u32[]{:S(2)}) %collective-permute-start.17) | collective-permute-done | bytes 622624 | tf_op jit(solution)/shard_map/ppermute | solution.py:71
  265.2 12.0 %attend.3 = (bf16[1280,256]{1,0:T(8,128)(2,1)S(1)}, f32[4,1280]{1,0:T(4,128)S(1)}) custom-call(s32[10,2]{1,0:T(8,128)S(1)} %copy.77.range_ref, s32[2,1280]{1,0:T(2,128)S(1)} %pad_add_fusion.span_ref, bf16[1280,768]{1,0:T(8,128)(2,1)S(1)} %fusion.29.qkv_ref), custom_call_target="tpu_custom_call" | custom-call | flops 419430 | bytes 1 | tf_op jit(solution)/shard_map/attend/pallas_call | solution.py:257
  277.3 2.8 collective-permute-done.24
  281.1 9.0 %collective-permute-done.25 = bf16[608,256]{1,0:T(8,128)(2,1)} collective-permute-done((bf16[608,256]{1,0:T(8,128)(2,1)S(1)}, bf16[608,256]{1,0:T(8,128)(2,1)}, u32[]{:S(2)}, u32[]{:S(2)}) %collective-permute-start.25) | collective-permute-done | bytes 311328 | tf_op jit(solution)/shard_map/ppermute | solution.py:71
  290.1 6.2 %all-gather.11.cloned.1.call-done.refs_0_.refs_1_ = bf16[1024,4608]{1,0:T(8,128)(2,1)} async-done(((bf16[256,4608]{1,0:T(8,128)(2,1)}), bf16[1024,4608]{1,0:T(8,128)(2,1)}) %all-gather.11.cloned.1.call-update) | async-done | bytes 9437200 | tf_op jit(solution)/shard_map/all_gather | solution.py:84
  301.5 1.7 fusion.141
  306.0 11.7 %feed_forward.3 = (f32[304,1024]{1,0:T(8,128)S(1)}, bf16[304,1024]{1,0:T(8,128)(2,1)S(1)}, bf16[608,2048]{1,0:T(8,128)(2,1)S(1)}) custom-call(bf16[1024,4608]{1,0:T(8,128)(2,1)} %all-gather.11.cloned.1.call-done.refs_0_.refs_1_, bf16[1024,4608]{1,0:T(8,128)(2,1)} %all-gather.11.cloned.1.call-done.refs_0_.refs_1_, bf16[304,1024]{1,0:T(8,128)(2,1)S(1)} %fusion.33.refs_2_, ...), custom_call_target="tpu_custom_call" | custom-call | flops 1275068 | bytes 1 | tf_op jit(solution)/shard_map/feed_forward/pallas_call | solution.py:403
  318.1 1.7 collective-permute-done.28
  322.7 1.7 collective-permute-done.29.refs_3_
  324.4 8.0 %feed_back.2 = (f32[304,1024]{1,0:T(8,128)S(1)}, bf16[304,1024]{1,0:T(8,128)(2,1)S(1)}) custom-call(bf16[1024,4608]{1,0:T(8,128)(2,1)} %all-gather.11.cloned.1.call-done.refs_0_.refs_1_, bf16[1024,4608]{1,0:T(8,128)(2,1)} %all-gather.11.cloned.1.call-done.refs_0_.refs_1_, bf16[304,1024]{1,0:T(8,128)(2,1)S(1)} %fusion.127.refs_2_, ...), custom_call_target="tpu_custom_call" | custom-call | flops 1275068 | bytes 1 | tf_op jit(solution)/shard_map/feed_back/pallas_call | solution.py:403
  332.8 1.7 collective-permute-done.30
  336.5 1.7 collective-permute-done.31
  338.2 1.7 convolution_convert_fusion.7
  339.9 1.6 collective-permute-start.32
  341.4 1.5 convolution_convert_fusion.6
  343.0 6.6 %collective-permute-done.32 = bf16[608,256]{1,0:T(8,128)(2,1)S(1)} collective-permute-done((bf16[608,256]{1,0:T(8,128)(2,1)S(1)}, bf16[608,256]{1,0:T(8,128)(2,1)S(1)}, u32[]{:S(2)}, u32[]{:S(2)}) %collective-permute-start.32) | collective-permute-done | bytes 311328 | tf_op jit(solution)/shard_map/ppermute | solution.py:71
  349.7 1.5 collective-permute-start.33
  351.9 17.1 %attend_back.2 = (bf16[1280,768]{1,0:T(8,128)(2,1)S(1)}, f32[2,64,256]{2,1,0:T(8,128)S(1)}) custom-call(s32[10,2]{1,0:T(8,128)S(1)} %copy.77.range_ref, s32[2,1280]{1,0:T(2,128)S(1)} %pad_add_fusion.span_ref, bf16[1280,768]{1,0:T(8,128)(2,1)S(1)} %fusion.29.qkv_ref, f32[4,1280]{1,0:T(4,128)S(1)} %get-tuple-element.87.lse_ref, ...), custom_call_target="tpu_custom_call" | custom-call | flops 1048576 | bytes 1 | tf_op jit(solution)/shard_map/attend_back/pallas_call | solution.py:272
  369.8 3.4 collective-permute-start.36
  376.5 15.5 %collective-permute-done.37 = bf16[304,1024]{1,0:T(8,128)(2,1)S(1)} collective-permute-done((bf16[304,1024]{1,0:T(8,128)(2,1)S(1)}, bf16[304,1024]{1,0:T(8,128)(2,1)S(1)}, u32[]{:S(2)}, u32[]{:S(2)}) %collective-permute-start.37) | collective-permute-done | bytes 622624 | tf_op jit(solution)/shard_map/ppermute | solution.py:71
  393.7 2.0 collective-permute-done.38.refs_5_
  395.8 8.9 %feed_back.3 = (f32[304,1024]{1,0:T(8,128)S(1)}, bf16[304,1024]{1,0:T(8,128)(2,1)S(1)}) custom-call(bf16[1024,2304]{1,0:T(8,128)(2,1)} %all-gather.7.cloned.1.call-done.refs_0_.refs_1_, bf16[1024,2304]{1,0:T(8,128)(2,1)} %all-gather.7.cloned.1.call-done.refs_0_.refs_1_, bf16[1024,3072]{1,0:T(8,128)(2,1)} %all-gather.9.cloned.1.call-done.refs_2_.refs_3_, ...), custom_call_target="tpu_custom_call" | custom-call | flops 1275068 | bytes 1 | tf_op jit(solution)/shard_map/feed_back/pallas_call | solution.py:403
  404.9 1.9 collective-permute-done.39
  408.4 1.9 collective-permute-done.40
  410.3 1.5 convolution_convert_fusion.5
  412.8 1.7 convolution_convert_fusion.4
  414.4 6.9 %collective-permute-done.41 = bf16[608,256]{1,0:T(8,128)(2,1)S(1)} collective-permute-done((bf16[608,256]{1,0:T(8,128)(2,1)S(1)}, bf16[608,256]{1,0:T(8,128)(2,1)S(1)}, u32[]{:S(2)}, u32[]{:S(2)}) %collective-permute-start.41) | collective-permute-done | bytes 311328 | tf_op jit(solution)/shard_map/ppermute | solution.py:71
  423.6 17.0 %attend_back.3 = (bf16[1280,768]{1,0:T(8,128)(2,1)S(1)}, f32[2,64,256]{2,1,0:T(8,128)S(1)}) custom-call(s32[10,2]{1,0:T(8,128)S(1)} %copy.77.range_ref, s32[2,1280]{1,0:T(2,128)S(1)} %pad_add_fusion.span_ref, bf16[1280,768]{1,0:T(8,128)(2,1)S(1)} %copy-done.1, f32[4,1280]{1,0:T(4,128)S(1)} %get-tuple-element.94.lse_ref, ...), custom_call_target="tpu_custom_call" | custom-call | flops 1048576 | bytes 1 | tf_op jit(solution)/shard_map/attend_back/pallas_call | solution.py:272
  441.3 1.7 collective-permute-start.45
  443.0 2.2 collective-permute-start.47
  446.7 4.9 collective-permute-done.47
  453.0 6.4 %collective-permute-done.48 = f32[2,2,64,256]{3,2,1,0:T(8,128)S(1)} collective-permute-done((f32[2,2,64,256]{3,2,1,0:T(8,128)S(1)}, f32[2,2,64,256]{3,2,1,0:T(8,128)S(1)}, u32[]{:S(2)}, u32[]{:S(2)}) %collective-permute-start.48) | collective-permute-done | bytes 262176 | tf_op jit(solution)/shard_map/ppermute | solution.py:492
  459.5 3.6 collective-permute-done.46
  465.4 3.7 collective-permute-start.52
  471.5 13.8 %collective-permute-done.52 = f32[2,64,256]{2,1,0:T(8,128)S(1)} collective-permute-done((f32[2,64,256]{2,1,0:T(8,128)S(1)}, f32[2,64,256]{2,1,0:T(8,128)S(1)}, u32[]{:S(2)}, u32[]{:S(2)}) %collective-permute-start.52) | collective-permute-done | bytes 131104 | tf_op jit(solution)/shard_map/ppermute | solution.py:65
  486.1 5.9 %collective-permute-done.50 = bf16[304,1024]{1,0:T(8,128)(2,1)S(1)} collective-permute-done((bf16[304,1024]{1,0:T(8,128)(2,1)S(1)}, bf16[304,1024]{1,0:T(8,128)(2,1)S(1)}, u32[]{:S(2)}, u32[]{:S(2)}) %collective-permute-start.50) | collective-permute-done | bytes 622624 | tf_op jit(solution)/shard_map/ppermute | solution.py:65
  (313 shorter events, 84.2 us)
Async XLA Ops:
  7.2 59.4 %all-gather.5.cloned.1.call-start = ((), (), s32[]{:S(2)}) async-start(), calls=%async_computation | async-start | bytes 1966080 | tf_op jit(solution)/shard_map/all_gather | solution.py:84
  10.3 8.2 %collective-permute-start = (bf16[336,768]{1,0:T(8,128)(2,1)S(1)}, bf16[336,768]{1,0:T(8,128)(2,1)S(1)}, u32[]{:S(2)}, u32[]{:S(2)}) collective-permute-start(bf16[336,768]{1,0:T(8,128)(2,1)S(1)} %pad_maximum_fusion.9), channel_id=1, source_target_pairs={{0,0},{1,1},{2,16},{3,17},{4,4},{5,5},{6,20},{7,21},{8,8},{9,9},{1... | collective-permute-start | bytes 1548296 | tf_op jit(solution)/shard_map/ppermute | solution.py:65
  11.2 13.2 %collective-permute-start.1 = (bf16[336,768]{1,0:T(8,128)(2,1)S(1)}, bf16[336,768]{1,0:T(8,128)(2,1)}, u32[]{:S(2)}, u32[]{:S(2)}) collective-permute-start(bf16[336,768]{1,0:T(8,128)(2,1)S(1)} %pad_maximum_fusion.9), channel_id=1, source_target_pairs={{0,2},{1,3},{2,18},{3,19},{4,6},{5,7},{6,22},{7,23},{8,10},{9,11},... | collective-permute-start | bytes 1548296 | tf_op jit(solution)/shard_map/ppermute | solution.py:65
  26.5 99.6 %all-gather.7.cloned.1.call-start = ((), (), s32[]{:S(2)}) async-start(), calls=%async_computation.1 | async-start | bytes 5898240 | tf_op jit(solution)/shard_map/all_gather | solution.py:84
  26.7 10.3 %collective-permute-start.2 = (bf16[272,2304]{1,0:T(8,128)(2,1)S(1)}, bf16[272,2304]{1,0:T(8,128)(2,1)S(1)}, u32[]{:S(2)}, u32[]{:S(2)}) collective-permute-start(bf16[272,2304]{1,0:T(8,128)(2,1)S(1)} %pad_maximum_fusion.1), channel_id=1, source_target_pairs={{0,0},{1,1},{2,16},{3,17},{4,4},{5,5},{6,20},{7,21},{8,8},{9,9},{1... | collective-permute-start | bytes 3760136 | tf_op jit(solution)/shard_map/ppermute | solution.py:65
  27.5 24.0 %collective-permute-start.3 = (bf16[272,2304]{1,0:T(8,128)(2,1)S(1)}, bf16[272,2304]{1,0:T(8,128)(2,1)S(1)}, u32[]{:S(2)}, u32[]{:S(2)}) collective-permute-start(bf16[272,2304]{1,0:T(8,128)(2,1)S(1)} %pad_maximum_fusion.1), channel_id=1, source_target_pairs={{0,2},{1,3},{2,18},{3,19},{4,6},{5,7},{6,22},{7,23},{8,10},{9,11},... | collective-permute-start | bytes 3760136 | tf_op jit(solution)/shard_map/ppermute | solution.py:65
  66.7 133.9 %all-gather.9.cloned.1.call-start = ((), (), s32[]{:S(2)}) async-start(), calls=%async_computation.2 | async-start | bytes 7864320 | tf_op jit(solution)/shard_map/all_gather | solution.py:84
  66.7 4.2 collective-permute-start.4
  68.0 3.7 collective-permute-start.5
  69.5 42.8 %collective-permute-start.11 = (bf16[272,2304]{1,0:T(8,128)(2,1)S(1)}, bf16[272,2304]{1,0:T(8,128)(2,1)}, u32[]{:S(2)}, u32[]{:S(2)}) collective-permute-start(bf16[272,2304]{1,0:T(8,128)(2,1)S(1)} %broadcast_select_fusion.1), channel_id=1, source_target_pairs={{0,1},{1,0},{2,3},{3,2},{4,5},{5,4},{6,7},{7,6},{8,9},{9,8},{10,11... | collective-permute-start | bytes 3760136 | tf_op jit(solution)/shard_map/ppermute | solution.py:71
  72.8 39.4 %copy-start.16 = (bf16[336,768]{1,0:T(8,128)(2,1)}, bf16[336,768]{1,0:T(8,128)(2,1)S(1)}, u32[]{:S(2)}) copy-start(bf16[336,768]{1,0:T(8,128)(2,1)S(1)} %broadcast_select_fusion.2) | copy-start | bytes 1548292
  74.2 36.9 %collective-permute-start.6 = (bf16[304,1024]{1,0:T(8,128)(2,1)S(1)}, bf16[304,1024]{1,0:T(8,128)(2,1)}, u32[]{:S(2)}, u32[]{:S(2)}) collective-permute-start(bf16[304,1024]{1,0:T(8,128)(2,1)S(1)} %dynamic-slice_bitcast_fusion.1), channel_id=1, source_target_pairs={{0,2},{1,3},{18,16},{19,17},{4,6},{5,7},{22,20},{23,21},{8,10},{9,... | collective-permute-start | bytes 1867784 | tf_op jit(solution)/shard_map/ppermute | solution.py:65
  112.2 55.9 %copy-start.12 = (bf16[304,1024]{1,0:T(8,128)(2,1)}, bf16[304,1024]{1,0:T(8,128)(2,1)S(1)}, u32[]{:S(2)}) copy-start(bf16[304,1024]{1,0:T(8,128)(2,1)S(1)} %bitcast_select_fusion.1) | copy-start | bytes 1867780
  126.2 170.1 %all-gather.11.cloned.1.call-start = ((), (), s32[]{:S(2)}) async-start(), calls=%async_computation.3 | async-start | bytes 11796480 | tf_op jit(solution)/shard_map/all_gather | solution.py:84
  129.0 34.1 %copy-start.39 = (s32[8]{0:T(128)S(1)}, s32[8]{0:T(128)}, u32[]{:S(2)}) copy-start(s32[8]{0:T(128)} %constant.148.clone) | copy-start | bytes 100
  130.2 34.9 %collective-permute-start.19 = (bf16[272,2304]{1,0:T(8,128)(2,1)}, bf16[272,2304]{1,0:T(8,128)(2,1)S(1)}, u32[]{:S(2)}, u32[]{:S(2)}) collective-permute-start(bf16[272,2304]{1,0:T(8,128)(2,1)} %pad_maximum_fusion.2), channel_id=1, source_target_pairs={{16,0},{17,1},{18,16},{19,17},{20,4},{21,5},{22,20},{23,21},{24,8}... | collective-permute-start | bytes 3760136 | tf_op jit(solution)/shard_map/ppermute | solution.py:65
  131.5 33.7 %collective-permute-start.20 = (bf16[272,2304]{1,0:T(8,128)(2,1)}, bf16[272,2304]{1,0:T(8,128)(2,1)}, u32[]{:S(2)}, u32[]{:S(2)}) collective-permute-start(bf16[272,2304]{1,0:T(8,128)(2,1)} %pad_maximum_fusion.2), channel_id=1, source_target_pairs={{16,2},{17,3},{18,18},{19,19},{20,6},{21,7},{22,22},{23,23},{24,10... | collective-permute-start | bytes 3760136 | tf_op jit(solution)/shard_map/ppermute | solution.py:65
  133.8 22.0 %collective-permute-start.8 = (bf16[304,1024]{1,0:T(8,128)(2,1)S(1)}, bf16[304,1024]{1,0:T(8,128)(2,1)}, u32[]{:S(2)}, u32[]{:S(2)}) collective-permute-start(bf16[304,1024]{1,0:T(8,128)(2,1)S(1)} %bitcast_select_fusion.1), channel_id=1, source_target_pairs={{0,1},{1,0},{2,3},{3,2},{4,5},{5,4},{6,7},{7,6},{8,9},{9,8},{10,11... | collective-permute-start | bytes 1867784 | tf_op jit(solution)/shard_map/ppermute | solution.py:71
  135.6 28.7 %collective-permute-start.7 = (bf16[304,1024]{1,0:T(8,128)(2,1)S(1)}, bf16[304,1024]{1,0:T(8,128)(2,1)}, u32[]{:S(2)}, u32[]{:S(2)}) collective-permute-start(bf16[304,1024]{1,0:T(8,128)(2,1)S(1)} %bitcast_select_fusion.1), channel_id=1, source_target_pairs={{0,16},{16,0},{1,17},{17,1},{2,18},{18,2},{3,19},{19,3},{4,20},{20... | collective-permute-start | bytes 1867784 | tf_op jit(solution)/shard_map/ppermute | solution.py:68
  155.8 9.3 %collective-permute-start.9 = (bf16[304,1024]{1,0:T(8,128)(2,1)}, bf16[304,1024]{1,0:T(8,128)(2,1)}, u32[]{:S(2)}, u32[]{:S(2)}) collective-permute-start(bf16[304,1024]{1,0:T(8,128)(2,1)} %collective-permute-done.8), channel_id=1, source_target_pairs={{0,16},{16,0},{1,17},{17,1},{2,18},{18,2},{3,19},{19,3},{4,20},{20... | collective-permute-start | bytes 1867784 | tf_op jit(solution)/shard_map/ppermute | solution.py:68
  165.3 33.9 %copy-start.9 = (bf16[272,2304]{1,0:T(8,128)(2,1)}, bf16[272,2304]{1,0:T(8,128)(2,1)S(1)}, u32[]{:S(2)}) copy-start(bf16[272,2304]{1,0:T(8,128)(2,1)S(1)} %broadcast_select_fusion) | copy-start | bytes 3760132
  165.3 30.2 %collective-permute-start.21 = (bf16[272,2304]{1,0:T(8,128)(2,1)S(1)}, bf16[272,2304]{1,0:T(8,128)(2,1)S(1)}, u32[]{:S(2)}, u32[]{:S(2)}) collective-permute-start(bf16[272,2304]{1,0:T(8,128)(2,1)S(1)} %broadcast_select_fusion), channel_id=1, source_target_pairs={{0,1},{1,0},{2,3},{3,2},{4,5},{5,4},{6,7},{7,6},{8,9},{9,8},{10,11... | collective-permute-start | bytes 3760136 | tf_op jit(solution)/shard_map/ppermute | solution.py:71
  201.3 2.0 collective-permute-start.13
  201.5 9.8 %collective-permute-start.10 = (bf16[608,256]{1,0:T(8,128)(2,1)S(1)}, bf16[608,256]{1,0:T(8,128)(2,1)S(1)}, u32[]{:S(2)}, u32[]{:S(2)}) collective-permute-start(bf16[608,256]{1,0:T(8,128)(2,1)S(1)} %pad_maximum_fusion.10), channel_id=1, source_target_pairs={{0,1},{1,0},{2,3},{3,2},{4,5},{5,4},{6,7},{7,6},{8,9},{9,8},{10,11... | collective-permute-start | bytes 933896 | tf_op jit(solution)/shard_map/ppermute | solution.py:71
  212.8 2.1 collective-permute-start.12
  216.9 45.6 %slice-start = ((s8[6291456]{0:T(1024)(128)(4,1)}), s8[4194304]{0:T(1024)(128)(4,1)S(1)}, s32[]{:S(2)}) async-start(s8[6291456]{0:T(1024)(128)(4,1)} %bitcast.137), calls=%async_computation.4 | async-start | bytes 8388608
  217.2 2.1 collective-permute-start.14
  218.5 44.0 %slice-start.1 = ((s8[6291456]{0:T(1024)(128)(4,1)}), s8[2097152]{0:T(1024)(128)(4,1)S(1)}, s32[]{:S(2)}) async-start(s8[6291456]{0:T(1024)(128)(4,1)} %bitcast.137), calls=%async_computation.5 | async-start | bytes 4194304
  231.9 2.1 collective-permute-start.15
  235.7 22.8 %collective-permute-start.17 = (bf16[304,1024]{1,0:T(8,128)(2,1)S(1)}, bf16[304,1024]{1,0:T(8,128)(2,1)S(1)}, u32[]{:S(2)}, u32[]{:S(2)}) collective-permute-start(bf16[304,1024]{1,0:T(8,128)(2,1)S(1)} %add_convert_fusion.1), channel_id=1, source_target_pairs={{0,1},{1,0},{2,3},{3,2},{4,5},{5,4},{6,7},{7,6},{8,9},{9,8},{10,11... | collective-permute-start | bytes 1867784 | tf_op jit(solution)/shard_map/ppermute | solution.py:71
  237.4 21.1 %collective-permute-start.22 = (bf16[304,1024]{1,0:T(8,128)(2,1)S(1)}, bf16[304,1024]{1,0:T(8,128)(2,1)S(1)}, u32[]{:S(2)}, u32[]{:S(2)}) collective-permute-start(bf16[304,1024]{1,0:T(8,128)(2,1)S(1)} %dynamic-slice_bitcast_fusion), channel_id=1, source_target_pairs={{0,2},{1,3},{18,16},{19,17},{4,6},{5,7},{22,20},{23,21},{8,10},{9,... | collective-permute-start | bytes 1867784 | tf_op jit(solution)/shard_map/ppermute | solution.py:65
  240.2 19.4 %collective-permute-start.16 = (bf16[304,1024]{1,0:T(8,128)(2,1)S(1)}, bf16[304,1024]{1,0:T(8,128)(2,1)S(1)}, u32[]{:S(2)}, u32[]{:S(2)}) collective-permute-start(bf16[304,1024]{1,0:T(8,128)(2,1)S(1)} %add_convert_fusion.1), channel_id=1, source_target_pairs={{0,16},{16,0},{1,17},{17,1},{2,18},{18,2},{3,19},{19,3},{4,20},{20... | collective-permute-start | bytes 1867784 | tf_op jit(solution)/shard_map/ppermute | solution.py:68
  258.4 2.1 collective-permute-start.18
  260.5 16.8 %collective-permute-start.23 = (bf16[304,1024]{1,0:T(8,128)(2,1)S(1)}, bf16[304,1024]{1,0:T(8,128)(2,1)S(1)}, u32[]{:S(2)}, u32[]{:S(2)}) collective-permute-start(bf16[304,1024]{1,0:T(8,128)(2,1)S(1)} %add_convert_fusion.1), channel_id=1, source_target_pairs={{0,0},{1,1},{16,2},{17,3},{4,4},{5,5},{20,6},{21,7},{8,8},{9,9},{2... | collective-permute-start | bytes 1867784 | tf_op jit(solution)/shard_map/ppermute | solution.py:65
  261.2 18.9 %collective-permute-start.24 = (bf16[304,1024]{1,0:T(8,128)(2,1)S(1)}, bf16[304,1024]{1,0:T(8,128)(2,1)S(1)}, u32[]{:S(2)}, u32[]{:S(2)}) collective-permute-start(bf16[304,1024]{1,0:T(8,128)(2,1)S(1)} %add_convert_fusion.1), channel_id=1, source_target_pairs={{2,0},{3,1},{18,2},{19,3},{6,4},{7,5},{22,6},{23,7},{10,8},{11,9},... | collective-permute-start | bytes 1867784 | tf_op jit(solution)/shard_map/ppermute | solution.py:65
  281.0 9.1 %collective-permute-start.25 = (bf16[608,256]{1,0:T(8,128)(2,1)S(1)}, bf16[608,256]{1,0:T(8,128)(2,1)}, u32[]{:S(2)}, u32[]{:S(2)}) collective-permute-start(bf16[608,256]{1,0:T(8,128)(2,1)S(1)} %pad_maximum_fusion.11), channel_id=1, source_target_pairs={{0,1},{1,0},{2,3},{3,2},{4,5},{5,4},{6,7},{7,6},{8,9},{9,8},{10,11... | collective-permute-start | bytes 933896 | tf_op jit(solution)/shard_map/ppermute | solution.py:71
  299.2 2.3 collective-permute-start.26
  303.8 2.2 collective-permute-start.27
  317.6 2.1 collective-permute-start.28
  322.3 2.1 collective-permute-start.29
  332.4 2.1 collective-permute-start.30
  336.0 2.1 collective-permute-start.31
  338.2 30.9 %slice-start.2 = ((s8[6291456]{0:T(1024)(128)(4,1)}), s8[4194304]{0:T(1024)(128)(4,1)S(1)}, s32[]{:S(2)}) async-start(s8[6291456]{0:T(1024)(128)(4,1)} %bitcast.139), calls=%async_computation.6 | async-start | bytes 8388608
  339.9 9.7 %collective-permute-start.32 = (bf16[608,256]{1,0:T(8,128)(2,1)S(1)}, bf16[608,256]{1,0:T(8,128)(2,1)S(1)}, u32[]{:S(2)}, u32[]{:S(2)}) collective-permute-start(bf16[608,256]{1,0:T(8,128)(2,1)S(1)} %convolution_convert_fusion.7), channel_id=1, source_target_pairs={{0,1},{1,0},{2,3},{3,2},{4,5},{5,4},{6,7},{7,6},{8,9},{9,8},{10,11... | collective-permute-start | bytes 933896 | tf_op jit(solution)/shard_map/ppermute | solution.py:71
  349.7 19.4 %collective-permute-start.33 = (bf16[304,1024]{1,0:T(8,128)(2,1)S(1)}, bf16[304,1024]{1,0:T(8,128)(2,1)S(1)}, u32[]{:S(2)}, u32[]{:S(2)}) collective-permute-start(bf16[304,1024]{1,0:T(8,128)(2,1)S(1)} %get-tuple-element.86), channel_id=1, source_target_pairs={{0,16},{1,17},{16,18},{17,19},{4,20},{5,21},{20,22},{21,23},{8,24}... | collective-permute-start | bytes 1867784 | tf_op jit(solution)/shard_map/ppermute | solution.py:65
  351.2 17.9 %collective-permute-start.34 = (bf16[304,1024]{1,0:T(8,128)(2,1)S(1)}, bf16[304,1024]{1,0:T(8,128)(2,1)S(1)}, u32[]{:S(2)}, u32[]{:S(2)}) collective-permute-start(bf16[304,1024]{1,0:T(8,128)(2,1)S(1)} %get-tuple-element.86), channel_id=1, source_target_pairs={{2,16},{3,17},{18,18},{19,19},{6,20},{7,21},{22,22},{23,23},{10,24... | collective-permute-start | bytes 1867784 | tf_op jit(solution)/shard_map/ppermute | solution.py:65
  369.8 5.1 %collective-permute-start.36 = (bf16[304,1024]{1,0:T(8,128)(2,1)S(1)}, bf16[304,1024]{1,0:T(8,128)(2,1)S(1)}, u32[]{:S(2)}, u32[]{:S(2)}) collective-permute-start(bf16[304,1024]{1,0:T(8,128)(2,1)S(1)} %convolution_convert_fusion.2), channel_id=1, source_target_pairs={{0,16},{16,0},{1,17},{17,1},{2,18},{18,2},{3,19},{19,3},{4,20},{20... | collective-permute-start | bytes 1867784 | tf_op jit(solution)/shard_map/ppermute | solution.py:68
  373.9 2.6 collective-permute-start.35
  375.6 16.4 %collective-permute-start.37 = (bf16[304,1024]{1,0:T(8,128)(2,1)S(1)}, bf16[304,1024]{1,0:T(8,128)(2,1)S(1)}, u32[]{:S(2)}, u32[]{:S(2)}) collective-permute-start(bf16[304,1024]{1,0:T(8,128)(2,1)S(1)} %fusion.12), channel_id=1, source_target_pairs={{0,1},{1,0},{2,3},{3,2},{4,5},{5,4},{6,7},{7,6},{8,9},{9,8},{10,11... | collective-permute-start | bytes 1867784 | tf_op jit(solution)/shard_map/ppermute | solution.py:71
  393.6 2.1 collective-permute-start.38
  404.7 2.1 collective-permute-start.39
  408.2 2.1 collective-permute-start.40
  411.9 9.5 %collective-permute-start.41 = (bf16[608,256]{1,0:T(8,128)(2,1)S(1)}, bf16[608,256]{1,0:T(8,128)(2,1)S(1)}, u32[]{:S(2)}, u32[]{:S(2)}) collective-permute-start(bf16[608,256]{1,0:T(8,128)(2,1)S(1)} %convolution_convert_fusion.5), channel_id=1, source_target_pairs={{0,1},{1,0},{2,3},{3,2},{4,5},{5,4},{6,7},{7,6},{8,9},{9,8},{10,11... | collective-permute-start | bytes 933896 | tf_op jit(solution)/shard_map/ppermute | solution.py:71
  421.5 19.1 %collective-permute-start.42 = (bf16[304,1024]{1,0:T(8,128)(2,1)S(1)}, bf16[304,1024]{1,0:T(8,128)(2,1)S(1)}, u32[]{:S(2)}, u32[]{:S(2)}) collective-permute-start(bf16[304,1024]{1,0:T(8,128)(2,1)S(1)} %get-tuple-element.93), channel_id=1, source_target_pairs={{0,16},{1,17},{16,18},{17,19},{4,20},{5,21},{20,22},{21,23},{8,24}... | collective-permute-start | bytes 1867784 | tf_op jit(solution)/shard_map/ppermute | solution.py:65
  422.8 17.8 %collective-permute-start.43 = (bf16[304,1024]{1,0:T(8,128)(2,1)S(1)}, bf16[304,1024]{1,0:T(8,128)(2,1)S(1)}, u32[]{:S(2)}, u32[]{:S(2)}) collective-permute-start(bf16[304,1024]{1,0:T(8,128)(2,1)S(1)} %get-tuple-element.93), channel_id=1, source_target_pairs={{2,16},{3,17},{18,18},{19,19},{6,20},{7,21},{22,22},{23,23},{10,24... | collective-permute-start | bytes 1867784 | tf_op jit(solution)/shard_map/ppermute | solution.py:65
  441.3 4.6 collective-permute-start.45
  443.0 8.6 %collective-permute-start.47 = (f32[2,2,64,256]{3,2,1,0:T(8,128)S(1)}, f32[2,2,64,256]{3,2,1,0:T(8,128)S(1)}, u32[]{:S(2)}, u32[]{:S(2)}) collective-permute-start(f32[2,2,64,256]{3,2,1,0:T(8,128)S(1)} %pad_maximum_fusion.12), channel_id=1, source_target_pairs={{0,4},{4,0},{8,12},{12,8},{1,5},{5,1},{9,13},{13,9},{2,6},{6,2},{1... | collective-permute-start | bytes 786440 | tf_op jit(solution)/shard_map/ppermute | solution.py:492
  445.8 17.3 %collective-permute-start.44 = (bf16[304,1024]{1,0:T(8,128)(2,1)S(1)}, bf16[304,1024]{1,0:T(8,128)(2,1)S(1)}, u32[]{:S(2)}, u32[]{:S(2)}) collective-permute-start(bf16[304,1024]{1,0:T(8,128)(2,1)S(1)} %convolution_convert_fusion.1), channel_id=1, source_target_pairs={{0,16},{16,0},{1,17},{17,1},{2,18},{18,2},{3,19},{19,3},{4,20},{20... | collective-permute-start | bytes 1867784 | tf_op jit(solution)/shard_map/ppermute | solution.py:68
  446.6 16.5 %collective-permute-start.46 = (bf16[304,1024]{1,0:T(8,128)(2,1)S(1)}, bf16[304,1024]{1,0:T(8,128)(2,1)S(1)}, u32[]{:S(2)}, u32[]{:S(2)}) collective-permute-start(bf16[304,1024]{1,0:T(8,128)(2,1)S(1)} %fusion.13), channel_id=1, source_target_pairs={{0,1},{1,0},{2,3},{3,2},{4,5},{5,4},{6,7},{7,6},{8,9},{9,8},{10,11... | collective-permute-start | bytes 1867784 | tf_op jit(solution)/shard_map/ppermute | solution.py:71
  451.7 7.8 %collective-permute-start.48 = (f32[2,2,64,256]{3,2,1,0:T(8,128)S(1)}, f32[2,2,64,256]{3,2,1,0:T(8,128)S(1)}, u32[]{:S(2)}, u32[]{:S(2)}) collective-permute-start(f32[2,2,64,256]{3,2,1,0:T(8,128)S(1)} %fusion.126), channel_id=1, source_target_pairs={{0,8},{4,12},{8,0},{12,4},{1,9},{5,13},{9,1},{13,5},{2,10},{6,14},... | collective-permute-start | bytes 786440 | tf_op jit(solution)/shard_map/ppermute | solution.py:492
  463.9 22.1 %collective-permute-start.49 = (bf16[304,1024]{1,0:T(8,128)(2,1)S(1)}, bf16[304,1024]{1,0:T(8,128)(2,1)S(1)}, u32[]{:S(2)}, u32[]{:S(2)}) collective-permute-start(bf16[304,1024]{1,0:T(8,128)(2,1)S(1)} %fusion.8), channel_id=1, source_target_pairs={{0,0},{1,1},{16,2},{17,3},{4,4},{5,5},{20,6},{21,7},{8,8},{9,9},{2... | collective-permute-start | bytes 1867784 | tf_op jit(solution)/shard_map/ppermute | solution.py:65
  464.7 6.8 %collective-permute-start.51 = (f32[2,64,256]{2,1,0:T(8,128)S(1)}, f32[2,64,256]{2,1,0:T(8,128)S(1)}, u32[]{:S(2)}, u32[]{:S(2)}) collective-permute-start(f32[2,64,256]{2,1,0:T(8,128)S(1)} %get-tuple-element.144), channel_id=1, source_target_pairs={{0,0},{1,1},{2,16},{3,17},{16,2},{17,3},{18,18},{19,19},{4,4},{5,5... | collective-permute-start | bytes 393224 | tf_op jit(solution)/shard_map/ppermute | solution.py:65
  465.4 20.0 %collective-permute-start.52 = (f32[2,64,256]{2,1,0:T(8,128)S(1)}, f32[2,64,256]{2,1,0:T(8,128)S(1)}, u32[]{:S(2)}, u32[]{:S(2)}) collective-permute-start(f32[2,64,256]{2,1,0:T(8,128)S(1)} %get-tuple-element.143), channel_id=1, source_target_pairs={{0,16},{1,17},{2,0},{3,1},{16,18},{17,19},{18,2},{19,3},{4,20},{5,... | collective-permute-start | bytes 393224 | tf_op jit(solution)/shard_map/ppermute | solution.py:65
  469.1 22.9 %collective-permute-start.50 = (bf16[304,1024]{1,0:T(8,128)(2,1)S(1)}, bf16[304,1024]{1,0:T(8,128)(2,1)S(1)}, u32[]{:S(2)}, u32[]{:S(2)}) collective-permute-start(bf16[304,1024]{1,0:T(8,128)(2,1)S(1)} %fusion.8), channel_id=1, source_target_pairs={{2,0},{3,1},{18,2},{19,3},{6,4},{7,5},{22,6},{23,7},{10,8},{11,9},... | collective-permute-start | bytes 1867784 | tf_op jit(solution)/shard_map/ppermute | solution.py:65
  (38 other events, 297.0 us)
Sparse Core Ops, SparseCore 0:
  26.7 39.9 all-gather.4
  69.0 57.0 all-gather.6
  128.0 70.1 all-gather.8
  200.7 95.4 all-gather.10

commit v5 on v4

--- a/solution.py
+++ b/solution.py
@@ -109,7 +109,8 @@
 
 
 def own_shard(place, l, out, up, up_bias, down):
-    block = jnp.concatenate([up[0].astype(BF), down[0].astype(BF).T, out[0].astype(BF).T], axis=1)
+    parts = [up[0].astype(BF), down[0].astype(BF).T, out[0].astype(BF).T]
+    block = jnp.concatenate(parts[: 3 - l], axis=1)
     bias = jnp.stack(high_low(up_bias[0]))
     bias = jnp.pad(bias, ((0, 14), (0, block.shape[1] - bias.shape[1])))
     block = jnp.concatenate([block, bias], 0)
@@ -487,9 +488,15 @@
     return da, go
 
 
-def swap_add(value, bit):
-    count = lax.axis_size("dp")
-    return value + lax.ppermute(value, "dp", [(i, i ^ bit) for i in range(count)])
+def total_dp(value):
+    count, low = lax.axis_size("dp"), value.astype(BF)
+    terms = [low] + [
+        lax.ppermute(low, "dp", [(i, i ^ x) for i in range(count)]) for x in range(1, count)
+    ]
+    terms = [term.astype(F32) for term in terms]
+    while len(terms) > 1:
+        terms = [terms[i] + terms[i + 1] for i in range(0, len(terms), 2)]
+    return terms[0]
 
 
 def input_back(place, order, da, back, qkv_w, kv=None):
@@ -502,10 +509,11 @@
         else:
             sent.append(place.chip(summed.astype(BF), j))
     if kv is not None:
-        bit = 1
-        while bit < lax.axis_size("dp"):
-            kv = swap_add(kv, bit)
-            bit *= 2
+        kv = total_dp(kv)
+        first = place.m == 0
+        kv = place.send(jnp.where(first, kv[0], kv[1]), lambda c, m, p: (m, c, p)) + place.send(
+            jnp.where(first, kv[1], kv[0]), lambda c, m, p: (1 - m, c, p)
+        )
         sent = tie(sent, kv)
     for value in sent:
         total = total + value.astype(F32)
@@ -558,23 +566,26 @@
         return own_shard(place, l, *held)
 
     shard0 = merged(place, shard_of(0, thin0))
-    shards0 = [shard0] + [place.chip(shard0, j) for j in range(1, g)]
-    thin1 = merged(place, own_layer(place, 1, tie(block, shard0)))
-    w1, qkv_b1, pre1 = cut_qkv(thin1, dim, prefix)
-
-    def panel_of(shards, *more):
+    extra = jnp.pad(out_weight[0].astype(BF).T, ((0, block.shape[0] - dim), (0, 0)))
+    wide = jnp.concatenate([block, extra], axis=1)
+    thin1 = merged(place, own_layer(place, 1, tie(wide, shard0)))
+    w1, qkv_b1, pre1 = cut_qkv(thin1[:, : 3 * width], dim, prefix)
+    out1 = thin1[:dim, 3 * width :]
+    outs1 = [out1] + [place.chip(out1, j) for j in range(1, g)]
+
+    def panel_of(shards, kinds, *more):
         cuts = [cut_shard(v, dim, ff) for v in shards]
-        parts = [v[k] for k in range(3) for v in cuts] + list(more)
+        parts = [v[k] for k in range(kinds) for v in cuts] + list(more)
         return jnp.concatenate(parts, axis=1), jnp.concatenate([v[3] for v in cuts])[None]
 
-    def outs_of(panel, count):
-        start = 2 * count * ff
+    def outs_of(panel, start, count):
         return [panel[:, start + j * width : start + (j + 1) * width] for j in range(count)]
 
-    part_a, bias_a = panel_of(shards0[:1])
+    part_a, bias_a = panel_of([shard0], 3)
     panel_a = gather(tie(part_a, w0))
     x = own_rows(tie(tokens, thin1))
-    part_b, bias_b = panel_of(shards0[1:], w1)
+    shards0 = [place.chip(tie(shard0, thin1), j) for j in range(1, g)]
+    part_b, bias_b = panel_of(shards0, 3, w1, *outs1)
     panel_b = gather(tie(part_b, panel_a, x))
     shard1 = shard_of(1, x)
     blocks = spread_rows(place, x)
@@ -582,26 +593,31 @@
     parts = out_parts(place, order, o0)
     shard1 = merged(place, tie(shard1, blocks))
     shards1 = [shard1] + [place.chip(shard1, j) for j in range(1, g)]
-    second, bias1 = panel_of(tie(shards1, o0))
+    second, bias1 = panel_of(tie(shards1, parts), 2)
     panel1 = gather(tie(second, panel_b))
-    grad = own_rows(tie(cotangent, second))
     panels0 = [(panel_a, ff), (panel_b, (g - 1) * ff)]
     panels1 = [(panel1, g * ff)]
 
-    w1 = panel_b[:, (g - 1) * (2 * ff + width) :]
-    outs = [outs_of(panel_a, 1) + outs_of(tie(panel_b, parts), g - 1), outs_of(panel1, g)]
+    at = (g - 1) * (2 * ff + width)
+    w1 = panel_b[:, at : at + 3 * width]
+    outs = [
+        outs_of(panel_a, 2 * ff, 1) + outs_of(tie(panel_b, parts), 2 * (g - 1) * ff, g - 1),
+        outs_of(panel_b, at + 3 * width, g),
+    ]
     a0, x1 = out_project(place, order, x, parts, outs[0], fixed[0])
     low = x1.astype(BF)
     mine, theirs, slope0 = feed(
         "forward", panels0, low, place.core(low), [bias_a, bias_b], keep=True
     )
+    grad = own_rows(tie(cotangent, low))
+    mine = tie(mine, grad)
     z0 = x1 + both_cores(place, mine, theirs) + fixed[0][1]
     y0 = (norm_stats(z0)[0] * fixed[0][3] + fixed[0][5]).astype(BF)
 
     def home(value, l, half):
         return place.send(value, lambda c, m, p: (l, c, p) if m == half else None)
 
-    blocks = tie(spread_rows(place, y0), grad)
+    blocks = spread_rows(place, y0)
     results0 = [home(tie(y0, blocks), 0, h) for h in range(2)]
     qkv1, o1, lse1 = attention(place, order, blocks, (w1, qkv_b1, pre1), where)
     a1, x1 = out_project(place, order, y0, out_parts(place, order, tie(o1, results0)), outs[1], fixed[1])
@@ -615,7 +631,6 @@
     mine, theirs = feed("back", panels1, low, place.core(low), slopes=[slope1])
     dx1 = dz + both_cores(place, mine, theirs)
 
-    first = m == 0
     da, go = out_back(place, order, dx1, a1, outs[1], fixed[1])
     results1 = [home(tie(y1, go), 1, h) for h in range(2)]
     back, kv1 = attend_back(*where, qkv1, lse1, o1, go, prefix, width // HD)
@@ -632,9 +647,6 @@
     back = tie(back, gouts)
     grad0, kv = input_back(place, order, da, back, w0, jnp.stack([kv0, kv1]))
     gouts = [gouts[h] + home(grad0, 0, h) for h in range(2)]
-    kv = place.send(jnp.where(first, kv[0], kv[1]), lambda c, m, p: (m, c, p)) + place.send(
-        jnp.where(first, kv[1], kv[0]), lambda c, m, p: (1 - m, c, p)
-    )
     results = jnp.stack([results0[h] + results1[h] for h in range(2)])[:, :, None]
     gouts = jnp.stack(gouts)[:, :, None]
     return results[None], gouts[None], kv[None, 0], kv[None, 1]

time: 506 us -> 499 us (0.986)
  Pallas kernels: 99 us -> 83.8 us
  matrix products: 33.1 us -> 24.3 us
  starting transfers between devices: 92.5 us -> 101 us
  other arithmetic: 23.2 us -> 30.5 us
    all_gather x4, waiting for transfers between devices: 30.9 us -> 43.1 us  [gather(): return lax.all_gather(block, 'dp', axis=0, tiled=True)]
    pallas_call x2, Pallas kernels: 34.2 us -> 23.6 us  [attend_back(): pl.pallas_call(partial(attn_bwd, prefix, heads), grid_spec=pltpu.Prefetch...]
    dot_general x28, matrix products: 33.1 us -> 24.3 us  [dot(): return lax.dot_general(a, b, (dims, ((), ())), preferred_element_type=F32)]
    ppermute x2 -> x3, waiting for transfers between devices: 11.4 us -> 4.63 us  [total_dp(): lax.ppermute(low, 'dp', [(i, i ^ x) for i in range(count)])]
    ppermute x20, starting transfers between devices: 57.9 us -> 64.5 us  [send(): return lax.ppermute(value, ('section', 'mp'), pairs)]
    ppermute x10 -> x11, waiting for transfers between devices: 93.2 us -> 87.7 us  [chip(): return lax.ppermute(value, 'mp', [(z, z ^ j) for z in range(self.mp)])]
    ppermute x10 -> x11, starting transfers between devices: 12.1 us -> 9 us  [chip(): return lax.ppermute(value, 'mp', [(z, z ^ j) for z in range(self.mp)])]
    unnamed x94 -> x106, local copies, waits for them, and re-layouts: 10.2 us -> 11 us
  transfers between devices with their start and end apart: 57 -> 59, of which waited for: 34 -> 36; matrix products, arithmetic and copies ran while one was open for 10% -> 9% of each run, Pallas kernels for 14% -> 11%
where the time goes in v5:
time: 499 us; the launch traced here: 493 us
  waiting for transfers between devices  218 us (44%)
  starting transfers between devices  101 us (20%)
  Pallas kernels  83.8 us (17%)
  other arithmetic  30.5 us (6%)
  matrix products  24.3 us (5%)
  local copies, waits for them, and re-layouts  20.5 us (4%)
  between operations  15.7 us (3%)
    ppermute x11, waiting for transfers between devices, chip(): return lax.ppermute(value, 'mp', [(z, z ^ j) for z in range(self.mp)])  87.7 us
    ppermute x20, starting transfers between devices, send(): return lax.ppermute(value, ('section', 'mp'), pairs)  64.5 us
    ppermute x20, waiting for transfers between devices, send(): return lax.ppermute(value, ('section', 'mp'), pairs)  62.5 us
    all_gather x4, waiting for transfers between devices, gather(): return lax.all_gather(block, 'dp', axis=0, tiled=True)  43.1 us
    pallas_call x4, Pallas kernels, feed(): pl.pallas_call(lambda *refs: feed_kernel(mode, cuts, refs), grid=(at,), i...  41.4 us
    dot_general x28, matrix products, dot(): return lax.dot_general(a, b, (dims, ((), ())), preferred_element_type=F32)  24.3 us
    pallas_call x2, Pallas kernels, attend_back(): pl.pallas_call(partial(attn_bwd, prefix, heads), grid_spec=pltpu.Prefetch...  23.6 us
    ppermute x21, starting transfers between devices, core(): return lax.ppermute(value, 'section', [(0, 1), (1, 0)])  22.6 us
  transfers between devices with their start and end apart: 59, of which 36 were waited for; matrix products, arithmetic and copies ran while one was open for 9% of the time, Pallas kernels for 11%

profile of v5, /device:TPU:0, one launch (start us, length us, event | category | flops | bytes accessed | tf_op | source)
XLA Modules:
  0.0 493.4 jit_solution(9169494484076291215)
XLA Ops:
  11.1 7.4 %collective-permute-start.1 = (bf16[336,768]{1,0:T(8,128)(2,1)S(1)}, bf16[336,768]{1,0:T(8,128)(2,1)}, u32[]{:S(2)}, u32[]{:S(2)}) collective-permute-start(bf16[336,768]{1,0:T(8,128)(2,1)S(1)} %pad_maximum_fusion.10), channel_id=1, source_target_pairs={{0,2},{1,3},{2,18},{3,19},{4,6},{5,7},{6,22},{7,23},{8,10},{9,11},... | collective-permute-start | bytes 1548296 | tf_op jit(solution)/shard_map/ppermute | solution.py:65
  18.5 5.8 %collective-permute-done.1 = bf16[336,768]{1,0:T(8,128)(2,1)} collective-permute-done((bf16[336,768]{1,0:T(8,128)(2,1)S(1)}, bf16[336,768]{1,0:T(8,128)(2,1)}, u32[]{:S(2)}, u32[]{:S(2)}) %collective-permute-start.1) | collective-permute-done | bytes 516128 | tf_op jit(solution)/shard_map/ppermute | solution.py:65
  29.0 9.6 %collective-permute-start.3 = (bf16[272,2304]{1,0:T(8,128)(2,1)S(1)}, bf16[272,2304]{1,0:T(8,128)(2,1)S(1)}, u32[]{:S(2)}, u32[]{:S(2)}) collective-permute-start(bf16[272,2304]{1,0:T(8,128)(2,1)S(1)} %pad_maximum_fusion.2), channel_id=1, source_target_pairs={{0,2},{1,3},{2,18},{3,19},{4,6},{5,7},{6,22},{7,23},{8,10},{9,11},... | collective-permute-start | bytes 3760136 | tf_op jit(solution)/shard_map/ppermute | solution.py:65
  38.6 14.4 %collective-permute-done.3 = bf16[272,2304]{1,0:T(8,128)(2,1)S(1)} collective-permute-done((bf16[272,2304]{1,0:T(8,128)(2,1)S(1)}, bf16[272,2304]{1,0:T(8,128)(2,1)S(1)}, u32[]{:S(2)}, u32[]{:S(2)}) %collective-permute-start.3) | collective-permute-done | bytes 1253408 | tf_op jit(solution)/shard_map/ppermute | solution.py:65
  54.3 12.8 %all-gather.5.cloned.1.call-done = bf16[1024,768]{1,0:T(8,128)(2,1)} async-done(((bf16[256,768]{1,0:T(8,128)(2,1)}), bf16[1024,768]{1,0:T(8,128)(2,1)}) %all-gather.5.cloned.1.call-update) | async-done | bytes 1572880 | tf_op jit(solution)/shard_map/all_gather | solution.py:84
  69.4 2.0 collective-permute-done.4
  72.3 2.0 collective-permute-start.11
  75.5 21.9 %collective-permute-start.6 = (bf16[304,1024]{1,0:T(8,128)(2,1)S(1)}, bf16[304,1024]{1,0:T(8,128)(2,1)}, u32[]{:S(2)}, u32[]{:S(2)}) collective-permute-start(bf16[304,1024]{1,0:T(8,128)(2,1)S(1)} %dynamic-slice_bitcast_fusion.1), channel_id=1, source_target_pairs={{0,2},{1,3},{18,16},{19,17},{4,6},{5,7},{22,20},{23,21},{8,10},{9,... | collective-permute-start | bytes 1867784 | tf_op jit(solution)/shard_map/ppermute | solution.py:65
  98.3 12.6 %collective-permute-done.6 = bf16[304,1024]{1,0:T(8,128)(2,1)} collective-permute-done((bf16[304,1024]{1,0:T(8,128)(2,1)S(1)}, bf16[304,1024]{1,0:T(8,128)(2,1)}, u32[]{:S(2)}, u32[]{:S(2)}) %collective-permute-start.6) | collective-permute-done | bytes 622624 | tf_op jit(solution)/shard_map/ppermute | solution.py:65
  112.2 1.6 slice.300
  113.8 1.4 pad_maximum_fusion.1
  115.2 12.0 %all-gather.7.cloned.1.call-done.refs_0_.refs_1_ = bf16[1024,2304]{1,0:T(8,128)(2,1)} async-done(((bf16[256,2304]{1,0:T(8,128)(2,1)}), bf16[1024,2304]{1,0:T(8,128)(2,1)}) %all-gather.7.cloned.1.call-update) | async-done | bytes 4718608 | tf_op jit(solution)/shard_map/all_gather | solution.py:84
  127.9 1.5 collective-permute-start.8
  132.0 1.4 collective-permute-start.25
  133.4 2.3 collective-permute-start.26
  135.9 4.1 collective-permute-start.7
  140.0 10.9 %collective-permute-done.8 = bf16[304,1024]{1,0:T(8,128)(2,1)} collective-permute-done((bf16[304,1024]{1,0:T(8,128)(2,1)S(1)}, bf16[304,1024]{1,0:T(8,128)(2,1)}, u32[]{:S(2)}, u32[]{:S(2)}) %collective-permute-start.8) | collective-permute-done | bytes 622624 | tf_op jit(solution)/shard_map/ppermute | solution.py:71
  156.1 2.1 fusion.20
  158.9 9.2 %attend.2 = (bf16[1280,256]{1,0:T(8,128)(2,1)S(1)}, f32[4,1280]{1,0:T(4,128)S(1)}) custom-call(s32[10,2]{1,0:T(8,128)S(1)} %copy.78.range_ref, s32[2,1280]{1,0:T(2,128)S(1)} %pad_add_fusion.span_ref, bf16[1280,768]{1,0:T(8,128)(2,1)S(1)} %fusion.22.qkv_ref), custom_call_target="tpu_custom_call" | custom-call | flops 419430 | bytes 1 | tf_op jit(solution)/shard_map/attend/pallas_call | solution.py:258
  168.1 1.7 collective-permute-start.10
  169.9 19.5 %collective-permute-done.10 = bf16[608,256]{1,0:T(8,128)(2,1)S(1)} collective-permute-done((bf16[608,256]{1,0:T(8,128)(2,1)S(1)}, bf16[608,256]{1,0:T(8,128)(2,1)S(1)}, u32[]{:S(2)}, u32[]{:S(2)}) %collective-permute-start.10) | collective-permute-done | bytes 311328 | tf_op jit(solution)/shard_map/ppermute | solution.py:71
  190.4 1.6 pad_maximum_fusion
  192.0 16.0 %all-gather.9.cloned.1.call-done.refs_2_.refs_3_ = bf16[1024,3584]{1,0:T(8,128)(2,1)} async-done(((bf16[256,3584]{1,0:T(8,128)(2,1)}), bf16[1024,3584]{1,0:T(8,128)(2,1)}) %all-gather.9.cloned.1.call-update) | async-done | bytes 7340048 | tf_op jit(solution)/shard_map/all_gather | solution.py:84
  209.4 1.4 fusion.53
  210.8 1.4 fusion.11
  212.5 1.4 fusion.55
  214.3 1.7 fusion.140
  218.9 5.6 %collective-permute-start.16 = (bf16[304,1024]{1,0:T(8,128)(2,1)}, bf16[304,1024]{1,0:T(8,128)(2,1)}, u32[]{:S(2)}, u32[]{:S(2)}) collective-permute-start(bf16[304,1024]{1,0:T(8,128)(2,1)} %dynamic-slice_bitcast_fusion), channel_id=1, source_target_pairs={{0,2},{1,3},{18,16},{19,17},{4,6},{5,7},{22,20},{23,21},{8,10},{9,... | collective-permute-start | bytes 1867784 | tf_op jit(solution)/shard_map/ppermute | solution.py:65
  225.3 12.6 %feed_forward.2 = (f32[304,1024]{1,0:T(8,128)S(1)}, bf16[304,1024]{1,0:T(8,128)(2,1)S(1)}, bf16[608,2048]{1,0:T(8,128)(2,1)S(1)}) custom-call(bf16[1024,2304]{1,0:T(8,128)(2,1)} %all-gather.7.cloned.1.call-done.refs_0_.refs_1_, bf16[1024,2304]{1,0:T(8,128)(2,1)} %all-gather.7.cloned.1.call-done.refs_0_.refs_1_, ...), custom_call_target="tpu_custom_call" | custom-call | flops 1275068 | bytes 1 | tf_op jit(solution)/shard_map/feed_forward/pallas_call | solution.py:404
  241.7 1.5 collective-permute-start.19
  243.3 14.7 %collective-permute-done.19 = bf16[304,1024]{1,0:T(8,128)(2,1)S(1)} collective-permute-done((bf16[304,1024]{1,0:T(8,128)(2,1)S(1)}, bf16[304,1024]{1,0:T(8,128)(2,1)S(1)}, u32[]{:S(2)}, u32[]{:S(2)}) %collective-permute-start.19) | collective-permute-done | bytes 622624 | tf_op jit(solution)/shard_map/ppermute | solution.py:71
  264.1 9.6 %attend.3 = (bf16[1280,256]{1,0:T(8,128)(2,1)S(1)}, f32[4,1280]{1,0:T(4,128)S(1)}) custom-call(s32[10,2]{1,0:T(8,128)S(1)} %copy.78.range_ref, s32[2,1280]{1,0:T(2,128)S(1)} %pad_add_fusion.span_ref, bf16[1280,768]{1,0:T(8,128)(2,1)S(1)} %fusion.30.qkv_ref), custom_call_target="tpu_custom_call" | custom-call | flops 419430 | bytes 1 | tf_op jit(solution)/shard_map/attend/pallas_call | solution.py:258
  273.8 6.9 %collective-permute-done.22 = bf16[304,1024]{1,0:T(8,128)(2,1)S(1)} collective-permute-done((bf16[304,1024]{1,0:T(8,128)(2,1)S(1)}, bf16[304,1024]{1,0:T(8,128)(2,1)S(1)}, u32[]{:S(2)}, u32[]{:S(2)}) %collective-permute-start.22) | collective-permute-done | bytes 622624 | tf_op jit(solution)/shard_map/ppermute | solution.py:65
  281.4 6.2 %collective-permute-done.23 = bf16[608,256]{1,0:T(8,128)(2,1)S(1)} collective-permute-done((bf16[608,256]{1,0:T(8,128)(2,1)S(1)}, bf16[608,256]{1,0:T(8,128)(2,1)S(1)}, u32[]{:S(2)}, u32[]{:S(2)}) %collective-permute-start.23) | collective-permute-done | bytes 311328 | tf_op jit(solution)/shard_map/ppermute | solution.py:71
  295.0 2.3 all-gather.11.cloned.1.call-done.refs_0_.refs_1_
  299.5 11.8 %feed_forward.3 = (f32[304,1024]{1,0:T(8,128)S(1)}, bf16[304,1024]{1,0:T(8,128)(2,1)S(1)}, bf16[608,2048]{1,0:T(8,128)(2,1)S(1)}) custom-call(bf16[1024,4096]{1,0:T(8,128)(2,1)} %all-gather.11.cloned.1.call-done.refs_0_.refs_1_, bf16[1024,4096]{1,0:T(8,128)(2,1)} %all-gather.11.cloned.1.call-done.refs_0_.refs_1_, bf16[304,1024]{1,0:T(8,128)(2,1)S(1)} %copy-done.3, ...), custom_call_target="tpu_custom_call" | custom-call | flops 1275068 | bytes 1 | tf_op jit(solution)/shard_map/feed_forward/pallas_call | solution.py:404
  311.4 2.0 collective-permute-done.29
  316.6 1.9 collective-permute-done.30.refs_3_
  318.5 8.1 %feed_back.2 = (f32[304,1024]{1,0:T(8,128)S(1)}, bf16[304,1024]{1,0:T(8,128)(2,1)S(1)}) custom-call(bf16[1024,4096]{1,0:T(8,128)(2,1)} %all-gather.11.cloned.1.call-done.refs_0_.refs_1_, bf16[1024,4096]{1,0:T(8,128)(2,1)} %all-gather.11.cloned.1.call-done.refs_0_.refs_1_, bf16[304,1024]{1,0:T(8,128)(2,1)S(1)} %fusion.125.refs_2_, ...), custom_call_target="tpu_custom_call" | custom-call | flops 1275068 | bytes 1 | tf_op jit(solution)/shard_map/feed_back/pallas_call | solution.py:404
  326.8 1.9 collective-permute-done.31
  328.8 3.0 fusion.128
  331.8 1.4 fusion.130
  333.4 1.9 collective-permute-done.32
  335.8 1.6 collective-permute-start.33
  337.8 7.4 %collective-permute-done.33 = bf16[608,256]{1,0:T(8,128)(2,1)S(1)} collective-permute-done((bf16[608,256]{1,0:T(8,128)(2,1)S(1)}, bf16[608,256]{1,0:T(8,128)(2,1)S(1)}, u32[]{:S(2)}, u32[]{:S(2)}) %collective-permute-start.33) | collective-permute-done | bytes 311328 | tf_op jit(solution)/shard_map/ppermute | solution.py:71
  347.5 11.8 %attend_back.2 = (bf16[1280,768]{1,0:T(8,128)(2,1)S(1)}, f32[2,64,256]{2,1,0:T(8,128)S(1)}) custom-call(s32[10,2]{1,0:T(8,128)S(1)} %copy.78.range_ref, s32[2,1280]{1,0:T(2,128)S(1)} %pad_add_fusion.span_ref, bf16[1280,768]{1,0:T(8,128)(2,1)S(1)} %fusion.30.qkv_ref, f32[4,1280]{1,0:T(4,128)S(1)} %get-tuple-element.81.lse_ref, ...), custom_call_target="tpu_custom_call" | custom-call | flops 1048576 | bytes 1 | tf_op jit(solution)/shard_map/attend_back/pallas_call | solution.py:273
  360.3 8.4 %collective-permute-start.37 = (bf16[304,1024]{1,0:T(8,128)(2,1)S(1)}, bf16[304,1024]{1,0:T(8,128)(2,1)S(1)}, u32[]{:S(2)}, u32[]{:S(2)}) collective-permute-start(bf16[304,1024]{1,0:T(8,128)(2,1)S(1)} %convolution_convert_fusion.2), channel_id=1, source_target_pairs={{0,16},{16,0},{1,17},{17,1},{2,18},{18,2},{3,19},{19,3},{4,20},{20... | collective-permute-start | bytes 1867784 | tf_op jit(solution)/shard_map/ppermute | solution.py:68
  371.5 15.9 %collective-permute-done.38 = bf16[304,1024]{1,0:T(8,128)(2,1)S(1)} collective-permute-done((bf16[304,1024]{1,0:T(8,128)(2,1)S(1)}, bf16[304,1024]{1,0:T(8,128)(2,1)S(1)}, u32[]{:S(2)}, u32[]{:S(2)}) %collective-permute-start.38) | collective-permute-done | bytes 622624 | tf_op jit(solution)/shard_map/ppermute | solution.py:71
  389.1 2.0 collective-permute-done.39.refs_5_
  391.2 8.9 %feed_back.3 = (f32[304,1024]{1,0:T(8,128)S(1)}, bf16[304,1024]{1,0:T(8,128)(2,1)S(1)}) custom-call(bf16[1024,2304]{1,0:T(8,128)(2,1)} %all-gather.7.cloned.1.call-done.refs_0_.refs_1_, bf16[1024,2304]{1,0:T(8,128)(2,1)} %all-gather.7.cloned.1.call-done.refs_0_.refs_1_, bf16[1024,3584]{1,0:T(8,128)(2,1)} %all-gather.9.cloned.1.call-done.refs_2_.refs_3_, ...), custom_call_target="tpu_custom_call" | custom-call | flops 1275068 | bytes 1 | tf_op jit(solution)/shard_map/feed_back/pallas_call | solution.py:404
  400.3 1.9 collective-permute-done.40
  403.8 1.9 collective-permute-done.41
  405.7 1.5 convolution_convert_fusion.5
  407.6 1.5 convolution_convert_fusion.4
  409.2 7.6 %collective-permute-done.42 = bf16[608,256]{1,0:T(8,128)(2,1)S(1)} collective-permute-done((bf16[608,256]{1,0:T(8,128)(2,1)S(1)}, bf16[608,256]{1,0:T(8,128)(2,1)S(1)}, u32[]{:S(2)}, u32[]{:S(2)}) %collective-permute-start.42) | collective-permute-done | bytes 311328 | tf_op jit(solution)/shard_map/ppermute | solution.py:71
  419.0 11.8 %attend_back.3 = (bf16[1280,768]{1,0:T(8,128)(2,1)S(1)}, f32[2,64,256]{2,1,0:T(8,128)S(1)}) custom-call(s32[10,2]{1,0:T(8,128)S(1)} %copy.78.range_ref, s32[2,1280]{1,0:T(2,128)S(1)} %pad_add_fusion.span_ref, bf16[1280,768]{1,0:T(8,128)(2,1)S(1)} %copy-done.1, f32[4,1280]{1,0:T(4,128)S(1)} %get-tuple-element.88.lse_ref, ...), custom_call_target="tpu_custom_call" | custom-call | flops 1048576 | bytes 1 | tf_op jit(solution)/shard_map/attend_back/pallas_call | solution.py:273
  431.5 7.4 %collective-permute-start.46 = (bf16[304,1024]{1,0:T(8,128)(2,1)S(1)}, bf16[304,1024]{1,0:T(8,128)(2,1)S(1)}, u32[]{:S(2)}, u32[]{:S(2)}) collective-permute-start(bf16[304,1024]{1,0:T(8,128)(2,1)S(1)} %convolution_convert_fusion), channel_id=1, source_target_pairs={{0,16},{16,0},{1,17},{17,1},{2,18},{18,2},{3,19},{19,3},{4,20},{20... | collective-permute-start | bytes 1867784 | tf_op jit(solution)/shard_map/ppermute | solution.py:68
  439.6 2.4 collective-permute-start.49
  445.0 2.8 collective-permute-done.49
  447.8 1.8 collective-permute-done.50
  450.4 4.1 collective-permute-start.52
  454.6 4.2 collective-permute-done.52
  458.8 5.4 %collective-permute-done.47 = bf16[304,1024]{1,0:T(8,128)(2,1)S(1)} collective-permute-done((bf16[304,1024]{1,0:T(8,128)(2,1)S(1)}, bf16[304,1024]{1,0:T(8,128)(2,1)S(1)}, u32[]{:S(2)}, u32[]{:S(2)}) %collective-permute-start.47) | collective-permute-done | bytes 622624 | tf_op jit(solution)/shard_map/ppermute | solution.py:71
  468.9 16.5 %collective-permute-done.54 = bf16[304,1024]{1,0:T(8,128)(2,1)S(1)} collective-permute-done((bf16[304,1024]{1,0:T(8,128)(2,1)S(1)}, bf16[304,1024]{1,0:T(8,128)(2,1)S(1)}, u32[]{:S(2)}, u32[]{:S(2)}) %collective-permute-start.54) | collective-permute-done | bytes 622624 | tf_op jit(solution)/shard_map/ppermute | solution.py:65
  (333 shorter events, 79.6 us)
Async XLA Ops:
  7.2 59.9 %all-gather.5.cloned.1.call-start = ((), (), s32[]{:S(2)}) async-start(), calls=%async_computation | async-start | bytes 1966080 | tf_op jit(solution)/shard_map/all_gather | solution.py:84
  10.3 8.2 %collective-permute-start = (bf16[336,768]{1,0:T(8,128)(2,1)S(1)}, bf16[336,768]{1,0:T(8,128)(2,1)S(1)}, u32[]{:S(2)}, u32[]{:S(2)}) collective-permute-start(bf16[336,768]{1,0:T(8,128)(2,1)S(1)} %pad_maximum_fusion.10), channel_id=1, source_target_pairs={{0,0},{1,1},{2,16},{3,17},{4,4},{5,5},{6,20},{7,21},{8,8},{9,9},{1... | collective-permute-start | bytes 1548296 | tf_op jit(solution)/shard_map/ppermute | solution.py:65
  11.1 13.2 %collective-permute-start.1 = (bf16[336,768]{1,0:T(8,128)(2,1)S(1)}, bf16[336,768]{1,0:T(8,128)(2,1)}, u32[]{:S(2)}, u32[]{:S(2)}) collective-permute-start(bf16[336,768]{1,0:T(8,128)(2,1)S(1)} %pad_maximum_fusion.10), channel_id=1, source_target_pairs={{0,2},{1,3},{2,18},{3,19},{4,6},{5,7},{6,22},{7,23},{8,10},{9,11},... | collective-permute-start | bytes 1548296 | tf_op jit(solution)/shard_map/ppermute | solution.py:65
  27.0 100.2 %all-gather.7.cloned.1.call-start = ((), (), s32[]{:S(2)}) async-start(), calls=%async_computation.1 | async-start | bytes 5898240 | tf_op jit(solution)/shard_map/all_gather | solution.py:84
  28.2 10.3 %collective-permute-start.2 = (bf16[272,2304]{1,0:T(8,128)(2,1)S(1)}, bf16[272,2304]{1,0:T(8,128)(2,1)S(1)}, u32[]{:S(2)}, u32[]{:S(2)}) collective-permute-start(bf16[272,2304]{1,0:T(8,128)(2,1)S(1)} %pad_maximum_fusion.2), channel_id=1, source_target_pairs={{0,0},{1,1},{2,16},{3,17},{4,4},{5,5},{6,20},{7,21},{8,8},{9,9},{1... | collective-permute-start | bytes 3760136 | tf_op jit(solution)/shard_map/ppermute | solution.py:65
  29.0 24.0 %collective-permute-start.3 = (bf16[272,2304]{1,0:T(8,128)(2,1)S(1)}, bf16[272,2304]{1,0:T(8,128)(2,1)S(1)}, u32[]{:S(2)}, u32[]{:S(2)}) collective-permute-start(bf16[272,2304]{1,0:T(8,128)(2,1)S(1)} %pad_maximum_fusion.2), channel_id=1, source_target_pairs={{0,2},{1,3},{2,18},{3,19},{4,6},{5,7},{6,22},{7,23},{8,10},{9,11},... | collective-permute-start | bytes 3760136 | tf_op jit(solution)/shard_map/ppermute | solution.py:65
  67.1 140.9 %all-gather.9.cloned.1.call-start = ((), (), s32[]{:S(2)}) async-start(), calls=%async_computation.2 | async-start | bytes 9175040 | tf_op jit(solution)/shard_map/all_gather | solution.py:84
  67.3 4.0 collective-permute-start.4
  68.6 2.7 collective-permute-start.5
  72.3 39.8 %collective-permute-start.11 = (bf16[272,2304]{1,0:T(8,128)(2,1)S(1)}, bf16[272,2304]{1,0:T(8,128)(2,1)}, u32[]{:S(2)}, u32[]{:S(2)}) collective-permute-start(bf16[272,2304]{1,0:T(8,128)(2,1)S(1)} %broadcast_select_fusion), channel_id=1, source_target_pairs={{0,1},{1,0},{2,3},{3,2},{4,5},{5,4},{6,7},{7,6},{8,9},{9,8},{10,11... | collective-permute-start | bytes 3760136 | tf_op jit(solution)/shard_map/ppermute | solution.py:71
  75.5 35.5 %collective-permute-start.6 = (bf16[304,1024]{1,0:T(8,128)(2,1)S(1)}, bf16[304,1024]{1,0:T(8,128)(2,1)}, u32[]{:S(2)}, u32[]{:S(2)}) collective-permute-start(bf16[304,1024]{1,0:T(8,128)(2,1)S(1)} %dynamic-slice_bitcast_fusion.1), channel_id=1, source_target_pairs={{0,2},{1,3},{18,16},{19,17},{4,6},{5,7},{22,20},{23,21},{8,10},{9,... | collective-permute-start | bytes 1867784 | tf_op jit(solution)/shard_map/ppermute | solution.py:65
  98.3 15.5 %collective-permute-start.12 = (bf16[256,256]{1,0:T(8,128)(2,1)S(1)}, bf16[256,256]{1,0:T(8,128)(2,1)S(1)}, u32[]{:S(2)}, u32[]{:S(2)}) collective-permute-start(bf16[256,256]{1,0:T(8,128)(2,1)S(1)} %slice.302), channel_id=1, source_target_pairs={{0,1},{1,0},{2,3},{3,2},{4,5},{5,4},{6,7},{7,6},{8,9},{9,8},{10,11... | collective-permute-start | bytes 393224 | tf_op jit(solution)/shard_map/ppermute | solution.py:71
  112.1 41.1 %copy-start.21 = (bf16[304,1024]{1,0:T(8,128)(2,1)}, bf16[304,1024]{1,0:T(8,128)(2,1)S(1)}, u32[]{:S(2)}) copy-start(bf16[304,1024]{1,0:T(8,128)(2,1)S(1)} %bitcast_select_fusion.1) | copy-start | bytes 1867780
  127.2 170.1 %all-gather.11.cloned.1.call-start = ((), (), s32[]{:S(2)}) async-start(), calls=%async_computation.3 | async-start | bytes 10485760 | tf_op jit(solution)/shard_map/all_gather | solution.py:84
  127.9 23.1 %collective-permute-start.8 = (bf16[304,1024]{1,0:T(8,128)(2,1)S(1)}, bf16[304,1024]{1,0:T(8,128)(2,1)}, u32[]{:S(2)}, u32[]{:S(2)}) collective-permute-start(bf16[304,1024]{1,0:T(8,128)(2,1)S(1)} %bitcast_select_fusion.1), channel_id=1, source_target_pairs={{0,1},{1,0},{2,3},{3,2},{4,5},{5,4},{6,7},{7,6},{8,9},{9,8},{10,11... | collective-permute-start | bytes 1867784 | tf_op jit(solution)/shard_map/ppermute | solution.py:71
  132.0 22.6 %collective-permute-start.25 = (bf16[272,2048]{1,0:T(8,128)(2,1)}, bf16[272,2048]{1,0:T(8,128)(2,1)}, u32[]{:S(2)}, u32[]{:S(2)}) collective-permute-start(bf16[272,2048]{1,0:T(8,128)(2,1)} %pad_maximum_fusion.5), channel_id=1, source_target_pairs={{16,0},{17,1},{18,16},{19,17},{20,4},{21,5},{22,20},{23,21},{24,8}... | collective-permute-start | bytes 3342344 | tf_op jit(solution)/shard_map/ppermute | solution.py:65
  133.4 21.2 %collective-permute-start.26 = (bf16[272,2048]{1,0:T(8,128)(2,1)}, bf16[272,2048]{1,0:T(8,128)(2,1)}, u32[]{:S(2)}, u32[]{:S(2)}) collective-permute-start(bf16[272,2048]{1,0:T(8,128)(2,1)} %pad_maximum_fusion.5), channel_id=1, source_target_pairs={{16,2},{17,3},{18,18},{19,19},{20,6},{21,7},{22,22},{23,23},{24,10... | collective-permute-start | bytes 3342344 | tf_op jit(solution)/shard_map/ppermute | solution.py:65
  135.9 18.0 %collective-permute-start.7 = (bf16[304,1024]{1,0:T(8,128)(2,1)S(1)}, bf16[304,1024]{1,0:T(8,128)(2,1)S(1)}, u32[]{:S(2)}, u32[]{:S(2)}) collective-permute-start(bf16[304,1024]{1,0:T(8,128)(2,1)S(1)} %bitcast_select_fusion.1), channel_id=1, source_target_pairs={{0,16},{16,0},{1,17},{17,1},{2,18},{18,2},{3,19},{19,3},{4,20},{20... | collective-permute-start | bytes 1867784 | tf_op jit(solution)/shard_map/ppermute | solution.py:68
  150.9 3.7 collective-permute-start.9
  156.0 33.4 %copy-start.17 = (bf16[272,2048]{1,0:T(8,128)(2,1)}, bf16[272,2048]{1,0:T(8,128)(2,1)S(1)}, u32[]{:S(2)}) copy-start(bf16[272,2048]{1,0:T(8,128)(2,1)S(1)} %broadcast_select_fusion.1) | copy-start | bytes 3342340
  156.0 33.4 %collective-permute-start.27 = (bf16[272,2048]{1,0:T(8,128)(2,1)S(1)}, bf16[272,2048]{1,0:T(8,128)(2,1)S(1)}, u32[]{:S(2)}, u32[]{:S(2)}) collective-permute-start(bf16[272,2048]{1,0:T(8,128)(2,1)S(1)} %broadcast_select_fusion.1), channel_id=1, source_target_pairs={{0,1},{1,0},{2,3},{3,2},{4,5},{5,4},{6,7},{7,6},{8,9},{9,8},{10,11... | collective-permute-start | bytes 3342344 | tf_op jit(solution)/shard_map/ppermute | solution.py:71
  168.1 21.3 %collective-permute-start.10 = (bf16[608,256]{1,0:T(8,128)(2,1)S(1)}, bf16[608,256]{1,0:T(8,128)(2,1)S(1)}, u32[]{:S(2)}, u32[]{:S(2)}) collective-permute-start(bf16[608,256]{1,0:T(8,128)(2,1)S(1)} %pad_maximum_fusion.11), channel_id=1, source_target_pairs={{0,1},{1,0},{2,3},{3,2},{4,5},{5,4},{6,7},{7,6},{8,9},{9,8},{10,11... | collective-permute-start | bytes 933896 | tf_op jit(solution)/shard_map/ppermute | solution.py:71
  208.1 1.3 collective-permute-start.14
  212.2 2.1 collective-permute-start.13
  216.0 24.0 %copy-start.8 = (f32[304,1024]{1,0:T(8,128)}, f32[304,1024]{1,0:T(8,128)S(1)}, u32[]{:S(2)}) copy-start(f32[304,1024]{1,0:T(8,128)S(1)} %get-tuple-element.168) | copy-start | bytes 3735556
  216.6 8.7 %collective-permute-start.15 = (bf16[304,1024]{1,0:T(8,128)(2,1)S(1)}, bf16[304,1024]{1,0:T(8,128)(2,1)S(1)}, u32[]{:S(2)}, u32[]{:S(2)}) collective-permute-start(bf16[304,1024]{1,0:T(8,128)(2,1)S(1)} %fusion.33.refs_4_), channel_id=1, source_target_pairs={{0,16},{16,0},{1,17},{17,1},{2,18},{18,2},{3,19},{19,3},{4,20},{20... | collective-permute-start | bytes 1867784 | tf_op jit(solution)/shard_map/ppermute | solution.py:68
  218.0 40.2 %slice-start = ((s8[7340032]{0:T(1024)(128)(4,1)}), s8[4194304]{0:T(1024)(128)(4,1)S(1)}, s32[]{:S(2)}) async-start(s8[7340032]{0:T(1024)(128)(4,1)} %bitcast.135), calls=%async_computation.4 | async-start | bytes 8388608
  218.9 19.0 %collective-permute-start.16 = (bf16[304,1024]{1,0:T(8,128)(2,1)}, bf16[304,1024]{1,0:T(8,128)(2,1)}, u32[]{:S(2)}, u32[]{:S(2)}) collective-permute-start(bf16[304,1024]{1,0:T(8,128)(2,1)} %dynamic-slice_bitcast_fusion), channel_id=1, source_target_pairs={{0,2},{1,3},{18,16},{19,17},{4,6},{5,7},{22,20},{23,21},{8,10},{9,... | collective-permute-start | bytes 1867784 | tf_op jit(solution)/shard_map/ppermute | solution.py:65
  225.2 33.0 %slice-start.1 = ((s8[7340032]{0:T(1024)(128)(4,1)}), s8[3145728]{0:T(1024)(128)(4,1)S(1)}, s32[]{:S(2)}) async-start(s8[7340032]{0:T(1024)(128)(4,1)} %bitcast.135), calls=%async_computation.5 | async-start | bytes 6291456
  237.9 2.1 collective-permute-start.17
  241.7 16.4 %collective-permute-start.19 = (bf16[304,1024]{1,0:T(8,128)(2,1)S(1)}, bf16[304,1024]{1,0:T(8,128)(2,1)S(1)}, u32[]{:S(2)}, u32[]{:S(2)}) collective-permute-start(bf16[304,1024]{1,0:T(8,128)(2,1)S(1)} %add_convert_fusion.1), channel_id=1, source_target_pairs={{0,1},{1,0},{2,3},{3,2},{4,5},{5,4},{6,7},{7,6},{8,9},{9,8},{10,11... | collective-permute-start | bytes 1867784 | tf_op jit(solution)/shard_map/ppermute | solution.py:71
  243.1 15.8 %collective-permute-start.18 = (bf16[304,1024]{1,0:T(8,128)(2,1)S(1)}, bf16[304,1024]{1,0:T(8,128)(2,1)S(1)}, u32[]{:S(2)}, u32[]{:S(2)}) collective-permute-start(bf16[304,1024]{1,0:T(8,128)(2,1)S(1)} %add_convert_fusion.1), channel_id=1, source_target_pairs={{0,16},{16,0},{1,17},{17,1},{2,18},{18,2},{3,19},{19,3},{4,20},{20... | collective-permute-start | bytes 1867784 | tf_op jit(solution)/shard_map/ppermute | solution.py:68
  258.1 2.1 collective-permute-start.20
  260.1 13.6 %collective-permute-start.21 = (bf16[304,1024]{1,0:T(8,128)(2,1)S(1)}, bf16[304,1024]{1,0:T(8,128)(2,1)S(1)}, u32[]{:S(2)}, u32[]{:S(2)}) collective-permute-start(bf16[304,1024]{1,0:T(8,128)(2,1)S(1)} %add_convert_fusion.1), channel_id=1, source_target_pairs={{0,0},{1,1},{16,2},{17,3},{4,4},{5,5},{20,6},{21,7},{8,8},{9,9},{2... | collective-permute-start | bytes 1867784 | tf_op jit(solution)/shard_map/ppermute | solution.py:65
  260.8 19.8 %collective-permute-start.22 = (bf16[304,1024]{1,0:T(8,128)(2,1)S(1)}, bf16[304,1024]{1,0:T(8,128)(2,1)S(1)}, u32[]{:S(2)}, u32[]{:S(2)}) collective-permute-start(bf16[304,1024]{1,0:T(8,128)(2,1)S(1)} %add_convert_fusion.1), channel_id=1, source_target_pairs={{2,0},{3,1},{18,2},{19,3},{6,4},{7,5},{22,6},{23,7},{10,8},{11,9},... | collective-permute-start | bytes 1867784 | tf_op jit(solution)/shard_map/ppermute | solution.py:65
  280.7 7.0 %collective-permute-start.23 = (bf16[608,256]{1,0:T(8,128)(2,1)S(1)}, bf16[608,256]{1,0:T(8,128)(2,1)S(1)}, u32[]{:S(2)}, u32[]{:S(2)}) collective-permute-start(bf16[608,256]{1,0:T(8,128)(2,1)S(1)} %pad_maximum_fusion.13), channel_id=1, source_target_pairs={{0,1},{1,0},{2,3},{3,2},{4,5},{5,4},{6,7},{7,6},{8,9},{9,8},{10,11... | collective-permute-start | bytes 933896 | tf_op jit(solution)/shard_map/ppermute | solution.py:71
  288.4 2.1 collective-permute-start.24
  292.1 2.1 collective-permute-start.28
  311.3 2.1 collective-permute-start.29
  316.4 2.1 collective-permute-start.30
  326.6 2.1 collective-permute-start.31
  333.2 2.1 collective-permute-start.32
  335.8 9.5 %collective-permute-start.33 = (bf16[608,256]{1,0:T(8,128)(2,1)S(1)}, bf16[608,256]{1,0:T(8,128)(2,1)S(1)}, u32[]{:S(2)}, u32[]{:S(2)}) collective-permute-start(bf16[608,256]{1,0:T(8,128)(2,1)S(1)} %convolution_convert_fusion.7), channel_id=1, source_target_pairs={{0,1},{1,0},{2,3},{3,2},{4,5},{5,4},{6,7},{7,6},{8,9},{9,8},{10,11... | collective-permute-start | bytes 933896 | tf_op jit(solution)/shard_map/ppermute | solution.py:71
  345.4 13.9 %collective-permute-start.34 = (bf16[304,1024]{1,0:T(8,128)(2,1)S(1)}, bf16[304,1024]{1,0:T(8,128)(2,1)S(1)}, u32[]{:S(2)}, u32[]{:S(2)}) collective-permute-start(bf16[304,1024]{1,0:T(8,128)(2,1)S(1)} %get-tuple-element.80), channel_id=1, source_target_pairs={{0,16},{1,17},{16,18},{17,19},{4,20},{5,21},{20,22},{21,23},{8,24}... | collective-permute-start | bytes 1867784 | tf_op jit(solution)/shard_map/ppermute | solution.py:65
  346.8 12.6 %collective-permute-start.35 = (bf16[304,1024]{1,0:T(8,128)(2,1)S(1)}, bf16[304,1024]{1,0:T(8,128)(2,1)S(1)}, u32[]{:S(2)}, u32[]{:S(2)}) collective-permute-start(bf16[304,1024]{1,0:T(8,128)(2,1)S(1)} %get-tuple-element.80), channel_id=1, source_target_pairs={{2,16},{3,17},{18,18},{19,19},{6,20},{7,21},{22,22},{23,23},{10,24... | collective-permute-start | bytes 1867784 | tf_op jit(solution)/shard_map/ppermute | solution.py:65
  360.3 10.1 %collective-permute-start.37 = (bf16[304,1024]{1,0:T(8,128)(2,1)S(1)}, bf16[304,1024]{1,0:T(8,128)(2,1)S(1)}, u32[]{:S(2)}, u32[]{:S(2)}) collective-permute-start(bf16[304,1024]{1,0:T(8,128)(2,1)S(1)} %convolution_convert_fusion.2), channel_id=1, source_target_pairs={{0,16},{16,0},{1,17},{17,1},{2,18},{18,2},{3,19},{19,3},{4,20},{20... | collective-permute-start | bytes 1867784 | tf_op jit(solution)/shard_map/ppermute | solution.py:68
  369.4 2.1 collective-permute-start.36
  371.1 16.4 %collective-permute-start.38 = (bf16[304,1024]{1,0:T(8,128)(2,1)S(1)}, bf16[304,1024]{1,0:T(8,128)(2,1)S(1)}, u32[]{:S(2)}, u32[]{:S(2)}) collective-permute-start(bf16[304,1024]{1,0:T(8,128)(2,1)S(1)} %fusion.13), channel_id=1, source_target_pairs={{0,1},{1,0},{2,3},{3,2},{4,5},{5,4},{6,7},{7,6},{8,9},{9,8},{10,11... | collective-permute-start | bytes 1867784 | tf_op jit(solution)/shard_map/ppermute | solution.py:71
  389.0 2.1 collective-permute-start.39
  400.1 2.1 collective-permute-start.40
  403.6 2.1 collective-permute-start.41
  407.3 9.5 %collective-permute-start.42 = (bf16[608,256]{1,0:T(8,128)(2,1)S(1)}, bf16[608,256]{1,0:T(8,128)(2,1)S(1)}, u32[]{:S(2)}, u32[]{:S(2)}) collective-permute-start(bf16[608,256]{1,0:T(8,128)(2,1)S(1)} %convolution_convert_fusion.5), channel_id=1, source_target_pairs={{0,1},{1,0},{2,3},{3,2},{4,5},{5,4},{6,7},{7,6},{8,9},{9,8},{10,11... | collective-permute-start | bytes 933896 | tf_op jit(solution)/shard_map/ppermute | solution.py:71
  416.9 13.9 %collective-permute-start.43 = (bf16[304,1024]{1,0:T(8,128)(2,1)S(1)}, bf16[304,1024]{1,0:T(8,128)(2,1)S(1)}, u32[]{:S(2)}, u32[]{:S(2)}) collective-permute-start(bf16[304,1024]{1,0:T(8,128)(2,1)S(1)} %get-tuple-element.87), channel_id=1, source_target_pairs={{0,16},{1,17},{16,18},{17,19},{4,20},{5,21},{20,22},{21,23},{8,24}... | collective-permute-start | bytes 1867784 | tf_op jit(solution)/shard_map/ppermute | solution.py:65
  418.2 12.5 %collective-permute-start.44 = (bf16[304,1024]{1,0:T(8,128)(2,1)S(1)}, bf16[304,1024]{1,0:T(8,128)(2,1)S(1)}, u32[]{:S(2)}, u32[]{:S(2)}) collective-permute-start(bf16[304,1024]{1,0:T(8,128)(2,1)S(1)} %get-tuple-element.87), channel_id=1, source_target_pairs={{2,16},{3,17},{18,18},{19,19},{6,20},{7,21},{22,22},{23,23},{10,24... | collective-permute-start | bytes 1867784 | tf_op jit(solution)/shard_map/ppermute | solution.py:65
  431.5 12.7 %collective-permute-start.46 = (bf16[304,1024]{1,0:T(8,128)(2,1)S(1)}, bf16[304,1024]{1,0:T(8,128)(2,1)S(1)}, u32[]{:S(2)}, u32[]{:S(2)}) collective-permute-start(bf16[304,1024]{1,0:T(8,128)(2,1)S(1)} %convolution_convert_fusion), channel_id=1, source_target_pairs={{0,16},{16,0},{1,17},{17,1},{2,18},{18,2},{3,19},{19,3},{4,20},{20... | collective-permute-start | bytes 1867784 | tf_op jit(solution)/shard_map/ppermute | solution.py:68
  438.9 6.0 %collective-permute-start.48 = (bf16[2,2,64,256]{3,2,1,0:T(8,128)(2,1)S(1)}, bf16[2,2,64,256]{3,2,1,0:T(8,128)(2,1)S(1)}, u32[]{:S(2)}, u32[]{:S(2)}) collective-permute-start(bf16[2,2,64,256]{3,2,1,0:T(8,128)(2,1)S(1)} %pad_maximum_fusion.14), channel_id=1, source_target_pairs={{0,4},{4,0},{8,12},{12,8},{1,5},{5,1},{9,13},{13,9},{2,6},{6,2},{1... | collective-permute-start | bytes 393224 | tf_op jit(solution)/shard_map/ppermute | solution.py:494
  439.6 8.1 %collective-permute-start.49 = (bf16[2,2,64,256]{3,2,1,0:T(8,128)(2,1)S(1)}, bf16[2,2,64,256]{3,2,1,0:T(8,128)(2,1)S(1)}, u32[]{:S(2)}, u32[]{:S(2)}) collective-permute-start(bf16[2,2,64,256]{3,2,1,0:T(8,128)(2,1)S(1)} %pad_maximum_fusion.14), channel_id=1, source_target_pairs={{0,8},{4,12},{8,0},{12,4},{1,9},{5,13},{9,1},{13,5},{2,10},{6,14},... | collective-permute-start | bytes 393224 | tf_op jit(solution)/shard_map/ppermute | solution.py:494
  442.0 7.6 %collective-permute-start.50 = (bf16[2,2,64,256]{3,2,1,0:T(8,128)(2,1)S(1)}, bf16[2,2,64,256]{3,2,1,0:T(8,128)(2,1)S(1)}, u32[]{:S(2)}, u32[]{:S(2)}) collective-permute-start(bf16[2,2,64,256]{3,2,1,0:T(8,128)(2,1)S(1)} %pad_maximum_fusion.14), channel_id=1, source_target_pairs={{0,12},{4,8},{8,4},{12,0},{1,13},{5,9},{9,5},{13,1},{2,14},{6,10},... | collective-permute-start | bytes 393224 | tf_op jit(solution)/shard_map/ppermute | solution.py:494
  444.1 20.1 %collective-permute-start.45 = (bf16[304,1024]{1,0:T(8,128)(2,1)S(1)}, bf16[304,1024]{1,0:T(8,128)(2,1)S(1)}, u32[]{:S(2)}, u32[]{:S(2)}) collective-permute-start(bf16[304,1024]{1,0:T(8,128)(2,1)S(1)} %convolution_convert_fusion.1), channel_id=1, source_target_pairs={{0,16},{16,0},{1,17},{17,1},{2,18},{18,2},{3,19},{19,3},{4,20},{20... | collective-permute-start | bytes 1867784 | tf_op jit(solution)/shard_map/ppermute | solution.py:68
  444.9 19.3 %collective-permute-start.47 = (bf16[304,1024]{1,0:T(8,128)(2,1)S(1)}, bf16[304,1024]{1,0:T(8,128)(2,1)S(1)}, u32[]{:S(2)}, u32[]{:S(2)}) collective-permute-start(bf16[304,1024]{1,0:T(8,128)(2,1)S(1)} %fusion.14), channel_id=1, source_target_pairs={{0,1},{1,0},{2,3},{3,2},{4,5},{5,4},{6,7},{7,6},{8,9},{9,8},{10,11... | collective-permute-start | bytes 1867784 | tf_op jit(solution)/shard_map/ppermute | solution.py:71
  449.7 4.9 collective-permute-start.51
  450.4 8.4 %collective-permute-start.52 = (f32[2,64,256]{2,1,0:T(8,128)S(1)}, f32[2,64,256]{2,1,0:T(8,128)S(1)}, u32[]{:S(2)}, u32[]{:S(2)}) collective-permute-start(f32[2,64,256]{2,1,0:T(8,128)S(1)} %get-tuple-element.143), channel_id=1, source_target_pairs={{0,16},{1,17},{2,0},{3,1},{16,18},{17,19},{18,2},{19,3},{4,20},{5,... | collective-permute-start | bytes 393224 | tf_op jit(solution)/shard_map/ppermute | solution.py:65
  465.0 3.9 collective-permute-start.53
  465.8 19.7 %collective-permute-start.54 = (bf16[304,1024]{1,0:T(8,128)(2,1)S(1)}, bf16[304,1024]{1,0:T(8,128)(2,1)S(1)}, u32[]{:S(2)}, u32[]{:S(2)}) collective-permute-start(bf16[304,1024]{1,0:T(8,128)(2,1)S(1)} %fusion.9), channel_id=1, source_target_pairs={{2,0},{3,1},{18,2},{19,3},{6,4},{7,5},{22,6},{23,7},{10,8},{11,9},... | collective-permute-start | bytes 1867784 | tf_op jit(solution)/shard_map/ppermute | solution.py:65
  (48 other events, 365.5 us)
Sparse Core Ops, SparseCore 0:
  27.1 39.9 all-gather.4
  69.5 57.6 all-gather.6
  129.1 78.8 all-gather.8
  209.7 87.6 all-gather.10

commit v6 on v5

--- a/solution.py
+++ b/solution.py
@@ -142,8 +142,14 @@
             body(pl.multiple_of(range_ref[t, 0], TQ), size * TQ)
 
 def pieces(prefix, start, size):
-    out = [(r, r, KC, False) for r in range(0, prefix, KC)]
-    return out + [(prefix + r, start + r, KC, True) for r in range(0, size, KC)]
+    out = [(r, start + r, KC, True) for r in range(0, size, KC)]
+    return out + [(size + r, r, KC, False) for r in range(0, prefix, KC)]
+
+def both_rows(ref, at, prefix, lane, width):
+    return jnp.concatenate([ref[at, lane:lane+width], ref[0:prefix, lane:lane+width]], 0)
+
+def both_lanes(ref, at, prefix, lane, width):
+    return jnp.concatenate([ref[lane:lane+width, at], ref[lane:lane+width, 0:prefix]], 1)
 
 def piece_mask(first, span_ref, heads):
     key = lax.broadcasted_iota(jnp.int32, (KC, TQ), 0) + first
@@ -166,8 +172,7 @@
         lanes = range(0, w, pw)
         for g, lane in enumerate(lanes):
             q = spread_heads(qkv_ref[here, lane:lane+pw] * BF(HD ** -0.5), pair)
-            s_ref[g, 0:prefix] = nt(qkv_ref[0:prefix, w+lane:w+lane+pw], q)
-            s_ref[g, prefix:prefix+size] = nt(qkv_ref[at, w+lane:w+lane+pw], q)
+            s_ref[g, 0:size+prefix] = nt(both_rows(qkv_ref, at, prefix, w+lane, pw), q)
         for g, lane in enumerate(lanes):
             peak = jnp.full((8, pair*TQ), -1e30, F32)
             for row, first, n, masked in pieces(prefix, start, size):
@@ -183,7 +188,7 @@
                 p_ref[g, row:row+n] = e.astype(BF)
                 total = total + jnp.sum(e.reshape(n//8, 8, -1), axis=0)
             total = jnp.sum(total, axis=0, keepdims=True)
-            acc = nn(vt_ref[lane:lane+pw, 0:prefix], p_ref[g, 0:prefix]) + nn(vt_ref[lane:lane+pw, at], p_ref[g, prefix:prefix+size])
+            acc = nn(both_lanes(vt_ref, at, prefix, lane, pw), p_ref[g, 0:size+prefix])
             outs.append(own_columns(acc * (1.0 / total), pair))
             lse = peak + jnp.log(total)
             for h in range(pair):
@@ -210,7 +215,7 @@
         both = (do_ref[...].astype(F32) * o_ref[...].astype(F32)).T
         outs = []
         at = pl.ds(start, size)
-        parts = ((slice(0, prefix), slice(0, prefix)), (at, slice(prefix, prefix+size)))
+        rows_in = slice(0, size + prefix)
         lanes = range(0, w, pw)
         qs, dos = [], []
         for g, lane in enumerate(lanes):
@@ -218,24 +223,26 @@
             do = spread_heads(do_ref[:, lane:lane+pw], pair)
             qs.append(q)
             dos.append(do)
-            for src, dst in parts:
-                s_ref[g, dst] = nt(qkv_ref[src, w+lane:w+lane+pw], q)
-                dp_ref[g, dst] = nt(qkv_ref[src, 2*w+lane:2*w+lane+pw], do)
+            s_ref[g, rows_in] = nt(both_rows(qkv_ref, at, prefix, w+lane, pw), q)
+            dp_ref[g, rows_in] = nt(both_rows(qkv_ref, at, prefix, 2*w+lane, pw), do)
+        deltas, lses = [], []
         for g, lane in enumerate(lanes):
             rows = range(lane // HD, lane // HD + pair)
-            delta = jnp.concatenate([jnp.sum(both[h*HD:(h+1)*HD], axis=0, keepdims=True) for h in rows], 1)
-            lse = jnp.concatenate([lse_ref[h:h+1, :] for h in rows], 1)
-            for row, first, n, masked in pieces(prefix, start, size):
-                prob = jnp.exp(s_ref[g, row:row+n] - lse)
+            deltas.append(jnp.concatenate([jnp.sum(both[h*HD:(h+1)*HD], axis=0, keepdims=True) for h in rows], 1))
+            lses.append(jnp.concatenate([lse_ref[h:h+1, :] for h in rows], 1))
+        for row, first, n, masked in pieces(prefix, start, size):
+            mask = piece_mask(first, span_ref, pair) if masked else None
+            for g in range(len(lanes)):
+                prob = jnp.exp(s_ref[g, row:row+n] - lses[g])
                 if masked:
-                    prob = jnp.where(piece_mask(first, span_ref, pair), prob, 0.0)
+                    prob = jnp.where(mask, prob, 0.0)
                 p_ref[g, row:row+n] = prob.astype(BF)
-                ds_ref[g, row:row+n] = (prob * (dp_ref[g, row:row+n] - delta)).astype(BF)
-            dq = 0.0
-            for src, dst in parts:
-                dv_ref[src, lane:lane+pw] += nn(p_ref[g, dst], dos[g])
-                dk_ref[src, lane:lane+pw] += nn(ds_ref[g, dst], qs[g])
-                dq = dq + nn(kt_ref[lane:lane+pw, src], ds_ref[g, dst])
+                ds_ref[g, row:row+n] = (prob * (dp_ref[g, row:row+n] - deltas[g])).astype(BF)
+        for g, lane in enumerate(lanes):
+            for to_ref, value in ((dv_ref, nn(p_ref[g, rows_in], dos[g])), (dk_ref, nn(ds_ref[g, rows_in], qs[g]))):
+                to_ref[at, lane:lane+pw] += value[0:size]
+                to_ref[0:prefix, lane:lane+pw] += value[size:size+prefix]
+            dq = nn(both_lanes(kt_ref, at, prefix, lane, pw), ds_ref[g, rows_in])
             outs.append(own_columns(dq, pair))
         out_ref[here, 0:w] = (jnp.concatenate(outs, 0) * HD ** -0.5).T.astype(BF)
     each_size(range_ref, t, body)

time: 499 us -> 497 us (level)
  starting transfers between devices: 101 us -> 94.7 us
  transfers between devices with their start and end apart: 59 -> 59, of which waited for: 36 -> 36; matrix products, arithmetic and copies ran while one was open for 9% -> 9% of each run, Pallas kernels for 11% -> 12%
where the time goes in v6:
time: 497 us; the launch traced here: 491 us
  waiting for transfers between devices  219 us (44%)
  starting transfers between devices  94.7 us (19%)
  Pallas kernels  86.4 us (17%)
  other arithmetic  30.5 us (6%)
  matrix products  24.3 us (5%)
  local copies, waits for them, and re-layouts  20.5 us (4%)
  between operations  15.6 us (3%)
    ppermute x11, waiting for transfers between devices, chip(): return lax.ppermute(value, 'mp', [(z, z ^ j) for z in range(self.mp)])  89 us
    ppermute x20, starting transfers between devices, send(): return lax.ppermute(value, ('section', 'mp'), pairs)  62.1 us
    ppermute x20, waiting for transfers between devices, send(): return lax.ppermute(value, ('section', 'mp'), pairs)  62 us
    all_gather x4, waiting for transfers between devices, gather(): return lax.all_gather(block, 'dp', axis=0, tiled=True)  43 us
    pallas_call x4, Pallas kernels, feed(): pl.pallas_call(lambda *refs: feed_kernel(mode, cuts, refs), grid=(at,), i...  41.4 us
    pallas_call x2, Pallas kernels, attend_back(): pl.pallas_call(partial(attn_bwd, prefix, heads), grid_spec=pltpu.Prefetch...  25.2 us
    dot_general x28, matrix products, dot(): return lax.dot_general(a, b, (dims, ((), ())), preferred_element_type=F32)  24.3 us
    ppermute x21, waiting for transfers between devices, core(): return lax.ppermute(value, 'section', [(0, 1), (1, 0)])  19.9 us
  transfers between devices with their start and end apart: 59, of which 36 were waited for; matrix products, arithmetic and copies ran while one was open for 9% of the time, Pallas kernels for 12%

profile of v6, /device:TPU:0, one launch (start us, length us, event | category | flops | bytes accessed | tf_op | source)
XLA Modules:
  0.0 490.6 jit_solution(204442696943701225)
XLA Ops:
  11.1 7.4 %collective-permute-start.1 = (bf16[336,768]{1,0:T(8,128)(2,1)S(1)}, bf16[336,768]{1,0:T(8,128)(2,1)}, u32[]{:S(2)}, u32[]{:S(2)}) collective-permute-start(bf16[336,768]{1,0:T(8,128)(2,1)S(1)} %pad_maximum_fusion.10), channel_id=1, source_target_pairs={{0,2},{1,3},{2,18},{3,19},{4,6},{5,7},{6,22},{7,23},{8,10},{9,11},... | collective-permute-start | bytes 1548296 | tf_op jit(solution)/shard_map/ppermute | solution.py:65
  18.5 5.8 %collective-permute-done.1 = bf16[336,768]{1,0:T(8,128)(2,1)} collective-permute-done((bf16[336,768]{1,0:T(8,128)(2,1)S(1)}, bf16[336,768]{1,0:T(8,128)(2,1)}, u32[]{:S(2)}, u32[]{:S(2)}) %collective-permute-start.1) | collective-permute-done | bytes 516128 | tf_op jit(solution)/shard_map/ppermute | solution.py:65
  29.0 9.6 %collective-permute-start.3 = (bf16[272,2304]{1,0:T(8,128)(2,1)S(1)}, bf16[272,2304]{1,0:T(8,128)(2,1)S(1)}, u32[]{:S(2)}, u32[]{:S(2)}) collective-permute-start(bf16[272,2304]{1,0:T(8,128)(2,1)S(1)} %pad_maximum_fusion.2), channel_id=1, source_target_pairs={{0,2},{1,3},{2,18},{3,19},{4,6},{5,7},{6,22},{7,23},{8,10},{9,11},... | collective-permute-start | bytes 3760136 | tf_op jit(solution)/shard_map/ppermute | solution.py:65
  38.6 14.4 %collective-permute-done.3 = bf16[272,2304]{1,0:T(8,128)(2,1)S(1)} collective-permute-done((bf16[272,2304]{1,0:T(8,128)(2,1)S(1)}, bf16[272,2304]{1,0:T(8,128)(2,1)S(1)}, u32[]{:S(2)}, u32[]{:S(2)}) %collective-permute-start.3) | collective-permute-done | bytes 1253408 | tf_op jit(solution)/shard_map/ppermute | solution.py:65
  54.3 12.8 %all-gather.5.cloned.1.call-done = bf16[1024,768]{1,0:T(8,128)(2,1)} async-done(((bf16[256,768]{1,0:T(8,128)(2,1)}), bf16[1024,768]{1,0:T(8,128)(2,1)}) %all-gather.5.cloned.1.call-update) | async-done | bytes 1572880 | tf_op jit(solution)/shard_map/all_gather | solution.py:84
  69.4 2.0 collective-permute-done.4
  72.3 2.0 collective-permute-start.11
  75.5 21.9 %collective-permute-start.6 = (bf16[304,1024]{1,0:T(8,128)(2,1)S(1)}, bf16[304,1024]{1,0:T(8,128)(2,1)}, u32[]{:S(2)}, u32[]{:S(2)}) collective-permute-start(bf16[304,1024]{1,0:T(8,128)(2,1)S(1)} %dynamic-slice_bitcast_fusion.1), channel_id=1, source_target_pairs={{0,2},{1,3},{18,16},{19,17},{4,6},{5,7},{22,20},{23,21},{8,10},{9,... | collective-permute-start | bytes 1867784 | tf_op jit(solution)/shard_map/ppermute | solution.py:65
  98.3 12.6 %collective-permute-done.6 = bf16[304,1024]{1,0:T(8,128)(2,1)} collective-permute-done((bf16[304,1024]{1,0:T(8,128)(2,1)S(1)}, bf16[304,1024]{1,0:T(8,128)(2,1)}, u32[]{:S(2)}, u32[]{:S(2)}) %collective-permute-start.6) | collective-permute-done | bytes 622624 | tf_op jit(solution)/shard_map/ppermute | solution.py:65
  112.2 1.6 slice.300
  113.8 1.4 pad_maximum_fusion.1
  115.2 12.0 %all-gather.7.cloned.1.call-done.refs_0_.refs_1_ = bf16[1024,2304]{1,0:T(8,128)(2,1)} async-done(((bf16[256,2304]{1,0:T(8,128)(2,1)}), bf16[1024,2304]{1,0:T(8,128)(2,1)}) %all-gather.7.cloned.1.call-update) | async-done | bytes 4718608 | tf_op jit(solution)/shard_map/all_gather | solution.py:84
  127.9 1.5 collective-permute-start.8
  132.0 1.4 collective-permute-start.25
  133.4 1.9 collective-permute-start.26
  135.5 4.1 collective-permute-start.7
  139.7 11.2 %collective-permute-done.8 = bf16[304,1024]{1,0:T(8,128)(2,1)} collective-permute-done((bf16[304,1024]{1,0:T(8,128)(2,1)S(1)}, bf16[304,1024]{1,0:T(8,128)(2,1)}, u32[]{:S(2)}, u32[]{:S(2)}) %collective-permute-start.8) | collective-permute-done | bytes 622624 | tf_op jit(solution)/shard_map/ppermute | solution.py:71
  156.1 2.1 fusion.20
  158.9 9.9 %attend.2 = (bf16[1280,256]{1,0:T(8,128)(2,1)S(1)}, f32[4,1280]{1,0:T(4,128)S(1)}) custom-call(s32[10,2]{1,0:T(8,128)S(1)} %copy.78.range_ref, s32[2,1280]{1,0:T(2,128)S(1)} %pad_add_fusion.span_ref, bf16[1280,768]{1,0:T(8,128)(2,1)S(1)} %fusion.22.qkv_ref), custom_call_target="tpu_custom_call" | custom-call | flops 419430 | bytes 1 | tf_op jit(solution)/shard_map/attend/pallas_call | solution.py:265
  168.8 1.8 collective-permute-start.10
  170.6 18.8 %collective-permute-done.10 = bf16[608,256]{1,0:T(8,128)(2,1)S(1)} collective-permute-done((bf16[608,256]{1,0:T(8,128)(2,1)S(1)}, bf16[608,256]{1,0:T(8,128)(2,1)S(1)}, u32[]{:S(2)}, u32[]{:S(2)}) %collective-permute-start.10) | collective-permute-done | bytes 311328 | tf_op jit(solution)/shard_map/ppermute | solution.py:71
  190.4 1.6 pad_maximum_fusion
  192.0 16.0 %all-gather.9.cloned.1.call-done.refs_2_.refs_3_ = bf16[1024,3584]{1,0:T(8,128)(2,1)} async-done(((bf16[256,3584]{1,0:T(8,128)(2,1)}), bf16[1024,3584]{1,0:T(8,128)(2,1)}) %all-gather.9.cloned.1.call-update) | async-done | bytes 7340048 | tf_op jit(solution)/shard_map/all_gather | solution.py:84
  210.8 1.4 fusion.11
  212.5 1.4 fusion.55
  214.3 1.7 fusion.140
  218.9 5.7 %collective-permute-start.16 = (bf16[304,1024]{1,0:T(8,128)(2,1)}, bf16[304,1024]{1,0:T(8,128)(2,1)}, u32[]{:S(2)}, u32[]{:S(2)}) collective-permute-start(bf16[304,1024]{1,0:T(8,128)(2,1)} %dynamic-slice_bitcast_fusion), channel_id=1, source_target_pairs={{0,2},{1,3},{18,16},{19,17},{4,6},{5,7},{22,20},{23,21},{8,10},{9,... | collective-permute-start | bytes 1867784 | tf_op jit(solution)/shard_map/ppermute | solution.py:65
  225.3 12.6 %feed_forward.2 = (f32[304,1024]{1,0:T(8,128)S(1)}, bf16[304,1024]{1,0:T(8,128)(2,1)S(1)}, bf16[608,2048]{1,0:T(8,128)(2,1)S(1)}) custom-call(bf16[1024,2304]{1,0:T(8,128)(2,1)} %all-gather.7.cloned.1.call-done.refs_0_.refs_1_, bf16[1024,2304]{1,0:T(8,128)(2,1)} %all-gather.7.cloned.1.call-done.refs_0_.refs_1_, ...), custom_call_target="tpu_custom_call" | custom-call | flops 1275068 | bytes 1 | tf_op jit(solution)/shard_map/feed_forward/pallas_call | solution.py:411
  241.8 1.4 collective-permute-start.19
  243.3 14.8 %collective-permute-done.19 = bf16[304,1024]{1,0:T(8,128)(2,1)S(1)} collective-permute-done((bf16[304,1024]{1,0:T(8,128)(2,1)S(1)}, bf16[304,1024]{1,0:T(8,128)(2,1)S(1)}, u32[]{:S(2)}, u32[]{:S(2)}) %collective-permute-start.19) | collective-permute-done | bytes 622624 | tf_op jit(solution)/shard_map/ppermute | solution.py:71
  260.9 1.7 collective-permute-start.22
  264.6 9.9 %attend.3 = (bf16[1280,256]{1,0:T(8,128)(2,1)S(1)}, f32[4,1280]{1,0:T(4,128)S(1)}) custom-call(s32[10,2]{1,0:T(8,128)S(1)} %copy.78.range_ref, s32[2,1280]{1,0:T(2,128)S(1)} %pad_add_fusion.span_ref, bf16[1280,768]{1,0:T(8,128)(2,1)S(1)} %fusion.30.qkv_ref), custom_call_target="tpu_custom_call" | custom-call | flops 419430 | bytes 1 | tf_op jit(solution)/shard_map/attend/pallas_call | solution.py:265
  274.5 6.2 %collective-permute-done.22 = bf16[304,1024]{1,0:T(8,128)(2,1)S(1)} collective-permute-done((bf16[304,1024]{1,0:T(8,128)(2,1)S(1)}, bf16[304,1024]{1,0:T(8,128)(2,1)S(1)}, u32[]{:S(2)}, u32[]{:S(2)}) %collective-permute-start.22) | collective-permute-done | bytes 622624 | tf_op jit(solution)/shard_map/ppermute | solution.py:65
  281.5 6.2 %collective-permute-done.23 = bf16[608,256]{1,0:T(8,128)(2,1)S(1)} collective-permute-done((bf16[608,256]{1,0:T(8,128)(2,1)S(1)}, bf16[608,256]{1,0:T(8,128)(2,1)S(1)}, u32[]{:S(2)}, u32[]{:S(2)}) %collective-permute-start.23) | collective-permute-done | bytes 311328 | tf_op jit(solution)/shard_map/ppermute | solution.py:71
  295.1 2.2 all-gather.11.cloned.1.call-done.refs_0_.refs_1_
  299.5 11.8 %feed_forward.3 = (f32[304,1024]{1,0:T(8,128)S(1)}, bf16[304,1024]{1,0:T(8,128)(2,1)S(1)}, bf16[608,2048]{1,0:T(8,128)(2,1)S(1)}) custom-call(bf16[1024,4096]{1,0:T(8,128)(2,1)} %all-gather.11.cloned.1.call-done.refs_0_.refs_1_, bf16[1024,4096]{1,0:T(8,128)(2,1)} %all-gather.11.cloned.1.call-done.refs_0_.refs_1_, bf16[304,1024]{1,0:T(8,128)(2,1)S(1)} %copy-done.3, ...), custom_call_target="tpu_custom_call" | custom-call | flops 1275068 | bytes 1 | tf_op jit(solution)/shard_map/feed_forward/pallas_call | solution.py:411
  311.3 2.0 collective-permute-done.29
  316.6 1.9 collective-permute-done.30.refs_3_
  318.5 8.1 %feed_back.2 = (f32[304,1024]{1,0:T(8,128)S(1)}, bf16[304,1024]{1,0:T(8,128)(2,1)S(1)}) custom-call(bf16[1024,4096]{1,0:T(8,128)(2,1)} %all-gather.11.cloned.1.call-done.refs_0_.refs_1_, bf16[1024,4096]{1,0:T(8,128)(2,1)} %all-gather.11.cloned.1.call-done.refs_0_.refs_1_, bf16[304,1024]{1,0:T(8,128)(2,1)S(1)} %fusion.125.refs_2_, ...), custom_call_target="tpu_custom_call" | custom-call | flops 1275068 | bytes 1 | tf_op jit(solution)/shard_map/feed_back/pallas_call | solution.py:411
  326.8 1.9 collective-permute-done.31
  328.8 3.0 fusion.128
  331.8 1.4 fusion.130
  333.4 1.9 collective-permute-done.32
  335.8 1.6 collective-permute-start.33
  337.8 7.4 %collective-permute-done.33 = bf16[608,256]{1,0:T(8,128)(2,1)S(1)} collective-permute-done((bf16[608,256]{1,0:T(8,128)(2,1)S(1)}, bf16[608,256]{1,0:T(8,128)(2,1)S(1)}, u32[]{:S(2)}, u32[]{:S(2)}) %collective-permute-start.33) | collective-permute-done | bytes 311328 | tf_op jit(solution)/shard_map/ppermute | solution.py:71
  347.5 12.7 %attend_back.2 = (bf16[1280,768]{1,0:T(8,128)(2,1)S(1)}, f32[2,64,256]{2,1,0:T(8,128)S(1)}) custom-call(s32[10,2]{1,0:T(8,128)S(1)} %copy.78.range_ref, s32[2,1280]{1,0:T(2,128)S(1)} %pad_add_fusion.span_ref, bf16[1280,768]{1,0:T(8,128)(2,1)S(1)} %fusion.30.qkv_ref, f32[4,1280]{1,0:T(4,128)S(1)} %get-tuple-element.81.lse_ref, ...), custom_call_target="tpu_custom_call" | custom-call | flops 1048576 | bytes 1 | tf_op jit(solution)/shard_map/attend_back/pallas_call | solution.py:280
  361.2 7.5 %collective-permute-start.37 = (bf16[304,1024]{1,0:T(8,128)(2,1)S(1)}, bf16[304,1024]{1,0:T(8,128)(2,1)S(1)}, u32[]{:S(2)}, u32[]{:S(2)}) collective-permute-start(bf16[304,1024]{1,0:T(8,128)(2,1)S(1)} %convolution_convert_fusion.2), channel_id=1, source_target_pairs={{0,16},{16,0},{1,17},{17,1},{2,18},{18,2},{3,19},{19,3},{4,20},{20... | collective-permute-start | bytes 1867784 | tf_op jit(solution)/shard_map/ppermute | solution.py:68
  371.5 15.9 %collective-permute-done.38 = bf16[304,1024]{1,0:T(8,128)(2,1)S(1)} collective-permute-done((bf16[304,1024]{1,0:T(8,128)(2,1)S(1)}, bf16[304,1024]{1,0:T(8,128)(2,1)S(1)}, u32[]{:S(2)}, u32[]{:S(2)}) %collective-permute-start.38) | collective-permute-done | bytes 622624 | tf_op jit(solution)/shard_map/ppermute | solution.py:71
  389.1 2.0 collective-permute-done.39.refs_5_
  391.2 8.9 %feed_back.3 = (f32[304,1024]{1,0:T(8,128)S(1)}, bf16[304,1024]{1,0:T(8,128)(2,1)S(1)}) custom-call(bf16[1024,2304]{1,0:T(8,128)(2,1)} %all-gather.7.cloned.1.call-done.refs_0_.refs_1_, bf16[1024,2304]{1,0:T(8,128)(2,1)} %all-gather.7.cloned.1.call-done.refs_0_.refs_1_, bf16[1024,3584]{1,0:T(8,128)(2,1)} %all-gather.9.cloned.1.call-done.refs_2_.refs_3_, ...), custom_call_target="tpu_custom_call" | custom-call | flops 1275068 | bytes 1 | tf_op jit(solution)/shard_map/feed_back/pallas_call | solution.py:411
  400.3 1.9 collective-permute-done.40
  403.8 1.9 collective-permute-done.41
  405.7 1.5 convolution_convert_fusion.5
  407.6 1.5 convolution_convert_fusion.4
  409.2 7.6 %collective-permute-done.42 = bf16[608,256]{1,0:T(8,128)(2,1)S(1)} collective-permute-done((bf16[608,256]{1,0:T(8,128)(2,1)S(1)}, bf16[608,256]{1,0:T(8,128)(2,1)S(1)}, u32[]{:S(2)}, u32[]{:S(2)}) %collective-permute-start.42) | collective-permute-done | bytes 311328 | tf_op jit(solution)/shard_map/ppermute | solution.py:71
  419.0 12.4 %attend_back.3 = (bf16[1280,768]{1,0:T(8,128)(2,1)S(1)}, f32[2,64,256]{2,1,0:T(8,128)S(1)}) custom-call(s32[10,2]{1,0:T(8,128)S(1)} %copy.78.range_ref, s32[2,1280]{1,0:T(2,128)S(1)} %pad_add_fusion.span_ref, bf16[1280,768]{1,0:T(8,128)(2,1)S(1)} %copy-done.1, f32[4,1280]{1,0:T(4,128)S(1)} %get-tuple-element.88.lse_ref, ...), custom_call_target="tpu_custom_call" | custom-call | flops 1048576 | bytes 1 | tf_op jit(solution)/shard_map/attend_back/pallas_call | solution.py:280
  432.1 5.6 %collective-permute-start.46 = (bf16[304,1024]{1,0:T(8,128)(2,1)S(1)}, bf16[304,1024]{1,0:T(8,128)(2,1)S(1)}, u32[]{:S(2)}, u32[]{:S(2)}) collective-permute-start(bf16[304,1024]{1,0:T(8,128)(2,1)S(1)} %convolution_convert_fusion), channel_id=1, source_target_pairs={{0,16},{16,0},{1,17},{17,1},{2,18},{18,2},{3,19},{19,3},{4,20},{20... | collective-permute-start | bytes 1867784 | tf_op jit(solution)/shard_map/ppermute | solution.py:68
  437.8 1.8 collective-permute-start.48
  439.9 1.5 collective-permute-start.50
  443.4 4.1 collective-permute-done.49
  448.3 1.6 collective-permute-start.52
  450.0 5.1 %collective-permute-done.52 = f32[2,64,256]{2,1,0:T(8,128)S(1)} collective-permute-done((f32[2,64,256]{2,1,0:T(8,128)S(1)}, f32[2,64,256]{2,1,0:T(8,128)S(1)}, u32[]{:S(2)}, u32[]{:S(2)}) %collective-permute-start.52) | collective-permute-done | bytes 131104 | tf_op jit(solution)/shard_map/ppermute | solution.py:65
  455.1 7.0 %collective-permute-done.47 = bf16[304,1024]{1,0:T(8,128)(2,1)S(1)} collective-permute-done((bf16[304,1024]{1,0:T(8,128)(2,1)S(1)}, bf16[304,1024]{1,0:T(8,128)(2,1)S(1)}, u32[]{:S(2)}, u32[]{:S(2)}) %collective-permute-start.47) | collective-permute-done | bytes 622624 | tf_op jit(solution)/shard_map/ppermute | solution.py:71
  466.9 15.8 %collective-permute-done.54 = bf16[304,1024]{1,0:T(8,128)(2,1)S(1)} collective-permute-done((bf16[304,1024]{1,0:T(8,128)(2,1)S(1)}, bf16[304,1024]{1,0:T(8,128)(2,1)S(1)}, u32[]{:S(2)}, u32[]{:S(2)}) %collective-permute-start.54) | collective-permute-done | bytes 622624 | tf_op jit(solution)/shard_map/ppermute | solution.py:65
  (333 shorter events, 78.4 us)
Async XLA Ops:
  7.2 59.9 %all-gather.5.cloned.1.call-start = ((), (), s32[]{:S(2)}) async-start(), calls=%async_computation | async-start | bytes 1966080 | tf_op jit(solution)/shard_map/all_gather | solution.py:84
  10.3 8.2 %collective-permute-start = (bf16[336,768]{1,0:T(8,128)(2,1)S(1)}, bf16[336,768]{1,0:T(8,128)(2,1)S(1)}, u32[]{:S(2)}, u32[]{:S(2)}) collective-permute-start(bf16[336,768]{1,0:T(8,128)(2,1)S(1)} %pad_maximum_fusion.10), channel_id=1, source_target_pairs={{0,0},{1,1},{2,16},{3,17},{4,4},{5,5},{6,20},{7,21},{8,8},{9,9},{1... | collective-permute-start | bytes 1548296 | tf_op jit(solution)/shard_map/ppermute | solution.py:65
  11.1 13.2 %collective-permute-start.1 = (bf16[336,768]{1,0:T(8,128)(2,1)S(1)}, bf16[336,768]{1,0:T(8,128)(2,1)}, u32[]{:S(2)}, u32[]{:S(2)}) collective-permute-start(bf16[336,768]{1,0:T(8,128)(2,1)S(1)} %pad_maximum_fusion.10), channel_id=1, source_target_pairs={{0,2},{1,3},{2,18},{3,19},{4,6},{5,7},{6,22},{7,23},{8,10},{9,11},... | collective-permute-start | bytes 1548296 | tf_op jit(solution)/shard_map/ppermute | solution.py:65
  27.0 100.2 %all-gather.7.cloned.1.call-start = ((), (), s32[]{:S(2)}) async-start(), calls=%async_computation.1 | async-start | bytes 5898240 | tf_op jit(solution)/shard_map/all_gather | solution.py:84
  28.2 10.3 %collective-permute-start.2 = (bf16[272,2304]{1,0:T(8,128)(2,1)S(1)}, bf16[272,2304]{1,0:T(8,128)(2,1)S(1)}, u32[]{:S(2)}, u32[]{:S(2)}) collective-permute-start(bf16[272,2304]{1,0:T(8,128)(2,1)S(1)} %pad_maximum_fusion.2), channel_id=1, source_target_pairs={{0,0},{1,1},{2,16},{3,17},{4,4},{5,5},{6,20},{7,21},{8,8},{9,9},{1... | collective-permute-start | bytes 3760136 | tf_op jit(solution)/shard_map/ppermute | solution.py:65
  29.0 24.0 %collective-permute-start.3 = (bf16[272,2304]{1,0:T(8,128)(2,1)S(1)}, bf16[272,2304]{1,0:T(8,128)(2,1)S(1)}, u32[]{:S(2)}, u32[]{:S(2)}) collective-permute-start(bf16[272,2304]{1,0:T(8,128)(2,1)S(1)} %pad_maximum_fusion.2), channel_id=1, source_target_pairs={{0,2},{1,3},{2,18},{3,19},{4,6},{5,7},{6,22},{7,23},{8,10},{9,11},... | collective-permute-start | bytes 3760136 | tf_op jit(solution)/shard_map/ppermute | solution.py:65
  67.1 140.9 %all-gather.9.cloned.1.call-start = ((), (), s32[]{:S(2)}) async-start(), calls=%async_computation.2 | async-start | bytes 9175040 | tf_op jit(solution)/shard_map/all_gather | solution.py:84
  67.3 4.0 collective-permute-start.4
  68.6 2.7 collective-permute-start.5
  72.3 39.8 %collective-permute-start.11 = (bf16[272,2304]{1,0:T(8,128)(2,1)S(1)}, bf16[272,2304]{1,0:T(8,128)(2,1)}, u32[]{:S(2)}, u32[]{:S(2)}) collective-permute-start(bf16[272,2304]{1,0:T(8,128)(2,1)S(1)} %broadcast_select_fusion), channel_id=1, source_target_pairs={{0,1},{1,0},{2,3},{3,2},{4,5},{5,4},{6,7},{7,6},{8,9},{9,8},{10,11... | collective-permute-start | bytes 3760136 | tf_op jit(solution)/shard_map/ppermute | solution.py:71
  75.5 35.5 %collective-permute-start.6 = (bf16[304,1024]{1,0:T(8,128)(2,1)S(1)}, bf16[304,1024]{1,0:T(8,128)(2,1)}, u32[]{:S(2)}, u32[]{:S(2)}) collective-permute-start(bf16[304,1024]{1,0:T(8,128)(2,1)S(1)} %dynamic-slice_bitcast_fusion.1), channel_id=1, source_target_pairs={{0,2},{1,3},{18,16},{19,17},{4,6},{5,7},{22,20},{23,21},{8,10},{9,... | collective-permute-start | bytes 1867784 | tf_op jit(solution)/shard_map/ppermute | solution.py:65
  98.3 15.5 %collective-permute-start.12 = (bf16[256,256]{1,0:T(8,128)(2,1)S(1)}, bf16[256,256]{1,0:T(8,128)(2,1)S(1)}, u32[]{:S(2)}, u32[]{:S(2)}) collective-permute-start(bf16[256,256]{1,0:T(8,128)(2,1)S(1)} %slice.302), channel_id=1, source_target_pairs={{0,1},{1,0},{2,3},{3,2},{4,5},{5,4},{6,7},{7,6},{8,9},{9,8},{10,11... | collective-permute-start | bytes 393224 | tf_op jit(solution)/shard_map/ppermute | solution.py:71
  112.1 41.1 %copy-start.21 = (bf16[304,1024]{1,0:T(8,128)(2,1)}, bf16[304,1024]{1,0:T(8,128)(2,1)S(1)}, u32[]{:S(2)}) copy-start(bf16[304,1024]{1,0:T(8,128)(2,1)S(1)} %bitcast_select_fusion.1) | copy-start | bytes 1867780
  127.2 170.1 %all-gather.11.cloned.1.call-start = ((), (), s32[]{:S(2)}) async-start(), calls=%async_computation.3 | async-start | bytes 10485760 | tf_op jit(solution)/shard_map/all_gather | solution.py:84
  127.9 23.1 %collective-permute-start.8 = (bf16[304,1024]{1,0:T(8,128)(2,1)S(1)}, bf16[304,1024]{1,0:T(8,128)(2,1)}, u32[]{:S(2)}, u32[]{:S(2)}) collective-permute-start(bf16[304,1024]{1,0:T(8,128)(2,1)S(1)} %bitcast_select_fusion.1), channel_id=1, source_target_pairs={{0,1},{1,0},{2,3},{3,2},{4,5},{5,4},{6,7},{7,6},{8,9},{9,8},{10,11... | collective-permute-start | bytes 1867784 | tf_op jit(solution)/shard_map/ppermute | solution.py:71
  132.0 22.6 %collective-permute-start.25 = (bf16[272,2048]{1,0:T(8,128)(2,1)}, bf16[272,2048]{1,0:T(8,128)(2,1)}, u32[]{:S(2)}, u32[]{:S(2)}) collective-permute-start(bf16[272,2048]{1,0:T(8,128)(2,1)} %pad_maximum_fusion.5), channel_id=1, source_target_pairs={{16,0},{17,1},{18,16},{19,17},{20,4},{21,5},{22,20},{23,21},{24,8}... | collective-permute-start | bytes 3342344 | tf_op jit(solution)/shard_map/ppermute | solution.py:65
  133.4 21.2 %collective-permute-start.26 = (bf16[272,2048]{1,0:T(8,128)(2,1)}, bf16[272,2048]{1,0:T(8,128)(2,1)}, u32[]{:S(2)}, u32[]{:S(2)}) collective-permute-start(bf16[272,2048]{1,0:T(8,128)(2,1)} %pad_maximum_fusion.5), channel_id=1, source_target_pairs={{16,2},{17,3},{18,18},{19,19},{20,6},{21,7},{22,22},{23,23},{24,10... | collective-permute-start | bytes 3342344 | tf_op jit(solution)/shard_map/ppermute | solution.py:65
  135.5 18.4 %collective-permute-start.7 = (bf16[304,1024]{1,0:T(8,128)(2,1)S(1)}, bf16[304,1024]{1,0:T(8,128)(2,1)S(1)}, u32[]{:S(2)}, u32[]{:S(2)}) collective-permute-start(bf16[304,1024]{1,0:T(8,128)(2,1)S(1)} %bitcast_select_fusion.1), channel_id=1, source_target_pairs={{0,16},{16,0},{1,17},{17,1},{2,18},{18,2},{3,19},{19,3},{4,20},{20... | collective-permute-start | bytes 1867784 | tf_op jit(solution)/shard_map/ppermute | solution.py:68
  150.9 3.7 collective-permute-start.9
  156.0 33.4 %copy-start.17 = (bf16[272,2048]{1,0:T(8,128)(2,1)}, bf16[272,2048]{1,0:T(8,128)(2,1)S(1)}, u32[]{:S(2)}) copy-start(bf16[272,2048]{1,0:T(8,128)(2,1)S(1)} %broadcast_select_fusion.1) | copy-start | bytes 3342340
  156.0 33.4 %collective-permute-start.27 = (bf16[272,2048]{1,0:T(8,128)(2,1)S(1)}, bf16[272,2048]{1,0:T(8,128)(2,1)S(1)}, u32[]{:S(2)}, u32[]{:S(2)}) collective-permute-start(bf16[272,2048]{1,0:T(8,128)(2,1)S(1)} %broadcast_select_fusion.1), channel_id=1, source_target_pairs={{0,1},{1,0},{2,3},{3,2},{4,5},{5,4},{6,7},{7,6},{8,9},{9,8},{10,11... | collective-permute-start | bytes 3342344 | tf_op jit(solution)/shard_map/ppermute | solution.py:71
  168.8 20.6 %collective-permute-start.10 = (bf16[608,256]{1,0:T(8,128)(2,1)S(1)}, bf16[608,256]{1,0:T(8,128)(2,1)S(1)}, u32[]{:S(2)}, u32[]{:S(2)}) collective-permute-start(bf16[608,256]{1,0:T(8,128)(2,1)S(1)} %pad_maximum_fusion.11), channel_id=1, source_target_pairs={{0,1},{1,0},{2,3},{3,2},{4,5},{5,4},{6,7},{7,6},{8,9},{9,8},{10,11... | collective-permute-start | bytes 933896 | tf_op jit(solution)/shard_map/ppermute | solution.py:71
  208.1 1.3 collective-permute-start.14
  212.2 2.1 collective-permute-start.13
  216.0 24.1 %copy-start.8 = (f32[304,1024]{1,0:T(8,128)}, f32[304,1024]{1,0:T(8,128)S(1)}, u32[]{:S(2)}) copy-start(f32[304,1024]{1,0:T(8,128)S(1)} %get-tuple-element.168) | copy-start | bytes 3735556
  216.6 8.8 %collective-permute-start.15 = (bf16[304,1024]{1,0:T(8,128)(2,1)S(1)}, bf16[304,1024]{1,0:T(8,128)(2,1)S(1)}, u32[]{:S(2)}, u32[]{:S(2)}) collective-permute-start(bf16[304,1024]{1,0:T(8,128)(2,1)S(1)} %fusion.33.refs_4_), channel_id=1, source_target_pairs={{0,16},{16,0},{1,17},{17,1},{2,18},{18,2},{3,19},{19,3},{4,20},{20... | collective-permute-start | bytes 1867784 | tf_op jit(solution)/shard_map/ppermute | solution.py:68
  218.0 40.3 %slice-start = ((s8[7340032]{0:T(1024)(128)(4,1)}), s8[4194304]{0:T(1024)(128)(4,1)S(1)}, s32[]{:S(2)}) async-start(s8[7340032]{0:T(1024)(128)(4,1)} %bitcast.135), calls=%async_computation.4 | async-start | bytes 8388608
  218.9 19.1 %collective-permute-start.16 = (bf16[304,1024]{1,0:T(8,128)(2,1)}, bf16[304,1024]{1,0:T(8,128)(2,1)}, u32[]{:S(2)}, u32[]{:S(2)}) collective-permute-start(bf16[304,1024]{1,0:T(8,128)(2,1)} %dynamic-slice_bitcast_fusion), channel_id=1, source_target_pairs={{0,2},{1,3},{18,16},{19,17},{4,6},{5,7},{22,20},{23,21},{8,10},{9,... | collective-permute-start | bytes 1867784 | tf_op jit(solution)/shard_map/ppermute | solution.py:65
  225.3 33.0 %slice-start.1 = ((s8[7340032]{0:T(1024)(128)(4,1)}), s8[3145728]{0:T(1024)(128)(4,1)S(1)}, s32[]{:S(2)}) async-start(s8[7340032]{0:T(1024)(128)(4,1)} %bitcast.135), calls=%async_computation.5 | async-start | bytes 6291456
  238.0 2.1 collective-permute-start.17
  241.8 16.4 %collective-permute-start.19 = (bf16[304,1024]{1,0:T(8,128)(2,1)S(1)}, bf16[304,1024]{1,0:T(8,128)(2,1)S(1)}, u32[]{:S(2)}, u32[]{:S(2)}) collective-permute-start(bf16[304,1024]{1,0:T(8,128)(2,1)S(1)} %add_convert_fusion.1), channel_id=1, source_target_pairs={{0,1},{1,0},{2,3},{3,2},{4,5},{5,4},{6,7},{7,6},{8,9},{9,8},{10,11... | collective-permute-start | bytes 1867784 | tf_op jit(solution)/shard_map/ppermute | solution.py:71
  243.2 15.8 %collective-permute-start.18 = (bf16[304,1024]{1,0:T(8,128)(2,1)S(1)}, bf16[304,1024]{1,0:T(8,128)(2,1)S(1)}, u32[]{:S(2)}, u32[]{:S(2)}) collective-permute-start(bf16[304,1024]{1,0:T(8,128)(2,1)S(1)} %add_convert_fusion.1), channel_id=1, source_target_pairs={{0,16},{16,0},{1,17},{17,1},{2,18},{18,2},{3,19},{19,3},{4,20},{20... | collective-permute-start | bytes 1867784 | tf_op jit(solution)/shard_map/ppermute | solution.py:68
  258.1 2.1 collective-permute-start.20
  260.2 14.3 %collective-permute-start.21 = (bf16[304,1024]{1,0:T(8,128)(2,1)S(1)}, bf16[304,1024]{1,0:T(8,128)(2,1)S(1)}, u32[]{:S(2)}, u32[]{:S(2)}) collective-permute-start(bf16[304,1024]{1,0:T(8,128)(2,1)S(1)} %add_convert_fusion.1), channel_id=1, source_target_pairs={{0,0},{1,1},{16,2},{17,3},{4,4},{5,5},{20,6},{21,7},{8,8},{9,9},{2... | collective-permute-start | bytes 1867784 | tf_op jit(solution)/shard_map/ppermute | solution.py:65
  260.9 19.8 %collective-permute-start.22 = (bf16[304,1024]{1,0:T(8,128)(2,1)S(1)}, bf16[304,1024]{1,0:T(8,128)(2,1)S(1)}, u32[]{:S(2)}, u32[]{:S(2)}) collective-permute-start(bf16[304,1024]{1,0:T(8,128)(2,1)S(1)} %add_convert_fusion.1), channel_id=1, source_target_pairs={{2,0},{3,1},{18,2},{19,3},{6,4},{7,5},{22,6},{23,7},{10,8},{11,9},... | collective-permute-start | bytes 1867784 | tf_op jit(solution)/shard_map/ppermute | solution.py:65
  280.8 7.0 %collective-permute-start.23 = (bf16[608,256]{1,0:T(8,128)(2,1)S(1)}, bf16[608,256]{1,0:T(8,128)(2,1)S(1)}, u32[]{:S(2)}, u32[]{:S(2)}) collective-permute-start(bf16[608,256]{1,0:T(8,128)(2,1)S(1)} %pad_maximum_fusion.13), channel_id=1, source_target_pairs={{0,1},{1,0},{2,3},{3,2},{4,5},{5,4},{6,7},{7,6},{8,9},{9,8},{10,11... | collective-permute-start | bytes 933896 | tf_op jit(solution)/shard_map/ppermute | solution.py:71
  288.4 2.1 collective-permute-start.24
  292.2 2.1 collective-permute-start.28
  311.3 2.1 collective-permute-start.29
  316.4 2.1 collective-permute-start.30
  326.6 2.1 collective-permute-start.31
  333.2 2.1 collective-permute-start.32
  335.8 9.5 %collective-permute-start.33 = (bf16[608,256]{1,0:T(8,128)(2,1)S(1)}, bf16[608,256]{1,0:T(8,128)(2,1)S(1)}, u32[]{:S(2)}, u32[]{:S(2)}) collective-permute-start(bf16[608,256]{1,0:T(8,128)(2,1)S(1)} %convolution_convert_fusion.7), channel_id=1, source_target_pairs={{0,1},{1,0},{2,3},{3,2},{4,5},{5,4},{6,7},{7,6},{8,9},{9,8},{10,11... | collective-permute-start | bytes 933896 | tf_op jit(solution)/shard_map/ppermute | solution.py:71
  345.4 14.8 %collective-permute-start.34 = (bf16[304,1024]{1,0:T(8,128)(2,1)S(1)}, bf16[304,1024]{1,0:T(8,128)(2,1)S(1)}, u32[]{:S(2)}, u32[]{:S(2)}) collective-permute-start(bf16[304,1024]{1,0:T(8,128)(2,1)S(1)} %get-tuple-element.80), channel_id=1, source_target_pairs={{0,16},{1,17},{16,18},{17,19},{4,20},{5,21},{20,22},{21,23},{8,24}... | collective-permute-start | bytes 1867784 | tf_op jit(solution)/shard_map/ppermute | solution.py:65
  346.7 13.5 %collective-permute-start.35 = (bf16[304,1024]{1,0:T(8,128)(2,1)S(1)}, bf16[304,1024]{1,0:T(8,128)(2,1)S(1)}, u32[]{:S(2)}, u32[]{:S(2)}) collective-permute-start(bf16[304,1024]{1,0:T(8,128)(2,1)S(1)} %get-tuple-element.80), channel_id=1, source_target_pairs={{2,16},{3,17},{18,18},{19,19},{6,20},{7,21},{22,22},{23,23},{10,24... | collective-permute-start | bytes 1867784 | tf_op jit(solution)/shard_map/ppermute | solution.py:65
  361.2 9.2 %collective-permute-start.37 = (bf16[304,1024]{1,0:T(8,128)(2,1)S(1)}, bf16[304,1024]{1,0:T(8,128)(2,1)S(1)}, u32[]{:S(2)}, u32[]{:S(2)}) collective-permute-start(bf16[304,1024]{1,0:T(8,128)(2,1)S(1)} %convolution_convert_fusion.2), channel_id=1, source_target_pairs={{0,16},{16,0},{1,17},{17,1},{2,18},{18,2},{3,19},{19,3},{4,20},{20... | collective-permute-start | bytes 1867784 | tf_op jit(solution)/shard_map/ppermute | solution.py:68
  369.4 2.1 collective-permute-start.36
  371.1 16.4 %collective-permute-start.38 = (bf16[304,1024]{1,0:T(8,128)(2,1)S(1)}, bf16[304,1024]{1,0:T(8,128)(2,1)S(1)}, u32[]{:S(2)}, u32[]{:S(2)}) collective-permute-start(bf16[304,1024]{1,0:T(8,128)(2,1)S(1)} %fusion.13), channel_id=1, source_target_pairs={{0,1},{1,0},{2,3},{3,2},{4,5},{5,4},{6,7},{7,6},{8,9},{9,8},{10,11... | collective-permute-start | bytes 1867784 | tf_op jit(solution)/shard_map/ppermute | solution.py:71
  389.0 2.1 collective-permute-start.39
  400.1 2.1 collective-permute-start.40
  403.6 2.1 collective-permute-start.41
  407.3 9.5 %collective-permute-start.42 = (bf16[608,256]{1,0:T(8,128)(2,1)S(1)}, bf16[608,256]{1,0:T(8,128)(2,1)S(1)}, u32[]{:S(2)}, u32[]{:S(2)}) collective-permute-start(bf16[608,256]{1,0:T(8,128)(2,1)S(1)} %convolution_convert_fusion.5), channel_id=1, source_target_pairs={{0,1},{1,0},{2,3},{3,2},{4,5},{5,4},{6,7},{7,6},{8,9},{9,8},{10,11... | collective-permute-start | bytes 933896 | tf_op jit(solution)/shard_map/ppermute | solution.py:71
  416.9 14.5 %collective-permute-start.43 = (bf16[304,1024]{1,0:T(8,128)(2,1)S(1)}, bf16[304,1024]{1,0:T(8,128)(2,1)S(1)}, u32[]{:S(2)}, u32[]{:S(2)}) collective-permute-start(bf16[304,1024]{1,0:T(8,128)(2,1)S(1)} %get-tuple-element.87), channel_id=1, source_target_pairs={{0,16},{1,17},{16,18},{17,19},{4,20},{5,21},{20,22},{21,23},{8,24}... | collective-permute-start | bytes 1867784 | tf_op jit(solution)/shard_map/ppermute | solution.py:65
  418.2 13.2 %collective-permute-start.44 = (bf16[304,1024]{1,0:T(8,128)(2,1)S(1)}, bf16[304,1024]{1,0:T(8,128)(2,1)S(1)}, u32[]{:S(2)}, u32[]{:S(2)}) collective-permute-start(bf16[304,1024]{1,0:T(8,128)(2,1)S(1)} %get-tuple-element.87), channel_id=1, source_target_pairs={{2,16},{3,17},{18,18},{19,19},{6,20},{7,21},{22,22},{23,23},{10,24... | collective-permute-start | bytes 1867784 | tf_op jit(solution)/shard_map/ppermute | solution.py:65
  432.1 9.9 %collective-permute-start.46 = (bf16[304,1024]{1,0:T(8,128)(2,1)S(1)}, bf16[304,1024]{1,0:T(8,128)(2,1)S(1)}, u32[]{:S(2)}, u32[]{:S(2)}) collective-permute-start(bf16[304,1024]{1,0:T(8,128)(2,1)S(1)} %convolution_convert_fusion), channel_id=1, source_target_pairs={{0,16},{16,0},{1,17},{17,1},{2,18},{18,2},{3,19},{19,3},{4,20},{20... | collective-permute-start | bytes 1867784 | tf_op jit(solution)/shard_map/ppermute | solution.py:68
  437.8 5.7 %collective-permute-start.48 = (bf16[2,2,64,256]{3,2,1,0:T(8,128)(2,1)S(1)}, bf16[2,2,64,256]{3,2,1,0:T(8,128)(2,1)S(1)}, u32[]{:S(2)}, u32[]{:S(2)}) collective-permute-start(bf16[2,2,64,256]{3,2,1,0:T(8,128)(2,1)S(1)} %pad_maximum_fusion.14), channel_id=1, source_target_pairs={{0,4},{4,0},{8,12},{12,8},{1,5},{5,1},{9,13},{13,9},{2,6},{6,2},{1... | collective-permute-start | bytes 393224 | tf_op jit(solution)/shard_map/ppermute | solution.py:501
  439.6 8.0 %collective-permute-start.49 = (bf16[2,2,64,256]{3,2,1,0:T(8,128)(2,1)S(1)}, bf16[2,2,64,256]{3,2,1,0:T(8,128)(2,1)S(1)}, u32[]{:S(2)}, u32[]{:S(2)}) collective-permute-start(bf16[2,2,64,256]{3,2,1,0:T(8,128)(2,1)S(1)} %pad_maximum_fusion.14), channel_id=1, source_target_pairs={{0,8},{4,12},{8,0},{12,4},{1,9},{5,13},{9,1},{13,5},{2,10},{6,14},... | collective-permute-start | bytes 393224 | tf_op jit(solution)/shard_map/ppermute | solution.py:501
  439.9 7.7 %collective-permute-start.50 = (bf16[2,2,64,256]{3,2,1,0:T(8,128)(2,1)S(1)}, bf16[2,2,64,256]{3,2,1,0:T(8,128)(2,1)S(1)}, u32[]{:S(2)}, u32[]{:S(2)}) collective-permute-start(bf16[2,2,64,256]{3,2,1,0:T(8,128)(2,1)S(1)} %pad_maximum_fusion.14), channel_id=1, source_target_pairs={{0,12},{4,8},{8,4},{12,0},{1,13},{5,9},{9,5},{13,1},{2,14},{6,10},... | collective-permute-start | bytes 393224 | tf_op jit(solution)/shard_map/ppermute | solution.py:501
  442.0 20.1 %collective-permute-start.45 = (bf16[304,1024]{1,0:T(8,128)(2,1)S(1)}, bf16[304,1024]{1,0:T(8,128)(2,1)S(1)}, u32[]{:S(2)}, u32[]{:S(2)}) collective-permute-start(bf16[304,1024]{1,0:T(8,128)(2,1)S(1)} %convolution_convert_fusion.1), channel_id=1, source_target_pairs={{0,16},{16,0},{1,17},{17,1},{2,18},{18,2},{3,19},{19,3},{4,20},{20... | collective-permute-start | bytes 1867784 | tf_op jit(solution)/shard_map/ppermute | solution.py:68
  442.8 19.3 %collective-permute-start.47 = (bf16[304,1024]{1,0:T(8,128)(2,1)S(1)}, bf16[304,1024]{1,0:T(8,128)(2,1)S(1)}, u32[]{:S(2)}, u32[]{:S(2)}) collective-permute-start(bf16[304,1024]{1,0:T(8,128)(2,1)S(1)} %fusion.14), channel_id=1, source_target_pairs={{0,1},{1,0},{2,3},{3,2},{4,5},{5,4},{6,7},{7,6},{8,9},{9,8},{10,11... | collective-permute-start | bytes 1867784 | tf_op jit(solution)/shard_map/ppermute | solution.py:71
  447.6 2.4 collective-permute-start.51
  448.3 6.8 %collective-permute-start.52 = (f32[2,64,256]{2,1,0:T(8,128)S(1)}, f32[2,64,256]{2,1,0:T(8,128)S(1)}, u32[]{:S(2)}, u32[]{:S(2)}) collective-permute-start(f32[2,64,256]{2,1,0:T(8,128)S(1)} %get-tuple-element.143), channel_id=1, source_target_pairs={{0,16},{1,17},{2,0},{3,1},{16,18},{17,19},{18,2},{19,3},{4,20},{5,... | collective-permute-start | bytes 393224 | tf_op jit(solution)/shard_map/ppermute | solution.py:65
  462.9 3.9 collective-permute-start.53
  463.7 19.0 %collective-permute-start.54 = (bf16[304,1024]{1,0:T(8,128)(2,1)S(1)}, bf16[304,1024]{1,0:T(8,128)(2,1)S(1)}, u32[]{:S(2)}, u32[]{:S(2)}) collective-permute-start(bf16[304,1024]{1,0:T(8,128)(2,1)S(1)} %fusion.9), channel_id=1, source_target_pairs={{2,0},{3,1},{18,2},{19,3},{6,4},{7,5},{22,6},{23,7},{10,8},{11,9},... | collective-permute-start | bytes 1867784 | tf_op jit(solution)/shard_map/ppermute | solution.py:65
  (48 other events, 361.1 us)
Sparse Core Ops, SparseCore 0:
  27.1 39.9 all-gather.4
  69.5 57.6 all-gather.6
  129.1 78.8 all-gather.8
  209.7 87.6 all-gather.10

commit v7 on v6

--- a/solution.py
+++ b/solution.py
@@ -517,14 +517,18 @@
             sent.append(place.chip(summed.astype(BF), j))
     if kv is not None:
         kv = total_dp(kv)
-        first = place.m == 0
-        kv = place.send(jnp.where(first, kv[0], kv[1]), lambda c, m, p: (m, c, p)) + place.send(
-            jnp.where(first, kv[1], kv[0]), lambda c, m, p: (1 - m, c, p)
-        )
         sent = tie(sent, kv)
     for value in sent:
         total = total + value.astype(F32)
-    return total.astype(BF) if kv is None else (total.astype(BF), kv)
+    total = total.astype(BF)
+    if kv is None:
+        return total
+    first, kv = place.m == 0, tie(kv, total).astype(BF)
+    halves = (
+        place.send(jnp.where(first, kv[0], kv[1]), lambda c, m, p: (m, c, p)),
+        place.send(jnp.where(first, kv[1], kv[0]), lambda c, m, p: (1 - m, c, p)),
+    )
+    return total, halves[0].astype(F32) + halves[1].astype(F32)
 
 
 def on_device(
@@ -653,7 +657,9 @@
     back, kv0 = attend_back(*where, qkv0, lse0, o0, go, prefix, width // HD)
     back = tie(back, gouts)
     grad0, kv = input_back(place, order, da, back, w0, jnp.stack([kv0, kv1]))
-    gouts = [gouts[h] + home(grad0, 0, h) for h in range(2)]
+    mine = place.send(grad0, lambda c, m, p: (m, c, p))
+    grads0 = [mine, place.core(mine)]
+    gouts = [jnp.where(c == 0, grads0[h], gouts[h]) for h in range(2)]
     results = jnp.stack([results0[h] + results1[h] for h in range(2)])[:, :, None]
     gouts = jnp.stack(gouts)[:, :, None]
     return results[None], gouts[None], kv[None, 0], kv[None, 1]

time: 497 us -> 494 us (level)
  starting transfers between devices: 94.7 us -> 112 us
  waiting for transfers between devices: 219 us -> 202 us
    ppermute x20 -> x19, waiting for transfers between devices: 62 us -> 43.5 us  [send(): return lax.ppermute(value, ('section', 'mp'), pairs)]
    ppermute x21 -> x22, starting transfers between devices: 19.9 us -> 35 us  [core(): return lax.ppermute(value, 'section', [(0, 1), (1, 0)])]
    ppermute x20 -> x19, starting transfers between devices: 62.1 us -> 64 us  [send(): return lax.ppermute(value, ('section', 'mp'), pairs)]
    ppermute x21 -> x22, waiting for transfers between devices: 19.9 us -> 20.8 us  [core(): return lax.ppermute(value, 'section', [(0, 1), (1, 0)])]
  transfers between devices with their start and end apart: 59 -> 59, of which waited for: 36 -> 36; matrix products, arithmetic and copies ran while one was open for 9% -> 9% of each run, Pallas kernels for 12% -> 11%
where the time goes in v7:
time: 494 us; the launch traced here: 488 us
  waiting for transfers between devices  202 us (41%)
  starting transfers between devices  112 us (23%)
  Pallas kernels  83.1 us (17%)
  other arithmetic  30.5 us (6%)
  matrix products  24.4 us (5%)
  local copies, waits for them, and re-layouts  20.5 us (4%)
  between operations  15.7 us (3%)
    ppermute x11, waiting for transfers between devices, chip(): return lax.ppermute(value, 'mp', [(z, z ^ j) for z in range(self.mp)])  88.3 us
    ppermute x19, starting transfers between devices, send(): return lax.ppermute(value, ('section', 'mp'), pairs)  64 us
    ppermute x19, waiting for transfers between devices, send(): return lax.ppermute(value, ('section', 'mp'), pairs)  43.5 us
    all_gather x4, waiting for transfers between devices, gather(): return lax.all_gather(block, 'dp', axis=0, tiled=True)  43.1 us
    pallas_call x4, Pallas kernels, feed(): pl.pallas_call(lambda *refs: feed_kernel(mode, cuts, refs), grid=(at,), i...  41.7 us
    ppermute x22, starting transfers between devices, core(): return lax.ppermute(value, 'section', [(0, 1), (1, 0)])  35 us
    dot_general x28, matrix products, dot(): return lax.dot_general(a, b, (dims, ((), ())), preferred_element_type=F32)  24.4 us
    pallas_call x2, Pallas kernels, attend_back(): pl.pallas_call(partial(attn_bwd, prefix, heads), grid_spec=pltpu.Prefetch...  22.8 us
  transfers between devices with their start and end apart: 59, of which 36 were waited for; matrix products, arithmetic and copies ran while one was open for 9% of the time, Pallas kernels for 11%

profile of v7, /device:TPU:0, one launch (start us, length us, event | category | flops | bytes accessed | tf_op | source)
XLA Modules:
  0.0 487.9 jit_solution(8670758844137804702)
XLA Ops:
  11.1 7.4 %collective-permute-start.1 = (bf16[336,768]{1,0:T(8,128)(2,1)S(1)}, bf16[336,768]{1,0:T(8,128)(2,1)}, u32[]{:S(2)}, u32[]{:S(2)}) collective-permute-start(bf16[336,768]{1,0:T(8,128)(2,1)S(1)} %pad_maximum_fusion.10), channel_id=1, source_target_pairs={{0,2},{1,3},{2,18},{3,19},{4,6},{5,7},{6,22},{7,23},{8,10},{9,11},... | collective-permute-start | bytes 1548296 | tf_op jit(solution)/shard_map/ppermute | solution.py:65
  18.5 5.8 %collective-permute-done.1 = bf16[336,768]{1,0:T(8,128)(2,1)} collective-permute-done((bf16[336,768]{1,0:T(8,128)(2,1)S(1)}, bf16[336,768]{1,0:T(8,128)(2,1)}, u32[]{:S(2)}, u32[]{:S(2)}) %collective-permute-start.1) | collective-permute-done | bytes 516128 | tf_op jit(solution)/shard_map/ppermute | solution.py:65
  29.0 9.6 %collective-permute-start.3 = (bf16[272,2304]{1,0:T(8,128)(2,1)S(1)}, bf16[272,2304]{1,0:T(8,128)(2,1)S(1)}, u32[]{:S(2)}, u32[]{:S(2)}) collective-permute-start(bf16[272,2304]{1,0:T(8,128)(2,1)S(1)} %pad_maximum_fusion.2), channel_id=1, source_target_pairs={{0,2},{1,3},{2,18},{3,19},{4,6},{5,7},{6,22},{7,23},{8,10},{9,11},... | collective-permute-start | bytes 3760136 | tf_op jit(solution)/shard_map/ppermute | solution.py:65
  38.6 14.4 %collective-permute-done.3 = bf16[272,2304]{1,0:T(8,128)(2,1)S(1)} collective-permute-done((bf16[272,2304]{1,0:T(8,128)(2,1)S(1)}, bf16[272,2304]{1,0:T(8,128)(2,1)S(1)}, u32[]{:S(2)}, u32[]{:S(2)}) %collective-permute-start.3) | collective-permute-done | bytes 1253408 | tf_op jit(solution)/shard_map/ppermute | solution.py:65
  54.3 12.8 %all-gather.5.cloned.1.call-done = bf16[1024,768]{1,0:T(8,128)(2,1)} async-done(((bf16[256,768]{1,0:T(8,128)(2,1)}), bf16[1024,768]{1,0:T(8,128)(2,1)}) %all-gather.5.cloned.1.call-update) | async-done | bytes 1572880 | tf_op jit(solution)/shard_map/all_gather | solution.py:84
  69.4 2.0 collective-permute-done.4
  72.3 2.0 collective-permute-start.11
  75.5 21.9 %collective-permute-start.6 = (bf16[304,1024]{1,0:T(8,128)(2,1)S(1)}, bf16[304,1024]{1,0:T(8,128)(2,1)}, u32[]{:S(2)}, u32[]{:S(2)}) collective-permute-start(bf16[304,1024]{1,0:T(8,128)(2,1)S(1)} %dynamic-slice_bitcast_fusion.1), channel_id=1, source_target_pairs={{0,2},{1,3},{18,16},{19,17},{4,6},{5,7},{22,20},{23,21},{8,10},{9,... | collective-permute-start | bytes 1867784 | tf_op jit(solution)/shard_map/ppermute | solution.py:65
  98.3 12.6 %collective-permute-done.6 = bf16[304,1024]{1,0:T(8,128)(2,1)} collective-permute-done((bf16[304,1024]{1,0:T(8,128)(2,1)S(1)}, bf16[304,1024]{1,0:T(8,128)(2,1)}, u32[]{:S(2)}, u32[]{:S(2)}) %collective-permute-start.6) | collective-permute-done | bytes 622624 | tf_op jit(solution)/shard_map/ppermute | solution.py:65
  112.2 1.6 slice.300
  113.8 1.4 pad_maximum_fusion.1
  115.2 12.0 %all-gather.7.cloned.1.call-done.refs_0_.refs_1_ = bf16[1024,2304]{1,0:T(8,128)(2,1)} async-done(((bf16[256,2304]{1,0:T(8,128)(2,1)}), bf16[1024,2304]{1,0:T(8,128)(2,1)}) %all-gather.7.cloned.1.call-update) | async-done | bytes 4718608 | tf_op jit(solution)/shard_map/all_gather | solution.py:84
  127.9 1.5 collective-permute-start.8
  132.0 1.4 collective-permute-start.25
  133.4 2.3 collective-permute-start.26
  135.9 4.1 collective-permute-start.7
  140.0 10.9 %collective-permute-done.8 = bf16[304,1024]{1,0:T(8,128)(2,1)} collective-permute-done((bf16[304,1024]{1,0:T(8,128)(2,1)S(1)}, bf16[304,1024]{1,0:T(8,128)(2,1)}, u32[]{:S(2)}, u32[]{:S(2)}) %collective-permute-start.8) | collective-permute-done | bytes 622624 | tf_op jit(solution)/shard_map/ppermute | solution.py:71
  156.1 2.1 fusion.20
  158.9 9.3 %attend.2 = (bf16[1280,256]{1,0:T(8,128)(2,1)S(1)}, f32[4,1280]{1,0:T(4,128)S(1)}) custom-call(s32[10,2]{1,0:T(8,128)S(1)} %copy.78.range_ref, s32[2,1280]{1,0:T(2,128)S(1)} %pad_add_fusion.span_ref, bf16[1280,768]{1,0:T(8,128)(2,1)S(1)} %fusion.22.qkv_ref), custom_call_target="tpu_custom_call" | custom-call | flops 419430 | bytes 1 | tf_op jit(solution)/shard_map/attend/pallas_call | solution.py:265
  168.3 1.8 collective-permute-start.10
  170.0 19.4 %collective-permute-done.10 = bf16[608,256]{1,0:T(8,128)(2,1)S(1)} collective-permute-done((bf16[608,256]{1,0:T(8,128)(2,1)S(1)}, bf16[608,256]{1,0:T(8,128)(2,1)S(1)}, u32[]{:S(2)}, u32[]{:S(2)}) %collective-permute-start.10) | collective-permute-done | bytes 311328 | tf_op jit(solution)/shard_map/ppermute | solution.py:71
  190.4 1.6 pad_maximum_fusion
  192.0 16.0 %all-gather.9.cloned.1.call-done.refs_2_.refs_3_ = bf16[1024,3584]{1,0:T(8,128)(2,1)} async-done(((bf16[256,3584]{1,0:T(8,128)(2,1)}), bf16[1024,3584]{1,0:T(8,128)(2,1)}) %all-gather.9.cloned.1.call-update) | async-done | bytes 7340048 | tf_op jit(solution)/shard_map/all_gather | solution.py:84
  212.5 1.4 fusion.55
  214.3 1.7 fusion.140
  218.9 5.6 %collective-permute-start.16 = (bf16[304,1024]{1,0:T(8,128)(2,1)}, bf16[304,1024]{1,0:T(8,128)(2,1)}, u32[]{:S(2)}, u32[]{:S(2)}) collective-permute-start(bf16[304,1024]{1,0:T(8,128)(2,1)} %dynamic-slice_bitcast_fusion), channel_id=1, source_target_pairs={{0,2},{1,3},{18,16},{19,17},{4,6},{5,7},{22,20},{23,21},{8,10},{9,... | collective-permute-start | bytes 1867784 | tf_op jit(solution)/shard_map/ppermute | solution.py:65
  225.3 12.6 %feed_forward.2 = (f32[304,1024]{1,0:T(8,128)S(1)}, bf16[304,1024]{1,0:T(8,128)(2,1)S(1)}, bf16[608,2048]{1,0:T(8,128)(2,1)S(1)}) custom-call(bf16[1024,2304]{1,0:T(8,128)(2,1)} %all-gather.7.cloned.1.call-done.refs_0_.refs_1_, bf16[1024,2304]{1,0:T(8,128)(2,1)} %all-gather.7.cloned.1.call-done.refs_0_.refs_1_, ...), custom_call_target="tpu_custom_call" | custom-call | flops 1275068 | bytes 1 | tf_op jit(solution)/shard_map/feed_forward/pallas_call | solution.py:411
  241.7 1.4 collective-permute-start.19
  243.3 14.8 %collective-permute-done.19 = bf16[304,1024]{1,0:T(8,128)(2,1)S(1)} collective-permute-done((bf16[304,1024]{1,0:T(8,128)(2,1)S(1)}, bf16[304,1024]{1,0:T(8,128)(2,1)S(1)}, u32[]{:S(2)}, u32[]{:S(2)}) %collective-permute-start.19) | collective-permute-done | bytes 622624 | tf_op jit(solution)/shard_map/ppermute | solution.py:71
  260.8 1.5 collective-permute-start.22
  264.4 9.3 %attend.3 = (bf16[1280,256]{1,0:T(8,128)(2,1)S(1)}, f32[4,1280]{1,0:T(4,128)S(1)}) custom-call(s32[10,2]{1,0:T(8,128)S(1)} %copy.78.range_ref, s32[2,1280]{1,0:T(2,128)S(1)} %pad_add_fusion.span_ref, bf16[1280,768]{1,0:T(8,128)(2,1)S(1)} %fusion.30.qkv_ref), custom_call_target="tpu_custom_call" | custom-call | flops 419430 | bytes 1 | tf_op jit(solution)/shard_map/attend/pallas_call | solution.py:265
  273.7 6.9 %collective-permute-done.22 = bf16[304,1024]{1,0:T(8,128)(2,1)S(1)} collective-permute-done((bf16[304,1024]{1,0:T(8,128)(2,1)S(1)}, bf16[304,1024]{1,0:T(8,128)(2,1)S(1)}, u32[]{:S(2)}, u32[]{:S(2)}) %collective-permute-start.22) | collective-permute-done | bytes 622624 | tf_op jit(solution)/shard_map/ppermute | solution.py:65
  281.5 6.2 %collective-permute-done.23 = bf16[608,256]{1,0:T(8,128)(2,1)S(1)} collective-permute-done((bf16[608,256]{1,0:T(8,128)(2,1)S(1)}, bf16[608,256]{1,0:T(8,128)(2,1)S(1)}, u32[]{:S(2)}, u32[]{:S(2)}) %collective-permute-start.23) | collective-permute-done | bytes 311328 | tf_op jit(solution)/shard_map/ppermute | solution.py:71
  295.0 2.3 all-gather.11.cloned.1.call-done.refs_0_.refs_1_
  299.5 12.0 %feed_forward.3 = (f32[304,1024]{1,0:T(8,128)S(1)}, bf16[304,1024]{1,0:T(8,128)(2,1)S(1)}, bf16[608,2048]{1,0:T(8,128)(2,1)S(1)}) custom-call(bf16[1024,4096]{1,0:T(8,128)(2,1)} %all-gather.11.cloned.1.call-done.refs_0_.refs_1_, bf16[1024,4096]{1,0:T(8,128)(2,1)} %all-gather.11.cloned.1.call-done.refs_0_.refs_1_, bf16[304,1024]{1,0:T(8,128)(2,1)S(1)} %copy-done.3, ...), custom_call_target="tpu_custom_call" | custom-call | flops 1275068 | bytes 1 | tf_op jit(solution)/shard_map/feed_forward/pallas_call | solution.py:411
  311.6 2.0 collective-permute-done.29
  316.8 1.9 collective-permute-done.30.refs_3_
  318.8 8.1 %feed_back.2 = (f32[304,1024]{1,0:T(8,128)S(1)}, bf16[304,1024]{1,0:T(8,128)(2,1)S(1)}) custom-call(bf16[1024,4096]{1,0:T(8,128)(2,1)} %all-gather.11.cloned.1.call-done.refs_0_.refs_1_, bf16[1024,4096]{1,0:T(8,128)(2,1)} %all-gather.11.cloned.1.call-done.refs_0_.refs_1_, bf16[304,1024]{1,0:T(8,128)(2,1)S(1)} %fusion.125.refs_2_, ...), custom_call_target="tpu_custom_call" | custom-call | flops 1275068 | bytes 1 | tf_op jit(solution)/shard_map/feed_back/pallas_call | solution.py:411
  327.1 1.9 collective-permute-done.31
  329.0 3.0 fusion.128
  332.1 1.4 fusion.130
  333.6 1.9 collective-permute-done.32
  336.0 1.6 collective-permute-start.33
  338.1 7.4 %collective-permute-done.33 = bf16[608,256]{1,0:T(8,128)(2,1)S(1)} collective-permute-done((bf16[608,256]{1,0:T(8,128)(2,1)S(1)}, bf16[608,256]{1,0:T(8,128)(2,1)S(1)}, u32[]{:S(2)}, u32[]{:S(2)}) %collective-permute-start.33) | collective-permute-done | bytes 311328 | tf_op jit(solution)/shard_map/ppermute | solution.py:71
  347.7 11.3 %attend_back.2 = (bf16[1280,768]{1,0:T(8,128)(2,1)S(1)}, f32[2,64,256]{2,1,0:T(8,128)S(1)}) custom-call(s32[10,2]{1,0:T(8,128)S(1)} %copy.78.range_ref, s32[2,1280]{1,0:T(2,128)S(1)} %pad_add_fusion.span_ref, bf16[1280,768]{1,0:T(8,128)(2,1)S(1)} %fusion.30.qkv_ref, f32[4,1280]{1,0:T(4,128)S(1)} %get-tuple-element.82.lse_ref, ...), custom_call_target="tpu_custom_call" | custom-call | flops 1048576 | bytes 1 | tf_op jit(solution)/shard_map/attend_back/pallas_call | solution.py:280
  360.1 8.9 %collective-permute-start.37 = (bf16[304,1024]{1,0:T(8,128)(2,1)S(1)}, bf16[304,1024]{1,0:T(8,128)(2,1)S(1)}, u32[]{:S(2)}, u32[]{:S(2)}) collective-permute-start(bf16[304,1024]{1,0:T(8,128)(2,1)S(1)} %convolution_convert_fusion.2), channel_id=1, source_target_pairs={{0,16},{16,0},{1,17},{17,1},{2,18},{18,2},{3,19},{19,3},{4,20},{20... | collective-permute-start | bytes 1867784 | tf_op jit(solution)/shard_map/ppermute | solution.py:68
  371.8 15.9 %collective-permute-done.38 = bf16[304,1024]{1,0:T(8,128)(2,1)S(1)} collective-permute-done((bf16[304,1024]{1,0:T(8,128)(2,1)S(1)}, bf16[304,1024]{1,0:T(8,128)(2,1)S(1)}, u32[]{:S(2)}, u32[]{:S(2)}) %collective-permute-start.38) | collective-permute-done | bytes 622624 | tf_op jit(solution)/shard_map/ppermute | solution.py:71
  389.3 2.0 collective-permute-done.39.refs_5_
  391.4 8.9 %feed_back.3 = (f32[304,1024]{1,0:T(8,128)S(1)}, bf16[304,1024]{1,0:T(8,128)(2,1)S(1)}) custom-call(bf16[1024,2304]{1,0:T(8,128)(2,1)} %all-gather.7.cloned.1.call-done.refs_0_.refs_1_, bf16[1024,2304]{1,0:T(8,128)(2,1)} %all-gather.7.cloned.1.call-done.refs_0_.refs_1_, bf16[1024,3584]{1,0:T(8,128)(2,1)} %all-gather.9.cloned.1.call-done.refs_2_.refs_3_, ...), custom_call_target="tpu_custom_call" | custom-call | flops 1275068 | bytes 1 | tf_op jit(solution)/shard_map/feed_back/pallas_call | solution.py:411
  400.5 1.9 collective-permute-done.40
  404.0 1.9 collective-permute-done.41
  406.0 1.5 convolution_convert_fusion.5
  407.9 1.7 convolution_convert_fusion.4
  409.5 7.4 %collective-permute-done.42 = bf16[608,256]{1,0:T(8,128)(2,1)S(1)} collective-permute-done((bf16[608,256]{1,0:T(8,128)(2,1)S(1)}, bf16[608,256]{1,0:T(8,128)(2,1)S(1)}, u32[]{:S(2)}, u32[]{:S(2)}) %collective-permute-start.42) | collective-permute-done | bytes 311328 | tf_op jit(solution)/shard_map/ppermute | solution.py:71
  419.2 11.5 %attend_back.3 = (bf16[1280,768]{1,0:T(8,128)(2,1)S(1)}, f32[2,64,256]{2,1,0:T(8,128)S(1)}) custom-call(s32[10,2]{1,0:T(8,128)S(1)} %copy.78.range_ref, s32[2,1280]{1,0:T(2,128)S(1)} %pad_add_fusion.span_ref, bf16[1280,768]{1,0:T(8,128)(2,1)S(1)} %copy-done.1, f32[4,1280]{1,0:T(4,128)S(1)} %get-tuple-element.88.lse_ref, ...), custom_call_target="tpu_custom_call" | custom-call | flops 1048576 | bytes 1 | tf_op jit(solution)/shard_map/attend_back/pallas_call | solution.py:280
  431.4 6.5 %collective-permute-start.46 = (bf16[304,1024]{1,0:T(8,128)(2,1)S(1)}, bf16[304,1024]{1,0:T(8,128)(2,1)S(1)}, u32[]{:S(2)}, u32[]{:S(2)}) collective-permute-start(bf16[304,1024]{1,0:T(8,128)(2,1)S(1)} %convolution_convert_fusion), channel_id=1, source_target_pairs={{0,16},{16,0},{1,17},{17,1},{2,18},{18,2},{3,19},{19,3},{4,20},{20... | collective-permute-start | bytes 1867784 | tf_op jit(solution)/shard_map/ppermute | solution.py:68
  440.4 1.7 collective-permute-start.48
  442.5 1.5 collective-permute-start.50
  444.1 2.4 collective-permute-done.48
  446.4 4.0 collective-permute-done.49
  450.5 6.2 %collective-permute-done.47 = bf16[304,1024]{1,0:T(8,128)(2,1)S(1)} collective-permute-done((bf16[304,1024]{1,0:T(8,128)(2,1)S(1)}, bf16[304,1024]{1,0:T(8,128)(2,1)S(1)}, u32[]{:S(2)}, u32[]{:S(2)}) %collective-permute-start.47) | collective-permute-done | bytes 622624 | tf_op jit(solution)/shard_map/ppermute | solution.py:71
  459.0 4.7 collective-permute-start.54
  464.8 12.7 %collective-permute-start.52 = (bf16[304,1024]{1,0:T(8,128)(2,1)S(1)}, bf16[304,1024]{1,0:T(8,128)(2,1)S(1)}, u32[]{:S(2)}, u32[]{:S(2)}) collective-permute-start(bf16[304,1024]{1,0:T(8,128)(2,1)S(1)} %collective-permute-done.51), channel_id=1, source_target_pairs={{0,16},{16,0},{1,17},{17,1},{2,18},{18,2},{3,19},{19,3},{4,20},{20... | collective-permute-start | bytes 1867784 | tf_op jit(solution)/shard_map/ppermute | solution.py:68
  477.6 1.6 collective-permute-done.54
  (333 shorter events, 78.9 us)
Async XLA Ops:
  7.2 59.9 %all-gather.5.cloned.1.call-start = ((), (), s32[]{:S(2)}) async-start(), calls=%async_computation | async-start | bytes 1966080 | tf_op jit(solution)/shard_map/all_gather | solution.py:84
  10.3 8.2 %collective-permute-start = (bf16[336,768]{1,0:T(8,128)(2,1)S(1)}, bf16[336,768]{1,0:T(8,128)(2,1)S(1)}, u32[]{:S(2)}, u32[]{:S(2)}) collective-permute-start(bf16[336,768]{1,0:T(8,128)(2,1)S(1)} %pad_maximum_fusion.10), channel_id=1, source_target_pairs={{0,0},{1,1},{2,16},{3,17},{4,4},{5,5},{6,20},{7,21},{8,8},{9,9},{1... | collective-permute-start | bytes 1548296 | tf_op jit(solution)/shard_map/ppermute | solution.py:65
  11.1 13.2 %collective-permute-start.1 = (bf16[336,768]{1,0:T(8,128)(2,1)S(1)}, bf16[336,768]{1,0:T(8,128)(2,1)}, u32[]{:S(2)}, u32[]{:S(2)}) collective-permute-start(bf16[336,768]{1,0:T(8,128)(2,1)S(1)} %pad_maximum_fusion.10), channel_id=1, source_target_pairs={{0,2},{1,3},{2,18},{3,19},{4,6},{5,7},{6,22},{7,23},{8,10},{9,11},... | collective-permute-start | bytes 1548296 | tf_op jit(solution)/shard_map/ppermute | solution.py:65
  27.0 100.2 %all-gather.7.cloned.1.call-start = ((), (), s32[]{:S(2)}) async-start(), calls=%async_computation.1 | async-start | bytes 5898240 | tf_op jit(solution)/shard_map/all_gather | solution.py:84
  28.2 10.3 %collective-permute-start.2 = (bf16[272,2304]{1,0:T(8,128)(2,1)S(1)}, bf16[272,2304]{1,0:T(8,128)(2,1)S(1)}, u32[]{:S(2)}, u32[]{:S(2)}) collective-permute-start(bf16[272,2304]{1,0:T(8,128)(2,1)S(1)} %pad_maximum_fusion.2), channel_id=1, source_target_pairs={{0,0},{1,1},{2,16},{3,17},{4,4},{5,5},{6,20},{7,21},{8,8},{9,9},{1... | collective-permute-start | bytes 3760136 | tf_op jit(solution)/shard_map/ppermute | solution.py:65
  29.0 24.0 %collective-permute-start.3 = (bf16[272,2304]{1,0:T(8,128)(2,1)S(1)}, bf16[272,2304]{1,0:T(8,128)(2,1)S(1)}, u32[]{:S(2)}, u32[]{:S(2)}) collective-permute-start(bf16[272,2304]{1,0:T(8,128)(2,1)S(1)} %pad_maximum_fusion.2), channel_id=1, source_target_pairs={{0,2},{1,3},{2,18},{3,19},{4,6},{5,7},{6,22},{7,23},{8,10},{9,11},... | collective-permute-start | bytes 3760136 | tf_op jit(solution)/shard_map/ppermute | solution.py:65
  67.1 140.9 %all-gather.9.cloned.1.call-start = ((), (), s32[]{:S(2)}) async-start(), calls=%async_computation.2 | async-start | bytes 9175040 | tf_op jit(solution)/shard_map/all_gather | solution.py:84
  67.3 4.0 collective-permute-start.4
  68.6 2.7 collective-permute-start.5
  72.3 39.8 %collective-permute-start.11 = (bf16[272,2304]{1,0:T(8,128)(2,1)S(1)}, bf16[272,2304]{1,0:T(8,128)(2,1)}, u32[]{:S(2)}, u32[]{:S(2)}) collective-permute-start(bf16[272,2304]{1,0:T(8,128)(2,1)S(1)} %broadcast_select_fusion), channel_id=1, source_target_pairs={{0,1},{1,0},{2,3},{3,2},{4,5},{5,4},{6,7},{7,6},{8,9},{9,8},{10,11... | collective-permute-start | bytes 3760136 | tf_op jit(solution)/shard_map/ppermute | solution.py:71
  75.5 35.5 %collective-permute-start.6 = (bf16[304,1024]{1,0:T(8,128)(2,1)S(1)}, bf16[304,1024]{1,0:T(8,128)(2,1)}, u32[]{:S(2)}, u32[]{:S(2)}) collective-permute-start(bf16[304,1024]{1,0:T(8,128)(2,1)S(1)} %dynamic-slice_bitcast_fusion.1), channel_id=1, source_target_pairs={{0,2},{1,3},{18,16},{19,17},{4,6},{5,7},{22,20},{23,21},{8,10},{9,... | collective-permute-start | bytes 1867784 | tf_op jit(solution)/shard_map/ppermute | solution.py:65
  98.3 15.5 %collective-permute-start.12 = (bf16[256,256]{1,0:T(8,128)(2,1)S(1)}, bf16[256,256]{1,0:T(8,128)(2,1)S(1)}, u32[]{:S(2)}, u32[]{:S(2)}) collective-permute-start(bf16[256,256]{1,0:T(8,128)(2,1)S(1)} %slice.302), channel_id=1, source_target_pairs={{0,1},{1,0},{2,3},{3,2},{4,5},{5,4},{6,7},{7,6},{8,9},{9,8},{10,11... | collective-permute-start | bytes 393224 | tf_op jit(solution)/shard_map/ppermute | solution.py:71
  112.1 41.1 %copy-start.21 = (bf16[304,1024]{1,0:T(8,128)(2,1)}, bf16[304,1024]{1,0:T(8,128)(2,1)S(1)}, u32[]{:S(2)}) copy-start(bf16[304,1024]{1,0:T(8,128)(2,1)S(1)} %bitcast_select_fusion.1) | copy-start | bytes 1867780
  127.2 170.1 %all-gather.11.cloned.1.call-start = ((), (), s32[]{:S(2)}) async-start(), calls=%async_computation.3 | async-start | bytes 10485760 | tf_op jit(solution)/shard_map/all_gather | solution.py:84
  127.9 23.1 %collective-permute-start.8 = (bf16[304,1024]{1,0:T(8,128)(2,1)S(1)}, bf16[304,1024]{1,0:T(8,128)(2,1)}, u32[]{:S(2)}, u32[]{:S(2)}) collective-permute-start(bf16[304,1024]{1,0:T(8,128)(2,1)S(1)} %bitcast_select_fusion.1), channel_id=1, source_target_pairs={{0,1},{1,0},{2,3},{3,2},{4,5},{5,4},{6,7},{7,6},{8,9},{9,8},{10,11... | collective-permute-start | bytes 1867784 | tf_op jit(solution)/shard_map/ppermute | solution.py:71
  132.0 22.6 %collective-permute-start.25 = (bf16[272,2048]{1,0:T(8,128)(2,1)}, bf16[272,2048]{1,0:T(8,128)(2,1)}, u32[]{:S(2)}, u32[]{:S(2)}) collective-permute-start(bf16[272,2048]{1,0:T(8,128)(2,1)} %pad_maximum_fusion.5), channel_id=1, source_target_pairs={{16,0},{17,1},{18,16},{19,17},{20,4},{21,5},{22,20},{23,21},{24,8}... | collective-permute-start | bytes 3342344 | tf_op jit(solution)/shard_map/ppermute | solution.py:65
  133.4 21.2 %collective-permute-start.26 = (bf16[272,2048]{1,0:T(8,128)(2,1)}, bf16[272,2048]{1,0:T(8,128)(2,1)}, u32[]{:S(2)}, u32[]{:S(2)}) collective-permute-start(bf16[272,2048]{1,0:T(8,128)(2,1)} %pad_maximum_fusion.5), channel_id=1, source_target_pairs={{16,2},{17,3},{18,18},{19,19},{20,6},{21,7},{22,22},{23,23},{24,10... | collective-permute-start | bytes 3342344 | tf_op jit(solution)/shard_map/ppermute | solution.py:65
  135.9 18.0 %collective-permute-start.7 = (bf16[304,1024]{1,0:T(8,128)(2,1)S(1)}, bf16[304,1024]{1,0:T(8,128)(2,1)S(1)}, u32[]{:S(2)}, u32[]{:S(2)}) collective-permute-start(bf16[304,1024]{1,0:T(8,128)(2,1)S(1)} %bitcast_select_fusion.1), channel_id=1, source_target_pairs={{0,16},{16,0},{1,17},{17,1},{2,18},{18,2},{3,19},{19,3},{4,20},{20... | collective-permute-start | bytes 1867784 | tf_op jit(solution)/shard_map/ppermute | solution.py:68
  150.9 3.7 collective-permute-start.9
  156.0 33.4 %copy-start.17 = (bf16[272,2048]{1,0:T(8,128)(2,1)}, bf16[272,2048]{1,0:T(8,128)(2,1)S(1)}, u32[]{:S(2)}) copy-start(bf16[272,2048]{1,0:T(8,128)(2,1)S(1)} %broadcast_select_fusion.1) | copy-start | bytes 3342340
  156.0 33.4 %collective-permute-start.27 = (bf16[272,2048]{1,0:T(8,128)(2,1)S(1)}, bf16[272,2048]{1,0:T(8,128)(2,1)S(1)}, u32[]{:S(2)}, u32[]{:S(2)}) collective-permute-start(bf16[272,2048]{1,0:T(8,128)(2,1)S(1)} %broadcast_select_fusion.1), channel_id=1, source_target_pairs={{0,1},{1,0},{2,3},{3,2},{4,5},{5,4},{6,7},{7,6},{8,9},{9,8},{10,11... | collective-permute-start | bytes 3342344 | tf_op jit(solution)/shard_map/ppermute | solution.py:71
  168.3 21.2 %collective-permute-start.10 = (bf16[608,256]{1,0:T(8,128)(2,1)S(1)}, bf16[608,256]{1,0:T(8,128)(2,1)S(1)}, u32[]{:S(2)}, u32[]{:S(2)}) collective-permute-start(bf16[608,256]{1,0:T(8,128)(2,1)S(1)} %pad_maximum_fusion.11), channel_id=1, source_target_pairs={{0,1},{1,0},{2,3},{3,2},{4,5},{5,4},{6,7},{7,6},{8,9},{9,8},{10,11... | collective-permute-start | bytes 933896 | tf_op jit(solution)/shard_map/ppermute | solution.py:71
  208.1 1.3 collective-permute-start.14
  212.2 2.1 collective-permute-start.13
  216.0 24.1 %copy-start.8 = (f32[304,1024]{1,0:T(8,128)}, f32[304,1024]{1,0:T(8,128)S(1)}, u32[]{:S(2)}) copy-start(f32[304,1024]{1,0:T(8,128)S(1)} %get-tuple-element.170) | copy-start | bytes 3735556
  216.6 8.7 %collective-permute-start.15 = (bf16[304,1024]{1,0:T(8,128)(2,1)S(1)}, bf16[304,1024]{1,0:T(8,128)(2,1)S(1)}, u32[]{:S(2)}, u32[]{:S(2)}) collective-permute-start(bf16[304,1024]{1,0:T(8,128)(2,1)S(1)} %fusion.33.refs_4_), channel_id=1, source_target_pairs={{0,16},{16,0},{1,17},{17,1},{2,18},{18,2},{3,19},{19,3},{4,20},{20... | collective-permute-start | bytes 1867784 | tf_op jit(solution)/shard_map/ppermute | solution.py:68
  218.0 40.2 %slice-start = ((s8[7340032]{0:T(1024)(128)(4,1)}), s8[4194304]{0:T(1024)(128)(4,1)S(1)}, s32[]{:S(2)}) async-start(s8[7340032]{0:T(1024)(128)(4,1)} %bitcast.135), calls=%async_computation.4 | async-start | bytes 8388608
  218.9 19.1 %collective-permute-start.16 = (bf16[304,1024]{1,0:T(8,128)(2,1)}, bf16[304,1024]{1,0:T(8,128)(2,1)}, u32[]{:S(2)}, u32[]{:S(2)}) collective-permute-start(bf16[304,1024]{1,0:T(8,128)(2,1)} %dynamic-slice_bitcast_fusion), channel_id=1, source_target_pairs={{0,2},{1,3},{18,16},{19,17},{4,6},{5,7},{22,20},{23,21},{8,10},{9,... | collective-permute-start | bytes 1867784 | tf_op jit(solution)/shard_map/ppermute | solution.py:65
  225.3 33.0 %slice-start.1 = ((s8[7340032]{0:T(1024)(128)(4,1)}), s8[3145728]{0:T(1024)(128)(4,1)S(1)}, s32[]{:S(2)}) async-start(s8[7340032]{0:T(1024)(128)(4,1)} %bitcast.135), calls=%async_computation.5 | async-start | bytes 6291456
  237.9 2.1 collective-permute-start.17
  241.7 16.4 %collective-permute-start.19 = (bf16[304,1024]{1,0:T(8,128)(2,1)S(1)}, bf16[304,1024]{1,0:T(8,128)(2,1)S(1)}, u32[]{:S(2)}, u32[]{:S(2)}) collective-permute-start(bf16[304,1024]{1,0:T(8,128)(2,1)S(1)} %add_convert_fusion.1), channel_id=1, source_target_pairs={{0,1},{1,0},{2,3},{3,2},{4,5},{5,4},{6,7},{7,6},{8,9},{9,8},{10,11... | collective-permute-start | bytes 1867784 | tf_op jit(solution)/shard_map/ppermute | solution.py:71
  243.1 15.8 %collective-permute-start.18 = (bf16[304,1024]{1,0:T(8,128)(2,1)S(1)}, bf16[304,1024]{1,0:T(8,128)(2,1)S(1)}, u32[]{:S(2)}, u32[]{:S(2)}) collective-permute-start(bf16[304,1024]{1,0:T(8,128)(2,1)S(1)} %add_convert_fusion.1), channel_id=1, source_target_pairs={{0,16},{16,0},{1,17},{17,1},{2,18},{18,2},{3,19},{19,3},{4,20},{20... | collective-permute-start | bytes 1867784 | tf_op jit(solution)/shard_map/ppermute | solution.py:68
  258.1 2.1 collective-permute-start.20
  260.1 13.5 %collective-permute-start.21 = (bf16[304,1024]{1,0:T(8,128)(2,1)S(1)}, bf16[304,1024]{1,0:T(8,128)(2,1)S(1)}, u32[]{:S(2)}, u32[]{:S(2)}) collective-permute-start(bf16[304,1024]{1,0:T(8,128)(2,1)S(1)} %add_convert_fusion.1), channel_id=1, source_target_pairs={{0,0},{1,1},{16,2},{17,3},{4,4},{5,5},{20,6},{21,7},{8,8},{9,9},{2... | collective-permute-start | bytes 1867784 | tf_op jit(solution)/shard_map/ppermute | solution.py:65
  260.8 19.8 %collective-permute-start.22 = (bf16[304,1024]{1,0:T(8,128)(2,1)S(1)}, bf16[304,1024]{1,0:T(8,128)(2,1)S(1)}, u32[]{:S(2)}, u32[]{:S(2)}) collective-permute-start(bf16[304,1024]{1,0:T(8,128)(2,1)S(1)} %add_convert_fusion.1), channel_id=1, source_target_pairs={{2,0},{3,1},{18,2},{19,3},{6,4},{7,5},{22,6},{23,7},{10,8},{11,9},... | collective-permute-start | bytes 1867784 | tf_op jit(solution)/shard_map/ppermute | solution.py:65
  280.7 7.0 %collective-permute-start.23 = (bf16[608,256]{1,0:T(8,128)(2,1)S(1)}, bf16[608,256]{1,0:T(8,128)(2,1)S(1)}, u32[]{:S(2)}, u32[]{:S(2)}) collective-permute-start(bf16[608,256]{1,0:T(8,128)(2,1)S(1)} %pad_maximum_fusion.13), channel_id=1, source_target_pairs={{0,1},{1,0},{2,3},{3,2},{4,5},{5,4},{6,7},{7,6},{8,9},{9,8},{10,11... | collective-permute-start | bytes 933896 | tf_op jit(solution)/shard_map/ppermute | solution.py:71
  288.4 2.1 collective-permute-start.24
  292.2 2.1 collective-permute-start.28
  311.5 2.1 collective-permute-start.29
  316.6 2.1 collective-permute-start.30
  326.9 2.1 collective-permute-start.31
  333.5 2.1 collective-permute-start.32
  336.0 9.5 %collective-permute-start.33 = (bf16[608,256]{1,0:T(8,128)(2,1)S(1)}, bf16[608,256]{1,0:T(8,128)(2,1)S(1)}, u32[]{:S(2)}, u32[]{:S(2)}) collective-permute-start(bf16[608,256]{1,0:T(8,128)(2,1)S(1)} %convolution_convert_fusion.7), channel_id=1, source_target_pairs={{0,1},{1,0},{2,3},{3,2},{4,5},{5,4},{6,7},{7,6},{8,9},{9,8},{10,11... | collective-permute-start | bytes 933896 | tf_op jit(solution)/shard_map/ppermute | solution.py:71
  345.6 13.4 %collective-permute-start.34 = (bf16[304,1024]{1,0:T(8,128)(2,1)S(1)}, bf16[304,1024]{1,0:T(8,128)(2,1)S(1)}, u32[]{:S(2)}, u32[]{:S(2)}) collective-permute-start(bf16[304,1024]{1,0:T(8,128)(2,1)S(1)} %get-tuple-element.81), channel_id=1, source_target_pairs={{0,16},{1,17},{16,18},{17,19},{4,20},{5,21},{20,22},{21,23},{8,24}... | collective-permute-start | bytes 1867784 | tf_op jit(solution)/shard_map/ppermute | solution.py:65
  347.0 12.0 %collective-permute-start.35 = (bf16[304,1024]{1,0:T(8,128)(2,1)S(1)}, bf16[304,1024]{1,0:T(8,128)(2,1)S(1)}, u32[]{:S(2)}, u32[]{:S(2)}) collective-permute-start(bf16[304,1024]{1,0:T(8,128)(2,1)S(1)} %get-tuple-element.81), channel_id=1, source_target_pairs={{2,16},{3,17},{18,18},{19,19},{6,20},{7,21},{22,22},{23,23},{10,24... | collective-permute-start | bytes 1867784 | tf_op jit(solution)/shard_map/ppermute | solution.py:65
  360.1 10.6 %collective-permute-start.37 = (bf16[304,1024]{1,0:T(8,128)(2,1)S(1)}, bf16[304,1024]{1,0:T(8,128)(2,1)S(1)}, u32[]{:S(2)}, u32[]{:S(2)}) collective-permute-start(bf16[304,1024]{1,0:T(8,128)(2,1)S(1)} %convolution_convert_fusion.2), channel_id=1, source_target_pairs={{0,16},{16,0},{1,17},{17,1},{2,18},{18,2},{3,19},{19,3},{4,20},{20... | collective-permute-start | bytes 1867784 | tf_op jit(solution)/shard_map/ppermute | solution.py:68
  369.7 2.1 collective-permute-start.36
  371.3 16.4 %collective-permute-start.38 = (bf16[304,1024]{1,0:T(8,128)(2,1)S(1)}, bf16[304,1024]{1,0:T(8,128)(2,1)S(1)}, u32[]{:S(2)}, u32[]{:S(2)}) collective-permute-start(bf16[304,1024]{1,0:T(8,128)(2,1)S(1)} %fusion.13), channel_id=1, source_target_pairs={{0,1},{1,0},{2,3},{3,2},{4,5},{5,4},{6,7},{7,6},{8,9},{9,8},{10,11... | collective-permute-start | bytes 1867784 | tf_op jit(solution)/shard_map/ppermute | solution.py:71
  389.3 2.1 collective-permute-start.39
  400.3 2.1 collective-permute-start.40
  403.8 2.1 collective-permute-start.41
  407.5 9.5 %collective-permute-start.42 = (bf16[608,256]{1,0:T(8,128)(2,1)S(1)}, bf16[608,256]{1,0:T(8,128)(2,1)S(1)}, u32[]{:S(2)}, u32[]{:S(2)}) collective-permute-start(bf16[608,256]{1,0:T(8,128)(2,1)S(1)} %convolution_convert_fusion.5), channel_id=1, source_target_pairs={{0,1},{1,0},{2,3},{3,2},{4,5},{5,4},{6,7},{7,6},{8,9},{9,8},{10,11... | collective-permute-start | bytes 933896 | tf_op jit(solution)/shard_map/ppermute | solution.py:71
  417.1 13.6 %collective-permute-start.43 = (bf16[304,1024]{1,0:T(8,128)(2,1)S(1)}, bf16[304,1024]{1,0:T(8,128)(2,1)S(1)}, u32[]{:S(2)}, u32[]{:S(2)}) collective-permute-start(bf16[304,1024]{1,0:T(8,128)(2,1)S(1)} %get-tuple-element.90), channel_id=1, source_target_pairs={{0,16},{1,17},{16,18},{17,19},{4,20},{5,21},{20,22},{21,23},{8,24}... | collective-permute-start | bytes 1867784 | tf_op jit(solution)/shard_map/ppermute | solution.py:65
  418.4 12.3 %collective-permute-start.44 = (bf16[304,1024]{1,0:T(8,128)(2,1)S(1)}, bf16[304,1024]{1,0:T(8,128)(2,1)S(1)}, u32[]{:S(2)}, u32[]{:S(2)}) collective-permute-start(bf16[304,1024]{1,0:T(8,128)(2,1)S(1)} %get-tuple-element.90), channel_id=1, source_target_pairs={{2,16},{3,17},{18,18},{19,19},{6,20},{7,21},{22,22},{23,23},{10,24... | collective-permute-start | bytes 1867784 | tf_op jit(solution)/shard_map/ppermute | solution.py:65
  431.4 8.2 %collective-permute-start.46 = (bf16[304,1024]{1,0:T(8,128)(2,1)S(1)}, bf16[304,1024]{1,0:T(8,128)(2,1)S(1)}, u32[]{:S(2)}, u32[]{:S(2)}) collective-permute-start(bf16[304,1024]{1,0:T(8,128)(2,1)S(1)} %convolution_convert_fusion), channel_id=1, source_target_pairs={{0,16},{16,0},{1,17},{17,1},{2,18},{18,2},{3,19},{19,3},{4,20},{20... | collective-permute-start | bytes 1867784 | tf_op jit(solution)/shard_map/ppermute | solution.py:68
  438.7 18.0 %collective-permute-start.45 = (bf16[304,1024]{1,0:T(8,128)(2,1)S(1)}, bf16[304,1024]{1,0:T(8,128)(2,1)S(1)}, u32[]{:S(2)}, u32[]{:S(2)}) collective-permute-start(bf16[304,1024]{1,0:T(8,128)(2,1)S(1)} %convolution_convert_fusion.1), channel_id=1, source_target_pairs={{0,16},{16,0},{1,17},{17,1},{2,18},{18,2},{3,19},{19,3},{4,20},{20... | collective-permute-start | bytes 1867784 | tf_op jit(solution)/shard_map/ppermute | solution.py:68
  440.3 16.4 %collective-permute-start.47 = (bf16[304,1024]{1,0:T(8,128)(2,1)S(1)}, bf16[304,1024]{1,0:T(8,128)(2,1)S(1)}, u32[]{:S(2)}, u32[]{:S(2)}) collective-permute-start(bf16[304,1024]{1,0:T(8,128)(2,1)S(1)} %fusion.14), channel_id=1, source_target_pairs={{0,1},{1,0},{2,3},{3,2},{4,5},{5,4},{6,7},{7,6},{8,9},{9,8},{10,11... | collective-permute-start | bytes 1867784 | tf_op jit(solution)/shard_map/ppermute | solution.py:71
  440.4 6.0 %collective-permute-start.48 = (bf16[2,2,64,256]{3,2,1,0:T(8,128)(2,1)S(1)}, bf16[2,2,64,256]{3,2,1,0:T(8,128)(2,1)S(1)}, u32[]{:S(2)}, u32[]{:S(2)}) collective-permute-start(bf16[2,2,64,256]{3,2,1,0:T(8,128)(2,1)S(1)} %pad_maximum_fusion.14), channel_id=1, source_target_pairs={{0,4},{4,0},{8,12},{12,8},{1,5},{5,1},{9,13},{13,9},{2,6},{6,2},{1... | collective-permute-start | bytes 393224 | tf_op jit(solution)/shard_map/ppermute | solution.py:501
  442.2 8.3 %collective-permute-start.49 = (bf16[2,2,64,256]{3,2,1,0:T(8,128)(2,1)S(1)}, bf16[2,2,64,256]{3,2,1,0:T(8,128)(2,1)S(1)}, u32[]{:S(2)}, u32[]{:S(2)}) collective-permute-start(bf16[2,2,64,256]{3,2,1,0:T(8,128)(2,1)S(1)} %pad_maximum_fusion.14), channel_id=1, source_target_pairs={{0,8},{4,12},{8,0},{12,4},{1,9},{5,13},{9,1},{13,5},{2,10},{6,14},... | collective-permute-start | bytes 393224 | tf_op jit(solution)/shard_map/ppermute | solution.py:501
  442.5 7.9 %collective-permute-start.50 = (bf16[2,2,64,256]{3,2,1,0:T(8,128)(2,1)S(1)}, bf16[2,2,64,256]{3,2,1,0:T(8,128)(2,1)S(1)}, u32[]{:S(2)}, u32[]{:S(2)}) collective-permute-start(bf16[2,2,64,256]{3,2,1,0:T(8,128)(2,1)S(1)} %pad_maximum_fusion.14), channel_id=1, source_target_pairs={{0,12},{4,8},{8,4},{12,0},{1,13},{5,9},{9,5},{13,1},{2,14},{6,10},... | collective-permute-start | bytes 393224 | tf_op jit(solution)/shard_map/ppermute | solution.py:501
  457.5 7.4 %collective-permute-start.51 = (bf16[304,1024]{1,0:T(8,128)(2,1)S(1)}, bf16[304,1024]{1,0:T(8,128)(2,1)S(1)}, u32[]{:S(2)}, u32[]{:S(2)}) collective-permute-start(bf16[304,1024]{1,0:T(8,128)(2,1)S(1)} %fusion.9), channel_id=1, source_target_pairs={{0,0},{1,1},{2,16},{3,17},{16,2},{17,3},{18,18},{19,19},{4,4},{5,5... | collective-permute-start | bytes 1867784 | tf_op jit(solution)/shard_map/ppermute | solution.py:65
  458.3 19.2 %collective-permute-start.53 = (bf16[2,64,256]{2,1,0:T(8,128)(2,1)S(1)}, bf16[2,64,256]{2,1,0:T(8,128)(2,1)S(1)}, u32[]{:S(2)}, u32[]{:S(2)}) collective-permute-start(bf16[2,64,256]{2,1,0:T(8,128)(2,1)S(1)} %get-tuple-element.147), channel_id=1, source_target_pairs={{0,0},{1,1},{2,16},{3,17},{16,2},{17,3},{18,18},{19,19},{4,4},{5,5... | collective-permute-start | bytes 196616 | tf_op jit(solution)/shard_map/ppermute | solution.py:65
  459.0 20.1 %collective-permute-start.54 = (bf16[2,64,256]{2,1,0:T(8,128)(2,1)S(1)}, bf16[2,64,256]{2,1,0:T(8,128)(2,1)S(1)}, u32[]{:S(2)}, u32[]{:S(2)}) collective-permute-start(bf16[2,64,256]{2,1,0:T(8,128)(2,1)S(1)} %get-tuple-element.148), channel_id=1, source_target_pairs={{0,16},{1,17},{2,0},{3,1},{16,18},{17,19},{18,2},{19,3},{4,20},{5,... | collective-permute-start | bytes 196616 | tf_op jit(solution)/shard_map/ppermute | solution.py:65
  464.8 15.0 %collective-permute-start.52 = (bf16[304,1024]{1,0:T(8,128)(2,1)S(1)}, bf16[304,1024]{1,0:T(8,128)(2,1)S(1)}, u32[]{:S(2)}, u32[]{:S(2)}) collective-permute-start(bf16[304,1024]{1,0:T(8,128)(2,1)S(1)} %collective-permute-done.51), channel_id=1, source_target_pairs={{0,16},{16,0},{1,17},{17,1},{2,18},{18,2},{3,19},{19,3},{4,20},{20... | collective-permute-start | bytes 1867784 | tf_op jit(solution)/shard_map/ppermute | solution.py:68
  (48 other events, 358.5 us)
Sparse Core Ops, SparseCore 0:
  27.1 39.9 all-gather.4
  69.5 57.6 all-gather.6
  129.1 78.8 all-gather.8
  209.7 87.6 all-gather.10
